TPU v7x, 32 devices: a whole 2x2x4 slice. The times are simulated.
32 devices in a mesh: row: 8 (over z, y), col: 4 (over x, core).
Axes of the slice: x: 2, y: 2, z: 4, core: 2. Of those that a mesh axis runs over, the one named last changes fastest.
Arguments:
- embeddings: bfloat16 [65536, 1024], P('row', 'col'), may hold values from -0.1875 to 0.1875
- quality: float32 [65536], P('row'), may hold values from 0.5 to 2
- probes: float32 [32, 65536], P(None, 'row'), may hold values from -6 to 6
- neighbors: int32 [512, 8], P('row'), may hold values from 0 to 511, as said below
Outputs:
- first: float32 [32, 65536], P(None, 'row')
- second: float32 [32, 65536], P(None, 'row')
Inputs may be any that keep to these rules, and one draw needn't show every extreme that they name: `neighbors`: block b is held by row index b // 64. Among the 512 entries of one row index's blocks, at most 32 name blocks of any one other row index, and on every row index some other index is named exactly 32 times; the remaining entries name the index's own blocks.
All inputs are finite; a program needn't handle non-finite values.
Results may differ from a plain program's by a relative error of at most 0.02.
Values may be sent and summed in bfloat16 or wider, within the bound.
No kernel may reach another device: no remote copies, remote signals or barrier semaphores. Data moves between devices by JAX's collectives and lax.ppermute only.
A program may use at most 64 MiB of HBM per device.

v0:
```python
import jax
import jax.numpy as jnp
from jax import lax
from jax.sharding import PartitionSpec as P


def body(embeddings, quality, probes, neighbors):
    nrow = lax.axis_size("row")
    myself = lax.axis_index("row")
    blk_count, list_len = neighbors.shape
    docs, width = embeddings.shape
    block_len = docs // blk_count
    nprobe = probes.shape[0]
    slots = max(2, blk_count * list_len // (2 * nrow))
    blocked = embeddings.reshape(blk_count, block_len, width)
    flat = neighbors.reshape(-1)
    owner = flat // blk_count
    local = flat % blk_count
    remote = owner != myself
    onehot = (owner[:, None] == jnp.arange(nrow, dtype=jnp.int32)[None, :]).astype(jnp.int32)
    slot = jnp.sum((jnp.cumsum(onehot, axis=0) - onehot) * onehot, axis=1)
    request = jnp.zeros((nrow, slots), jnp.int32)
    request = request.at[jnp.where(remote, owner, nrow), slot].set(local, mode="drop")
    wanted = lax.all_to_all(request, "row", split_axis=0, concat_axis=0, tiled=True)
    source = jnp.where(remote, blk_count + owner * slots + slot, local)

    def apply(vec):
        scaled = (vec * quality[None, :]).astype(jnp.bfloat16).reshape(nprobe, blk_count, block_len)
        own = jnp.einsum(
            "bdc,pbd->bcp", blocked, scaled, preferred_element_type=jnp.float32
        ).astype(jnp.bfloat16)
        outgoing = own.reshape(blk_count, width * nprobe)[wanted]
        arrived = lax.all_to_all(outgoing, "row", split_axis=0, concat_axis=0, tiled=True)
        table = jnp.concatenate([own, arrived.reshape(nrow * slots, width, nprobe)], axis=0)
        gathered = table[source].reshape(blk_count, list_len, width, nprobe)
        summed = jnp.sum(gathered, axis=1, dtype=jnp.float32).astype(jnp.bfloat16)
        partial_value = jnp.einsum(
            "bdc,bcp->pbd", blocked, summed, preferred_element_type=jnp.float32
        ).reshape(nprobe, docs)
        total = lax.psum(partial_value.astype(jnp.bfloat16), "col").astype(jnp.float32)
        return total * quality[None, :] - vec

    first = apply(probes)
    second = 2.0 * apply(first) - probes
    return (first, second)


def solution(mesh):
    placed = (P("row", "col"), P("row"), P(None, "row"), P("row", None))
    return jax.shard_map(
        body,
        mesh=mesh,
        in_specs=placed,
        out_specs=(P(None, "row"), P(None, "row")),
        check_vma=False,
    )
```

profile of v0, /device:TPU:0, one launch (start us, length us, event | category | flops | bytes accessed | tf_op | source)
XLA Modules:
  0.0 528.2 jit_solution(13360046506584150237)
XLA Ops:
  10.5 76.2 %scatter_fusion = s32[8,32]{1,0:T(8,128)} fusion(s32[8,32]{1,0:T(8,128)} %broadcast.250, s32[512]{0:T(512)S(1)} %bitcast.65, s32[512]{0:T(512)S(1)} %get-tuple-element.6), kind=kCustom, calls=%fused_computation.4 | custom fusion | bytes 10240 | tf_op jit(solution)/shard_map/scatter | solution.py:23
  86.8 7.1 %all-to-all-start = ((s32[8,1,32]{2,1,0:T(1,128)}), s32[8,1,32]{2,1,0:T(1,128)S(1)}, u32[]{:S(2)}, u32[]{:S(2)}) async-start(s32[8,1,32]{2,1,0:T(1,128)} %bitcast.8), calls=%async_computation | async-start | bytes 8192 | tf_op jit(solution)/shard_map/all_to_all | solution.py:24
  93.9 2.9 fusion
  96.7 4.5 copy.24
  103.2 5.1 gather_fusion
  108.3 6.0 %all-to-all-start.1 = ((bf16[8,32,8192]{2,1,0:T(8,128)(2,1)}), bf16[8,32,8192]{2,1,0:T(8,128)(2,1)}, u32[]{:S(2)}, u32[]{:S(2)}) async-start(bf16[8,32,8192]{2,1,0:T(8,128)(2,1)} %bitcast.66), calls=%async_computation.1 | async-start | bytes 8388608 | tf_op jit(solution)/shard_map/all_to_all | solution.py:33
  114.6 92.5 %all-to-all-done.1 = bf16[8,32,8192]{2,1,0:T(8,128)(2,1)} async-done(((bf16[8,32,8192]{2,1,0:T(8,128)(2,1)}), bf16[8,32,8192]{2,1,0:T(8,128)(2,1)}, u32[]{:S(2)}, u32[]{:S(2)}) %all-to-all-start.1) | async-done | bytes 4194336 | tf_op jit(solution)/shard_map/all_to_all | solution.py:33
  207.0 17.3 %reshape.270 = bf16[256,256,32]{2,1,0:T(8,128)(2,1)} reshape(bf16[8,32,8192]{2,1,0:T(8,128)(2,1)} %all-to-all-done.1) | data formatting | bytes 8388608 | tf_op jit(solution)/shard_map/reshape | solution.py:34
  224.4 14.3 %copy.30 = bf16[256,256,32]{1,2,0:T(8,128)(2,1)} copy(bf16[256,256,32]{2,1,0:T(8,128)(2,1)} %reshape.270) | data formatting | bytes 8388608 | tf_op jit(solution)/shard_map/reshape | solution.py:34
  238.7 5.0 pad_maximum_fusion
  243.7 22.1 %gather_fusion.1 = bf16[512,256,32]{1,2,0:T(8,128)(2,1)} fusion(bf16[320,256,32]{1,2,0:T(8,128)(2,1)} %pad_maximum_fusion, s32[1024]{0:T(1024)S(1)} %pad_clamp_fusion), kind=kCustom, calls=%fused_computation.1 | custom fusion | bytes 16779264 | tf_op jit(solution)/shard_map/gather | solution.py:35
  265.8 5.7 %bitcast_reduce_fusion.1 = bf16[64,256,32]{1,2,0:T(8,128)(2,1)S(1)} fusion(bf16[512,256,32]{1,2,0:T(8,128)(2,1)} %gather_fusion.1), kind=kLoop, calls=%fused_computation.6 | loop fusion | flops 3670016 | bytes 9437184
  274.3 32.1 %all-reduce.3.cloned.1.call-done = bf16[32,8192]{1,0:T(8,128)(2,1)} async-done(((bf16[32,8192]{1,0:T(8,128)(2,1)}), bf16[32,8192]{1,0:T(8,128)(2,1)}) %all-reduce.3.cloned.1.call-update) | async-done | bytes 524304 | tf_op jit(solution)/shard_map/psum | solution.py:40
  306.4 2.2 fusion.5
  308.6 2.9 fusion.1
  311.4 4.5 copy.35
  317.8 5.1 gather_fusion.2
  322.9 98.1 %all_to_all.22 = bf16[8,32,8192]{2,1,0:T(8,128)(2,1)} all-to-all(bf16[8,32,8192]{2,1,0:T(8,128)(2,1)} %bitcast.67), channel_id=1, replica_groups=mesh['row'=8,'col'=4] {'row'}, dimensions={0} | all-to-all | bytes 8388608 | tf_op jit(solution)/shard_map/all_to_all | solution.py:33
  421.0 17.3 %reshape.274 = bf16[256,256,32]{2,1,0:T(8,128)(2,1)} reshape(bf16[8,32,8192]{2,1,0:T(8,128)(2,1)} %all_to_all.22) | data formatting | bytes 8388608 | tf_op jit(solution)/shard_map/reshape | solution.py:34
  438.4 14.3 %copy.37 = bf16[256,256,32]{1,2,0:T(8,128)(2,1)} copy(bf16[256,256,32]{2,1,0:T(8,128)(2,1)} %reshape.274) | data formatting | bytes 8388608 | tf_op jit(solution)/shard_map/reshape | solution.py:34
  452.7 5.0 pad_maximum_fusion.1
  457.7 22.1 %gather_fusion.3 = bf16[512,256,32]{1,2,0:T(8,128)(2,1)} fusion(bf16[320,256,32]{1,2,0:T(8,128)(2,1)} %pad_maximum_fusion.1, s32[1024]{0:T(1024)S(1)} %pad_clamp_fusion), kind=kCustom, calls=%fused_computation.3 | custom fusion | bytes 16779264 | tf_op jit(solution)/shard_map/gather | solution.py:35
  479.8 5.7 %bitcast_reduce_fusion = bf16[64,256,32]{1,2,0:T(8,128)(2,1)S(1)} fusion(bf16[512,256,32]{1,2,0:T(8,128)(2,1)} %gather_fusion.3), kind=kLoop, calls=%fused_computation.5 | loop fusion | flops 3670016 | bytes 9437184
  488.0 31.2 %all-reduce.5.cloned.1.call-done = bf16[32,8192]{1,0:T(8,128)(2,1)} async-done(((bf16[32,8192]{1,0:T(8,128)(2,1)}), bf16[32,8192]{1,0:T(8,128)(2,1)}) %all-reduce.5.cloned.1.call-update) | async-done | bytes 524304 | tf_op jit(solution)/shard_map/psum | solution.py:40
  (41 shorter events, 14.8 us)
Async XLA Ops:
  7.2 86.7 %copy-start.2 = (f32[32,8192]{1,0:T(8,128)S(1)}, f32[32,8192]{1,0:T(8,128)}, u32[]{:S(2)}) copy-start(f32[32,8192]{1,0:T(8,128)} %param.6) | copy-start | bytes 3145732
  7.2 86.7 %copy-start.4 = (f32[8192]{0:T(1024)S(1)}, f32[8192]{0:T(1024)}, u32[]{:S(2)}) copy-start(f32[8192]{0:T(1024)} %param.5) | copy-start | bytes 98308
  86.8 16.4 %all-to-all-start = ((s32[8,1,32]{2,1,0:T(1,128)}), s32[8,1,32]{2,1,0:T(1,128)S(1)}, u32[]{:S(2)}, u32[]{:S(2)}) async-start(s32[8,1,32]{2,1,0:T(1,128)} %bitcast.8), calls=%async_computation | async-start | bytes 8192 | tf_op jit(solution)/shard_map/all_to_all | solution.py:24
  108.3 98.7 %all-to-all-start.1 = ((bf16[8,32,8192]{2,1,0:T(8,128)(2,1)}), bf16[8,32,8192]{2,1,0:T(8,128)(2,1)}, u32[]{:S(2)}, u32[]{:S(2)}) async-start(bf16[8,32,8192]{2,1,0:T(8,128)(2,1)} %bitcast.66), calls=%async_computation.1 | async-start | bytes 8388608 | tf_op jit(solution)/shard_map/all_to_all | solution.py:33
  114.3 192.0 %all-reduce.3.cloned.1.call-start = ((), (), s32[]{:S(2)}) async-start(), calls=%async_computation.3 | async-start | bytes 1048576 | tf_op jit(solution)/shard_map/psum | solution.py:40
  265.8 5.7 %copy-start = (bf16[8192,256]{1,0:T(8,128)(2,1)S(1)}, bf16[8192,256]{1,0:T(8,128)(2,1)}, u32[]{:S(2)}) copy-start(bf16[8192,256]{1,0:T(8,128)(2,1)} %param.4) | copy-start | bytes 12582916
  274.0 245.2 %all-reduce.5.cloned.1.call-start = ((), (), s32[]{:S(2)}) async-start(), calls=%async_computation.4 | async-start | bytes 1048576 | tf_op jit(solution)/shard_map/psum | solution.py:40
  479.8 5.7 %copy-start.1 = (bf16[8192,256]{1,0:T(8,128)(2,1)S(1)}, bf16[8192,256]{1,0:T(8,128)(2,1)}, u32[]{:S(2)}) copy-start(bf16[8192,256]{1,0:T(8,128)(2,1)} %param.4) | copy-start | bytes 12582916
  485.5 33.6 %copy-start.3 = (f32[32,8192]{1,0:T(8,128)S(1)}, f32[32,8192]{1,0:T(8,128)}, u32[]{:S(2)}) copy-start(f32[32,8192]{1,0:T(8,128)} %get-tuple-element.3) | copy-start | bytes 3145732
Sparse Core Ops, SparseCore 0:
  274.1 32.2 all-reduce.2
  488.1 31.0 all-reduce.4
where the time goes:
time: 532 us; the launch traced here: 528 us
  local copies, waits for them, and re-layouts  211 us (40%)
  waiting for transfers between devices  156 us (29%)
  blocking collectives  98.1 us (18%)
  other arithmetic  27.1 us (5%)
  between operations  14.3 us (3%)
  starting transfers between devices  13.6 us (3%)
  matrix products  8.78 us (2%)
    all_to_all x1, blocking collectives, apply(): lax.all_to_all(outgoing, 'row', split_axis=0, concat_axis=0, tiled=True)  98.1 us
    all_to_all x1, waiting for transfers between devices, apply(): lax.all_to_all(outgoing, 'row', split_axis=0, concat_axis=0, tiled=True)  92.5 us
    scatter x1, local copies, waits for them, and re-layouts, body(): request.at[jnp.where(remote, owner, nrow), slot].set(local, mode='drop')  76.2 us
    psum x2, waiting for transfers between devices, apply(): lax.psum(partial_value.astype(jnp.bfloat16), 'col').astype(jnp.float32)  63.3 us
    reshape x4, local copies, waits for them, and re-layouts, apply(): arrived.reshape(nrow * slots, width, nprobe)  63.2 us
    gather x2, local copies, waits for them, and re-layouts, apply(): gathered = table[source].reshape(blk_count, list_len, width, nprobe)  44.3 us
    unnamed x3, other arithmetic  13.5 us
  transfers between devices with their start and end apart: 4, of which 3 were waited for; matrix products, arithmetic and copies ran while one was open for 2% of the time, Pallas kernels for 0%

commit v1 on v0

v1 whole, which is shorter than its diff:
```python
import functools

import jax
import jax.numpy as jnp
from jax import lax
from jax.experimental import pallas as pl
from jax.experimental.pallas import tpu as pltpu
from jax.sharding import PartitionSpec as P

CHUNKS = 2
TILE_BLOCKS = 8
VMEM_LIMIT = 32 * 1024 * 1024


def params(**kw):
    return pltpu.CompilerParams(vmem_limit_bytes=VMEM_LIMIT, **kw)


def cost(flops, nbytes):
    return pl.CostEstimate(flops=int(flops), bytes_accessed=int(nbytes), transcendentals=0)


def swap(value, axis, size, mask):
    return lax.ppermute(value, axis, [(i, i ^ mask) for i in range(size)])


def project(block_len, scaled, emb_ref, sums_ref):
    for b in range(sums_ref.shape[0]):
        docs = slice(b * block_len, (b + 1) * block_len)
        sums_ref[b] = jnp.dot(
            scaled[:, docs], emb_ref[docs, :], preferred_element_type=jnp.float32
        ).astype(jnp.bfloat16)


def first_sums_kernel(block_len, vec_ref, quality_ref, emb_ref, sums_ref):
    scaled = (vec_ref[...] * quality_ref[...]).astype(jnp.bfloat16)
    project(block_len, scaled, emb_ref, sums_ref)


def next_sums_kernel(block_len, mine_ref, other_ref, vec_ref, quality_ref, emb_ref, out_ref, sums_ref):
    total = mine_ref[...].astype(jnp.float32) + other_ref[...].astype(jnp.float32)
    quality = quality_ref[...]
    out = total * quality - vec_ref[...]
    out_ref[...] = out
    project(block_len, (out * quality).astype(jnp.bfloat16), emb_ref, sums_ref)


def combine_kernel(ids_ref, *refs):
    *shards, out_ref, table, sems = refs
    blocks = shards[0].shape[0]
    copies = [
        pltpu.make_async_copy(ref, table.at[pl.ds(i * blocks, blocks)], sems.at[i])
        for i, ref in enumerate(shards)
    ]
    for copy in copies:
        copy.start()
    table[len(shards) * blocks] = jnp.zeros(table.shape[1:], table.dtype)
    for copy in copies:
        copy.wait()
    entries = ids_ref.shape[0] // out_ref.shape[0]

    def step(b, carry):
        total = table[ids_ref[b * entries]].astype(jnp.float32)
        for k in range(1, entries):
            total = total + table[ids_ref[b * entries + k]].astype(jnp.float32)
        out_ref[b] = total.astype(out_ref.dtype)
        return carry

    lax.fori_loop(0, out_ref.shape[0], step, 0, unroll=4)


def expand_kernel(block_len, own_ref, arrived_ref, emb_ref, out_ref):
    for b in range(own_ref.shape[0]):
        docs = slice(b * block_len, (b + 1) * block_len)
        gathered = (own_ref[b] + arrived_ref[b].astype(jnp.float32)).astype(jnp.bfloat16)
        out_ref[:, docs] = lax.dot_general(
            gathered, emb_ref[docs, :], (((1,), (1,)), ((), ())),
            preferred_element_type=jnp.float32,
        ).astype(jnp.bfloat16)


def body(embeddings, quality, probes, neighbors):
    nrow, ncol = lax.axis_size("row"), lax.axis_size("col")
    me = lax.axis_index("row")
    blk_count, list_len = neighbors.shape
    docs, width = embeddings.shape
    block_len = docs // blk_count
    nprobe = probes.shape[0]
    part = nprobe // CHUNKS
    bits = nrow.bit_length() - 1
    gather_bits = [m for m in (2, 1) if m < nrow]
    near = sum(gather_bits)
    reduce_bits = [1 << i for i in reversed(range(bits)) if not (1 << i) & near]
    far = sum(reduce_bits)

    def table_ids(lists):
        flat = lists.reshape(-1)
        apart = (flat // blk_count) ^ me
        inside = (apart & far) == 0
        place = jnp.where(inside, apart & near, 0) * blk_count + flat % blk_count
        return jnp.where(inside, place, (near + 1) * blk_count)

    dests = [0]
    for m in reduce_bits:
        dests = dests + [d | m for d in dests]
    ids = {d: table_ids(neighbors if d == 0 else swap(neighbors, "row", nrow, d)) for d in dests}

    qrow = quality[None, :]
    tile_docs = TILE_BLOCKS * block_len
    steps = blk_count // TILE_BLOCKS
    shard_shape = (blk_count, part, width)
    shard_size = blk_count * part * width
    mac = 2 * part * docs * width
    emb_spec = pl.BlockSpec((tile_docs, width), lambda j: (j, 0))
    vec_spec = pl.BlockSpec((part, tile_docs), lambda j: (0, j))
    q_spec = pl.BlockSpec((1, tile_docs), lambda j: (0, j))
    shard_spec = pl.BlockSpec((TILE_BLOCKS, part, width), lambda j: (j, 0, 0))

    def chunk_spec(c):
        return pl.BlockSpec((part, tile_docs), lambda j: (c, j))

    def first_sums(c):
        return pl.pallas_call(
            functools.partial(first_sums_kernel, block_len),
            grid=(steps,),
            in_specs=[chunk_spec(c), q_spec, emb_spec],
            out_specs=shard_spec,
            out_shape=jax.ShapeDtypeStruct(shard_shape, jnp.bfloat16),
            compiler_params=params(),
            cost_estimate=cost(mac, 2 * docs * width + 4 * part * docs + 2 * shard_size),
        )(probes, qrow, embeddings)

    def next_sums(c, mine, other):
        return pl.pallas_call(
            functools.partial(next_sums_kernel, block_len),
            grid=(steps,),
            in_specs=[vec_spec, vec_spec, chunk_spec(c), q_spec, emb_spec],
            out_specs=[vec_spec, shard_spec],
            out_shape=[
                jax.ShapeDtypeStruct((part, docs), jnp.float32),
                jax.ShapeDtypeStruct(shard_shape, jnp.bfloat16),
            ],
            compiler_params=params(),
            cost_estimate=cost(mac, 2 * docs * width + 12 * part * docs + 2 * shard_size),
        )(mine, other, probes, qrow, embeddings)

    def combine(dest, shards, dtype):
        count = len(shards)
        return pl.pallas_call(
            combine_kernel,
            in_specs=[pl.BlockSpec(memory_space=pltpu.SMEM)] + [pl.BlockSpec(memory_space=pl.ANY)] * count,
            out_specs=pl.BlockSpec(memory_space=pltpu.VMEM),
            out_shape=jax.ShapeDtypeStruct(shard_shape, dtype),
            scratch_shapes=[
                pltpu.VMEM((count * blk_count + 1, part, width), jnp.bfloat16),
                pltpu.SemaphoreType.DMA((count,)),
            ],
            compiler_params=params(),
            cost_estimate=cost(list_len * shard_size, 2 * count * shard_size + 4 * shard_size),
        )(ids[dest], *shards)

    def expand(own, arrived):
        return pl.pallas_call(
            functools.partial(expand_kernel, block_len),
            grid=(steps,),
            in_specs=[shard_spec, shard_spec, emb_spec],
            out_specs=vec_spec,
            out_shape=jax.ShapeDtypeStruct((part, docs), jnp.bfloat16),
            compiler_params=params(),
            cost_estimate=cost(mac, 2 * docs * width + 2 * part * docs + 6 * shard_size),
        )(own, arrived, embeddings)

    def exchange(sums):
        shards = {0: sums}
        for m in gather_bits:
            shards.update({k | m: swap(v, "row", nrow, m) for k, v in list(shards.items())})
        shards = [shards[k] for k in sorted(shards)]
        outgoing = {d: combine(d, shards, jnp.bfloat16) for d in dests if d}
        own = combine(0, shards, jnp.float32)
        arrived = None
        for m in reduce_bits:
            taken = {d ^ m: swap(outgoing.pop(d), "row", nrow, m) for d in list(outgoing) if d & m}
            for d, value in taken.items():
                if d in outgoing:
                    outgoing[d] = (
                        outgoing[d].astype(jnp.float32) + value.astype(jnp.float32)
                    ).astype(jnp.bfloat16)
                else:
                    arrived = value if arrived is None else (
                        arrived.astype(jnp.float32) + value.astype(jnp.float32)
                    ).astype(jnp.bfloat16)
        return own, arrived

    def col_sum(value):
        masks = [1 << i for i in range(ncol.bit_length() - 1)]
        for m in masks[:-1]:
            other = swap(value, "col", ncol, m)
            value = (value.astype(jnp.float32) + other.astype(jnp.float32)).astype(jnp.bfloat16)
        return value, swap(value, "col", ncol, masks[-1])

    sums = [first_sums(c) for c in range(CHUNKS)]
    halves = [col_sum(expand(*exchange(s))) for s in sums]
    firsts, sums = zip(*[next_sums(c, *h) for c, h in enumerate(halves)])
    halves = [col_sum(expand(*exchange(s))) for s in sums]
    seconds = []
    for c, (mine, other) in enumerate(halves):
        total = mine.astype(jnp.float32) + other.astype(jnp.float32)
        seconds.append(2.0 * (total * qrow - firsts[c]) - probes[c * part:(c + 1) * part])
    return jnp.concatenate(firsts, axis=0), jnp.concatenate(seconds, axis=0)


def solution(mesh):
    placed = (P("row", "col"), P("row"), P(None, "row"), P("row", None))
    return jax.shard_map(
        body,
        mesh=mesh,
        in_specs=placed,
        out_specs=(P(None, "row"), P(None, "row")),
        check_vma=False,
    )
```

time: 532 us -> 203 us (0.38)
  local copies, waits for them, and re-layouts: 211 us -> 6.73 us
  blocking collectives: 98.1 us -> 0 us
  Pallas kernels: 0 us -> 37.2 us
  waiting for transfers between devices: 156 us -> 120 us
  other arithmetic: 27.1 us -> 2.65 us
  starting transfers between devices: 13.6 us -> 34.7 us
  between operations: 14.3 us -> 0.9 us
  matrix products: 8.78 us -> 0 us
    ppermute x0 -> x25, waiting for transfers between devices: none -> 120 us  [swap(): return lax.ppermute(value, axis, [(i, i ^ mask) for i in range(size)])]
    all_to_all x1 -> x0, blocking collectives: 98.1 us -> none  [apply(): lax.all_to_all(outgoing, 'row', split_axis=0, concat_axis=0, tiled=True)]
    all_to_all x2 -> x0, waiting for transfers between devices: 92.5 us -> none  [the longest x1 92.5 us: apply(): lax.all_to_all(outgoing, 'row', split_axis=0, concat_axis=0, tiled=True)]
    scatter x1 -> x0, local copies, waits for them, and re-layouts: 76.2 us -> none  [body(): request.at[jnp.where(remote, owner, nrow), slot].set(local, mode='drop')]
    reshape x9 -> x2, local copies, waits for them, and re-layouts: 67.3 us -> 0.18 us  [table_ids(): flat = lists.reshape(-1)]
    psum x2 -> x0, waiting for transfers between devices: 63.3 us -> none  [apply(): lax.psum(partial_value.astype(jnp.bfloat16), 'col').astype(jnp.float32)]
    gather x4 -> x0, local copies, waits for them, and re-layouts: 54.5 us -> none  [the longest x2 44.3 us: apply(): gathered = table[source].reshape(blk_count, list_len, width, nprobe)]
    pallas_call x0 -> x16, Pallas kernels: none -> 37.2 us  [the longest x8 17.2 us: combine(): pl.pallas_call(combine_kernel, in_specs=[pl.BlockSpec(memory_space=pltpu....]
  transfers between devices with their start and end apart: 4 -> 25, of which waited for: 3 -> 17; matrix products, arithmetic and copies ran while one was open for 2% -> 1% of each run, Pallas kernels for 0% -> 18%
where the time goes in v1:
time: 203 us; the launch traced here: 202 us
  waiting for transfers between devices  120 us (59%)
  Pallas kernels  37.2 us (18%)
  starting transfers between devices  34.7 us (17%)
  local copies, waits for them, and re-layouts  6.73 us (3%)
  other arithmetic  2.65 us (1%)
    ppermute x25, waiting for transfers between devices, swap(): return lax.ppermute(value, axis, [(i, i ^ mask) for i in range(size)])  120 us
    ppermute x25, starting transfers between devices, swap(): return lax.ppermute(value, axis, [(i, i ^ mask) for i in range(size)])  34.7 us
    pallas_call x8, Pallas kernels, combine(): pl.pallas_call(combine_kernel, in_specs=[pl.BlockSpec(memory_space=pltpu....  17.2 us
    pallas_call x4, Pallas kernels, expand(): pl.pallas_call(functools.partial(expand_kernel, block_len), grid=(steps,)...  13.8 us
    unnamed x17, local copies, waits for them, and re-layouts  6.46 us
  transfers between devices with their start and end apart: 25, of which 17 were waited for; matrix products, arithmetic and copies ran while one was open for 1% of the time, Pallas kernels for 18%

profile of v1, /device:TPU:0, one launch (start us, length us, event | category | flops | bytes accessed | tf_op | source)
XLA Modules:
  0.0 202.0 jit_solution(15026509013794741262)
XLA Ops:
  6.4 3.1 %collective-permute-start.1 = (bf16[64,16,256]{2,1,0:T(8,128)(2,1)S(1)}, bf16[64,16,256]{2,1,0:T(8,128)(2,1)S(1)}, u32[]{:S(2)}, u32[]{:S(2)}) collective-permute-start(bf16[64,16,256]{2,1,0:T(8,128)(2,1)S(1)} %shard_map.59.refs_0_), channel_id=1, source_target_pairs={{0,8},{4,12},{8,0},{12,4},{16,24},{20,28},{24,16},{28,20},{1,9},{5... | collective-permute-start | bytes 1572872 | tf_op jit(solution)/shard_map/ppermute | solution.py:24
  13.0 9.2 %collective-permute-done.1.refs_2_ = bf16[64,16,256]{2,1,0:T(8,128)(2,1)S(1)} collective-permute-done((bf16[64,16,256]{2,1,0:T(8,128)(2,1)S(1)}, bf16[64,16,256]{2,1,0:T(8,128)(2,1)S(1)}, u32[]{:S(2)}, u32[]{:S(2)}) %collective-permute-start.1) | collective-permute-done | bytes 524320 | tf_op jit(solution)/shard_map/ppermute | solution.py:24
  24.2 8.4 %collective-permute-done.8.refs_2_ = bf16[64,16,256]{2,1,0:T(8,128)(2,1)S(1)} collective-permute-done((bf16[64,16,256]{2,1,0:T(8,128)(2,1)S(1)}, bf16[64,16,256]{2,1,0:T(8,128)(2,1)S(1)}, u32[]{:S(2)}, u32[]{:S(2)}) %collective-permute-start.8) | collective-permute-done | bytes 524320 | tf_op jit(solution)/shard_map/ppermute | solution.py:24
  39.0 3.2 %shard_map.61 = bf16[64,16,256]{2,1,0:T(8,128)(2,1)} custom-call(s32[512]{0:T(512)S(1)} %fusion.5.ids_ref, bf16[64,16,256]{2,1,0:T(8,128)(2,1)S(1)} %shard_map.59.refs_0_, bf16[64,16,256]{2,1,0:T(8,128)(2,1)S(1)} %collective-permute-done.refs_1_, bf16[64,16,256]{2,1,0:T(8,128)(2,1)S(1)} %collective-permute-done.1.refs_2_, ...), custom_call_target="tpu_custom_call" | custom-call | flops 2097152 | bytes 3145728 | tf_op jit(solution)/shard_map/pallas_call | solution.py:149
  42.3 2.7 %collective-permute-start.4 = (bf16[64,16,256]{2,1,0:T(8,128)(2,1)}, bf16[64,16,256]{2,1,0:T(8,128)(2,1)}, u32[]{:S(2)}, u32[]{:S(2)}) collective-permute-start(bf16[64,16,256]{2,1,0:T(8,128)(2,1)} %shard_map.61), channel_id=1, source_target_pairs={{0,16},{4,20},{8,24},{12,28},{16,0},{20,4},{24,8},{28,12},{1,17},{... | collective-permute-start | bytes 1572872 | tf_op jit(solution)/shard_map/ppermute | solution.py:24
  44.9 3.4 %collective-permute-done.7.refs_1_ = bf16[64,16,256]{2,1,0:T(8,128)(2,1)S(1)} collective-permute-done((bf16[64,16,256]{2,1,0:T(8,128)(2,1)S(1)}, bf16[64,16,256]{2,1,0:T(8,128)(2,1)S(1)}, u32[]{:S(2)}, u32[]{:S(2)}) %collective-permute-start.7) | collective-permute-done | bytes 524320 | tf_op jit(solution)/shard_map/ppermute | solution.py:24
  48.3 10.0 %collective-permute-done.9.refs_3_ = bf16[64,16,256]{2,1,0:T(8,128)(2,1)} collective-permute-done((bf16[64,16,256]{2,1,0:T(8,128)(2,1)S(1)}, bf16[64,16,256]{2,1,0:T(8,128)(2,1)}, u32[]{:S(2)}, u32[]{:S(2)}) %collective-permute-start.9) | collective-permute-done | bytes 524320 | tf_op jit(solution)/shard_map/ppermute | solution.py:24
  58.3 3.2 %shard_map.66 = bf16[64,16,256]{2,1,0:T(8,128)(2,1)} custom-call(s32[512]{0:T(512)S(1)} %fusion.5.ids_ref, bf16[64,16,256]{2,1,0:T(8,128)(2,1)S(1)} %shard_map.64.refs_0_, bf16[64,16,256]{2,1,0:T(8,128)(2,1)S(1)} %collective-permute-done.7.refs_1_, bf16[64,16,256]{2,1,0:T(8,128)(2,1)S(1)} %collective-permute-done.8.refs_2_, ...), custom_call_target="tpu_custom_call" | custom-call | flops 2097152 | bytes 3145728 | tf_op jit(solution)/shard_map/pallas_call | solution.py:149
  61.6 2.7 %collective-permute-start.10 = (bf16[64,16,256]{2,1,0:T(8,128)(2,1)}, bf16[64,16,256]{2,1,0:T(8,128)(2,1)}, u32[]{:S(2)}, u32[]{:S(2)}) collective-permute-start(bf16[64,16,256]{2,1,0:T(8,128)(2,1)} %shard_map.66), channel_id=1, source_target_pairs={{0,16},{4,20},{8,24},{12,28},{16,0},{20,4},{24,8},{28,12},{1,17},{... | collective-permute-start | bytes 1572872 | tf_op jit(solution)/shard_map/ppermute | solution.py:24
  67.0 11.7 %collective-permute-done.4.arrived_ref = bf16[64,16,256]{2,1,0:T(8,128)(2,1)} collective-permute-done((bf16[64,16,256]{2,1,0:T(8,128)(2,1)}, bf16[64,16,256]{2,1,0:T(8,128)(2,1)}, u32[]{:S(2)}, u32[]{:S(2)}) %collective-permute-start.4) | collective-permute-done | bytes 524320 | tf_op jit(solution)/shard_map/ppermute | solution.py:24
  80.9 4.9 %shard_map.62 = bf16[16,8192]{1,0:T(8,128)(2,1)S(1)} custom-call(f32[64,16,256]{2,1,0:T(8,128)S(1)} %shard_map.60.own_ref, bf16[64,16,256]{2,1,0:T(8,128)(2,1)} %collective-permute-done.4.arrived_ref, bf16[8192,256]{1,0:T(8,128)(2,1)S(1)} %copy-done.1), custom_call_target="tpu_custom_call" | custom-call | flops 67108864 | bytes 6029312 | tf_op jit(solution)/shard_map/pallas_call | solution.py:163
  88.7 4.7 %shard_map.67 = bf16[16,8192]{1,0:T(8,128)(2,1)S(1)} custom-call(f32[64,16,256]{2,1,0:T(8,128)S(1)} %shard_map.65.own_ref, bf16[64,16,256]{2,1,0:T(8,128)(2,1)} %collective-permute-done.10.arrived_ref, bf16[8192,256]{1,0:T(8,128)(2,1)S(1)} %copy-done.2), custom_call_target="tpu_custom_call" | custom-call | flops 67108864 | bytes 6029312 | tf_op jit(solution)/shard_map/pallas_call | solution.py:163
  96.6 6.3 %collective-permute-done.6.other_ref = bf16[16,8192]{1,0:T(8,128)(2,1)S(1)} collective-permute-done((bf16[16,8192]{1,0:T(8,128)(2,1)S(1)}, bf16[16,8192]{1,0:T(8,128)(2,1)S(1)}, u32[]{:S(2)}, u32[]{:S(2)}) %collective-permute-start.6) | collective-permute-done | bytes 262176 | tf_op jit(solution)/shard_map/ppermute | solution.py:24
  105.1 2.8 %collective-permute-done.12.other_ref = bf16[16,8192]{1,0:T(8,128)(2,1)S(1)} collective-permute-done((bf16[16,8192]{1,0:T(8,128)(2,1)S(1)}, bf16[16,8192]{1,0:T(8,128)(2,1)S(1)}, u32[]{:S(2)}, u32[]{:S(2)}) %collective-permute-start.12) | collective-permute-done | bytes 262176 | tf_op jit(solution)/shard_map/ppermute | solution.py:24
  110.8 8.6 %collective-permute-done.14.refs_2_ = bf16[64,16,256]{2,1,0:T(8,128)(2,1)S(1)} collective-permute-done((bf16[64,16,256]{2,1,0:T(8,128)(2,1)S(1)}, bf16[64,16,256]{2,1,0:T(8,128)(2,1)S(1)}, u32[]{:S(2)}, u32[]{:S(2)}) %collective-permute-start.14) | collective-permute-done | bytes 524320 | tf_op jit(solution)/shard_map/ppermute | solution.py:24
  121.5 7.2 %collective-permute-done.20.refs_2_ = bf16[64,16,256]{2,1,0:T(8,128)(2,1)S(1)} collective-permute-done((bf16[64,16,256]{2,1,0:T(8,128)(2,1)S(1)}, bf16[64,16,256]{2,1,0:T(8,128)(2,1)S(1)}, u32[]{:S(2)}, u32[]{:S(2)}) %collective-permute-start.20) | collective-permute-done | bytes 524320 | tf_op jit(solution)/shard_map/ppermute | solution.py:24
  129.5 6.9 %collective-permute-done.15.refs_3_ = bf16[64,16,256]{2,1,0:T(8,128)(2,1)S(1)} collective-permute-done((bf16[64,16,256]{2,1,0:T(8,128)(2,1)S(1)}, bf16[64,16,256]{2,1,0:T(8,128)(2,1)S(1)}, u32[]{:S(2)}, u32[]{:S(2)}) %collective-permute-start.15) | collective-permute-done | bytes 524320 | tf_op jit(solution)/shard_map/ppermute | solution.py:24
  137.9 3.4 %collective-permute-start.16 = (bf16[64,16,256]{2,1,0:T(8,128)(2,1)S(1)}, bf16[64,16,256]{2,1,0:T(8,128)(2,1)S(1)}, u32[]{:S(2)}, u32[]{:S(2)}) collective-permute-start(bf16[64,16,256]{2,1,0:T(8,128)(2,1)S(1)} %shard_map.70), channel_id=1, source_target_pairs={{0,16},{4,20},{8,24},{12,28},{16,0},{20,4},{24,8},{28,12},{1,17},{... | collective-permute-start | bytes 1572872 | tf_op jit(solution)/shard_map/ppermute | solution.py:24
  141.3 6.3 %collective-permute-done.19.refs_1_ = bf16[64,16,256]{2,1,0:T(8,128)(2,1)S(1)} collective-permute-done((bf16[64,16,256]{2,1,0:T(8,128)(2,1)S(1)}, bf16[64,16,256]{2,1,0:T(8,128)(2,1)S(1)}, u32[]{:S(2)}, u32[]{:S(2)}) %collective-permute-start.19) | collective-permute-done | bytes 524320 | tf_op jit(solution)/shard_map/ppermute | solution.py:24
  147.7 9.6 %collective-permute-done.21.refs_3_ = bf16[64,16,256]{2,1,0:T(8,128)(2,1)S(1)} collective-permute-done((bf16[64,16,256]{2,1,0:T(8,128)(2,1)S(1)}, bf16[64,16,256]{2,1,0:T(8,128)(2,1)S(1)}, u32[]{:S(2)}, u32[]{:S(2)}) %collective-permute-start.21) | collective-permute-done | bytes 524320 | tf_op jit(solution)/shard_map/ppermute | solution.py:24
  158.7 3.4 %collective-permute-start.22 = (bf16[64,16,256]{2,1,0:T(8,128)(2,1)S(1)}, bf16[64,16,256]{2,1,0:T(8,128)(2,1)S(1)}, u32[]{:S(2)}, u32[]{:S(2)}) collective-permute-start(bf16[64,16,256]{2,1,0:T(8,128)(2,1)S(1)} %shard_map.73), channel_id=1, source_target_pairs={{0,16},{4,20},{8,24},{12,28},{16,0},{20,4},{24,8},{28,12},{1,17},{... | collective-permute-start | bytes 1572872 | tf_op jit(solution)/shard_map/ppermute | solution.py:24
  167.3 16.7 %collective-permute-done.22.arrived_ref = bf16[64,16,256]{2,1,0:T(8,128)(2,1)S(1)} collective-permute-done((bf16[64,16,256]{2,1,0:T(8,128)(2,1)S(1)}, bf16[64,16,256]{2,1,0:T(8,128)(2,1)S(1)}, u32[]{:S(2)}, u32[]{:S(2)}) %collective-permute-start.22) | collective-permute-done | bytes 524320 | tf_op jit(solution)/shard_map/ppermute | solution.py:24
  190.4 5.1 %collective-permute-done.18 = bf16[16,8192]{1,0:T(8,128)(2,1)S(1)} collective-permute-done((bf16[16,8192]{1,0:T(8,128)(2,1)S(1)}, bf16[16,8192]{1,0:T(8,128)(2,1)S(1)}, u32[]{:S(2)}, u32[]{:S(2)}) %collective-permute-start.18) | collective-permute-done | bytes 262176 | tf_op jit(solution)/shard_map/ppermute | solution.py:24
  195.4 5.2 %collective-permute-done.24 = bf16[16,8192]{1,0:T(8,128)(2,1)S(1)} collective-permute-done((bf16[16,8192]{1,0:T(8,128)(2,1)S(1)}, bf16[16,8192]{1,0:T(8,128)(2,1)S(1)}, u32[]{:S(2)}, u32[]{:S(2)}) %collective-permute-start.24) | collective-permute-done | bytes 262176 | tf_op jit(solution)/shard_map/ppermute | solution.py:24
  (71 shorter events, 52.2 us)
Async XLA Ops:
  6.4 15.8 %collective-permute-start.1 = (bf16[64,16,256]{2,1,0:T(8,128)(2,1)S(1)}, bf16[64,16,256]{2,1,0:T(8,128)(2,1)S(1)}, u32[]{:S(2)}, u32[]{:S(2)}) collective-permute-start(bf16[64,16,256]{2,1,0:T(8,128)(2,1)S(1)} %shard_map.59.refs_0_), channel_id=1, source_target_pairs={{0,8},{4,12},{8,0},{12,4},{16,24},{20,28},{24,16},{28,20},{1,9},{5... | collective-permute-start | bytes 1572872 | tf_op jit(solution)/shard_map/ppermute | solution.py:24
  11.0 21.6 %collective-permute-start.8 = (bf16[64,16,256]{2,1,0:T(8,128)(2,1)S(1)}, bf16[64,16,256]{2,1,0:T(8,128)(2,1)S(1)}, u32[]{:S(2)}, u32[]{:S(2)}) collective-permute-start(bf16[64,16,256]{2,1,0:T(8,128)(2,1)S(1)} %shard_map.64.refs_0_), channel_id=1, source_target_pairs={{0,8},{4,12},{8,0},{12,4},{16,24},{20,28},{24,16},{28,20},{1,9},{5... | collective-permute-start | bytes 1572872 | tf_op jit(solution)/shard_map/ppermute | solution.py:24
  11.1 27.9 %collective-permute-start = (bf16[64,16,256]{2,1,0:T(8,128)(2,1)S(1)}, bf16[64,16,256]{2,1,0:T(8,128)(2,1)S(1)}, u32[]{:S(2)}, u32[]{:S(2)}) collective-permute-start(bf16[64,16,256]{2,1,0:T(8,128)(2,1)S(1)} %shard_map.59.refs_0_), channel_id=1, source_target_pairs={{0,4},{4,0},{8,12},{12,8},{16,20},{20,16},{24,28},{28,24},{1,5},{5... | collective-permute-start | bytes 1572872 | tf_op jit(solution)/shard_map/ppermute | solution.py:24
  22.2 16.8 %collective-permute-start.2 = (bf16[64,16,256]{2,1,0:T(8,128)(2,1)S(1)}, bf16[64,16,256]{2,1,0:T(8,128)(2,1)}, u32[]{:S(2)}, u32[]{:S(2)}) collective-permute-start(bf16[64,16,256]{2,1,0:T(8,128)(2,1)S(1)} %collective-permute-done.1.refs_2_), channel_id=1, source_target_pairs={{0,4},{4,0},{8,12},{12,8},{16,20},{20,16},{24,28},{28,24},{1,5},{5... | collective-permute-start | bytes 1572872 | tf_op jit(solution)/shard_map/ppermute | solution.py:24
  24.2 24.1 %collective-permute-start.7 = (bf16[64,16,256]{2,1,0:T(8,128)(2,1)S(1)}, bf16[64,16,256]{2,1,0:T(8,128)(2,1)S(1)}, u32[]{:S(2)}, u32[]{:S(2)}) collective-permute-start(bf16[64,16,256]{2,1,0:T(8,128)(2,1)S(1)} %shard_map.64.refs_0_), channel_id=1, source_target_pairs={{0,4},{4,0},{8,12},{12,8},{16,20},{20,16},{24,28},{28,24},{1,5},{5... | collective-permute-start | bytes 1572872 | tf_op jit(solution)/shard_map/ppermute | solution.py:24
  32.6 25.7 %collective-permute-start.9 = (bf16[64,16,256]{2,1,0:T(8,128)(2,1)S(1)}, bf16[64,16,256]{2,1,0:T(8,128)(2,1)}, u32[]{:S(2)}, u32[]{:S(2)}) collective-permute-start(bf16[64,16,256]{2,1,0:T(8,128)(2,1)S(1)} %collective-permute-done.8.refs_2_), channel_id=1, source_target_pairs={{0,4},{4,0},{8,12},{12,8},{16,20},{20,16},{24,28},{28,24},{1,5},{5... | collective-permute-start | bytes 1572872 | tf_op jit(solution)/shard_map/ppermute | solution.py:24
  34.3 4.5 %collective-permute-start.3 = (s32[64,8]{0,1:T(8,128)S(1)}, s32[64,8]{0,1:T(8,128)S(1)}, u32[]{:S(2)}, u32[]{:S(2)}) collective-permute-start(s32[64,8]{0,1:T(8,128)S(1)} %copy-done.7), channel_id=1, source_target_pairs={{0,16},{4,20},{8,24},{12,28},{16,0},{20,4},{24,8},{28,12},{1,17},{... | collective-permute-start | bytes 6152 | tf_op jit(solution)/shard_map/ppermute | solution.py:24
  42.3 36.4 %collective-permute-start.4 = (bf16[64,16,256]{2,1,0:T(8,128)(2,1)}, bf16[64,16,256]{2,1,0:T(8,128)(2,1)}, u32[]{:S(2)}, u32[]{:S(2)}) collective-permute-start(bf16[64,16,256]{2,1,0:T(8,128)(2,1)} %shard_map.61), channel_id=1, source_target_pairs={{0,16},{4,20},{8,24},{12,28},{16,0},{20,4},{24,8},{28,12},{1,17},{... | collective-permute-start | bytes 1572872 | tf_op jit(solution)/shard_map/ppermute | solution.py:24
  61.6 27.1 %collective-permute-start.10 = (bf16[64,16,256]{2,1,0:T(8,128)(2,1)}, bf16[64,16,256]{2,1,0:T(8,128)(2,1)}, u32[]{:S(2)}, u32[]{:S(2)}) collective-permute-start(bf16[64,16,256]{2,1,0:T(8,128)(2,1)} %shard_map.66), channel_id=1, source_target_pairs={{0,16},{4,20},{8,24},{12,28},{16,0},{20,4},{24,8},{28,12},{1,17},{... | collective-permute-start | bytes 1572872 | tf_op jit(solution)/shard_map/ppermute | solution.py:24
  85.7 7.9 %collective-permute-start.5 = (bf16[16,8192]{1,0:T(8,128)(2,1)S(1)}, bf16[16,8192]{1,0:T(8,128)(2,1)S(1)}, u32[]{:S(2)}, u32[]{:S(2)}) collective-permute-start(bf16[16,8192]{1,0:T(8,128)(2,1)S(1)} %shard_map.62), channel_id=1, source_target_pairs={{0,1},{1,0},{2,3},{3,2},{4,5},{5,4},{6,7},{7,6},{8,9},{9,8},{10,11... | collective-permute-start | bytes 786440 | tf_op jit(solution)/shard_map/ppermute | solution.py:24
  93.4 1.9 collective-permute-start.11
  93.7 9.2 %collective-permute-start.6 = (bf16[16,8192]{1,0:T(8,128)(2,1)S(1)}, bf16[16,8192]{1,0:T(8,128)(2,1)S(1)}, u32[]{:S(2)}, u32[]{:S(2)}) collective-permute-start(bf16[16,8192]{1,0:T(8,128)(2,1)S(1)} %add_convert_fusion.3.mine_ref), channel_id=1, source_target_pairs={{0,2},{1,3},{2,0},{3,1},{4,6},{5,7},{6,4},{7,5},{8,10},{9,11},{10,... | collective-permute-start | bytes 786440 | tf_op jit(solution)/shard_map/ppermute | solution.py:24
  95.3 12.6 %collective-permute-start.12 = (bf16[16,8192]{1,0:T(8,128)(2,1)S(1)}, bf16[16,8192]{1,0:T(8,128)(2,1)S(1)}, u32[]{:S(2)}, u32[]{:S(2)}) collective-permute-start(bf16[16,8192]{1,0:T(8,128)(2,1)S(1)} %add_convert_fusion.2.mine_ref), channel_id=1, source_target_pairs={{0,2},{1,3},{2,0},{3,1},{4,6},{5,7},{6,4},{7,5},{8,10},{9,11},{10,... | collective-permute-start | bytes 786440 | tf_op jit(solution)/shard_map/ppermute | solution.py:24
  104.5 14.9 %collective-permute-start.14 = (bf16[64,16,256]{2,1,0:T(8,128)(2,1)S(1)}, bf16[64,16,256]{2,1,0:T(8,128)(2,1)S(1)}, u32[]{:S(2)}, u32[]{:S(2)}) collective-permute-start(bf16[64,16,256]{2,1,0:T(8,128)(2,1)S(1)} %get-tuple-element.8.refs_0_), channel_id=1, source_target_pairs={{0,8},{4,12},{8,0},{12,4},{16,24},{20,28},{24,16},{28,20},{1,9},{5... | collective-permute-start | bytes 1572872 | tf_op jit(solution)/shard_map/ppermute | solution.py:24
  109.6 19.1 %collective-permute-start.20 = (bf16[64,16,256]{2,1,0:T(8,128)(2,1)S(1)}, bf16[64,16,256]{2,1,0:T(8,128)(2,1)S(1)}, u32[]{:S(2)}, u32[]{:S(2)}) collective-permute-start(bf16[64,16,256]{2,1,0:T(8,128)(2,1)S(1)} %get-tuple-element.9.refs_0_), channel_id=1, source_target_pairs={{0,8},{4,12},{8,0},{12,4},{16,24},{20,28},{24,16},{28,20},{1,9},{5... | collective-permute-start | bytes 1572872 | tf_op jit(solution)/shard_map/ppermute | solution.py:24
  110.3 19.2 %collective-permute-start.13 = (bf16[64,16,256]{2,1,0:T(8,128)(2,1)S(1)}, bf16[64,16,256]{2,1,0:T(8,128)(2,1)S(1)}, u32[]{:S(2)}, u32[]{:S(2)}) collective-permute-start(bf16[64,16,256]{2,1,0:T(8,128)(2,1)S(1)} %get-tuple-element.8.refs_0_), channel_id=1, source_target_pairs={{0,4},{4,0},{8,12},{12,8},{16,20},{20,16},{24,28},{28,24},{1,5},{5... | collective-permute-start | bytes 1572872 | tf_op jit(solution)/shard_map/ppermute | solution.py:24
  119.5 17.0 %collective-permute-start.15 = (bf16[64,16,256]{2,1,0:T(8,128)(2,1)S(1)}, bf16[64,16,256]{2,1,0:T(8,128)(2,1)S(1)}, u32[]{:S(2)}, u32[]{:S(2)}) collective-permute-start(bf16[64,16,256]{2,1,0:T(8,128)(2,1)S(1)} %collective-permute-done.14.refs_2_), channel_id=1, source_target_pairs={{0,4},{4,0},{8,12},{12,8},{16,20},{20,16},{24,28},{28,24},{1,5},{5... | collective-permute-start | bytes 1572872 | tf_op jit(solution)/shard_map/ppermute | solution.py:24
  120.0 27.7 %collective-permute-start.19 = (bf16[64,16,256]{2,1,0:T(8,128)(2,1)S(1)}, bf16[64,16,256]{2,1,0:T(8,128)(2,1)S(1)}, u32[]{:S(2)}, u32[]{:S(2)}) collective-permute-start(bf16[64,16,256]{2,1,0:T(8,128)(2,1)S(1)} %get-tuple-element.9.refs_0_), channel_id=1, source_target_pairs={{0,4},{4,0},{8,12},{12,8},{16,20},{20,16},{24,28},{28,24},{1,5},{5... | collective-permute-start | bytes 1572872 | tf_op jit(solution)/shard_map/ppermute | solution.py:24
  128.7 28.6 %collective-permute-start.21 = (bf16[64,16,256]{2,1,0:T(8,128)(2,1)S(1)}, bf16[64,16,256]{2,1,0:T(8,128)(2,1)S(1)}, u32[]{:S(2)}, u32[]{:S(2)}) collective-permute-start(bf16[64,16,256]{2,1,0:T(8,128)(2,1)S(1)} %collective-permute-done.20.refs_2_), channel_id=1, source_target_pairs={{0,4},{4,0},{8,12},{12,8},{16,20},{20,16},{24,28},{28,24},{1,5},{5... | collective-permute-start | bytes 1572872 | tf_op jit(solution)/shard_map/ppermute | solution.py:24
  137.9 25.8 %collective-permute-start.16 = (bf16[64,16,256]{2,1,0:T(8,128)(2,1)S(1)}, bf16[64,16,256]{2,1,0:T(8,128)(2,1)S(1)}, u32[]{:S(2)}, u32[]{:S(2)}) collective-permute-start(bf16[64,16,256]{2,1,0:T(8,128)(2,1)S(1)} %shard_map.70), channel_id=1, source_target_pairs={{0,16},{4,20},{8,24},{12,28},{16,0},{20,4},{24,8},{28,12},{1,17},{... | collective-permute-start | bytes 1572872 | tf_op jit(solution)/shard_map/ppermute | solution.py:24
  158.7 25.3 %collective-permute-start.22 = (bf16[64,16,256]{2,1,0:T(8,128)(2,1)S(1)}, bf16[64,16,256]{2,1,0:T(8,128)(2,1)S(1)}, u32[]{:S(2)}, u32[]{:S(2)}) collective-permute-start(bf16[64,16,256]{2,1,0:T(8,128)(2,1)S(1)} %shard_map.73), channel_id=1, source_target_pairs={{0,16},{4,20},{8,24},{12,28},{16,0},{20,4},{24,8},{28,12},{1,17},{... | collective-permute-start | bytes 1572872 | tf_op jit(solution)/shard_map/ppermute | solution.py:24
  165.8 20.4 %collective-permute-start.17 = (bf16[16,8192]{1,0:T(8,128)(2,1)S(1)}, bf16[16,8192]{1,0:T(8,128)(2,1)S(1)}, u32[]{:S(2)}, u32[]{:S(2)}) collective-permute-start(bf16[16,8192]{1,0:T(8,128)(2,1)S(1)} %shard_map.71), channel_id=1, source_target_pairs={{0,1},{1,0},{2,3},{3,2},{4,5},{5,4},{6,7},{7,6},{8,9},{9,8},{10,11... | collective-permute-start | bytes 786440 | tf_op jit(solution)/shard_map/ppermute | solution.py:24
  186.3 9.2 %collective-permute-start.18 = (bf16[16,8192]{1,0:T(8,128)(2,1)S(1)}, bf16[16,8192]{1,0:T(8,128)(2,1)S(1)}, u32[]{:S(2)}, u32[]{:S(2)}) collective-permute-start(bf16[16,8192]{1,0:T(8,128)(2,1)S(1)} %add_convert_fusion.1), channel_id=1, source_target_pairs={{0,2},{1,3},{2,0},{3,1},{4,6},{5,7},{6,4},{7,5},{8,10},{9,11},{10,... | collective-permute-start | bytes 786440 | tf_op jit(solution)/shard_map/ppermute | solution.py:24
  187.9 12.7 %collective-permute-start.24 = (bf16[16,8192]{1,0:T(8,128)(2,1)S(1)}, bf16[16,8192]{1,0:T(8,128)(2,1)S(1)}, u32[]{:S(2)}, u32[]{:S(2)}) collective-permute-start(bf16[16,8192]{1,0:T(8,128)(2,1)S(1)} %add_convert_fusion), channel_id=1, source_target_pairs={{0,2},{1,3},{2,0},{3,1},{4,6},{5,7},{6,4},{7,5},{8,10},{9,11},{10,... | collective-permute-start | bytes 786440 | tf_op jit(solution)/shard_map/ppermute | solution.py:24
  (9 other events, 73.2 us)

commit v2 on v1

v2 whole, which is shorter than its diff:
```python
import functools

import jax
import jax.numpy as jnp
from jax import lax
from jax.experimental import pallas as pl
from jax.experimental.pallas import tpu as pltpu
from jax.sharding import PartitionSpec as P

TILE_BLOCKS = 8
VMEM_LIMIT = 8 * 1024 * 1024
NEAR = 3


def params():
    return pltpu.CompilerParams(vmem_limit_bytes=VMEM_LIMIT)


def cost(flops, nbytes):
    return pl.CostEstimate(flops=int(flops), bytes_accessed=int(nbytes), transcendentals=0)


def swap(value, axis, size, mask):
    return lax.ppermute(value, axis, [(i, i ^ mask) for i in range(size)])


def add_bf16(a, b):
    return (a.astype(jnp.float32) + b.astype(jnp.float32)).astype(jnp.bfloat16)


def project(block_len, scaled, emb_ref, sums_refs):
    count = len(sums_refs)
    part = emb_ref.shape[1] // count
    for b in range(sums_refs[0].shape[0]):
        docs = slice(b * block_len, (b + 1) * block_len)
        sums = jnp.dot(
            scaled[:, docs], emb_ref[docs, :], preferred_element_type=jnp.float32
        ).astype(jnp.bfloat16)
        for i, ref in enumerate(sums_refs):
            ref[b] = sums[:, i * part:(i + 1) * part]


def first_sums_kernel(block_len, vec_ref, quality_ref, emb_ref, *sums_refs):
    scaled = (vec_ref[...] * quality_ref[...]).astype(jnp.bfloat16)
    project(block_len, scaled, emb_ref, sums_refs)


def next_sums_kernel(block_len, mine_ref, other_ref, vec_ref, quality_ref, emb_ref, out_ref, *sums_refs):
    total = mine_ref[...].astype(jnp.float32) + other_ref[...].astype(jnp.float32)
    quality = quality_ref[...]
    out = total * quality - vec_ref[...]
    out_ref[...] = out
    project(block_len, (out * quality).astype(jnp.bfloat16), emb_ref, sums_refs)


def finish_kernel(mine_ref, other_ref, first_ref, vec_ref, quality_ref, out_ref):
    total = mine_ref[...].astype(jnp.float32) + other_ref[...].astype(jnp.float32)
    out_ref[...] = 2.0 * (total * quality_ref[...] - first_ref[...]) - vec_ref[...]


def combine_kernel(ids_ref, *refs):
    *shards, out_ref, table, sems = refs
    blocks = shards[0].shape[0]
    copies = [
        pltpu.make_async_copy(ref, table.at[pl.ds(i * blocks, blocks)], sems.at[i])
        for i, ref in enumerate(shards)
    ]
    for copy in copies:
        copy.start()
    table[len(shards) * blocks] = jnp.zeros(table.shape[1:], table.dtype)
    for copy in copies:
        copy.wait()
    entries = ids_ref.shape[0] // out_ref.shape[0]

    def step(b, carry):
        total = table[ids_ref[b * entries]].astype(jnp.float32)
        for k in range(1, entries):
            total = total + table[ids_ref[b * entries + k]].astype(jnp.float32)
        out_ref[b] = total.astype(out_ref.dtype)
        return carry

    lax.fori_loop(0, out_ref.shape[0], step, 0, unroll=4)


def expand_kernel(block_len, counts, *refs):
    *refs, emb_ref, out_ref = refs
    for b in range(refs[0].shape[0]):
        docs = slice(b * block_len, (b + 1) * block_len)
        parts, at = [], 0
        for count in counts:
            total = refs[at][b]
            for ref in refs[at + 1:at + count]:
                total = total + ref[b].astype(jnp.float32)
            parts.append(total.astype(jnp.bfloat16))
            at += count
        out_ref[:, docs] = lax.dot_general(
            jnp.concatenate(parts, axis=1), emb_ref[docs, :], (((1,), (1,)), ((), ())),
            preferred_element_type=jnp.float32,
        ).astype(jnp.bfloat16)


def body(embeddings, quality, probes, neighbors):
    nrow, ncol = lax.axis_size("row"), lax.axis_size("col")
    me = lax.axis_index("row")
    blk_count, list_len = neighbors.shape
    docs, width = embeddings.shape
    block_len = docs // blk_count
    nprobe = probes.shape[0]
    bits = [1 << i for i in reversed(range(nrow.bit_length() - 1))]
    near = [m for m in bits if m & NEAR]
    far = [m for m in bits if not m & NEAR]
    plans = [(far, near[::-1]), (near, far)]
    nparts = len(plans)
    part = width // nparts

    dests = []
    for _, reduce_bits in plans:
        found = [0]
        for m in reversed(reduce_bits):
            found = [d | m for d in found] + found
        dests.append(found)
    lists = {d: swap(neighbors, "row", nrow, d) for found in dests for d in found if d}
    lists[0] = neighbors

    def table_ids(dest, gather_bits):
        flat = lists[dest].reshape(-1)
        apart = (flat // blk_count) ^ me
        inside = (apart & ~sum(gather_bits)) == 0
        slot = sum(((apart & m) != 0).astype(jnp.int32) << i for i, m in enumerate(gather_bits))
        return jnp.where(inside, slot * blk_count + flat % blk_count, blk_count << len(gather_bits))

    qrow = quality[None, :]
    tile_docs = TILE_BLOCKS * block_len
    steps = blk_count // TILE_BLOCKS
    shard_shape = (blk_count, nprobe, part)
    shard_size = blk_count * nprobe * part
    mac = 2 * nprobe * docs * width
    emb_spec = pl.BlockSpec((tile_docs, width), lambda j: (j, 0))
    vec_spec = pl.BlockSpec((nprobe, tile_docs), lambda j: (0, j))
    q_spec = pl.BlockSpec((1, tile_docs), lambda j: (0, j))
    shard_spec = pl.BlockSpec((TILE_BLOCKS, nprobe, part), lambda j: (j, 0, 0))
    shard_out = jax.ShapeDtypeStruct(shard_shape, jnp.bfloat16)
    vec_out = jax.ShapeDtypeStruct((nprobe, docs), jnp.float32)

    def first_sums(qrow):
        return pl.pallas_call(
            functools.partial(first_sums_kernel, block_len),
            grid=(steps,),
            in_specs=[vec_spec, q_spec, emb_spec],
            out_specs=[shard_spec] * nparts,
            out_shape=[shard_out] * nparts,
            compiler_params=params(),
            cost_estimate=cost(mac, 2 * docs * width + 4 * nprobe * docs + 4 * shard_size),
        )(probes, qrow, embeddings)

    def next_sums(mine, other):
        first, *sums = pl.pallas_call(
            functools.partial(next_sums_kernel, block_len),
            grid=(steps,),
            in_specs=[vec_spec, vec_spec, vec_spec, q_spec, emb_spec],
            out_specs=[vec_spec] + [shard_spec] * nparts,
            out_shape=[vec_out] + [shard_out] * nparts,
            compiler_params=params(),
            cost_estimate=cost(mac, 2 * docs * width + 12 * nprobe * docs + 4 * shard_size),
        )(mine, other, probes, qrow, embeddings)
        return first, sums

    def finish(mine, other, first):
        return pl.pallas_call(
            finish_kernel,
            grid=(steps // 2,),
            in_specs=[pl.BlockSpec((nprobe, 2 * tile_docs), lambda j: (0, j))] * 4
            + [pl.BlockSpec((1, 2 * tile_docs), lambda j: (0, j))],
            out_specs=pl.BlockSpec((nprobe, 2 * tile_docs), lambda j: (0, j)),
            out_shape=vec_out,
            compiler_params=params(),
            cost_estimate=cost(6 * nprobe * docs, 16 * nprobe * docs),
        )(mine, other, first, probes, qrow)

    def combine(ids, shards, dtype):
        count = len(shards)
        return pl.pallas_call(
            combine_kernel,
            in_specs=[pl.BlockSpec(memory_space=pltpu.SMEM)] + [pl.BlockSpec(memory_space=pl.ANY)] * count,
            out_specs=pl.BlockSpec(memory_space=pltpu.VMEM),
            out_shape=jax.ShapeDtypeStruct(shard_shape, dtype),
            scratch_shapes=[
                pltpu.VMEM((count * blk_count + 1, nprobe, part), jnp.bfloat16),
                pltpu.SemaphoreType.DMA((count,)),
            ],
            compiler_params=params(),
            cost_estimate=cost(list_len * shard_size, 2 * count * shard_size + 4 * shard_size),
        )(ids, *shards)

    def expand(groups):
        values = [v for group in groups for v in group]
        return pl.pallas_call(
            functools.partial(expand_kernel, block_len, [len(group) for group in groups]),
            grid=(steps,),
            in_specs=[shard_spec] * len(values) + [emb_spec],
            out_specs=vec_spec,
            out_shape=jax.ShapeDtypeStruct((nprobe, docs), jnp.bfloat16),
            compiler_params=params(),
            cost_estimate=cost(mac, 2 * docs * width + 2 * nprobe * docs + 6 * len(values) * shard_size // 2),
        )(*values, embeddings)

    ids = [{d: table_ids(d, gather_bits) for d in found} for found, (gather_bits, _) in zip(dests, plans)]

    def gather(sums, gather_bits):
        shards = [sums]
        for m in gather_bits:
            shards = shards + [swap(v, "row", nrow, m) for v in shards]
        return shards

    def reduce(outgoing, reduce_bits):
        arrived = []
        for m in reduce_bits:
            taken = {d ^ m: swap(outgoing.pop(d), "row", nrow, m) for d in list(outgoing) if d & m}
            for d, value in taken.items():
                if d:
                    outgoing[d] = add_bf16(outgoing[d], value)
                else:
                    arrived.append(value)
        return arrived

    def exchange(sums):
        shards = [gather(s, gather_bits) for s, (gather_bits, _) in zip(sums, plans)]
        order = [(i, found[k]) for k in range(nrow) for i, found in enumerate(dests) if k + 1 < len(found)]
        combined, last = [{} for _ in plans], None
        for i, d in order + [(i, 0) for i in range(nparts)]:
            picks = ids[i][d] if last is None else lax.optimization_barrier((ids[i][d], last))[0]
            last = combine(picks, shards[i], jnp.bfloat16 if d else jnp.float32)
            combined[i][d] = last
        own = [found.pop(0) for found in combined]
        return [[o] + reduce(c, reduce_bits) for o, c, (_, reduce_bits) in zip(own, combined, plans)]

    def col_sum(value):
        masks = [1 << i for i in range(ncol.bit_length() - 1)]
        for m in masks[:-1]:
            value = add_bf16(value, swap(value, "col", ncol, m))
        return value, swap(value, "col", ncol, masks[-1])

    halves = col_sum(expand(exchange(first_sums(lax.optimization_barrier((qrow, lists))[0]))))
    first, sums = next_sums(*halves)
    halves = col_sum(expand(exchange(sums)))
    return first, finish(*halves, first)


def solution(mesh):
    placed = (P("row", "col"), P("row"), P(None, "row"), P("row", None))
    return jax.shard_map(
        body,
        mesh=mesh,
        in_specs=placed,
        out_specs=(P(None, "row"), P(None, "row")),
        check_vma=False,
    )
```

time: 203 us -> 201 us (level)
  waiting for transfers between devices: 120 us -> 142 us
  starting transfers between devices: 34.7 us -> 17 us
  Pallas kernels: 37.2 us -> 33.5 us
    ppermute x25 -> x24, waiting for transfers between devices: 120 us -> 142 us  [swap(): return lax.ppermute(value, axis, [(i, i ^ mask) for i in range(size)])]
    ppermute x25 -> x24, starting transfers between devices: 34.7 us -> 17 us  [swap(): return lax.ppermute(value, axis, [(i, i ^ mask) for i in range(size)])]
    pallas_call x4 -> x3, Pallas kernels: 13.8 us -> 9.32 us  [the longest x2 7.5 us: expand(): pl.pallas_call(functools.partial(expand_kernel, block_len, [len(group) fo...]
    unnamed x17, local copies, waits for them, and re-layouts: 6.46 us -> 4.28 us
    convert_element_type x4, other arithmetic: 0.27 us -> 2.36 us  [add_bf16(): return (a.astype(jnp.float32) + b.astype(jnp.float32)).astype(jnp.bfloat16)]
    concatenate x2 -> x0, other arithmetic: 2.08 us -> none  [body(): return (jnp.concatenate(firsts, axis=0), jnp.concatenate(seconds, axis=0))]
    pallas_call x8 -> x12, Pallas kernels: 17.2 us -> 19.1 us  [combine(): pl.pallas_call(combine_kernel, in_specs=[pl.BlockSpec(memory_space=pltpu....]
  transfers between devices with their start and end apart: 25 -> 24, of which waited for: 17 -> 21; matrix products, arithmetic and copies ran while one was open for 1% -> 2% of each run, Pallas kernels for 18% -> 10%
where the time goes in v2:
time: 201 us
  waiting for transfers between devices  142 us (71%)
  Pallas kernels  33.5 us (17%)
  starting transfers between devices  17 us (8%)
  local copies, waits for them, and re-layouts  5.08 us (3%)
  other arithmetic  2.43 us (1%)
    ppermute x24, waiting for transfers between devices, swap(): return lax.ppermute(value, axis, [(i, i ^ mask) for i in range(size)])  142 us
    pallas_call x12, Pallas kernels, combine(): pl.pallas_call(combine_kernel, in_specs=[pl.BlockSpec(memory_space=pltpu....  19.1 us
    ppermute x24, starting transfers between devices, swap(): return lax.ppermute(value, axis, [(i, i ^ mask) for i in range(size)])  17 us
    pallas_call x2, Pallas kernels, expand(): pl.pallas_call(functools.partial(expand_kernel, block_len, [len(group) fo...  7.5 us
    unnamed x17, local copies, waits for them, and re-layouts  4.28 us
  transfers between devices with their start and end apart: 24, of which 21 were waited for; matrix products, arithmetic and copies ran while one was open for 2% of the time, Pallas kernels for 10%

profile of v2, /device:TPU:0, one launch (start us, length us, event | category | flops | bytes accessed | tf_op | source)
XLA Modules:
  0.0 200.5 jit_solution(13293711688710426936)
XLA Ops:
  0.6 4.1 %collective-permute-start.2 = (s32[64,8]{0,1:T(8,128)}, s32[64,8]{0,1:T(8,128)S(1)}, u32[]{:S(2)}, u32[]{:S(2)}) collective-permute-start(s32[64,8]{0,1:T(8,128)} %param.7), channel_id=1, source_target_pairs={{0,16},{4,20},{8,24},{12,28},{16,0},{20,4},{24,8},{28,12},{1,17},{... | collective-permute-start | bytes 6152 | tf_op jit(solution)/shard_map/ppermute | solution.py:24
  10.1 2.5 %collective-permute-done.3 = s32[64,8]{0,1:T(8,128)S(1)} collective-permute-done((s32[64,8]{0,1:T(8,128)}, s32[64,8]{0,1:T(8,128)S(1)}, u32[]{:S(2)}, u32[]{:S(2)}) %collective-permute-start.3) | collective-permute-done | bytes 2080 | tf_op jit(solution)/shard_map/ppermute | solution.py:24
  12.5 2.2 %copy-done = bf16[8192,256]{1,0:T(8,128)(2,1)S(1)} copy-done((bf16[8192,256]{1,0:T(8,128)(2,1)S(1)}, bf16[8192,256]{1,0:T(8,128)(2,1)}, u32[]{:S(2)}) %copy-start) | copy-done | bytes 4194328
  19.8 20.5 %collective-permute-done.5.refs_1_ = bf16[64,32,128]{2,1,0:T(8,128)(2,1)S(1)} collective-permute-done((bf16[64,32,128]{2,1,0:T(8,128)(2,1)S(1)}, bf16[64,32,128]{2,1,0:T(8,128)(2,1)S(1)}, u32[]{:S(2)}, u32[]{:S(2)}) %collective-permute-start.5) | collective-permute-done | bytes 524320 | tf_op jit(solution)/shard_map/ppermute | solution.py:24
  42.6 2.2 %shard_map.60 = bf16[64,32,128]{2,1,0:T(8,128)(2,1)} custom-call(s32[512]{0:T(512)S(1)} %fusion.12.ids_ref, bf16[64,32,128]{2,1,0:T(8,128)(2,1)S(1)} %get-tuple-element.19.refs_0_, bf16[64,32,128]{2,1,0:T(8,128)(2,1)S(1)} %collective-permute-done.4.refs_1_), custom_call_target="tpu_custom_call" | custom-call | flops 2097152 | bytes 2097152 | tf_op jit(solution)/shard_map/pallas_call | solution.py:182
  45.9 9.2 %collective-permute-done.7.refs_3_ = bf16[64,32,128]{2,1,0:T(8,128)(2,1)S(1)} collective-permute-done((bf16[64,32,128]{2,1,0:T(8,128)(2,1)S(1)}, bf16[64,32,128]{2,1,0:T(8,128)(2,1)S(1)}, u32[]{:S(2)}, u32[]{:S(2)}) %collective-permute-start.7) | collective-permute-done | bytes 524320 | tf_op jit(solution)/shard_map/ppermute | solution.py:24
  55.1 2.3 %shard_map.61 = bf16[64,32,128]{2,1,0:T(8,128)(2,1)} custom-call(s32[512]{0:T(512)S(1)} %get-tuple-element.28.ids_ref, bf16[64,32,128]{2,1,0:T(8,128)(2,1)S(1)} %get-tuple-element.21.refs_0_, bf16[64,32,128]{2,1,0:T(8,128)(2,1)S(1)} %collective-permute-done.5.refs_1_, bf16[64,32,128]{2,1,0:T(8,128)(2,1)S(1)} %collective-permute-done.6.refs_2_, ...), custom_call_target="tpu_custom_call" | custom-call | flops 2097152 | bytes 3145728 | tf_op jit(solution)/shard_map/pallas_call | solution.py:182
  57.5 2.2 %shard_map.62 = bf16[64,32,128]{2,1,0:T(8,128)(2,1)} custom-call(s32[512]{0:T(512)S(1)} %fusion.6.ids_ref, bf16[64,32,128]{2,1,0:T(8,128)(2,1)S(1)} %get-tuple-element.19.refs_0_, bf16[64,32,128]{2,1,0:T(8,128)(2,1)S(1)} %collective-permute-done.4.refs_1_), custom_call_target="tpu_custom_call" | custom-call | flops 2097152 | bytes 2097152 | tf_op jit(solution)/shard_map/pallas_call | solution.py:182
  61.6 4.9 %collective-permute-done.9 = bf16[64,32,128]{2,1,0:T(8,128)(2,1)} collective-permute-done((bf16[64,32,128]{2,1,0:T(8,128)(2,1)}, bf16[64,32,128]{2,1,0:T(8,128)(2,1)}, u32[]{:S(2)}, u32[]{:S(2)}) %collective-permute-start.9) | collective-permute-done | bytes 524320 | tf_op jit(solution)/shard_map/ppermute | solution.py:24
  71.5 4.1 %collective-permute-done.8.refs_1_ = bf16[64,32,128]{2,1,0:T(8,128)(2,1)} collective-permute-done((bf16[64,32,128]{2,1,0:T(8,128)(2,1)}, bf16[64,32,128]{2,1,0:T(8,128)(2,1)}, u32[]{:S(2)}, u32[]{:S(2)}) %collective-permute-start.8) | collective-permute-done | bytes 524320 | tf_op jit(solution)/shard_map/ppermute | solution.py:24
  75.5 3.1 %collective-permute-done.11.refs_4_ = bf16[64,32,128]{2,1,0:T(8,128)(2,1)} collective-permute-done((bf16[64,32,128]{2,1,0:T(8,128)(2,1)}, bf16[64,32,128]{2,1,0:T(8,128)(2,1)}, u32[]{:S(2)}, u32[]{:S(2)}) %collective-permute-start.11) | collective-permute-done | bytes 524320 | tf_op jit(solution)/shard_map/ppermute | solution.py:24
  78.6 9.6 %collective-permute-done.10.refs_2_ = bf16[64,32,128]{2,1,0:T(8,128)(2,1)} collective-permute-done((bf16[64,32,128]{2,1,0:T(8,128)(2,1)}, bf16[64,32,128]{2,1,0:T(8,128)(2,1)}, u32[]{:S(2)}, u32[]{:S(2)}) %collective-permute-start.10) | collective-permute-done | bytes 524320 | tf_op jit(solution)/shard_map/ppermute | solution.py:24
  88.3 5.2 %shard_map.66 = bf16[32,8192]{1,0:T(8,128)(2,1)S(1)} custom-call(f32[64,32,128]{2,1,0:T(8,128)S(1)} %shard_map.64.refs_0_, bf16[64,32,128]{2,1,0:T(8,128)(2,1)} %collective-permute-done.8.refs_1_, bf16[64,32,128]{2,1,0:T(8,128)(2,1)} %collective-permute-done.10.refs_2_, f32[64,32,128]{2,1,0:T(8,128)S(1)} %shard_map.65.refs_3_, ...), custom_call_target="tpu_custom_call" | custom-call | flops 134217728 | bytes 8650752 | tf_op jit(solution)/shard_map/pallas_call | solution.py:197
  97.1 12.5 %collective-permute-done.13.other_ref = bf16[32,8192]{1,0:T(8,128)(2,1)S(1)} collective-permute-done((bf16[32,8192]{1,0:T(8,128)(2,1)S(1)}, bf16[32,8192]{1,0:T(8,128)(2,1)S(1)}, u32[]{:S(2)}, u32[]{:S(2)}) %collective-permute-start.13) | collective-permute-done | bytes 524320 | tf_op jit(solution)/shard_map/ppermute | solution.py:24
  109.6 3.3 %shard_map.67 = (f32[32,8192]{1,0:T(8,128)}, bf16[64,32,128]{2,1,0:T(8,128)(2,1)S(1)}, bf16[64,32,128]{2,1,0:T(8,128)(2,1)S(1)}) custom-call(bf16[32,8192]{1,0:T(8,128)(2,1)S(1)} %add_convert_fusion.2.mine_ref, bf16[32,8192]{1,0:T(8,128)(2,1)S(1)} %collective-permute-done.13.other_ref, f32[32,8192]{1,0:T(8,128)S(1)} %copy-done.3, f32[1,8192]{1,0:T(1,128)S(1)} %bitcast.2, ...), custom_call_target="tpu_custom_call" | custom-call | flops 134217728 | bytes 8388608 | tf_op jit(solution)/shard_map/pallas_call | solution.py:157
  113.7 19.4 %collective-permute-done.15.refs_1_ = bf16[64,32,128]{2,1,0:T(8,128)(2,1)S(1)} collective-permute-done((bf16[64,32,128]{2,1,0:T(8,128)(2,1)S(1)}, bf16[64,32,128]{2,1,0:T(8,128)(2,1)S(1)}, u32[]{:S(2)}, u32[]{:S(2)}) %collective-permute-start.15) | collective-permute-done | bytes 524320 | tf_op jit(solution)/shard_map/ppermute | solution.py:24
  133.6 4.6 %collective-permute-done.14.refs_1_ = bf16[64,32,128]{2,1,0:T(8,128)(2,1)S(1)} collective-permute-done((bf16[64,32,128]{2,1,0:T(8,128)(2,1)S(1)}, bf16[64,32,128]{2,1,0:T(8,128)(2,1)S(1)}, u32[]{:S(2)}, u32[]{:S(2)}) %collective-permute-start.14) | collective-permute-done | bytes 524320 | tf_op jit(solution)/shard_map/ppermute | solution.py:24
  140.4 7.5 %collective-permute-done.17.refs_3_ = bf16[64,32,128]{2,1,0:T(8,128)(2,1)S(1)} collective-permute-done((bf16[64,32,128]{2,1,0:T(8,128)(2,1)S(1)}, bf16[64,32,128]{2,1,0:T(8,128)(2,1)S(1)}, u32[]{:S(2)}, u32[]{:S(2)}) %collective-permute-start.17) | collective-permute-done | bytes 524320 | tf_op jit(solution)/shard_map/ppermute | solution.py:24
  153.1 6.0 %collective-permute-done.19 = bf16[64,32,128]{2,1,0:T(8,128)(2,1)S(1)} collective-permute-done((bf16[64,32,128]{2,1,0:T(8,128)(2,1)S(1)}, bf16[64,32,128]{2,1,0:T(8,128)(2,1)S(1)}, u32[]{:S(2)}, u32[]{:S(2)}) %collective-permute-start.19) | collective-permute-done | bytes 524320 | tf_op jit(solution)/shard_map/ppermute | solution.py:24
  162.2 6.2 %collective-permute-done.18.refs_1_ = bf16[64,32,128]{2,1,0:T(8,128)(2,1)S(1)} collective-permute-done((bf16[64,32,128]{2,1,0:T(8,128)(2,1)S(1)}, bf16[64,32,128]{2,1,0:T(8,128)(2,1)S(1)}, u32[]{:S(2)}, u32[]{:S(2)}) %collective-permute-start.18) | collective-permute-done | bytes 524320 | tf_op jit(solution)/shard_map/ppermute | solution.py:24
  168.4 3.8 %collective-permute-done.21.refs_4_ = bf16[64,32,128]{2,1,0:T(8,128)(2,1)S(1)} collective-permute-done((bf16[64,32,128]{2,1,0:T(8,128)(2,1)S(1)}, bf16[64,32,128]{2,1,0:T(8,128)(2,1)S(1)}, u32[]{:S(2)}, u32[]{:S(2)}) %collective-permute-start.21) | collective-permute-done | bytes 524320 | tf_op jit(solution)/shard_map/ppermute | solution.py:24
  172.2 8.0 %collective-permute-done.20.refs_2_ = bf16[64,32,128]{2,1,0:T(8,128)(2,1)S(1)} collective-permute-done((bf16[64,32,128]{2,1,0:T(8,128)(2,1)S(1)}, bf16[64,32,128]{2,1,0:T(8,128)(2,1)S(1)}, u32[]{:S(2)}, u32[]{:S(2)}) %collective-permute-start.20) | collective-permute-done | bytes 524320 | tf_op jit(solution)/shard_map/ppermute | solution.py:24
  180.2 2.4 %shard_map.74 = bf16[32,8192]{1,0:T(8,128)(2,1)S(1)} custom-call(f32[64,32,128]{2,1,0:T(8,128)S(1)} %shard_map.72.refs_0_, bf16[64,32,128]{2,1,0:T(8,128)(2,1)S(1)} %collective-permute-done.18.refs_1_, bf16[64,32,128]{2,1,0:T(8,128)(2,1)S(1)} %collective-permute-done.20.refs_2_, f32[64,32,128]{2,1,0:T(8,128)S(1)} %shard_map.73.refs_3_, ...), custom_call_target="tpu_custom_call" | custom-call | flops 134217728 | bytes 8650752 | tf_op jit(solution)/shard_map/pallas_call | solution.py:197
  186.2 12.5 %collective-permute-done.23.other_ref = bf16[32,8192]{1,0:T(8,128)(2,1)S(1)} collective-permute-done((bf16[32,8192]{1,0:T(8,128)(2,1)S(1)}, bf16[32,8192]{1,0:T(8,128)(2,1)S(1)}, u32[]{:S(2)}, u32[]{:S(2)}) %collective-permute-start.23) | collective-permute-done | bytes 524320 | tf_op jit(solution)/shard_map/ppermute | solution.py:24
  (75 shorter events, 41.7 us)
Async XLA Ops:
  0.6 7.6 %collective-permute-start.2 = (s32[64,8]{0,1:T(8,128)}, s32[64,8]{0,1:T(8,128)S(1)}, u32[]{:S(2)}, u32[]{:S(2)}) collective-permute-start(s32[64,8]{0,1:T(8,128)} %param.7), channel_id=1, source_target_pairs={{0,16},{4,20},{8,24},{12,28},{16,0},{20,4},{24,8},{28,12},{1,17},{... | collective-permute-start | bytes 6152 | tf_op jit(solution)/shard_map/ppermute | solution.py:24
  4.7 3.8 %collective-permute-start.1 = (s32[64,8]{0,1:T(8,128)}, s32[64,8]{0,1:T(8,128)S(1)}, u32[]{:S(2)}, u32[]{:S(2)}) collective-permute-start(s32[64,8]{0,1:T(8,128)} %param.7), channel_id=1, source_target_pairs={{0,4},{4,0},{8,12},{12,8},{16,20},{20,16},{24,28},{28,24},{1,5},{5... | collective-permute-start | bytes 6152 | tf_op jit(solution)/shard_map/ppermute | solution.py:24
  6.3 3.8 %collective-permute-start = (s32[64,8]{0,1:T(8,128)}, s32[64,8]{0,1:T(8,128)S(1)}, u32[]{:S(2)}, u32[]{:S(2)}) collective-permute-start(s32[64,8]{0,1:T(8,128)} %param.7), channel_id=1, source_target_pairs={{0,8},{4,12},{8,0},{12,4},{16,24},{20,28},{24,16},{28,20},{1,9},{5... | collective-permute-start | bytes 6152 | tf_op jit(solution)/shard_map/ppermute | solution.py:24
  7.8 4.7 %collective-permute-start.3 = (s32[64,8]{0,1:T(8,128)}, s32[64,8]{0,1:T(8,128)S(1)}, u32[]{:S(2)}, u32[]{:S(2)}) collective-permute-start(s32[64,8]{0,1:T(8,128)} %param.7), channel_id=1, source_target_pairs={{0,12},{4,8},{8,4},{12,0},{16,28},{20,24},{24,20},{28,16},{1,13},{... | collective-permute-start | bytes 6152 | tf_op jit(solution)/shard_map/ppermute | solution.py:24
  18.5 21.8 %collective-permute-start.5 = (bf16[64,32,128]{2,1,0:T(8,128)(2,1)S(1)}, bf16[64,32,128]{2,1,0:T(8,128)(2,1)S(1)}, u32[]{:S(2)}, u32[]{:S(2)}) collective-permute-start(bf16[64,32,128]{2,1,0:T(8,128)(2,1)S(1)} %get-tuple-element.21.refs_0_), channel_id=1, source_target_pairs={{0,8},{4,12},{8,0},{12,4},{16,24},{20,28},{24,16},{28,20},{1,9},{5... | collective-permute-start | bytes 1572872 | tf_op jit(solution)/shard_map/ppermute | solution.py:24
  19.0 23.6 %collective-permute-start.4 = (bf16[64,32,128]{2,1,0:T(8,128)(2,1)S(1)}, bf16[64,32,128]{2,1,0:T(8,128)(2,1)S(1)}, u32[]{:S(2)}, u32[]{:S(2)}) collective-permute-start(bf16[64,32,128]{2,1,0:T(8,128)(2,1)S(1)} %get-tuple-element.19.refs_0_), channel_id=1, source_target_pairs={{0,16},{4,20},{8,24},{12,28},{16,0},{20,4},{24,8},{28,12},{1,17},{... | collective-permute-start | bytes 1572872 | tf_op jit(solution)/shard_map/ppermute | solution.py:24
  19.4 26.6 %collective-permute-start.6 = (bf16[64,32,128]{2,1,0:T(8,128)(2,1)S(1)}, bf16[64,32,128]{2,1,0:T(8,128)(2,1)S(1)}, u32[]{:S(2)}, u32[]{:S(2)}) collective-permute-start(bf16[64,32,128]{2,1,0:T(8,128)(2,1)S(1)} %get-tuple-element.21.refs_0_), channel_id=1, source_target_pairs={{0,4},{4,0},{8,12},{12,8},{16,20},{20,16},{24,28},{28,24},{1,5},{5... | collective-permute-start | bytes 1572872 | tf_op jit(solution)/shard_map/ppermute | solution.py:24
  40.3 14.9 %collective-permute-start.7 = (bf16[64,32,128]{2,1,0:T(8,128)(2,1)S(1)}, bf16[64,32,128]{2,1,0:T(8,128)(2,1)S(1)}, u32[]{:S(2)}, u32[]{:S(2)}) collective-permute-start(bf16[64,32,128]{2,1,0:T(8,128)(2,1)S(1)} %collective-permute-done.5.refs_1_), channel_id=1, source_target_pairs={{0,4},{4,0},{8,12},{12,8},{16,20},{20,16},{24,28},{28,24},{1,5},{5... | collective-permute-start | bytes 1572872 | tf_op jit(solution)/shard_map/ppermute | solution.py:24
  44.8 21.7 %collective-permute-start.9 = (bf16[64,32,128]{2,1,0:T(8,128)(2,1)}, bf16[64,32,128]{2,1,0:T(8,128)(2,1)}, u32[]{:S(2)}, u32[]{:S(2)}) collective-permute-start(bf16[64,32,128]{2,1,0:T(8,128)(2,1)} %shard_map.60), channel_id=1, source_target_pairs={{0,4},{4,0},{8,12},{12,8},{16,20},{20,16},{24,28},{28,24},{1,5},{5... | collective-permute-start | bytes 1572872 | tf_op jit(solution)/shard_map/ppermute | solution.py:24
  57.4 21.2 %collective-permute-start.11 = (bf16[64,32,128]{2,1,0:T(8,128)(2,1)}, bf16[64,32,128]{2,1,0:T(8,128)(2,1)}, u32[]{:S(2)}, u32[]{:S(2)}) collective-permute-start(bf16[64,32,128]{2,1,0:T(8,128)(2,1)} %shard_map.61), channel_id=1, source_target_pairs={{0,16},{4,20},{8,24},{12,28},{16,0},{20,4},{24,8},{28,12},{1,17},{... | collective-permute-start | bytes 1572872 | tf_op jit(solution)/shard_map/ppermute | solution.py:24
  59.7 15.9 %collective-permute-start.8 = (bf16[64,32,128]{2,1,0:T(8,128)(2,1)}, bf16[64,32,128]{2,1,0:T(8,128)(2,1)}, u32[]{:S(2)}, u32[]{:S(2)}) collective-permute-start(bf16[64,32,128]{2,1,0:T(8,128)(2,1)} %shard_map.62), channel_id=1, source_target_pairs={{0,4},{4,0},{8,12},{12,8},{16,20},{20,16},{24,28},{28,24},{1,5},{5... | collective-permute-start | bytes 1572872 | tf_op jit(solution)/shard_map/ppermute | solution.py:24
  68.4 19.8 %collective-permute-start.10 = (bf16[64,32,128]{2,1,0:T(8,128)(2,1)}, bf16[64,32,128]{2,1,0:T(8,128)(2,1)}, u32[]{:S(2)}, u32[]{:S(2)}) collective-permute-start(bf16[64,32,128]{2,1,0:T(8,128)(2,1)} %add_convert_fusion.3), channel_id=1, source_target_pairs={{0,8},{4,12},{8,0},{12,4},{16,24},{20,28},{24,16},{28,20},{1,9},{5... | collective-permute-start | bytes 1572872 | tf_op jit(solution)/shard_map/ppermute | solution.py:24
  93.4 2.0 collective-permute-start.12
  95.5 14.0 %collective-permute-start.13 = (bf16[32,8192]{1,0:T(8,128)(2,1)S(1)}, bf16[32,8192]{1,0:T(8,128)(2,1)S(1)}, u32[]{:S(2)}, u32[]{:S(2)}) collective-permute-start(bf16[32,8192]{1,0:T(8,128)(2,1)S(1)} %add_convert_fusion.2.mine_ref), channel_id=1, source_target_pairs={{0,2},{1,3},{2,0},{3,1},{4,6},{5,7},{6,4},{7,5},{8,10},{9,11},{10,... | collective-permute-start | bytes 1572872 | tf_op jit(solution)/shard_map/ppermute | solution.py:24
  112.9 20.2 %collective-permute-start.15 = (bf16[64,32,128]{2,1,0:T(8,128)(2,1)S(1)}, bf16[64,32,128]{2,1,0:T(8,128)(2,1)S(1)}, u32[]{:S(2)}, u32[]{:S(2)}) collective-permute-start(bf16[64,32,128]{2,1,0:T(8,128)(2,1)S(1)} %get-tuple-element.29.refs_0_), channel_id=1, source_target_pairs={{0,8},{4,12},{8,0},{12,4},{16,24},{20,28},{24,16},{28,20},{1,9},{5... | collective-permute-start | bytes 1572872 | tf_op jit(solution)/shard_map/ppermute | solution.py:24
  112.9 25.3 %collective-permute-start.14 = (bf16[64,32,128]{2,1,0:T(8,128)(2,1)S(1)}, bf16[64,32,128]{2,1,0:T(8,128)(2,1)S(1)}, u32[]{:S(2)}, u32[]{:S(2)}) collective-permute-start(bf16[64,32,128]{2,1,0:T(8,128)(2,1)S(1)} %get-tuple-element.27.refs_0_), channel_id=1, source_target_pairs={{0,16},{4,20},{8,24},{12,28},{16,0},{20,4},{24,8},{28,12},{1,17},{... | collective-permute-start | bytes 1572872 | tf_op jit(solution)/shard_map/ppermute | solution.py:24
  112.9 27.6 %collective-permute-start.16 = (bf16[64,32,128]{2,1,0:T(8,128)(2,1)S(1)}, bf16[64,32,128]{2,1,0:T(8,128)(2,1)S(1)}, u32[]{:S(2)}, u32[]{:S(2)}) collective-permute-start(bf16[64,32,128]{2,1,0:T(8,128)(2,1)S(1)} %get-tuple-element.29.refs_0_), channel_id=1, source_target_pairs={{0,4},{4,0},{8,12},{12,8},{16,20},{20,16},{24,28},{28,24},{1,5},{5... | collective-permute-start | bytes 1572872 | tf_op jit(solution)/shard_map/ppermute | solution.py:24
  133.0 14.9 %collective-permute-start.17 = (bf16[64,32,128]{2,1,0:T(8,128)(2,1)S(1)}, bf16[64,32,128]{2,1,0:T(8,128)(2,1)S(1)}, u32[]{:S(2)}, u32[]{:S(2)}) collective-permute-start(bf16[64,32,128]{2,1,0:T(8,128)(2,1)S(1)} %collective-permute-done.15.refs_1_), channel_id=1, source_target_pairs={{0,4},{4,0},{8,12},{12,8},{16,20},{20,16},{24,28},{28,24},{1,5},{5... | collective-permute-start | bytes 1572872 | tf_op jit(solution)/shard_map/ppermute | solution.py:24
  139.6 19.6 %collective-permute-start.19 = (bf16[64,32,128]{2,1,0:T(8,128)(2,1)S(1)}, bf16[64,32,128]{2,1,0:T(8,128)(2,1)S(1)}, u32[]{:S(2)}, u32[]{:S(2)}) collective-permute-start(bf16[64,32,128]{2,1,0:T(8,128)(2,1)S(1)} %shard_map.68), channel_id=1, source_target_pairs={{0,4},{4,0},{8,12},{12,8},{16,20},{20,16},{24,28},{28,24},{1,5},{5... | collective-permute-start | bytes 1572872 | tf_op jit(solution)/shard_map/ppermute | solution.py:24
  150.7 17.6 %collective-permute-start.18 = (bf16[64,32,128]{2,1,0:T(8,128)(2,1)S(1)}, bf16[64,32,128]{2,1,0:T(8,128)(2,1)S(1)}, u32[]{:S(2)}, u32[]{:S(2)}) collective-permute-start(bf16[64,32,128]{2,1,0:T(8,128)(2,1)S(1)} %shard_map.70), channel_id=1, source_target_pairs={{0,4},{4,0},{8,12},{12,8},{16,20},{20,16},{24,28},{28,24},{1,5},{5... | collective-permute-start | bytes 1572872 | tf_op jit(solution)/shard_map/ppermute | solution.py:24
  151.3 20.9 %collective-permute-start.21 = (bf16[64,32,128]{2,1,0:T(8,128)(2,1)S(1)}, bf16[64,32,128]{2,1,0:T(8,128)(2,1)S(1)}, u32[]{:S(2)}, u32[]{:S(2)}) collective-permute-start(bf16[64,32,128]{2,1,0:T(8,128)(2,1)S(1)} %shard_map.69), channel_id=1, source_target_pairs={{0,16},{4,20},{8,24},{12,28},{16,0},{20,4},{24,8},{28,12},{1,17},{... | collective-permute-start | bytes 1572872 | tf_op jit(solution)/shard_map/ppermute | solution.py:24
  159.3 20.9 %collective-permute-start.20 = (bf16[64,32,128]{2,1,0:T(8,128)(2,1)S(1)}, bf16[64,32,128]{2,1,0:T(8,128)(2,1)S(1)}, u32[]{:S(2)}, u32[]{:S(2)}) collective-permute-start(bf16[64,32,128]{2,1,0:T(8,128)(2,1)S(1)} %add_convert_fusion.1), channel_id=1, source_target_pairs={{0,8},{4,12},{8,0},{12,4},{16,24},{20,28},{24,16},{28,20},{1,9},{5... | collective-permute-start | bytes 1572872 | tf_op jit(solution)/shard_map/ppermute | solution.py:24
  182.6 2.0 collective-permute-start.22
  184.7 14.0 %collective-permute-start.23 = (bf16[32,8192]{1,0:T(8,128)(2,1)S(1)}, bf16[32,8192]{1,0:T(8,128)(2,1)S(1)}, u32[]{:S(2)}, u32[]{:S(2)}) collective-permute-start(bf16[32,8192]{1,0:T(8,128)(2,1)S(1)} %add_convert_fusion.mine_ref), channel_id=1, source_target_pairs={{0,2},{1,3},{2,0},{3,1},{4,6},{5,7},{6,4},{7,5},{8,10},{9,11},{10,... | collective-permute-start | bytes 1572872 | tf_op jit(solution)/shard_map/ppermute | solution.py:24
  (8 other events, 164.2 us)

commit v3 on v2

v3 whole, which is shorter than its diff:
```python
import functools

import jax
import jax.numpy as jnp
from jax import lax
from jax.experimental import pallas as pl
from jax.experimental.pallas import tpu as pltpu
from jax.sharding import PartitionSpec as P

GROUPS = 2
PARTS = 2
TILE_BLOCKS = 8
VMEM_LIMIT = 8 * 1024 * 1024
SIDE, NEXT = 1, 2

ORDER = (
    "As Bs Al Af1",
    "Af2 Ao1 Aw1 Ao2",
    "Az1 Aw2 Bf1 Bf2",
    "Ae Bo1 Bw1 Bo2",
    "Bw2 Bz1 As Be",
    "Af1 Af2 Ao1 Aw1",
    "Bs Ao2 Az1 Aw2",
    "Bf1 Bf2 Ae Bo1",
    "Bw1 Bo2 Bw2 Bz1",
    "Ar Be Br",
)


def params():
    return pltpu.CompilerParams(vmem_limit_bytes=VMEM_LIMIT)


def swap(value, axis, size, mask):
    return lax.ppermute(value, axis, [(i, i ^ mask) for i in range(size)])


def add_bf16(a, b):
    return (a.astype(jnp.float32) + b.astype(jnp.float32)).astype(jnp.bfloat16)


def tree_sum(values):
    values = [v.astype(jnp.float32) for v in values]
    while len(values) > 1:
        values = [values[i] + values[i + 1] for i in range(0, len(values), 2)]
    return values[0]


def project(block_len, scaled, emb_ref, sums_refs):
    count = len(sums_refs)
    part = emb_ref.shape[1] // count
    for b in range(sums_refs[0].shape[0]):
        docs = slice(b * block_len, (b + 1) * block_len)
        sums = jnp.dot(
            scaled[:, docs], emb_ref[docs, :], preferred_element_type=jnp.float32
        ).astype(jnp.bfloat16)
        for i, ref in enumerate(sums_refs):
            ref[b] = sums[:, i * part:(i + 1) * part]


def first_sums_kernel(block_len, vec_ref, quality_ref, emb_ref, *sums_refs):
    scaled = (vec_ref[...] * quality_ref[...]).astype(jnp.bfloat16)
    project(block_len, scaled, emb_ref, sums_refs)


def next_sums_kernel(block_len, nsum, *refs):
    vec_ref, quality_ref, emb_ref = refs[nsum:nsum + 3]
    out_ref, *sums_refs = refs[-1 - PARTS:]
    quality = quality_ref[...]
    out = tree_sum([ref[...] for ref in refs[:nsum]]) * quality - vec_ref[...]
    out_ref[...] = out
    project(block_len, (out * quality).astype(jnp.bfloat16), emb_ref, sums_refs)


def finish_kernel(nsum, *refs):
    first_ref, vec_ref, quality_ref = refs[nsum:nsum + 3]
    total = tree_sum([ref[...] for ref in refs[:nsum]])
    refs[-1][...] = 2.0 * (total * quality_ref[...] - first_ref[...]) - vec_ref[...]


def combine_kernel(ids_ref, *refs):
    *shards, out_ref, table, sems = refs
    blocks = shards[0].shape[0]
    copies = [
        pltpu.make_async_copy(ref, table.at[pl.ds(i * blocks, blocks)], sems.at[i])
        for i, ref in enumerate(shards)
    ]
    for copy in copies:
        copy.start()
    table[len(shards) * blocks] = jnp.zeros(table.shape[1:], table.dtype)
    for copy in copies:
        copy.wait()
    entries = ids_ref.shape[0] // out_ref.shape[0]

    def step(b, carry):
        total = table[ids_ref[b * entries]].astype(jnp.float32)
        for k in range(1, entries):
            total = total + table[ids_ref[b * entries + k]].astype(jnp.float32)
        out_ref[b] = total.astype(out_ref.dtype)
        return carry

    lax.fori_loop(0, out_ref.shape[0], step, 0, unroll=4)


def expand_kernel(block_len, counts, *refs):
    *refs, emb_ref, out_ref = refs
    for b in range(refs[0].shape[0]):
        docs = slice(b * block_len, (b + 1) * block_len)
        parts, at = [], 0
        for count in counts:
            total = refs[at][b]
            for ref in refs[at + 1:at + count]:
                total = total + ref[b].astype(jnp.float32)
            parts.append(total.astype(jnp.bfloat16))
            at += count
        out_ref[:, docs] = lax.dot_general(
            jnp.concatenate(parts, axis=1), emb_ref[docs, :], (((1,), (1,)), ((), ())),
            preferred_element_type=jnp.float32,
        ).astype(jnp.bfloat16)


def body(embeddings, quality, probes, neighbors):
    nrow, ncol = lax.axis_size("row"), lax.axis_size("col")
    me = lax.axis_index("row")
    blk_count, list_len = neighbors.shape
    docs, width = embeddings.shape
    block_len = docs // blk_count
    nprobe = probes.shape[0]
    group, part = nprobe // GROUPS, width // PARTS
    reduce_bits = [1 << i for i in reversed(range(nrow.bit_length() - 1)) if 1 << i not in (SIDE, NEXT)]
    dests = [0]
    for m in reversed(reduce_bits):
        dests = [d | m for d in dests] + dests
    shards = (0, NEXT, SIDE, NEXT | SIDE)

    def table_ids(lists):
        flat = lists.reshape(-1)
        apart = (flat // blk_count) ^ me
        place = flat % blk_count
        for i, shard in enumerate(shards):
            place = jnp.where(apart == shard, i * blk_count + flat % blk_count, place)
        return jnp.where((apart & ~(NEXT | SIDE)) == 0, place, len(shards) * blk_count)

    qrow = quality[None, :]
    tile_docs = TILE_BLOCKS * block_len
    steps = blk_count // TILE_BLOCKS
    shard_shape = (blk_count, group, part)
    nsum = ncol
    emb_spec = pl.BlockSpec((tile_docs, width), lambda j: (j, 0))
    vec_spec = pl.BlockSpec((group, tile_docs), lambda j: (0, j))
    q_spec = pl.BlockSpec((1, tile_docs), lambda j: (0, j))
    shard_spec = pl.BlockSpec((TILE_BLOCKS, group, part), lambda j: (j, 0, 0))
    any_spec = pl.BlockSpec(memory_space=pl.ANY)
    shard_out = jax.ShapeDtypeStruct(shard_shape, jnp.bfloat16)
    vec_out = jax.ShapeDtypeStruct((nprobe, docs), jnp.float32)

    def group_spec(c):
        return pl.BlockSpec((group, tile_docs), lambda j: (c, j))

    def first_sums(c, qrow):
        return pl.pallas_call(
            functools.partial(first_sums_kernel, block_len),
            grid=(steps,),
            in_specs=[group_spec(c), q_spec, emb_spec],
            out_specs=[shard_spec] * PARTS,
            out_shape=[shard_out] * PARTS,
            compiler_params=params(),
        )(probes, qrow, embeddings)

    def next_sums(c, first, values):
        held = [] if first is None else [first]
        first, *sums = pl.pallas_call(
            functools.partial(next_sums_kernel, block_len, nsum),
            grid=(steps,),
            in_specs=[vec_spec] * nsum + [group_spec(c), q_spec, emb_spec] + [any_spec] * len(held),
            out_specs=[group_spec(c)] + [shard_spec] * PARTS,
            out_shape=[vec_out] + [shard_out] * PARTS,
            input_output_aliases={nsum + 3: 0} if held else {},
            compiler_params=params(),
        )(*values, probes, qrow, embeddings, *held)
        return first, sums

    def finish(c, first, second, values):
        held = [] if second is None else [second]
        wide = pl.BlockSpec((group, 2 * tile_docs), lambda j: (0, j))
        here = pl.BlockSpec((group, 2 * tile_docs), lambda j: (c, j))
        wide_q = pl.BlockSpec((1, 2 * tile_docs), lambda j: (0, j))
        return pl.pallas_call(
            functools.partial(finish_kernel, nsum),
            grid=(steps // 2,),
            in_specs=[wide] * nsum + [here, here, wide_q] + [any_spec] * len(held),
            out_specs=here,
            out_shape=vec_out,
            input_output_aliases={nsum + 3: 0} if held else {},
            compiler_params=params(),
        )(*values, first, probes, qrow, *held)

    def combine(ids, shards, dtype):
        count = len(shards)
        return pl.pallas_call(
            combine_kernel,
            in_specs=[pl.BlockSpec(memory_space=pltpu.SMEM)] + [any_spec] * count,
            out_specs=pl.BlockSpec(memory_space=pltpu.VMEM),
            out_shape=jax.ShapeDtypeStruct(shard_shape, dtype),
            scratch_shapes=[
                pltpu.VMEM((count * blk_count + 1, group, part), jnp.bfloat16),
                pltpu.SemaphoreType.DMA((count,)),
            ],
            compiler_params=params(),
        )(ids, *shards)

    def expand(parts):
        values = [v for values in parts for v in values]
        return pl.pallas_call(
            functools.partial(expand_kernel, block_len, [len(values) for values in parts]),
            grid=(steps,),
            in_specs=[shard_spec] * len(values) + [emb_spec],
            out_specs=vec_spec,
            out_shape=jax.ShapeDtypeStruct((group, docs), jnp.bfloat16),
            compiler_params=params(),
        )(*values, embeddings)

    def reduce(outgoing):
        arrived = []
        for m in reduce_bits:
            taken = {d ^ m: swap(outgoing.pop(d), "row", nrow, m) for d in list(outgoing) if d & m}
            for d, value in taken.items():
                if d:
                    outgoing[d] = add_bf16(outgoing[d], value)
                else:
                    arrived.append(value)
        return arrived

    token = []

    def take(*values):
        if token:
            values = lax.optimization_barrier(values + (token.pop(),))[:-1]
        return values

    lists = {d: swap(neighbors, "row", nrow, d) if d else neighbors for d in dests}
    first = second = None
    tables = [[None] * PARTS for _ in range(GROUPS)]
    own = [[None] * PARTS for _ in range(GROUPS)]
    arrived = [[None] * PARTS for _ in range(GROUPS)]
    products = [None] * GROUPS
    for word in (word for line in ORDER for word in line.split()):
        c, step, p = ord(word[0]) - ord("A"), word[1], int(word[2:] or 0) - 1
        if step == "l":
            taken = take(*(lists[d] for d in dests))
            ids = dict(zip(dests, lax.optimization_barrier(tuple(table_ids(v) for v in taken))))
            token.append(ids[0])
        elif step == "s":
            if products[c] is None:
                sums = first_sums(c, *take(qrow))
            else:
                first, sums = next_sums(c, first, take(*products[c]))
            token.append(sums[0])
            for i, value in enumerate(sums):
                tables[c][i] = {0: value}
                for m in (NEXT, SIDE):
                    tables[c][i][m] = swap(value, "row", nrow, m)
        elif step == "f":
            table = tables[c][p]
            table[NEXT], table[SIDE] = take(table[NEXT], table[SIDE])
            table[NEXT | SIDE] = swap(table[NEXT], "row", nrow, SIDE)
            token.append(table[NEXT])
        elif step == "o":
            tables[c][p] = take(*(tables[c][p][m] for m in shards))
            outgoing = {d: combine(ids[d], tables[c][p], jnp.bfloat16) for d in dests if d}
            token.append(outgoing[reduce_bits[-1]])
            arrived[c][p] = reduce(outgoing)
        elif step == "w":
            own[c][p] = combine(ids[0], take(*tables[c][p]), jnp.float32)
            token.append(own[c][p])
        elif step == "z":
            arrived[c][p] = take(*arrived[c][p])
            token.append(arrived[c][p][-1])
        elif step == "e":
            flat = take(*own[c], *(v for values in arrived[c] for v in values))
            later = [flat[PARTS + i * len(reduce_bits):PARTS + (i + 1) * len(reduce_bits)] for i in range(PARTS)]
            value = expand([(flat[i], *later[i]) for i in range(PARTS)])
            products[c] = [value] + [swap(value, "col", ncol, m) for m in range(1, ncol)]
            token.append(value)
        else:
            second = finish(c, first, second, take(*products[c]))
            token.append(second)
    return first, second


def solution(mesh):
    placed = (P("row", "col"), P("row"), P(None, "row"), P("row", None))
    return jax.shard_map(
        body,
        mesh=mesh,
        in_specs=placed,
        out_specs=(P(None, "row"), P(None, "row")),
        check_vma=False,
    )
```

time: 201 us -> 181 us (0.900)
  waiting for transfers between devices: 142 us -> 80.9 us
  starting transfers between devices: 17 us -> 51.7 us
  Pallas kernels: 33.5 us -> 42.1 us
  other arithmetic: 2.43 us -> 0.02 us
    ppermute x24 -> x45, waiting for transfers between devices: 142 us -> 80.9 us  [swap(): return lax.ppermute(value, axis, [(i, i ^ mask) for i in range(size)])]
    ppermute x24 -> x45, starting transfers between devices: 17 us -> 51.7 us  [swap(): return lax.ppermute(value, axis, [(i, i ^ mask) for i in range(size)])]
    pallas_call x4 -> x8, Pallas kernels: 12.6 us -> 17.8 us  [the longest x4 8.33 us: expand(): pl.pallas_call(functools.partial(expand_kernel, block_len, [len(values) f...]
    convert_element_type x4 -> x0, other arithmetic: 2.36 us -> none  [add_bf16(): return (a.astype(jnp.float32) + b.astype(jnp.float32)).astype(jnp.bfloat16)]
    pallas_call x12 -> x16, Pallas kernels: 19.1 us -> 21.2 us  [combine(): pl.pallas_call(combine_kernel, in_specs=[pl.BlockSpec(memory_space=pltpu....]
    unnamed x17 -> x16, local copies, waits for them, and re-layouts: 4.28 us -> 4.19 us
  transfers between devices with their start and end apart: 24 -> 45, of which waited for: 21 -> 20; matrix products, arithmetic and copies ran while one was open for 2% -> 0% of each run, Pallas kernels for 10% -> 20%
where the time goes in v3:
time: 181 us; the launch traced here: 180 us
  waiting for transfers between devices  80.9 us (45%)
  starting transfers between devices  51.7 us (29%)
  Pallas kernels  42.1 us (23%)
  local copies, waits for them, and re-layouts  4.54 us (3%)
    ppermute x45, waiting for transfers between devices, swap(): return lax.ppermute(value, axis, [(i, i ^ mask) for i in range(size)])  80.9 us
    ppermute x45, starting transfers between devices, swap(): return lax.ppermute(value, axis, [(i, i ^ mask) for i in range(size)])  51.7 us
    pallas_call x16, Pallas kernels, combine(): pl.pallas_call(combine_kernel, in_specs=[pl.BlockSpec(memory_space=pltpu....  21.2 us
    pallas_call x4, Pallas kernels, expand(): pl.pallas_call(functools.partial(expand_kernel, block_len, [len(values) f...  8.33 us
    pallas_call x2, Pallas kernels, next_sums(): pl.pallas_call(functools.partial(next_sums_kernel, block_len, nsum), grid...  6.18 us
    unnamed x16, local copies, waits for them, and re-layouts  4.19 us
  transfers between devices with their start and end apart: 45, of which 20 were waited for; matrix products, arithmetic and copies ran while one was open for 0% of the time, Pallas kernels for 20%

profile of v3, /device:TPU:0, one launch (start us, length us, event | category | flops | bytes accessed | tf_op | source)
XLA Modules:
  0.0 180.3 jit_solution(8202411504342619684)
XLA Ops:
  0.6 2.2 %copy-done = bf16[8192,256]{1,0:T(8,128)(2,1)S(1)} copy-done((bf16[8192,256]{1,0:T(8,128)(2,1)S(1)}, bf16[8192,256]{1,0:T(8,128)(2,1)}, u32[]{:S(2)}) %copy-start) | copy-done | bytes 4194328
  6.3 3.1 %collective-permute-start.5 = (bf16[64,16,128]{2,1,0:T(8,128)(2,1)S(1)}, bf16[64,16,128]{2,1,0:T(8,128)(2,1)S(1)}, u32[]{:S(2)}, u32[]{:S(2)}) collective-permute-start(bf16[64,16,128]{2,1,0:T(8,128)(2,1)S(1)} %get-tuple-element.149.refs_0_), channel_id=1, source_target_pairs={{0,8},{4,12},{8,0},{12,4},{16,24},{20,28},{24,16},{28,20},{1,9},{5... | collective-permute-start | bytes 786440 | tf_op jit(solution)/shard_map/ppermute | solution.py:35
  11.0 2.6 %collective-permute-start = (s32[64,8]{0,1:T(8,128)S(1)}, s32[64,8]{0,1:T(8,128)S(1)}, u32[]{:S(2)}, u32[]{:S(2)}) collective-permute-start(s32[64,8]{0,1:T(8,128)S(1)} %copy-done.7), channel_id=1, source_target_pairs={{0,16},{4,20},{8,24},{12,28},{16,0},{20,4},{24,8},{28,12},{1,17},{... | collective-permute-start | bytes 6152 | tf_op jit(solution)/shard_map/ppermute | solution.py:35
  21.4 2.8 %collective-permute-done.4.refs_2_ = bf16[64,16,128]{2,1,0:T(8,128)(2,1)S(1)} collective-permute-done((bf16[64,16,128]{2,1,0:T(8,128)(2,1)S(1)}, bf16[64,16,128]{2,1,0:T(8,128)(2,1)S(1)}, u32[]{:S(2)}, u32[]{:S(2)}) %collective-permute-start.4) | collective-permute-done | bytes 262176 | tf_op jit(solution)/shard_map/ppermute | solution.py:35
  25.8 4.1 %collective-permute-done.8.refs_3_ = bf16[64,16,128]{2,1,0:T(8,128)(2,1)S(1)} collective-permute-done((bf16[64,16,128]{2,1,0:T(8,128)(2,1)S(1)}, bf16[64,16,128]{2,1,0:T(8,128)(2,1)S(1)}, u32[]{:S(2)}, u32[]{:S(2)}) %collective-permute-start.8) | collective-permute-done | bytes 262176 | tf_op jit(solution)/shard_map/ppermute | solution.py:35
  31.2 2.7 %collective-permute-start.9 = (bf16[64,16,128]{2,1,0:T(8,128)(2,1)S(1)}, bf16[64,16,128]{2,1,0:T(8,128)(2,1)S(1)}, u32[]{:S(2)}, u32[]{:S(2)}) collective-permute-start(bf16[64,16,128]{2,1,0:T(8,128)(2,1)S(1)} %shard_map.61), channel_id=1, source_target_pairs={{0,16},{4,20},{8,24},{12,28},{16,0},{20,4},{24,8},{28,12},{1,17},{... | collective-permute-start | bytes 786440 | tf_op jit(solution)/shard_map/ppermute | solution.py:35
  40.7 2.5 %collective-permute-done.9.refs_1_ = bf16[64,16,128]{2,1,0:T(8,128)(2,1)S(1)} collective-permute-done((bf16[64,16,128]{2,1,0:T(8,128)(2,1)S(1)}, bf16[64,16,128]{2,1,0:T(8,128)(2,1)S(1)}, u32[]{:S(2)}, u32[]{:S(2)}) %collective-permute-start.9) | collective-permute-done | bytes 262176 | tf_op jit(solution)/shard_map/ppermute | solution.py:35
  45.4 2.7 %collective-permute-done.1.refs_1_ = bf16[64,16,128]{2,1,0:T(8,128)(2,1)S(1)} collective-permute-done((bf16[64,16,128]{2,1,0:T(8,128)(2,1)S(1)}, bf16[64,16,128]{2,1,0:T(8,128)(2,1)S(1)}, u32[]{:S(2)}, u32[]{:S(2)}) %collective-permute-start.1) | collective-permute-done | bytes 262176 | tf_op jit(solution)/shard_map/ppermute | solution.py:35
  49.6 3.9 %collective-permute-done.12.refs_1_ = bf16[64,16,128]{2,1,0:T(8,128)(2,1)S(1)} collective-permute-done((bf16[64,16,128]{2,1,0:T(8,128)(2,1)S(1)}, bf16[64,16,128]{2,1,0:T(8,128)(2,1)S(1)}, u32[]{:S(2)}, u32[]{:S(2)}) %collective-permute-start.12) | collective-permute-done | bytes 262176 | tf_op jit(solution)/shard_map/ppermute | solution.py:35
  65.3 2.5 %collective-permute-start.16 = (bf16[64,16,128]{2,1,0:T(8,128)(2,1)S(1)}, bf16[64,16,128]{2,1,0:T(8,128)(2,1)S(1)}, u32[]{:S(2)}, u32[]{:S(2)}) collective-permute-start(bf16[64,16,128]{2,1,0:T(8,128)(2,1)S(1)} %shard_map.68), channel_id=1, source_target_pairs={{0,16},{4,20},{8,24},{12,28},{16,0},{20,4},{24,8},{28,12},{1,17},{... | collective-permute-start | bytes 786440 | tf_op jit(solution)/shard_map/ppermute | solution.py:35
  69.0 9.4 %collective-permute-done.15.refs_1_ = bf16[64,16,128]{2,1,0:T(8,128)(2,1)S(1)} collective-permute-done((bf16[64,16,128]{2,1,0:T(8,128)(2,1)S(1)}, bf16[64,16,128]{2,1,0:T(8,128)(2,1)S(1)}, u32[]{:S(2)}, u32[]{:S(2)}) %collective-permute-start.15) | collective-permute-done | bytes 262176 | tf_op jit(solution)/shard_map/ppermute | solution.py:35
  78.4 3.1 %shard_map.70 = (f32[32,8192]{1,0:T(8,128)}, bf16[64,16,128]{2,1,0:T(8,128)(2,1)S(1)}, bf16[64,16,128]{2,1,0:T(8,128)(2,1)S(1)}) custom-call(bf16[16,8192]{1,0:T(8,128)(2,1)S(1)} %shard_map.65.refs_0_, bf16[16,8192]{1,0:T(8,128)(2,1)S(1)} %collective-permute-done.17.refs_1_, bf16[16,8192]{1,0:T(8,128)(2,1)S(1)} %collective-permute-done.18.refs_2_, ...), custom_call_target="tpu_custom_call" | custom-call | tf_op jit(solution)/shard_map/pallas_call | solution.py:172
  87.7 3.1 %collective-permute-done.23.refs_1_ = bf16[64,16,128]{2,1,0:T(8,128)(2,1)S(1)} collective-permute-done((bf16[64,16,128]{2,1,0:T(8,128)(2,1)S(1)}, bf16[64,16,128]{2,1,0:T(8,128)(2,1)S(1)}, u32[]{:S(2)}, u32[]{:S(2)}) %collective-permute-start.23) | collective-permute-done | bytes 262176 | tf_op jit(solution)/shard_map/ppermute | solution.py:35
  94.2 2.2 %collective-permute-done.27.refs_2_ = bf16[64,16,128]{2,1,0:T(8,128)(2,1)S(1)} collective-permute-done((bf16[64,16,128]{2,1,0:T(8,128)(2,1)S(1)}, bf16[64,16,128]{2,1,0:T(8,128)(2,1)S(1)}, u32[]{:S(2)}, u32[]{:S(2)}) %collective-permute-start.27) | collective-permute-done | bytes 262176 | tf_op jit(solution)/shard_map/ppermute | solution.py:35
  97.9 3.5 %collective-permute-done.25.refs_3_ = bf16[64,16,128]{2,1,0:T(8,128)(2,1)S(1)} collective-permute-done((bf16[64,16,128]{2,1,0:T(8,128)(2,1)S(1)}, bf16[64,16,128]{2,1,0:T(8,128)(2,1)S(1)}, u32[]{:S(2)}, u32[]{:S(2)}) %collective-permute-start.25) | collective-permute-done | bytes 262176 | tf_op jit(solution)/shard_map/ppermute | solution.py:35
  104.2 2.1 %collective-permute-done.22.refs_3_ = bf16[16,8192]{1,0:T(8,128)(2,1)S(1)} collective-permute-done((bf16[16,8192]{1,0:T(8,128)(2,1)S(1)}, bf16[16,8192]{1,0:T(8,128)(2,1)S(1)}, u32[]{:S(2)}, u32[]{:S(2)}) %collective-permute-start.22) | collective-permute-done | bytes 262176 | tf_op jit(solution)/shard_map/ppermute | solution.py:35
  106.3 3.1 %shard_map.74 = (f32[32,8192]{1,0:T(8,128)}, bf16[64,16,128]{2,1,0:T(8,128)(2,1)S(1)}, bf16[64,16,128]{2,1,0:T(8,128)(2,1)S(1)}) custom-call(bf16[16,8192]{1,0:T(8,128)(2,1)S(1)} %shard_map.71.refs_0_, bf16[16,8192]{1,0:T(8,128)(2,1)S(1)} %collective-permute-done.20.refs_1_, ...), custom_call_target="tpu_custom_call", output_to_operand_aliasing={{0}: (7, {})} | custom-call | tf_op jit(solution)/shard_map/pallas_call | solution.py:172
  114.7 2.6 %collective-permute-start.33 = (bf16[64,16,128]{2,1,0:T(8,128)(2,1)S(1)}, bf16[64,16,128]{2,1,0:T(8,128)(2,1)S(1)}, u32[]{:S(2)}, u32[]{:S(2)}) collective-permute-start(bf16[64,16,128]{2,1,0:T(8,128)(2,1)S(1)} %shard_map.75), channel_id=1, source_target_pairs={{0,16},{4,20},{8,24},{12,28},{16,0},{20,4},{24,8},{28,12},{1,17},{... | collective-permute-start | bytes 786440 | tf_op jit(solution)/shard_map/ppermute | solution.py:35
  118.7 5.4 %collective-permute-done.28.refs_1_ = bf16[64,16,128]{2,1,0:T(8,128)(2,1)S(1)} collective-permute-done((bf16[64,16,128]{2,1,0:T(8,128)(2,1)S(1)}, bf16[64,16,128]{2,1,0:T(8,128)(2,1)S(1)}, u32[]{:S(2)}, u32[]{:S(2)}) %collective-permute-start.28) | collective-permute-done | bytes 262176 | tf_op jit(solution)/shard_map/ppermute | solution.py:35
  125.0 4.5 %collective-permute-done.34.refs_1_ = bf16[64,16,128]{2,1,0:T(8,128)(2,1)S(1)} collective-permute-done((bf16[64,16,128]{2,1,0:T(8,128)(2,1)S(1)}, bf16[64,16,128]{2,1,0:T(8,128)(2,1)S(1)}, u32[]{:S(2)}, u32[]{:S(2)}) %collective-permute-start.34) | collective-permute-done | bytes 262176 | tf_op jit(solution)/shard_map/ppermute | solution.py:35
  143.2 14.3 %collective-permute-done.37.refs_1_ = bf16[64,16,128]{2,1,0:T(8,128)(2,1)S(1)} collective-permute-done((bf16[64,16,128]{2,1,0:T(8,128)(2,1)S(1)}, bf16[64,16,128]{2,1,0:T(8,128)(2,1)S(1)}, u32[]{:S(2)}, u32[]{:S(2)}) %collective-permute-start.37) | collective-permute-done | bytes 262176 | tf_op jit(solution)/shard_map/ppermute | solution.py:35
  159.2 3.3 %collective-permute-done.38.refs_3_ = bf16[64,16,128]{2,1,0:T(8,128)(2,1)S(1)} collective-permute-done((bf16[64,16,128]{2,1,0:T(8,128)(2,1)S(1)}, bf16[64,16,128]{2,1,0:T(8,128)(2,1)S(1)}, u32[]{:S(2)}, u32[]{:S(2)}) %collective-permute-start.38) | collective-permute-done | bytes 262176 | tf_op jit(solution)/shard_map/ppermute | solution.py:35
  166.6 7.2 %collective-permute-done.43.refs_2_ = bf16[16,8192]{1,0:T(8,128)(2,1)S(1)} collective-permute-done((bf16[16,8192]{1,0:T(8,128)(2,1)S(1)}, bf16[16,8192]{1,0:T(8,128)(2,1)S(1)}, u32[]{:S(2)}, u32[]{:S(2)}) %collective-permute-start.43) | collective-permute-done | bytes 262176 | tf_op jit(solution)/shard_map/ppermute | solution.py:35
  173.8 4.9 %collective-permute-done.44.refs_3_ = bf16[16,8192]{1,0:T(8,128)(2,1)S(1)} collective-permute-done((bf16[16,8192]{1,0:T(8,128)(2,1)S(1)}, bf16[16,8192]{1,0:T(8,128)(2,1)S(1)}, u32[]{:S(2)}, u32[]{:S(2)}) %collective-permute-start.44) | collective-permute-done | bytes 262176 | tf_op jit(solution)/shard_map/ppermute | solution.py:35
  (113 shorter events, 81.7 us)
Async XLA Ops:
  24.3 14.5 %collective-permute-start.7 = (bf16[64,16,128]{2,1,0:T(8,128)(2,1)S(1)}, bf16[64,16,128]{2,1,0:T(8,128)(2,1)S(1)}, u32[]{:S(2)}, u32[]{:S(2)}) collective-permute-start(bf16[64,16,128]{2,1,0:T(8,128)(2,1)S(1)} %collective-permute-done.3.refs_1_), channel_id=1, source_target_pairs={{0,4},{4,0},{8,12},{12,8},{16,20},{20,16},{24,28},{28,24},{1,5},{5... | collective-permute-start | bytes 786440 | tf_op jit(solution)/shard_map/ppermute | solution.py:35
  33.9 14.2 %collective-permute-start.1 = (bf16[64,16,128]{2,1,0:T(8,128)(2,1)S(1)}, bf16[64,16,128]{2,1,0:T(8,128)(2,1)S(1)}, u32[]{:S(2)}, u32[]{:S(2)}) collective-permute-start(bf16[64,16,128]{2,1,0:T(8,128)(2,1)S(1)} %get-tuple-element.174.refs_0_), channel_id=1, source_target_pairs={{0,8},{4,12},{8,0},{12,4},{16,24},{20,28},{24,16},{28,20},{1,9},{5... | collective-permute-start | bytes 786440 | tf_op jit(solution)/shard_map/ppermute | solution.py:35
  34.3 13.7 %collective-permute-start.2 = (bf16[64,16,128]{2,1,0:T(8,128)(2,1)S(1)}, bf16[64,16,128]{2,1,0:T(8,128)(2,1)S(1)}, u32[]{:S(2)}, u32[]{:S(2)}) collective-permute-start(bf16[64,16,128]{2,1,0:T(8,128)(2,1)S(1)} %get-tuple-element.174.refs_0_), channel_id=1, source_target_pairs={{0,4},{4,0},{8,12},{12,8},{16,20},{20,16},{24,28},{28,24},{1,5},{5... | collective-permute-start | bytes 786440 | tf_op jit(solution)/shard_map/ppermute | solution.py:35
  35.9 17.7 %collective-permute-start.12 = (bf16[64,16,128]{2,1,0:T(8,128)(2,1)S(1)}, bf16[64,16,128]{2,1,0:T(8,128)(2,1)S(1)}, u32[]{:S(2)}, u32[]{:S(2)}) collective-permute-start(bf16[64,16,128]{2,1,0:T(8,128)(2,1)S(1)} %get-tuple-element.183.refs_0_), channel_id=1, source_target_pairs={{0,8},{4,12},{8,0},{12,4},{16,24},{20,28},{24,16},{28,20},{1,9},{5... | collective-permute-start | bytes 786440 | tf_op jit(solution)/shard_map/ppermute | solution.py:35
  38.8 14.8 %collective-permute-start.13 = (bf16[64,16,128]{2,1,0:T(8,128)(2,1)S(1)}, bf16[64,16,128]{2,1,0:T(8,128)(2,1)S(1)}, u32[]{:S(2)}, u32[]{:S(2)}) collective-permute-start(bf16[64,16,128]{2,1,0:T(8,128)(2,1)S(1)} %get-tuple-element.183.refs_0_), channel_id=1, source_target_pairs={{0,4},{4,0},{8,12},{12,8},{16,20},{20,16},{24,28},{28,24},{1,5},{5... | collective-permute-start | bytes 786440 | tf_op jit(solution)/shard_map/ppermute | solution.py:35
  43.1 13.5 %collective-permute-start.11 = (bf16[64,16,128]{2,1,0:T(8,128)(2,1)S(1)}, bf16[64,16,128]{2,1,0:T(8,128)(2,1)S(1)}, u32[]{:S(2)}, u32[]{:S(2)}) collective-permute-start(bf16[64,16,128]{2,1,0:T(8,128)(2,1)S(1)} %shard_map.63), channel_id=1, source_target_pairs={{0,16},{4,20},{8,24},{12,28},{16,0},{20,4},{24,8},{28,12},{1,17},{... | collective-permute-start | bytes 786440 | tf_op jit(solution)/shard_map/ppermute | solution.py:35
  60.1 18.3 %collective-permute-start.15 = (bf16[64,16,128]{2,1,0:T(8,128)(2,1)S(1)}, bf16[64,16,128]{2,1,0:T(8,128)(2,1)S(1)}, u32[]{:S(2)}, u32[]{:S(2)}) collective-permute-start(bf16[64,16,128]{2,1,0:T(8,128)(2,1)S(1)} %shard_map.66), channel_id=1, source_target_pairs={{0,16},{4,20},{8,24},{12,28},{16,0},{20,4},{24,8},{28,12},{1,17},{... | collective-permute-start | bytes 786440 | tf_op jit(solution)/shard_map/ppermute | solution.py:35
  60.7 17.7 %collective-permute-start.17 = (bf16[16,8192]{1,0:T(8,128)(2,1)S(1)}, bf16[16,8192]{1,0:T(8,128)(2,1)S(1)}, u32[]{:S(2)}, u32[]{:S(2)}) collective-permute-start(bf16[16,8192]{1,0:T(8,128)(2,1)S(1)} %shard_map.65.refs_0_), channel_id=1, source_target_pairs={{0,1},{1,0},{2,3},{3,2},{4,5},{5,4},{6,7},{7,6},{8,9},{9,8},{10,11... | collective-permute-start | bytes 786440 | tf_op jit(solution)/shard_map/ppermute | solution.py:35
  60.7 17.7 %collective-permute-start.18 = (bf16[16,8192]{1,0:T(8,128)(2,1)S(1)}, bf16[16,8192]{1,0:T(8,128)(2,1)S(1)}, u32[]{:S(2)}, u32[]{:S(2)}) collective-permute-start(bf16[16,8192]{1,0:T(8,128)(2,1)S(1)} %shard_map.65.refs_0_), channel_id=1, source_target_pairs={{0,2},{1,3},{2,0},{3,1},{4,6},{5,7},{6,4},{7,5},{8,10},{9,11},{10,... | collective-permute-start | bytes 786440 | tf_op jit(solution)/shard_map/ppermute | solution.py:35
  62.2 16.2 %collective-permute-start.19 = (bf16[16,8192]{1,0:T(8,128)(2,1)S(1)}, bf16[16,8192]{1,0:T(8,128)(2,1)S(1)}, u32[]{:S(2)}, u32[]{:S(2)}) collective-permute-start(bf16[16,8192]{1,0:T(8,128)(2,1)S(1)} %shard_map.65.refs_0_), channel_id=1, source_target_pairs={{0,3},{1,2},{2,1},{3,0},{4,7},{5,6},{6,5},{7,4},{8,11},{9,10},{10,... | collective-permute-start | bytes 786440 | tf_op jit(solution)/shard_map/ppermute | solution.py:35
  65.3 20.3 %collective-permute-start.16 = (bf16[64,16,128]{2,1,0:T(8,128)(2,1)S(1)}, bf16[64,16,128]{2,1,0:T(8,128)(2,1)S(1)}, u32[]{:S(2)}, u32[]{:S(2)}) collective-permute-start(bf16[64,16,128]{2,1,0:T(8,128)(2,1)S(1)} %shard_map.68), channel_id=1, source_target_pairs={{0,16},{4,20},{8,24},{12,28},{16,0},{20,4},{24,8},{28,12},{1,17},{... | collective-permute-start | bytes 786440 | tf_op jit(solution)/shard_map/ppermute | solution.py:35
  93.8 12.5 %collective-permute-start.22 = (bf16[16,8192]{1,0:T(8,128)(2,1)S(1)}, bf16[16,8192]{1,0:T(8,128)(2,1)S(1)}, u32[]{:S(2)}, u32[]{:S(2)}) collective-permute-start(bf16[16,8192]{1,0:T(8,128)(2,1)S(1)} %shard_map.71.refs_0_), channel_id=1, source_target_pairs={{0,3},{1,2},{2,1},{3,0},{4,7},{5,6},{6,5},{7,4},{8,11},{9,10},{10,... | collective-permute-start | bytes 786440 | tf_op jit(solution)/shard_map/ppermute | solution.py:35
  96.4 15.5 %collective-permute-start.30 = (bf16[64,16,128]{2,1,0:T(8,128)(2,1)S(1)}, bf16[64,16,128]{2,1,0:T(8,128)(2,1)S(1)}, u32[]{:S(2)}, u32[]{:S(2)}) collective-permute-start(bf16[64,16,128]{2,1,0:T(8,128)(2,1)S(1)} %collective-permute-done.26.refs_1_), channel_id=1, source_target_pairs={{0,4},{4,0},{8,12},{12,8},{16,20},{20,16},{24,28},{28,24},{1,5},{5... | collective-permute-start | bytes 786440 | tf_op jit(solution)/shard_map/ppermute | solution.py:35
  109.3 14.8 %collective-permute-start.28 = (bf16[64,16,128]{2,1,0:T(8,128)(2,1)S(1)}, bf16[64,16,128]{2,1,0:T(8,128)(2,1)S(1)}, u32[]{:S(2)}, u32[]{:S(2)}) collective-permute-start(bf16[64,16,128]{2,1,0:T(8,128)(2,1)S(1)} %get-tuple-element.238.refs_0_), channel_id=1, source_target_pairs={{0,8},{4,12},{8,0},{12,4},{16,24},{20,28},{24,16},{28,20},{1,9},{5... | collective-permute-start | bytes 786440 | tf_op jit(solution)/shard_map/ppermute | solution.py:35
  111.4 12.8 %collective-permute-start.29 = (bf16[64,16,128]{2,1,0:T(8,128)(2,1)S(1)}, bf16[64,16,128]{2,1,0:T(8,128)(2,1)S(1)}, u32[]{:S(2)}, u32[]{:S(2)}) collective-permute-start(bf16[64,16,128]{2,1,0:T(8,128)(2,1)S(1)} %get-tuple-element.238.refs_0_), channel_id=1, source_target_pairs={{0,4},{4,0},{8,12},{12,8},{16,20},{20,16},{24,28},{28,24},{1,5},{5... | collective-permute-start | bytes 786440 | tf_op jit(solution)/shard_map/ppermute | solution.py:35
  111.9 17.7 %collective-permute-start.34 = (bf16[64,16,128]{2,1,0:T(8,128)(2,1)S(1)}, bf16[64,16,128]{2,1,0:T(8,128)(2,1)S(1)}, u32[]{:S(2)}, u32[]{:S(2)}) collective-permute-start(bf16[64,16,128]{2,1,0:T(8,128)(2,1)S(1)} %get-tuple-element.247.refs_0_), channel_id=1, source_target_pairs={{0,8},{4,12},{8,0},{12,4},{16,24},{20,28},{24,16},{28,20},{1,9},{5... | collective-permute-start | bytes 786440 | tf_op jit(solution)/shard_map/ppermute | solution.py:35
  111.9 17.7 %collective-permute-start.35 = (bf16[64,16,128]{2,1,0:T(8,128)(2,1)S(1)}, bf16[64,16,128]{2,1,0:T(8,128)(2,1)S(1)}, u32[]{:S(2)}, u32[]{:S(2)}) collective-permute-start(bf16[64,16,128]{2,1,0:T(8,128)(2,1)S(1)} %get-tuple-element.247.refs_0_), channel_id=1, source_target_pairs={{0,4},{4,0},{8,12},{12,8},{16,20},{20,16},{24,28},{28,24},{1,5},{5... | collective-permute-start | bytes 786440 | tf_op jit(solution)/shard_map/ppermute | solution.py:35
  114.7 15.9 %collective-permute-start.33 = (bf16[64,16,128]{2,1,0:T(8,128)(2,1)S(1)}, bf16[64,16,128]{2,1,0:T(8,128)(2,1)S(1)}, u32[]{:S(2)}, u32[]{:S(2)}) collective-permute-start(bf16[64,16,128]{2,1,0:T(8,128)(2,1)S(1)} %shard_map.75), channel_id=1, source_target_pairs={{0,16},{4,20},{8,24},{12,28},{16,0},{20,4},{24,8},{28,12},{1,17},{... | collective-permute-start | bytes 786440 | tf_op jit(solution)/shard_map/ppermute | solution.py:35
  132.8 24.7 %collective-permute-start.39 = (bf16[16,8192]{1,0:T(8,128)(2,1)S(1)}, bf16[16,8192]{1,0:T(8,128)(2,1)S(1)}, u32[]{:S(2)}, u32[]{:S(2)}) collective-permute-start(bf16[16,8192]{1,0:T(8,128)(2,1)S(1)} %shard_map.77.refs_0_), channel_id=1, source_target_pairs={{0,1},{1,0},{2,3},{3,2},{4,5},{5,4},{6,7},{7,6},{8,9},{9,8},{10,11... | collective-permute-start | bytes 786440 | tf_op jit(solution)/shard_map/ppermute | solution.py:35
  132.8 24.6 %collective-permute-start.40 = (bf16[16,8192]{1,0:T(8,128)(2,1)S(1)}, bf16[16,8192]{1,0:T(8,128)(2,1)S(1)}, u32[]{:S(2)}, u32[]{:S(2)}) collective-permute-start(bf16[16,8192]{1,0:T(8,128)(2,1)S(1)} %shard_map.77.refs_0_), channel_id=1, source_target_pairs={{0,2},{1,3},{2,0},{3,1},{4,6},{5,7},{6,4},{7,5},{8,10},{9,11},{10,... | collective-permute-start | bytes 786440 | tf_op jit(solution)/shard_map/ppermute | solution.py:35
  134.7 22.7 %collective-permute-start.41 = (bf16[16,8192]{1,0:T(8,128)(2,1)S(1)}, bf16[16,8192]{1,0:T(8,128)(2,1)S(1)}, u32[]{:S(2)}, u32[]{:S(2)}) collective-permute-start(bf16[16,8192]{1,0:T(8,128)(2,1)S(1)} %shard_map.77.refs_0_), channel_id=1, source_target_pairs={{0,3},{1,2},{2,1},{3,0},{4,7},{5,6},{6,5},{7,4},{8,11},{9,10},{10,... | collective-permute-start | bytes 786440 | tf_op jit(solution)/shard_map/ppermute | solution.py:35
  136.1 21.3 %collective-permute-start.37 = (bf16[64,16,128]{2,1,0:T(8,128)(2,1)S(1)}, bf16[64,16,128]{2,1,0:T(8,128)(2,1)S(1)}, u32[]{:S(2)}, u32[]{:S(2)}) collective-permute-start(bf16[64,16,128]{2,1,0:T(8,128)(2,1)S(1)} %shard_map.78), channel_id=1, source_target_pairs={{0,16},{4,20},{8,24},{12,28},{16,0},{20,4},{24,8},{28,12},{1,17},{... | collective-permute-start | bytes 786440 | tf_op jit(solution)/shard_map/ppermute | solution.py:35
  140.3 22.1 %collective-permute-start.38 = (bf16[64,16,128]{2,1,0:T(8,128)(2,1)S(1)}, bf16[64,16,128]{2,1,0:T(8,128)(2,1)S(1)}, u32[]{:S(2)}, u32[]{:S(2)}) collective-permute-start(bf16[64,16,128]{2,1,0:T(8,128)(2,1)S(1)} %shard_map.80), channel_id=1, source_target_pairs={{0,16},{4,20},{8,24},{12,28},{16,0},{20,4},{24,8},{28,12},{1,17},{... | collective-permute-start | bytes 786440 | tf_op jit(solution)/shard_map/ppermute | solution.py:35
  166.5 12.1 %collective-permute-start.44 = (bf16[16,8192]{1,0:T(8,128)(2,1)S(1)}, bf16[16,8192]{1,0:T(8,128)(2,1)S(1)}, u32[]{:S(2)}, u32[]{:S(2)}) collective-permute-start(bf16[16,8192]{1,0:T(8,128)(2,1)S(1)} %shard_map.83.refs_0_), channel_id=1, source_target_pairs={{0,3},{1,2},{2,1},{3,0},{4,7},{5,6},{6,5},{7,4},{8,11},{9,10},{10,... | collective-permute-start | bytes 786440 | tf_op jit(solution)/shard_map/ppermute | solution.py:35
  (29 other events, 319.8 us)

commit v4 on v3

v4 whole, which is shorter than its diff:
```python
import functools

import jax
import jax.numpy as jnp
from jax import lax
from jax.experimental import pallas as pl
from jax.experimental.pallas import tpu as pltpu
from jax.sharding import PartitionSpec as P

GROUPS = 2
PARTS = 2
TILE_BLOCKS = 8
VMEM_LIMIT = 8 * 1024 * 1024
SIDE, NEXT = 1, 2

ORDER = (
    "As Al Af1 Af2",
    "Ao1 Bs Ao2 Az1",
    "Aw Bg1 Ae Bo1",
    "Bg2 Ac Bo2 Bw",
    "Bz1 As Be Ag1",
    "Ag2 Bc Ao1 Bs",
    "Ao2 Az1 Bf1 Aw",
    "Ae Bo1 Bg2 Ac",
    "Ap Bo2 Bp Bw",
    "Bz1 Ar Be Bc",
    "Br",
)

VMEM = pl.BlockSpec(memory_space=pltpu.VMEM)
SMEM = pl.BlockSpec(memory_space=pltpu.SMEM)
ANY = pl.BlockSpec(memory_space=pl.ANY)
HBM = pl.BlockSpec(memory_space=pltpu.HBM)


def params():
    return pltpu.CompilerParams(vmem_limit_bytes=VMEM_LIMIT)


def swap(value, axis, size, mask):
    return lax.ppermute(value, axis, [(i, i ^ mask) for i in range(size)])


def add_bf16(a, b):
    return (a.astype(jnp.float32) + b.astype(jnp.float32)).astype(jnp.bfloat16)


def add_f32(a, b):
    return a.astype(jnp.float32) + b.astype(jnp.float32)


def store_sums(b, scaled, emb, sums_refs):
    sums = jnp.dot(scaled, emb, preferred_element_type=jnp.float32).astype(jnp.bfloat16)
    part = sums.shape[1] // len(sums_refs)
    for i, ref in enumerate(sums_refs):
        ref[b] = sums[:, i * part:(i + 1) * part]


def first_sums_kernel(rows, vec_ref, quality_ref, emb_ref, *refs):
    *sums_refs, vec, quality, emb, sems = refs
    tiles, tile_docs = emb.shape[:2]
    blocks = sums_refs[0].shape[0]
    block_len = tiles * tile_docs // blocks
    here = [
        pltpu.make_async_copy(quality_ref, quality, sems.at[tiles]),
        pltpu.make_async_copy(vec_ref.at[rows], vec, sems.at[tiles + 1]),
    ]

    def tile_copy(j):
        docs = pl.ds(pl.multiple_of(j * tile_docs, tile_docs), tile_docs)
        return pltpu.make_async_copy(emb_ref.at[docs], emb.at[j], sems.at[j])

    for copy in here:
        copy.start()
    for j in range(tiles):
        tile_copy(j).start()
    for copy in here:
        copy.wait()

    def step(j, carry):
        tile_copy(j).wait()
        for b in range(blocks // tiles):
            docs = pl.ds(pl.multiple_of(j * tile_docs + b * block_len, block_len), block_len)
            scaled = (vec[:, docs] * quality[:, docs]).astype(jnp.bfloat16)
            store_sums(j * (blocks // tiles) + b, scaled, emb[j, b * block_len:(b + 1) * block_len], sums_refs)
        return carry

    lax.fori_loop(0, tiles, step, 0)


def next_sums_kernel(rows, pair, vec_ref, quality_ref, emb_ref, *sums_refs):
    blocks = sums_refs[0].shape[0]
    block_len = emb_ref.shape[0] // blocks

    def step(b, carry):
        docs = pl.ds(pl.multiple_of(b * block_len, block_len), block_len)
        quality = quality_ref[:, docs]
        value = vec_ref[rows, docs]
        if pair:
            value = add_f32(pair[0][:, docs], pair[1][:, docs]) * quality - value
        store_sums(b, (value * quality).astype(jnp.bfloat16), emb_ref[docs], sums_refs)
        return carry

    lax.fori_loop(0, blocks, step, 0, unroll=TILE_BLOCKS)


def later_sums_kernel(rows, mine_ref, other_ref, *refs):
    next_sums_kernel(rows, (mine_ref, other_ref), *refs)


def fill_kernel(rows, second, mine_ref, other_ref, vec_ref, quality_ref, *refs):
    out_ref, out, sems = refs[-3:]
    tiles = sems.shape[0]
    tile_docs = out.shape[1] // tiles
    copies = []
    for j in range(tiles):
        docs = pl.ds(j * tile_docs, tile_docs)
        vec, quality = vec_ref[rows, docs], quality_ref[:, docs]
        total = add_f32(mine_ref[:, docs], other_ref[:, docs])
        if second:
            first = add_f32(refs[0][:, docs], refs[1][:, docs]) * quality - vec
            value = 2.0 * (total * quality - first) - vec
        else:
            value = total * quality - vec
        out[:, docs] = value
        copies.append(pltpu.make_async_copy(out.at[:, docs], out_ref.at[rows, docs], sems.at[j]))
        copies[-1].start()
    for copy in copies:
        copy.wait()


def lookup(ids_ref, tables, outs, entries):
    def step(b, carry):
        places = [ids_ref[b * entries + k] for k in range(entries)]
        for table, ref in zip(tables, outs):
            total = table[places[0]].astype(jnp.float32)
            for place in places[1:]:
                total = total + table[place].astype(jnp.float32)
            ref[b] = total.astype(ref.dtype)
        return carry

    lax.fori_loop(0, outs[0].shape[0], step, 0, unroll=4)


def table_kernel(ids_ref, *refs):
    *shards, out_ref, table, sems = refs
    blocks = shards[0].shape[0]
    copies = [
        pltpu.make_async_copy(ref, table.at[pl.ds(i * blocks, blocks)], sems.at[i])
        for i, ref in enumerate(shards)
    ]
    for copy in copies:
        copy.start()
    table[len(shards) * blocks] = jnp.zeros(table.shape[1:], table.dtype)
    for copy in copies:
        copy.wait()
    lookup(ids_ref, [table], [out_ref], ids_ref.shape[0] // blocks)


def lookup_kernel(ids_ref, *refs):
    count = len(refs) // 2
    lookup(ids_ref, refs[:count], refs[count:], ids_ref.shape[0] // refs[count].shape[0])


def expand_kernel(count, *refs):
    *refs, emb_ref, out_ref = refs
    blocks = refs[0].shape[0]
    block_len = emb_ref.shape[0] // blocks

    def step(b, carry):
        docs = pl.ds(pl.multiple_of(b * block_len, block_len), block_len)
        parts = []
        for at in range(0, len(refs), count):
            total = refs[at][b]
            for ref in refs[at + 1:at + count]:
                total = total + ref[b].astype(jnp.float32)
            parts.append(total.astype(jnp.bfloat16))
        out_ref[:, docs] = lax.dot_general(
            jnp.concatenate(parts, axis=1), emb_ref[docs], (((1,), (1,)), ((), ())),
            preferred_element_type=jnp.float32,
        ).astype(jnp.bfloat16)
        return carry

    lax.fori_loop(0, blocks, step, 0, unroll=TILE_BLOCKS)


def body(embeddings, quality, probes, neighbors):
    nrow, ncol = lax.axis_size("row"), lax.axis_size("col")
    me = lax.axis_index("row")
    blk_count, list_len = neighbors.shape
    docs, width = embeddings.shape
    nprobe = probes.shape[0]
    group, part = nprobe // GROUPS, width // PARTS
    tiles = blk_count // TILE_BLOCKS
    reduce_bits = [1 << i for i in reversed(range(nrow.bit_length() - 1)) if 1 << i not in (SIDE, NEXT)]
    dests = [0]
    for m in reversed(reduce_bits):
        dests = [d | m for d in dests] + dests
    shards = (0, NEXT, SIDE, NEXT | SIDE)

    def table_ids(lists):
        flat = lists.reshape(-1)
        apart = (flat // blk_count) ^ me
        place = flat % blk_count
        for i, shard in enumerate(shards):
            place = jnp.where(apart == shard, i * blk_count + flat % blk_count, place)
        return jnp.where((apart & ~(NEXT | SIDE)) == 0, place, len(shards) * blk_count)

    qrow = quality[None, :]
    shard_shape = (blk_count, group, part)
    shard_out = jax.ShapeDtypeStruct(shard_shape, jnp.bfloat16)
    vec_out = jax.ShapeDtypeStruct((nprobe, docs), jnp.float32)

    def rows(c):
        return pl.ds(c * group, group)

    def first_sums(c, qrow):
        if c:
            return pl.pallas_call(
                functools.partial(next_sums_kernel, rows(c), ()),
                in_specs=[VMEM] * 3,
                out_specs=[VMEM] * PARTS,
                out_shape=[shard_out] * PARTS,
                compiler_params=params(),
            )(probes, qrow, embeddings)
        return pl.pallas_call(
            functools.partial(first_sums_kernel, rows(c)),
            in_specs=[HBM] * 3,
            out_specs=[VMEM] * PARTS,
            out_shape=[shard_out] * PARTS,
            scratch_shapes=[
                pltpu.VMEM((group, docs), jnp.float32),
                pltpu.VMEM((1, docs), jnp.float32),
                pltpu.VMEM((tiles, docs // tiles, width), jnp.bfloat16),
                pltpu.SemaphoreType.DMA((tiles + 2,)),
            ],
            compiler_params=params(),
        )(*(pltpu.with_memory_space_constraint(v, pltpu.HBM) for v in (probes, qrow, embeddings)))

    def next_sums(c, pair):
        return pl.pallas_call(
            functools.partial(later_sums_kernel, rows(c)),
            in_specs=[VMEM] * 5,
            out_specs=[VMEM] * PARTS,
            out_shape=[shard_out] * PARTS,
            compiler_params=params(),
        )(*pair, probes, qrow, embeddings)

    def fill(c, held, pair, *others):
        held = [] if held is None else [held]
        return pl.pallas_call(
            functools.partial(fill_kernel, rows(c), bool(others)),
            in_specs=[VMEM] * (4 + len(others)) + [ANY] * len(held),
            out_specs=HBM,
            out_shape=vec_out,
            input_output_aliases={4 + len(others): 0} if held else {},
            scratch_shapes=[pltpu.VMEM((group, docs), jnp.float32), pltpu.SemaphoreType.DMA((4,))],
            compiler_params=params(),
        )(*pair, probes, qrow, *others, *held)

    def combine_far(ids, shards):
        rows_held = len(shards) * blk_count + 1
        return pl.pallas_call(
            table_kernel,
            in_specs=[SMEM] + [VMEM] * len(shards),
            out_specs=[VMEM] * 2,
            out_shape=[shard_out, jax.ShapeDtypeStruct((rows_held, group, part), jnp.bfloat16)],
            scratch_shapes=[pltpu.SemaphoreType.DMA((len(shards),))],
            compiler_params=params(),
        )(ids, *shards)

    def combine(ids, tables, dtype):
        return pl.pallas_call(
            lookup_kernel,
            in_specs=[SMEM] + [VMEM] * len(tables),
            out_specs=[VMEM] * len(tables),
            out_shape=[jax.ShapeDtypeStruct(shard_shape, dtype)] * len(tables),
            compiler_params=params(),
        )(ids, *tables)

    def expand(parts):
        values = [v for values in parts for v in values]
        return pl.pallas_call(
            functools.partial(expand_kernel, len(parts[0])),
            in_specs=[VMEM] * (len(values) + 1),
            out_specs=VMEM,
            out_shape=jax.ShapeDtypeStruct((group, docs), jnp.bfloat16),
            compiler_params=params(),
        )(*values, embeddings)

    def reduce(outgoing):
        arrived = []
        for m in reduce_bits:
            taken = {d ^ m: swap(outgoing.pop(d), "row", nrow, m) for d in list(outgoing) if d & m}
            for d, value in taken.items():
                if d:
                    outgoing[d] = add_bf16(outgoing[d], value)
                else:
                    arrived.append(value)
        return arrived

    token = []

    def take(*values):
        if token:
            values = lax.optimization_barrier(values + (token.pop(),))[:-1]
        return values

    lists = {d: swap(neighbors, "row", nrow, d) if d else neighbors for d in dests}
    first = second = None
    gathered = [[None] * PARTS for _ in range(GROUPS)]
    tables = [[None] * PARTS for _ in range(GROUPS)]
    own = [[None] * PARTS for _ in range(GROUPS)]
    arrived = [[None] * PARTS for _ in range(GROUPS)]
    products = [None] * GROUPS
    halves = [None] * GROUPS
    for word in (word for line in ORDER for word in line.split()):
        c, step, p = ord(word[0]) - ord("A"), word[1], int(word[2:] or 0) - 1
        if step == "l":
            taken = take(*(lists[d] for d in dests))
            ids = dict(zip(dests, lax.optimization_barrier(tuple(table_ids(v) for v in taken))))
            token.append(ids[0])
        elif step == "s":
            if products[c] is None:
                sums = first_sums(c, *take(qrow))
            else:
                sums = next_sums(c, take(*products[c]))
                halves[c] = products[c]
            token.append(sums[0])
            for i, value in enumerate(sums):
                gathered[c][i] = {0: value}
                for m in (NEXT, SIDE):
                    gathered[c][i][m] = swap(value, "row", nrow, m)
        elif step in "fg":
            held = gathered[c][p]
            if step == "g":
                held[NEXT], held[SIDE] = take(held[NEXT], held[SIDE])
            else:
                (held[NEXT],) = take(held[NEXT])
            held[NEXT | SIDE] = swap(held[NEXT], "row", nrow, SIDE)
            token.append(held[NEXT])
        elif step == "o":
            held = take(*(gathered[c][p][m] for m in shards))
            outgoing = {}
            for d in dests[:-1]:
                if outgoing:
                    outgoing[d] = combine(ids[d], [tables[c][p]], jnp.bfloat16)[0]
                else:
                    outgoing[d], tables[c][p] = combine_far(ids[d], held)
            token.append(outgoing[dests[-2]])
            arrived[c][p] = reduce(outgoing)
        elif step == "w":
            tables[c] = list(take(*tables[c]))
            own[c] = combine(ids[0], tables[c], jnp.float32)
            token.append(own[c][0])
        elif step == "z":
            arrived[c][p] = take(*arrived[c][p])
            token.append(arrived[c][p][-1])
        elif step == "e":
            flat = take(*own[c], *(v for values in arrived[c] for v in values))
            later = [flat[PARTS + i * len(reduce_bits):PARTS + (i + 1) * len(reduce_bits)] for i in range(PARTS)]
            value = expand([(flat[i], *later[i]) for i in range(PARTS)])
            products[c] = [value, swap(value, "col", ncol, 1)]
            token.append(value)
        elif step == "c":
            pair = take(*products[c])
            for i in range(1, ncol.bit_length() - 1):
                value = add_bf16(*pair)
                pair = [value, swap(value, "col", ncol, 1 << i)]
            products[c] = pair
            token.append(value)
        elif step == "p":
            first = fill(c, first, take(*halves[c]))
            token.append(first)
        else:
            second = fill(c, second, take(*products[c]), *halves[c])
            token.append(second)
    return first, second


def solution(mesh):
    placed = (P("row", "col"), P("row"), P(None, "row"), P("row", None))
    return jax.shard_map(
        body,
        mesh=mesh,
        in_specs=placed,
        out_specs=(P(None, "row"), P(None, "row")),
        check_vma=False,
    )
```

time: 181 us -> 167 us (0.923)
  waiting for transfers between devices: 80.9 us -> 71.6 us
  Pallas kernels: 42.1 us -> 35.5 us
  starting transfers between devices: 51.7 us -> 55.6 us
  local copies, waits for them, and re-layouts: 4.54 us -> 2.56 us
    ppermute x45 -> x41, waiting for transfers between devices: 80.9 us -> 71.6 us  [swap(): return lax.ppermute(value, axis, [(i, i ^ mask) for i in range(size)])]
    pallas_call x26 -> x24, Pallas kernels: 42.1 us -> 35.5 us  [the longest x8 10.6 us: combine_far(): pl.pallas_call(table_kernel, in_specs=[SMEM] + [VMEM] * len(shards), out_...]
    ppermute x45 -> x41, starting transfers between devices: 51.7 us -> 55.6 us  [swap(): return lax.ppermute(value, axis, [(i, i ^ mask) for i in range(size)])]
    unnamed x16 -> x10, local copies, waits for them, and re-layouts: 4.19 us -> 2.21 us
  transfers between devices with their start and end apart: 45 -> 41, of which waited for: 20 -> 21; matrix products, arithmetic and copies ran while one was open for 0% -> 0% of each run, Pallas kernels for 20% -> 18%
where the time goes in v4:
time: 167 us; the launch traced here: 166 us
  waiting for transfers between devices  71.6 us (43%)
  starting transfers between devices  55.6 us (33%)
  Pallas kernels  35.5 us (21%)
  local copies, waits for them, and re-layouts  2.56 us (2%)
    ppermute x41, waiting for transfers between devices, swap(): return lax.ppermute(value, axis, [(i, i ^ mask) for i in range(size)])  71.6 us
    ppermute x41, starting transfers between devices, swap(): return lax.ppermute(value, axis, [(i, i ^ mask) for i in range(size)])  55.6 us
    pallas_call x8, Pallas kernels, combine_far(): pl.pallas_call(table_kernel, in_specs=[SMEM] + [VMEM] * len(shards), out_...  10.6 us
    pallas_call x4, Pallas kernels, expand(): pl.pallas_call(functools.partial(expand_kernel, len(parts[0])), in_specs=...  8.16 us
    pallas_call x4, Pallas kernels, combine(): pl.pallas_call(lookup_kernel, in_specs=[SMEM] + [VMEM] * len(tables), out...  5.8 us
    pallas_call x4, Pallas kernels, fill(): pl.pallas_call(functools.partial(fill_kernel, rows(c), bool(others)), in_...  3.48 us
  transfers between devices with their start and end apart: 41, of which 21 were waited for; matrix products, arithmetic and copies ran while one was open for 0% of the time, Pallas kernels for 18%

profile of v4, /device:TPU:0, one launch (start us, length us, event | category | flops | bytes accessed | tf_op | source)
XLA Modules:
  0.0 166.5 jit_solution(2148808922689865064)
XLA Ops:
  0.6 2.8 %shard_map.59 = (bf16[64,16,128]{2,1,0:T(8,128)(2,1)S(1)}, bf16[64,16,128]{2,1,0:T(8,128)(2,1)S(1)}) custom-call(f32[32,8192]{1,0:T(8,128)} %vec_ref.11, f32[1,8192]{1,0:T(1,128)} %bitcast.1, bf16[8192,256]{1,0:T(8,128)(2,1)} %refs_4_.7), custom_call_target="tpu_custom_call" | custom-call | tf_op jit(solution)/shard_map/pallas_call | solution.py:226
  3.5 3.1 %collective-permute-start.1 = (bf16[64,16,128]{2,1,0:T(8,128)(2,1)S(1)}, bf16[64,16,128]{2,1,0:T(8,128)(2,1)S(1)}, u32[]{:S(2)}, u32[]{:S(2)}) collective-permute-start(bf16[64,16,128]{2,1,0:T(8,128)(2,1)S(1)} %get-tuple-element.140.refs_0_), channel_id=1, source_target_pairs={{0,8},{4,12},{8,0},{12,4},{16,24},{20,28},{24,16},{28,20},{1,9},{5... | collective-permute-start | bytes 786440 | tf_op jit(solution)/shard_map/ppermute | solution.py:41
  6.7 3.0 %collective-permute-start = (s32[64,8]{0,1:T(8,128)S(1)}, s32[64,8]{0,1:T(8,128)S(1)}, u32[]{:S(2)}, u32[]{:S(2)}) collective-permute-start(s32[64,8]{0,1:T(8,128)S(1)} %copy-done.4), channel_id=1, source_target_pairs={{0,16},{4,20},{8,24},{12,28},{16,0},{20,4},{24,8},{28,12},{1,17},{... | collective-permute-start | bytes 6152 | tf_op jit(solution)/shard_map/ppermute | solution.py:41
  11.1 6.7 %collective-permute-done = s32[64,8]{0,1:T(8,128)S(1)} collective-permute-done((s32[64,8]{0,1:T(8,128)S(1)}, s32[64,8]{0,1:T(8,128)S(1)}, u32[]{:S(2)}, u32[]{:S(2)}) %collective-permute-start) | collective-permute-done | bytes 2080 | tf_op jit(solution)/shard_map/ppermute | solution.py:41
  21.9 5.7 %collective-permute-done.3.refs_3_ = bf16[64,16,128]{2,1,0:T(8,128)(2,1)S(1)} collective-permute-done((bf16[64,16,128]{2,1,0:T(8,128)(2,1)S(1)}, bf16[64,16,128]{2,1,0:T(8,128)(2,1)S(1)}, u32[]{:S(2)}, u32[]{:S(2)}) %collective-permute-start.3) | collective-permute-done | bytes 262176 | tf_op jit(solution)/shard_map/ppermute | solution.py:41
  28.9 3.4 %collective-permute-start.9 = (bf16[64,16,128]{2,1,0:T(8,128)(2,1)S(1)}, bf16[64,16,128]{2,1,0:T(8,128)(2,1)S(1)}, u32[]{:S(2)}, u32[]{:S(2)}) collective-permute-start(bf16[64,16,128]{2,1,0:T(8,128)(2,1)S(1)} %get-tuple-element.144), channel_id=1, source_target_pairs={{0,16},{4,20},{8,24},{12,28},{16,0},{20,4},{24,8},{28,12},{1,17},{... | collective-permute-start | bytes 786440 | tf_op jit(solution)/shard_map/ppermute | solution.py:41
  32.3 2.2 %copy-done = bf16[8192,256]{1,0:T(8,128)(2,1)S(1)} copy-done((bf16[8192,256]{1,0:T(8,128)(2,1)S(1)}, bf16[8192,256]{1,0:T(8,128)(2,1)}, u32[]{:S(2)}) %copy-start) | copy-done | bytes 4194328
  40.1 3.4 %collective-permute-start.11 = (bf16[64,16,128]{2,1,0:T(8,128)(2,1)S(1)}, bf16[64,16,128]{2,1,0:T(8,128)(2,1)S(1)}, u32[]{:S(2)}, u32[]{:S(2)}) collective-permute-start(bf16[64,16,128]{2,1,0:T(8,128)(2,1)S(1)} %get-tuple-element.153), channel_id=1, source_target_pairs={{0,16},{4,20},{8,24},{12,28},{16,0},{20,4},{24,8},{28,12},{1,17},{... | collective-permute-start | bytes 786440 | tf_op jit(solution)/shard_map/ppermute | solution.py:41
  45.5 4.8 %collective-permute-start.10 = (bf16[64,16,128]{2,1,0:T(8,128)(2,1)S(1)}, bf16[64,16,128]{2,1,0:T(8,128)(2,1)S(1)}, u32[]{:S(2)}, u32[]{:S(2)}) collective-permute-start(bf16[64,16,128]{2,1,0:T(8,128)(2,1)S(1)} %collective-permute-done.5.refs_1_), channel_id=1, source_target_pairs={{0,4},{4,0},{8,12},{12,8},{16,20},{20,16},{24,28},{28,24},{1,5},{5... | collective-permute-start | bytes 786440 | tf_op jit(solution)/shard_map/ppermute | solution.py:41
  52.4 2.2 %collective-permute-done.10.refs_3_ = bf16[64,16,128]{2,1,0:T(8,128)(2,1)S(1)} collective-permute-done((bf16[64,16,128]{2,1,0:T(8,128)(2,1)S(1)}, bf16[64,16,128]{2,1,0:T(8,128)(2,1)S(1)}, u32[]{:S(2)}, u32[]{:S(2)}) %collective-permute-start.10) | collective-permute-done | bytes 262176 | tf_op jit(solution)/shard_map/ppermute | solution.py:41
  61.5 5.0 %collective-permute-done.14.refs_3_ = bf16[64,16,128]{2,1,0:T(8,128)(2,1)S(1)} collective-permute-done((bf16[64,16,128]{2,1,0:T(8,128)(2,1)S(1)}, bf16[64,16,128]{2,1,0:T(8,128)(2,1)S(1)}, u32[]{:S(2)}, u32[]{:S(2)}) %collective-permute-start.14) | collective-permute-done | bytes 262176 | tf_op jit(solution)/shard_map/ppermute | solution.py:41
  69.9 6.3 %collective-permute-done.16.refs_1_ = bf16[64,16,128]{2,1,0:T(8,128)(2,1)S(1)} collective-permute-done((bf16[64,16,128]{2,1,0:T(8,128)(2,1)S(1)}, bf16[64,16,128]{2,1,0:T(8,128)(2,1)S(1)}, u32[]{:S(2)}, u32[]{:S(2)}) %collective-permute-start.16) | collective-permute-done | bytes 262176 | tf_op jit(solution)/shard_map/ppermute | solution.py:41
  83.9 3.4 %collective-permute-done.22.refs_1_ = bf16[64,16,128]{2,1,0:T(8,128)(2,1)S(1)} collective-permute-done((bf16[64,16,128]{2,1,0:T(8,128)(2,1)S(1)}, bf16[64,16,128]{2,1,0:T(8,128)(2,1)S(1)}, u32[]{:S(2)}, u32[]{:S(2)}) %collective-permute-start.22) | collective-permute-done | bytes 262176 | tf_op jit(solution)/shard_map/ppermute | solution.py:41
  89.8 3.1 %collective-permute-done.20.refs_1_ = bf16[64,16,128]{2,1,0:T(8,128)(2,1)S(1)} collective-permute-done((bf16[64,16,128]{2,1,0:T(8,128)(2,1)S(1)}, bf16[64,16,128]{2,1,0:T(8,128)(2,1)S(1)}, u32[]{:S(2)}, u32[]{:S(2)}) %collective-permute-start.20) | collective-permute-done | bytes 262176 | tf_op jit(solution)/shard_map/ppermute | solution.py:41
  99.1 2.1 %collective-permute-done.24.other_ref.refs_1_ = bf16[16,8192]{1,0:T(8,128)(2,1)S(1)} collective-permute-done((bf16[16,8192]{1,0:T(8,128)(2,1)S(1)}, bf16[16,8192]{1,0:T(8,128)(2,1)S(1)}, u32[]{:S(2)}, u32[]{:S(2)}) %collective-permute-start.24) | collective-permute-done | bytes 262176 | tf_op jit(solution)/shard_map/ppermute | solution.py:41
  104.6 3.0 %collective-permute-start.33 = (bf16[64,16,128]{2,1,0:T(8,128)(2,1)S(1)}, bf16[64,16,128]{2,1,0:T(8,128)(2,1)S(1)}, u32[]{:S(2)}, u32[]{:S(2)}) collective-permute-start(bf16[64,16,128]{2,1,0:T(8,128)(2,1)S(1)} %get-tuple-element.214), channel_id=1, source_target_pairs={{0,16},{4,20},{8,24},{12,28},{16,0},{20,4},{24,8},{28,12},{1,17},{... | collective-permute-start | bytes 786440 | tf_op jit(solution)/shard_map/ppermute | solution.py:41
  107.6 2.1 %collective-permute-start.31 = (bf16[64,16,128]{2,1,0:T(8,128)(2,1)S(1)}, bf16[64,16,128]{2,1,0:T(8,128)(2,1)S(1)}, u32[]{:S(2)}, u32[]{:S(2)}) collective-permute-start(bf16[64,16,128]{2,1,0:T(8,128)(2,1)S(1)} %get-tuple-element.227.refs_0_), channel_id=1, source_target_pairs={{0,4},{4,0},{8,12},{12,8},{16,20},{20,16},{24,28},{28,24},{1,5},{5... | collective-permute-start | bytes 786440 | tf_op jit(solution)/shard_map/ppermute | solution.py:41
  109.7 6.8 %collective-permute-done.29.refs_1_ = bf16[64,16,128]{2,1,0:T(8,128)(2,1)S(1)} collective-permute-done((bf16[64,16,128]{2,1,0:T(8,128)(2,1)S(1)}, bf16[64,16,128]{2,1,0:T(8,128)(2,1)S(1)}, u32[]{:S(2)}, u32[]{:S(2)}) %collective-permute-start.29) | collective-permute-done | bytes 262176 | tf_op jit(solution)/shard_map/ppermute | solution.py:41
  121.2 2.3 %collective-permute-done.33.refs_3_ = bf16[64,16,128]{2,1,0:T(8,128)(2,1)S(1)} collective-permute-done((bf16[64,16,128]{2,1,0:T(8,128)(2,1)S(1)}, bf16[64,16,128]{2,1,0:T(8,128)(2,1)S(1)}, u32[]{:S(2)}, u32[]{:S(2)}) %collective-permute-start.33) | collective-permute-done | bytes 262176 | tf_op jit(solution)/shard_map/ppermute | solution.py:41
  132.1 3.7 %collective-permute-done.34.refs_3_ = bf16[64,16,128]{2,1,0:T(8,128)(2,1)S(1)} collective-permute-done((bf16[64,16,128]{2,1,0:T(8,128)(2,1)S(1)}, bf16[64,16,128]{2,1,0:T(8,128)(2,1)S(1)}, u32[]{:S(2)}, u32[]{:S(2)}) %collective-permute-start.34) | collective-permute-done | bytes 262176 | tf_op jit(solution)/shard_map/ppermute | solution.py:41
  137.2 2.6 %collective-permute-start.37 = (bf16[64,16,128]{2,1,0:T(8,128)(2,1)S(1)}, bf16[64,16,128]{2,1,0:T(8,128)(2,1)S(1)}, u32[]{:S(2)}, u32[]{:S(2)}) collective-permute-start(bf16[64,16,128]{2,1,0:T(8,128)(2,1)S(1)} %get-tuple-element.242), channel_id=1, source_target_pairs={{0,16},{4,20},{8,24},{12,28},{16,0},{20,4},{24,8},{28,12},{1,17},{... | collective-permute-start | bytes 786440 | tf_op jit(solution)/shard_map/ppermute | solution.py:41
  142.1 7.1 %collective-permute-done.36.refs_1_ = bf16[64,16,128]{2,1,0:T(8,128)(2,1)S(1)} collective-permute-done((bf16[64,16,128]{2,1,0:T(8,128)(2,1)S(1)}, bf16[64,16,128]{2,1,0:T(8,128)(2,1)S(1)}, u32[]{:S(2)}, u32[]{:S(2)}) %collective-permute-start.36) | collective-permute-done | bytes 262176 | tf_op jit(solution)/shard_map/ppermute | solution.py:41
  150.1 3.4 %collective-permute-done.37.refs_3_ = bf16[64,16,128]{2,1,0:T(8,128)(2,1)S(1)} collective-permute-done((bf16[64,16,128]{2,1,0:T(8,128)(2,1)S(1)}, bf16[64,16,128]{2,1,0:T(8,128)(2,1)S(1)}, u32[]{:S(2)}, u32[]{:S(2)}) %collective-permute-start.37) | collective-permute-done | bytes 262176 | tf_op jit(solution)/shard_map/ppermute | solution.py:41
  157.3 8.3 %collective-permute-done.40.other_ref = bf16[16,8192]{1,0:T(8,128)(2,1)S(1)} collective-permute-done((bf16[16,8192]{1,0:T(8,128)(2,1)S(1)}, bf16[16,8192]{1,0:T(8,128)(2,1)S(1)}, u32[]{:S(2)}, u32[]{:S(2)}) %collective-permute-start.40) | collective-permute-done | bytes 262176 | tf_op jit(solution)/shard_map/ppermute | solution.py:41
  (101 shorter events, 69.0 us)
Async XLA Ops:
  3.5 14.7 %collective-permute-start.1 = (bf16[64,16,128]{2,1,0:T(8,128)(2,1)S(1)}, bf16[64,16,128]{2,1,0:T(8,128)(2,1)S(1)}, u32[]{:S(2)}, u32[]{:S(2)}) collective-permute-start(bf16[64,16,128]{2,1,0:T(8,128)(2,1)S(1)} %get-tuple-element.140.refs_0_), channel_id=1, source_target_pairs={{0,8},{4,12},{8,0},{12,4},{16,24},{20,28},{24,16},{28,20},{1,9},{5... | collective-permute-start | bytes 786440 | tf_op jit(solution)/shard_map/ppermute | solution.py:41
  6.6 13.8 %collective-permute-start.4 = (bf16[64,16,128]{2,1,0:T(8,128)(2,1)S(1)}, bf16[64,16,128]{2,1,0:T(8,128)(2,1)S(1)}, u32[]{:S(2)}, u32[]{:S(2)}) collective-permute-start(bf16[64,16,128]{2,1,0:T(8,128)(2,1)S(1)} %get-tuple-element.148.refs_0_), channel_id=1, source_target_pairs={{0,8},{4,12},{8,0},{12,4},{16,24},{20,28},{24,16},{28,20},{1,9},{5... | collective-permute-start | bytes 786440 | tf_op jit(solution)/shard_map/ppermute | solution.py:41
  6.7 11.2 %collective-permute-start = (s32[64,8]{0,1:T(8,128)S(1)}, s32[64,8]{0,1:T(8,128)S(1)}, u32[]{:S(2)}, u32[]{:S(2)}) collective-permute-start(s32[64,8]{0,1:T(8,128)S(1)} %copy-done.4), channel_id=1, source_target_pairs={{0,16},{4,20},{8,24},{12,28},{16,0},{20,4},{24,8},{28,12},{1,17},{... | collective-permute-start | bytes 6152 | tf_op jit(solution)/shard_map/ppermute | solution.py:41
  9.6 12.2 %collective-permute-start.2 = (bf16[64,16,128]{2,1,0:T(8,128)(2,1)S(1)}, bf16[64,16,128]{2,1,0:T(8,128)(2,1)S(1)}, u32[]{:S(2)}, u32[]{:S(2)}) collective-permute-start(bf16[64,16,128]{2,1,0:T(8,128)(2,1)S(1)} %get-tuple-element.140.refs_0_), channel_id=1, source_target_pairs={{0,4},{4,0},{8,12},{12,8},{16,20},{20,16},{24,28},{28,24},{1,5},{5... | collective-permute-start | bytes 786440 | tf_op jit(solution)/shard_map/ppermute | solution.py:41
  19.8 17.9 %collective-permute-start.7 = (bf16[64,16,128]{2,1,0:T(8,128)(2,1)S(1)}, bf16[64,16,128]{2,1,0:T(8,128)(2,1)S(1)}, u32[]{:S(2)}, u32[]{:S(2)}) collective-permute-start(bf16[64,16,128]{2,1,0:T(8,128)(2,1)S(1)} %get-tuple-element.148.refs_0_), channel_id=1, source_target_pairs={{0,4},{4,0},{8,12},{12,8},{16,20},{20,16},{24,28},{28,24},{1,5},{5... | collective-permute-start | bytes 786440 | tf_op jit(solution)/shard_map/ppermute | solution.py:41
  20.3 18.4 %collective-permute-start.8 = (bf16[64,16,128]{2,1,0:T(8,128)(2,1)S(1)}, bf16[64,16,128]{2,1,0:T(8,128)(2,1)S(1)}, u32[]{:S(2)}, u32[]{:S(2)}) collective-permute-start(bf16[64,16,128]{2,1,0:T(8,128)(2,1)S(1)} %collective-permute-done.4.refs_1_), channel_id=1, source_target_pairs={{0,4},{4,0},{8,12},{12,8},{16,20},{20,16},{24,28},{28,24},{1,5},{5... | collective-permute-start | bytes 786440 | tf_op jit(solution)/shard_map/ppermute | solution.py:41
  28.9 14.7 %collective-permute-start.9 = (bf16[64,16,128]{2,1,0:T(8,128)(2,1)S(1)}, bf16[64,16,128]{2,1,0:T(8,128)(2,1)S(1)}, u32[]{:S(2)}, u32[]{:S(2)}) collective-permute-start(bf16[64,16,128]{2,1,0:T(8,128)(2,1)S(1)} %get-tuple-element.144), channel_id=1, source_target_pairs={{0,16},{4,20},{8,24},{12,28},{16,0},{20,4},{24,8},{28,12},{1,17},{... | collective-permute-start | bytes 786440 | tf_op jit(solution)/shard_map/ppermute | solution.py:41
  40.1 10.2 %collective-permute-start.11 = (bf16[64,16,128]{2,1,0:T(8,128)(2,1)S(1)}, bf16[64,16,128]{2,1,0:T(8,128)(2,1)S(1)}, u32[]{:S(2)}, u32[]{:S(2)}) collective-permute-start(bf16[64,16,128]{2,1,0:T(8,128)(2,1)S(1)} %get-tuple-element.153), channel_id=1, source_target_pairs={{0,16},{4,20},{8,24},{12,28},{16,0},{20,4},{24,8},{28,12},{1,17},{... | collective-permute-start | bytes 786440 | tf_op jit(solution)/shard_map/ppermute | solution.py:41
  56.0 20.2 %collective-permute-start.16 = (bf16[64,16,128]{2,1,0:T(8,128)(2,1)S(1)}, bf16[64,16,128]{2,1,0:T(8,128)(2,1)S(1)}, u32[]{:S(2)}, u32[]{:S(2)}) collective-permute-start(bf16[64,16,128]{2,1,0:T(8,128)(2,1)S(1)} %get-tuple-element.171), channel_id=1, source_target_pairs={{0,16},{4,20},{8,24},{12,28},{16,0},{20,4},{24,8},{28,12},{1,17},{... | collective-permute-start | bytes 786440 | tf_op jit(solution)/shard_map/ppermute | solution.py:41
  59.9 16.3 %collective-permute-start.18 = (bf16[16,8192]{1,0:T(8,128)(2,1)S(1)}, bf16[16,8192]{1,0:T(8,128)(2,1)S(1)}, u32[]{:S(2)}, u32[]{:S(2)}) collective-permute-start(bf16[16,8192]{1,0:T(8,128)(2,1)S(1)} %add_convert_fusion.3.mine_ref.refs_0_), channel_id=1, source_target_pairs={{0,2},{1,3},{2,0},{3,1},{4,6},{5,7},{6,4},{7,5},{8,10},{9,11},{10,... | collective-permute-start | bytes 786440 | tf_op jit(solution)/shard_map/ppermute | solution.py:41
  67.8 14.0 %collective-permute-start.17 = (bf16[64,16,128]{2,1,0:T(8,128)(2,1)S(1)}, bf16[64,16,128]{2,1,0:T(8,128)(2,1)S(1)}, u32[]{:S(2)}, u32[]{:S(2)}) collective-permute-start(bf16[64,16,128]{2,1,0:T(8,128)(2,1)S(1)} %get-tuple-element.181), channel_id=1, source_target_pairs={{0,16},{4,20},{8,24},{12,28},{16,0},{20,4},{24,8},{28,12},{1,17},{... | collective-permute-start | bytes 786440 | tf_op jit(solution)/shard_map/ppermute | solution.py:41
  77.7 9.6 %collective-permute-start.22 = (bf16[64,16,128]{2,1,0:T(8,128)(2,1)S(1)}, bf16[64,16,128]{2,1,0:T(8,128)(2,1)S(1)}, u32[]{:S(2)}, u32[]{:S(2)}) collective-permute-start(bf16[64,16,128]{2,1,0:T(8,128)(2,1)S(1)} %get-tuple-element.200.refs_0_), channel_id=1, source_target_pairs={{0,8},{4,12},{8,0},{12,4},{16,24},{20,28},{24,16},{28,20},{1,9},{5... | collective-permute-start | bytes 786440 | tf_op jit(solution)/shard_map/ppermute | solution.py:41
  80.5 12.3 %collective-permute-start.20 = (bf16[64,16,128]{2,1,0:T(8,128)(2,1)S(1)}, bf16[64,16,128]{2,1,0:T(8,128)(2,1)S(1)}, u32[]{:S(2)}, u32[]{:S(2)}) collective-permute-start(bf16[64,16,128]{2,1,0:T(8,128)(2,1)S(1)} %get-tuple-element.210.refs_0_), channel_id=1, source_target_pairs={{0,8},{4,12},{8,0},{12,4},{16,24},{20,28},{24,16},{28,20},{1,9},{5... | collective-permute-start | bytes 786440 | tf_op jit(solution)/shard_map/ppermute | solution.py:41
  81.8 11.4 %collective-permute-start.21 = (bf16[64,16,128]{2,1,0:T(8,128)(2,1)S(1)}, bf16[64,16,128]{2,1,0:T(8,128)(2,1)S(1)}, u32[]{:S(2)}, u32[]{:S(2)}) collective-permute-start(bf16[64,16,128]{2,1,0:T(8,128)(2,1)S(1)} %get-tuple-element.210.refs_0_), channel_id=1, source_target_pairs={{0,4},{4,0},{8,12},{12,8},{16,20},{20,16},{24,28},{28,24},{1,5},{5... | collective-permute-start | bytes 786440 | tf_op jit(solution)/shard_map/ppermute | solution.py:41
  87.7 9.8 %collective-permute-start.25 = (bf16[64,16,128]{2,1,0:T(8,128)(2,1)S(1)}, bf16[64,16,128]{2,1,0:T(8,128)(2,1)S(1)}, u32[]{:S(2)}, u32[]{:S(2)}) collective-permute-start(bf16[64,16,128]{2,1,0:T(8,128)(2,1)S(1)} %collective-permute-done.22.refs_1_), channel_id=1, source_target_pairs={{0,4},{4,0},{8,12},{12,8},{16,20},{20,16},{24,28},{28,24},{1,5},{5... | collective-permute-start | bytes 786440 | tf_op jit(solution)/shard_map/ppermute | solution.py:41
  98.9 17.7 %collective-permute-start.29 = (bf16[64,16,128]{2,1,0:T(8,128)(2,1)S(1)}, bf16[64,16,128]{2,1,0:T(8,128)(2,1)S(1)}, u32[]{:S(2)}, u32[]{:S(2)}) collective-permute-start(bf16[64,16,128]{2,1,0:T(8,128)(2,1)S(1)} %get-tuple-element.204), channel_id=1, source_target_pairs={{0,16},{4,20},{8,24},{12,28},{16,0},{20,4},{24,8},{28,12},{1,17},{... | collective-permute-start | bytes 786440 | tf_op jit(solution)/shard_map/ppermute | solution.py:41
  102.8 15.2 %collective-permute-start.28 = (bf16[64,16,128]{2,1,0:T(8,128)(2,1)S(1)}, bf16[64,16,128]{2,1,0:T(8,128)(2,1)S(1)}, u32[]{:S(2)}, u32[]{:S(2)}) collective-permute-start(bf16[64,16,128]{2,1,0:T(8,128)(2,1)S(1)} %get-tuple-element.227.refs_0_), channel_id=1, source_target_pairs={{0,8},{4,12},{8,0},{12,4},{16,24},{20,28},{24,16},{28,20},{1,9},{5... | collective-permute-start | bytes 786440 | tf_op jit(solution)/shard_map/ppermute | solution.py:41
  104.6 18.9 %collective-permute-start.33 = (bf16[64,16,128]{2,1,0:T(8,128)(2,1)S(1)}, bf16[64,16,128]{2,1,0:T(8,128)(2,1)S(1)}, u32[]{:S(2)}, u32[]{:S(2)}) collective-permute-start(bf16[64,16,128]{2,1,0:T(8,128)(2,1)S(1)} %get-tuple-element.214), channel_id=1, source_target_pairs={{0,16},{4,20},{8,24},{12,28},{16,0},{20,4},{24,8},{28,12},{1,17},{... | collective-permute-start | bytes 786440 | tf_op jit(solution)/shard_map/ppermute | solution.py:41
  107.6 18.0 %collective-permute-start.31 = (bf16[64,16,128]{2,1,0:T(8,128)(2,1)S(1)}, bf16[64,16,128]{2,1,0:T(8,128)(2,1)S(1)}, u32[]{:S(2)}, u32[]{:S(2)}) collective-permute-start(bf16[64,16,128]{2,1,0:T(8,128)(2,1)S(1)} %get-tuple-element.227.refs_0_), channel_id=1, source_target_pairs={{0,4},{4,0},{8,12},{12,8},{16,20},{20,16},{24,28},{28,24},{1,5},{5... | collective-permute-start | bytes 786440 | tf_op jit(solution)/shard_map/ppermute | solution.py:41
  109.6 18.2 %collective-permute-start.26 = (bf16[64,16,128]{2,1,0:T(8,128)(2,1)S(1)}, bf16[64,16,128]{2,1,0:T(8,128)(2,1)S(1)}, u32[]{:S(2)}, u32[]{:S(2)}) collective-permute-start(bf16[64,16,128]{2,1,0:T(8,128)(2,1)S(1)} %get-tuple-element.238.refs_0_), channel_id=1, source_target_pairs={{0,8},{4,12},{8,0},{12,4},{16,24},{20,28},{24,16},{28,20},{1,9},{5... | collective-permute-start | bytes 786440 | tf_op jit(solution)/shard_map/ppermute | solution.py:41
  116.5 11.3 %collective-permute-start.27 = (bf16[64,16,128]{2,1,0:T(8,128)(2,1)S(1)}, bf16[64,16,128]{2,1,0:T(8,128)(2,1)S(1)}, u32[]{:S(2)}, u32[]{:S(2)}) collective-permute-start(bf16[64,16,128]{2,1,0:T(8,128)(2,1)S(1)} %get-tuple-element.238.refs_0_), channel_id=1, source_target_pairs={{0,4},{4,0},{8,12},{12,8},{16,20},{20,16},{24,28},{28,24},{1,5},{5... | collective-permute-start | bytes 786440 | tf_op jit(solution)/shard_map/ppermute | solution.py:41
  127.8 21.4 %collective-permute-start.36 = (bf16[64,16,128]{2,1,0:T(8,128)(2,1)S(1)}, bf16[64,16,128]{2,1,0:T(8,128)(2,1)S(1)}, u32[]{:S(2)}, u32[]{:S(2)}) collective-permute-start(bf16[64,16,128]{2,1,0:T(8,128)(2,1)S(1)} %get-tuple-element.231), channel_id=1, source_target_pairs={{0,16},{4,20},{8,24},{12,28},{16,0},{20,4},{24,8},{28,12},{1,17},{... | collective-permute-start | bytes 786440 | tf_op jit(solution)/shard_map/ppermute | solution.py:41
  129.7 19.4 %collective-permute-start.38 = (bf16[16,8192]{1,0:T(8,128)(2,1)S(1)}, bf16[16,8192]{1,0:T(8,128)(2,1)S(1)}, u32[]{:S(2)}, u32[]{:S(2)}) collective-permute-start(bf16[16,8192]{1,0:T(8,128)(2,1)S(1)} %add_convert_fusion.1.mine_ref), channel_id=1, source_target_pairs={{0,2},{1,3},{2,0},{3,1},{4,6},{5,7},{6,4},{7,5},{8,10},{9,11},{10,... | collective-permute-start | bytes 786440 | tf_op jit(solution)/shard_map/ppermute | solution.py:41
  137.2 16.3 %collective-permute-start.37 = (bf16[64,16,128]{2,1,0:T(8,128)(2,1)S(1)}, bf16[64,16,128]{2,1,0:T(8,128)(2,1)S(1)}, u32[]{:S(2)}, u32[]{:S(2)}) collective-permute-start(bf16[64,16,128]{2,1,0:T(8,128)(2,1)S(1)} %get-tuple-element.242), channel_id=1, source_target_pairs={{0,16},{4,20},{8,24},{12,28},{16,0},{20,4},{24,8},{28,12},{1,17},{... | collective-permute-start | bytes 786440 | tf_op jit(solution)/shard_map/ppermute | solution.py:41
  (22 other events, 215.5 us)

commit v5 on v4

v5 whole, which is shorter than its diff:
```python
import functools

import jax
import jax.numpy as jnp
from jax import lax
from jax.experimental import pallas as pl
from jax.experimental.pallas import tpu as pltpu
from jax.sharding import PartitionSpec as P

GROUPS = 2
TILE_BLOCKS = 8
VMEM_LIMIT = 8 * 1024 * 1024
SIDE, NEXT = 1, 2

ORDER = (
    "As Bs Ag Al",
    "Bh Ao Bi Bj",
    "Aw Bn Bw Ae",
    "Be Ac Bc As",
    "Bs Ag Bh Ao",
    "Bi Ap Aw Bj",
    "Bn Bw Bp Ae",
    "Be Ac Bc Ar",
    "Br",
)

VMEM = pl.BlockSpec(memory_space=pltpu.VMEM)
SMEM = pl.BlockSpec(memory_space=pltpu.SMEM)
ANY = pl.BlockSpec(memory_space=pl.ANY)
HBM = pl.BlockSpec(memory_space=pltpu.HBM)


def params():
    return pltpu.CompilerParams(vmem_limit_bytes=VMEM_LIMIT)


def swap(value, axis, size, mask):
    return lax.ppermute(value, axis, [(i, i ^ mask) for i in range(size)])


def add_bf16(a, b):
    return (a.astype(jnp.float32) + b.astype(jnp.float32)).astype(jnp.bfloat16)


def add_f32(a, b):
    return a.astype(jnp.float32) + b.astype(jnp.float32)


def block_sum(scaled, emb):
    return jnp.dot(scaled, emb, preferred_element_type=jnp.float32).astype(jnp.bfloat16)


def first_sums_kernel(rows, vec_ref, quality_ref, emb_ref, *refs):
    sums_ref, vec, quality, emb, sems = refs
    tiles, tile_docs = emb.shape[:2]
    blocks = sums_ref.shape[0]
    block_len = tiles * tile_docs // blocks
    here = [
        pltpu.make_async_copy(quality_ref, quality, sems.at[tiles]),
        pltpu.make_async_copy(vec_ref.at[rows], vec, sems.at[tiles + 1]),
    ]

    def tile_copy(j):
        docs = pl.ds(pl.multiple_of(j * tile_docs, tile_docs), tile_docs)
        return pltpu.make_async_copy(emb_ref.at[docs], emb.at[j], sems.at[j])

    for copy in here:
        copy.start()
    for j in range(tiles):
        tile_copy(j).start()
    for copy in here:
        copy.wait()

    def step(j, carry):
        tile_copy(j).wait()
        for b in range(blocks // tiles):
            docs = pl.ds(pl.multiple_of(j * tile_docs + b * block_len, block_len), block_len)
            scaled = (vec[:, docs] * quality[:, docs]).astype(jnp.bfloat16)
            sums_ref[j * (blocks // tiles) + b] = block_sum(scaled, emb[j, b * block_len:(b + 1) * block_len])
        return carry

    lax.fori_loop(0, tiles, step, 0)


def next_sums_kernel(rows, pair, vec_ref, quality_ref, emb_ref, sums_ref):
    blocks = sums_ref.shape[0]
    block_len = emb_ref.shape[0] // blocks

    def step(b, carry):
        docs = pl.ds(pl.multiple_of(b * block_len, block_len), block_len)
        quality = quality_ref[:, docs]
        value = vec_ref[rows, docs]
        if pair:
            value = add_f32(pair[0][:, docs], pair[1][:, docs]) * quality - value
        sums_ref[b] = block_sum((value * quality).astype(jnp.bfloat16), emb_ref[docs])
        return carry

    lax.fori_loop(0, blocks, step, 0, unroll=TILE_BLOCKS)


def later_sums_kernel(rows, mine_ref, other_ref, *refs):
    next_sums_kernel(rows, (mine_ref, other_ref), *refs)


def fill_kernel(rows, second, mine_ref, other_ref, vec_ref, quality_ref, *refs):
    out_ref, out, sems = refs[-3:]
    tiles = sems.shape[0]
    tile_docs = out.shape[1] // tiles
    copies = []
    for j in range(tiles):
        docs = pl.ds(j * tile_docs, tile_docs)
        vec, quality = vec_ref[rows, docs], quality_ref[:, docs]
        total = add_f32(mine_ref[:, docs], other_ref[:, docs])
        if second:
            first = add_f32(refs[0][:, docs], refs[1][:, docs]) * quality - vec
            value = 2.0 * (total * quality - first) - vec
        else:
            value = total * quality - vec
        out[:, docs] = value
        copies.append(pltpu.make_async_copy(out.at[:, docs], out_ref.at[rows, docs], sems.at[j]))
        copies[-1].start()
    for copy in copies:
        copy.wait()


def lookup_kernel(ids_ref, table, out_ref):
    entries = ids_ref.shape[0] // out_ref.shape[0]

    def step(b, carry):
        total = table[ids_ref[b * entries]].astype(jnp.float32)
        for k in range(1, entries):
            total = total + table[ids_ref[b * entries + k]].astype(jnp.float32)
        out_ref[b] = total.astype(out_ref.dtype)
        return carry

    lax.fori_loop(0, out_ref.shape[0], step, 0, unroll=4)


def table_kernel(ids_ref, *refs):
    *shards, out_ref, table, sems = refs
    blocks = shards[0].shape[0]
    copies = [
        pltpu.make_async_copy(ref, table.at[pl.ds(i * blocks, blocks)], sems.at[i])
        for i, ref in enumerate(shards)
    ]
    for copy in copies:
        copy.start()
    table[len(shards) * blocks] = jnp.zeros(table.shape[1:], table.dtype)
    for copy in copies:
        copy.wait()
    lookup_kernel(ids_ref, table, out_ref)


def expand_kernel(own_ref, *refs):
    *arrived_refs, emb_ref, out_ref = refs
    blocks = own_ref.shape[0]
    block_len = emb_ref.shape[0] // blocks

    def step(b, carry):
        docs = pl.ds(pl.multiple_of(b * block_len, block_len), block_len)
        total = own_ref[b]
        for ref in arrived_refs:
            total = total + ref[b].astype(jnp.float32)
        out_ref[:, docs] = lax.dot_general(
            total.astype(jnp.bfloat16), emb_ref[docs], (((1,), (1,)), ((), ())),
            preferred_element_type=jnp.float32,
        ).astype(jnp.bfloat16)
        return carry

    lax.fori_loop(0, blocks, step, 0, unroll=TILE_BLOCKS)


def body(embeddings, quality, probes, neighbors):
    nrow, ncol = lax.axis_size("row"), lax.axis_size("col")
    me = lax.axis_index("row")
    blk_count, list_len = neighbors.shape
    docs, width = embeddings.shape
    nprobe = probes.shape[0]
    group = nprobe // GROUPS
    tiles = blk_count // TILE_BLOCKS
    near = [NEXT, SIDE]
    far = [1 << i for i in reversed(range(nrow.bit_length() - 1)) if 1 << i not in near]
    far_dests = [0]
    for m in reversed(far):
        far_dests = [d | m for d in far_dests] + far_dests

    def table_ids(lists, dest, bits):
        flat = lax.dynamic_slice_in_dim(lists, (me ^ dest) * blk_count, blk_count).reshape(-1)
        apart = (flat // blk_count) ^ me
        place = flat % blk_count
        for i, m in enumerate(bits):
            place = place + jnp.where((apart & m) != 0, blk_count << i, 0)
        return jnp.where((apart & ~sum(bits)) == 0, place, blk_count << len(bits))

    qrow = quality[None, :]

    def blocks_out(count, dtype):
        return jax.ShapeDtypeStruct((count, group, width), dtype)

    shard_out = blocks_out(blk_count, jnp.bfloat16)
    vec_out = jax.ShapeDtypeStruct((nprobe, docs), jnp.float32)

    def rows(c):
        return pl.ds(c * group, group)

    def first_sums(c, qrow):
        if c:
            return pl.pallas_call(
                functools.partial(next_sums_kernel, rows(c), ()),
                in_specs=[VMEM] * 3,
                out_specs=VMEM,
                out_shape=shard_out,
                compiler_params=params(),
            )(probes, qrow, embeddings)
        return pl.pallas_call(
            functools.partial(first_sums_kernel, rows(c)),
            in_specs=[HBM] * 3,
            out_specs=VMEM,
            out_shape=shard_out,
            scratch_shapes=[
                pltpu.VMEM((group, docs), jnp.float32),
                pltpu.VMEM((1, docs), jnp.float32),
                pltpu.VMEM((tiles, docs // tiles, width), jnp.bfloat16),
                pltpu.SemaphoreType.DMA((tiles + 2,)),
            ],
            compiler_params=params(),
        )(*(pltpu.with_memory_space_constraint(v, pltpu.HBM) for v in (probes, qrow, embeddings)))

    def next_sums(c, pair):
        return pl.pallas_call(
            functools.partial(later_sums_kernel, rows(c)),
            in_specs=[VMEM] * 5,
            out_specs=VMEM,
            out_shape=shard_out,
            compiler_params=params(),
        )(*pair, probes, qrow, embeddings)

    def fill(c, held, pair, *others):
        held = [] if held is None else [held]
        return pl.pallas_call(
            functools.partial(fill_kernel, rows(c), bool(others)),
            in_specs=[VMEM] * (4 + len(others)) + [ANY] * len(held),
            out_specs=HBM,
            out_shape=vec_out,
            input_output_aliases={4 + len(others): 0} if held else {},
            scratch_shapes=[pltpu.VMEM((group, docs), jnp.float32), pltpu.SemaphoreType.DMA((4,))],
            compiler_params=params(),
        )(*pair, probes, qrow, *others, *held)

    def combine_first(ids, shards):
        return pl.pallas_call(
            table_kernel,
            in_specs=[SMEM] + [VMEM] * len(shards),
            out_specs=[VMEM] * 2,
            out_shape=[shard_out, blocks_out(len(shards) * blk_count + 1, jnp.bfloat16)],
            scratch_shapes=[pltpu.SemaphoreType.DMA((len(shards),))],
            compiler_params=params(),
        )(ids, *shards)

    def combine(ids, table, dtype):
        return pl.pallas_call(
            lookup_kernel,
            in_specs=[SMEM, VMEM],
            out_specs=VMEM,
            out_shape=blocks_out(blk_count, dtype),
            compiler_params=params(),
        )(ids, table)

    def expand(own, arrived):
        return pl.pallas_call(
            expand_kernel,
            in_specs=[VMEM] * (len(arrived) + 2),
            out_specs=VMEM,
            out_shape=jax.ShapeDtypeStruct((group, docs), jnp.bfloat16),
            compiler_params=params(),
        )(own, *arrived, embeddings)

    def reduce(outgoing, bits):
        arrived = []
        for m in bits:
            taken = {d ^ m: swap(outgoing.pop(d), "row", nrow, m) for d in list(outgoing) if d & m}
            for d, value in taken.items():
                if d:
                    outgoing[d] = add_bf16(outgoing[d], value)
                else:
                    arrived.append(value)
        return arrived

    token = []

    def take(*values):
        if token:
            values = lax.optimization_barrier(values + (token.pop(),))[:-1]
        return values

    lists = lax.all_gather(neighbors, "row", axis=0, tiled=True)
    first = second = None
    gathered, tables, own, arrived, products, halves = ([None] * GROUPS for _ in range(6))
    for word in (word for line in ORDER for word in line.split()):
        c, step = ord(word[0]) - ord("A"), word[1]
        if step == "l":
            (lists,) = take(lists)
            ids = {(0, d): table_ids(lists, d, near) for d in far_dests}
            ids.update({(1, d): table_ids(lists, d, far) for d in (NEXT | SIDE, SIDE, NEXT, 0)})
            ids = lax.optimization_barrier(ids)
            token.append(ids[0, 0])
        elif step == "s":
            if products[c] is None:
                sums = first_sums(c, *take(qrow))
            else:
                sums = next_sums(c, take(*products[c]))
                halves[c] = products[c]
            token.append(sums)
            gathered[c] = [sums] + [swap(sums, "row", nrow, m) for m in (far[:1] if c else near)]
        elif step == "g":
            gathered[c] = list(take(*gathered[c]))
            gathered[c].append(swap(gathered[c][1], "row", nrow, SIDE))
            token.append(gathered[c][1])
        elif step == "o":
            held, table, outgoing = take(*gathered[c]), None, {}
            for d in far_dests[:-1]:
                if table is None:
                    outgoing[d], table = combine_first(ids[c, d], held)
                else:
                    outgoing[d] = combine(ids[c, d], table, jnp.bfloat16)
            tables[c] = table
            token.append(outgoing[far_dests[-2]])
            arrived[c] = reduce(outgoing, far)
        elif step == "h":
            for m in far[1:]:
                gathered[c] += [swap(v, "row", nrow, m) for v in gathered[c]]
            value, tables[c] = combine_first(ids[c, NEXT | SIDE], take(*gathered[c]))
            arrived[c] = [swap(value, "row", nrow, SIDE)]
            token.append(value)
        elif step == "i":
            (table,) = take(tables[c])
            value = combine(ids[c, SIDE], table, jnp.bfloat16)
            arrived[c].append(swap(value, "row", nrow, SIDE))
            token.append(value)
        elif step == "j":
            (table,) = take(tables[c])
            own[c] = combine(ids[c, NEXT], table, jnp.bfloat16)
            token.append(own[c])
        elif step == "n":
            value = add_bf16(*take(own[c], arrived[c].pop(0)))
            arrived[c].append(swap(value, "row", nrow, NEXT))
            token.append(value)
        elif step == "w":
            (table,) = take(tables[c])
            own[c] = combine(ids[c, 0], table, jnp.float32)
            token.append(own[c])
        elif step == "e":
            here, *later = take(own[c], *arrived[c])
            value = expand(here, later)
            products[c] = [value, swap(value, "col", ncol, 1)]
            token.append(value)
        elif step == "c":
            pair = take(*products[c])
            for i in range(1, ncol.bit_length() - 1):
                value = add_bf16(*pair)
                pair = [value, swap(value, "col", ncol, 1 << i)]
            products[c] = pair
            token.append(value)
        elif step == "p":
            first = fill(c, first, take(*halves[c]))
            token.append(first)
        else:
            second = fill(c, second, take(*products[c]), *halves[c])
            token.append(second)
    return first, second


def solution(mesh):
    placed = (P("row", "col"), P("row"), P(None, "row"), P("row", None))
    return jax.shard_map(
        body,
        mesh=mesh,
        in_specs=placed,
        out_specs=(P(None, "row"), P(None, "row")),
        check_vma=False,
    )
```

time: 167 us -> 191 us (1.14)
  blocking collectives: 0 us -> 44.5 us
  starting transfers between devices: 55.6 us -> 20.2 us
  waiting for transfers between devices: 71.6 us -> 87.5 us
    all_gather x0 -> x1, blocking collectives: none -> 44.5 us  [body(): lists = lax.all_gather(neighbors, 'row', axis=0, tiled=True)]
    ppermute x41 -> x24, starting transfers between devices: 55.6 us -> 20.2 us  [swap(): return lax.ppermute(value, axis, [(i, i ^ mask) for i in range(size)])]
    ppermute x41 -> x24, waiting for transfers between devices: 71.6 us -> 87.5 us  [swap(): return lax.ppermute(value, axis, [(i, i ^ mask) for i in range(size)])]
    unnamed x10, local copies, waits for them, and re-layouts: 2.21 us -> 0.03 us
  transfers between devices with their start and end apart: 41 -> 24, of which waited for: 21 -> 14; matrix products, arithmetic and copies ran while one was open for 0% -> 1% of each run, Pallas kernels for 18% -> 17%
where the time goes in v5:
time: 191 us
  waiting for transfers between devices  87.5 us (46%)
  blocking collectives  44.5 us (23%)
  Pallas kernels  36 us (19%)
  starting transfers between devices  20.2 us (11%)
    ppermute x24, waiting for transfers between devices, swap(): return lax.ppermute(value, axis, [(i, i ^ mask) for i in range(size)])  87.5 us
    all_gather x1, blocking collectives, body(): lists = lax.all_gather(neighbors, 'row', axis=0, tiled=True)  44.5 us
    ppermute x24, starting transfers between devices, swap(): return lax.ppermute(value, axis, [(i, i ^ mask) for i in range(size)])  20.2 us
    pallas_call x8, Pallas kernels, combine(): pl.pallas_call(lookup_kernel, in_specs=[SMEM, VMEM], out_specs=VMEM, out_...  10.1 us
    pallas_call x4, Pallas kernels, expand(): pl.pallas_call(expand_kernel, in_specs=[VMEM] * (len(arrived) + 2), out_s...  8.19 us
    pallas_call x4, Pallas kernels, combine_first(): pl.pallas_call(table_kernel, in_specs=[SMEM] + [VMEM] * len(shards), out_...  6.62 us
  transfers between devices with their start and end apart: 24, of which 14 were waited for; matrix products, arithmetic and copies ran while one was open for 1% of the time, Pallas kernels for 17%

profile of v5, /device:TPU:0, one launch (start us, length us, event | category | flops | bytes accessed | tf_op | source)
XLA Modules:
  0.0 190.8 jit_solution(13303317370729962219)
XLA Ops:
  0.7 3.0 %shard_map.59.refs_0_ = bf16[64,16,256]{2,1,0:T(8,128)(2,1)S(1)} custom-call(f32[32,8192]{1,0:T(8,128)} %vec_ref.11, f32[1,8192]{1,0:T(1,128)} %bitcast.4, bf16[8192,256]{1,0:T(8,128)(2,1)} %refs_2_.7), custom_call_target="tpu_custom_call" | custom-call | tf_op jit(solution)/shard_map/pallas_call | solution.py:215
  3.6 3.0 %collective-permute-start.1 = (bf16[64,16,256]{2,1,0:T(8,128)(2,1)S(1)}, bf16[64,16,256]{2,1,0:T(8,128)(2,1)S(1)}, u32[]{:S(2)}, u32[]{:S(2)}) collective-permute-start(bf16[64,16,256]{2,1,0:T(8,128)(2,1)S(1)} %shard_map.59.refs_0_), channel_id=1, source_target_pairs={{0,4},{4,0},{8,12},{12,8},{16,20},{20,16},{24,28},{28,24},{1,5},{5... | collective-permute-start | bytes 1572872 | tf_op jit(solution)/shard_map/ppermute | solution.py:38
  9.8 2.7 %collective-permute-start.2 = (bf16[64,16,256]{2,1,0:T(8,128)(2,1)S(1)}, bf16[64,16,256]{2,1,0:T(8,128)(2,1)}, u32[]{:S(2)}, u32[]{:S(2)}) collective-permute-start(bf16[64,16,256]{2,1,0:T(8,128)(2,1)S(1)} %shard_map.60.refs_0_), channel_id=1, source_target_pairs={{0,16},{4,20},{8,24},{12,28},{16,0},{20,4},{24,8},{28,12},{1,17},{... | collective-permute-start | bytes 1572872 | tf_op jit(solution)/shard_map/ppermute | solution.py:38
  12.4 44.5 %all-gather = s32[8,64,8]{1,2,0:T(8,128)S(1)} all-gather(s32[1,64,8]{1,2,0:T(8,128)S(1)} %bitcast.12), channel_id=1, replica_groups=mesh['row'=8,'col'=4] {'row'}, dimensions={0}, use_global_device_ids=true | all-gather | bytes 18432 | tf_op jit(solution)/shard_map/all_gather | solution.py:296
  60.0 2.1 %collective-permute-start.4 = (bf16[64,16,256]{2,1,0:T(8,128)(2,1)S(1)}, bf16[64,16,256]{2,1,0:T(8,128)(2,1)S(1)}, u32[]{:S(2)}, u32[]{:S(2)}) collective-permute-start(bf16[64,16,256]{2,1,0:T(8,128)(2,1)S(1)} %get-tuple-element.92), channel_id=1, source_target_pairs={{0,4},{4,0},{8,12},{12,8},{16,20},{20,16},{24,28},{28,24},{1,5},{5... | collective-permute-start | bytes 1572872 | tf_op jit(solution)/shard_map/ppermute | solution.py:38
  62.0 7.7 %collective-permute-done.3.refs_3_ = bf16[64,16,256]{2,1,0:T(8,128)(2,1)} collective-permute-done((bf16[64,16,256]{2,1,0:T(8,128)(2,1)S(1)}, bf16[64,16,256]{2,1,0:T(8,128)(2,1)}, u32[]{:S(2)}, u32[]{:S(2)}) %collective-permute-start.3) | collective-permute-done | bytes 524320 | tf_op jit(solution)/shard_map/ppermute | solution.py:38
  69.8 1.9 %shard_map.62 = (bf16[64,16,256]{2,1,0:T(8,128)(2,1)S(1)}, bf16[257,16,256]{2,1,0:T(8,128)(2,1)S(1)}) custom-call(s32[512]{0:T(512)S(1)} %get-tuple-element.89.ids_ref, bf16[64,16,256]{2,1,0:T(8,128)(2,1)S(1)} %shard_map.59.refs_0_, bf16[64,16,256]{2,1,0:T(8,128)(2,1)S(1)} %collective-permute-done.refs_1_, ...), custom_call_target="tpu_custom_call" | custom-call | tf_op jit(solution)/shard_map/pallas_call | solution.py:251
  75.7 4.3 %collective-permute-done.4 = bf16[64,16,256]{2,1,0:T(8,128)(2,1)S(1)} collective-permute-done((bf16[64,16,256]{2,1,0:T(8,128)(2,1)S(1)}, bf16[64,16,256]{2,1,0:T(8,128)(2,1)S(1)}, u32[]{:S(2)}, u32[]{:S(2)}) %collective-permute-start.4) | collective-permute-done | bytes 524320 | tf_op jit(solution)/shard_map/ppermute | solution.py:38
  81.5 5.2 %collective-permute-done.7.refs_0_ = bf16[64,16,256]{2,1,0:T(8,128)(2,1)S(1)} collective-permute-done((bf16[64,16,256]{2,1,0:T(8,128)(2,1)S(1)}, bf16[64,16,256]{2,1,0:T(8,128)(2,1)S(1)}, u32[]{:S(2)}, u32[]{:S(2)}) %collective-permute-start.7) | collective-permute-done | bytes 524320 | tf_op jit(solution)/shard_map/ppermute | solution.py:38
  86.7 2.0 %shard_map.67 = bf16[16,8192]{1,0:T(8,128)(2,1)S(1)} custom-call(f32[64,16,256]{2,1,0:T(8,128)S(1)} %shard_map.65.own_ref, bf16[64,16,256]{2,1,0:T(8,128)(2,1)S(1)} %collective-permute-done.7.refs_0_, bf16[8192,256]{1,0:T(8,128)(2,1)S(1)} %copy-done.1), custom_call_target="tpu_custom_call" | custom-call | tf_op jit(solution)/shard_map/pallas_call | solution.py:270
  88.8 3.4 %collective-permute-done.6.refs_1_ = bf16[64,16,256]{2,1,0:T(8,128)(2,1)S(1)} collective-permute-done((bf16[64,16,256]{2,1,0:T(8,128)(2,1)S(1)}, bf16[64,16,256]{2,1,0:T(8,128)(2,1)S(1)}, u32[]{:S(2)}, u32[]{:S(2)}) %collective-permute-start.6) | collective-permute-done | bytes 524320 | tf_op jit(solution)/shard_map/ppermute | solution.py:38
  92.2 2.0 %shard_map.68 = bf16[16,8192]{1,0:T(8,128)(2,1)S(1)} custom-call(f32[64,16,256]{2,1,0:T(8,128)S(1)} %shard_map.66.own_ref, bf16[64,16,256]{2,1,0:T(8,128)(2,1)S(1)} %collective-permute-done.5.refs_0_, bf16[64,16,256]{2,1,0:T(8,128)(2,1)S(1)} %collective-permute-done.6.refs_1_, bf16[8192,256]{1,0:T(8,128)(2,1)S(1)} %copy-done.1), custom_call_target="tpu_custom_call" | custom-call | tf_op jit(solution)/shard_map/pallas_call | solution.py:270
  97.5 6.1 %collective-permute-done.11.other_ref.refs_1_ = bf16[16,8192]{1,0:T(8,128)(2,1)S(1)} collective-permute-done((bf16[16,8192]{1,0:T(8,128)(2,1)S(1)}, bf16[16,8192]{1,0:T(8,128)(2,1)S(1)}, u32[]{:S(2)}, u32[]{:S(2)}) %collective-permute-start.11) | collective-permute-done | bytes 262176 | tf_op jit(solution)/shard_map/ppermute | solution.py:38
  106.2 2.6 %collective-permute-done.10.other_ref.refs_1_ = bf16[16,8192]{1,0:T(8,128)(2,1)S(1)} collective-permute-done((bf16[16,8192]{1,0:T(8,128)(2,1)S(1)}, bf16[16,8192]{1,0:T(8,128)(2,1)S(1)}, u32[]{:S(2)}, u32[]{:S(2)}) %collective-permute-start.10) | collective-permute-done | bytes 262176 | tf_op jit(solution)/shard_map/ppermute | solution.py:38
  110.4 7.9 %collective-permute-done.14.refs_2_ = bf16[64,16,256]{2,1,0:T(8,128)(2,1)S(1)} collective-permute-done((bf16[64,16,256]{2,1,0:T(8,128)(2,1)S(1)}, bf16[64,16,256]{2,1,0:T(8,128)(2,1)S(1)}, u32[]{:S(2)}, u32[]{:S(2)}) %collective-permute-start.14) | collective-permute-done | bytes 524320 | tf_op jit(solution)/shard_map/ppermute | solution.py:38
  118.3 6.4 %collective-permute-done.13.refs_1_ = bf16[64,16,256]{2,1,0:T(8,128)(2,1)S(1)} collective-permute-done((bf16[64,16,256]{2,1,0:T(8,128)(2,1)S(1)}, bf16[64,16,256]{2,1,0:T(8,128)(2,1)S(1)}, u32[]{:S(2)}, u32[]{:S(2)}) %collective-permute-start.13) | collective-permute-done | bytes 524320 | tf_op jit(solution)/shard_map/ppermute | solution.py:38
  125.7 10.4 %collective-permute-done.12.refs_1_ = bf16[64,16,256]{2,1,0:T(8,128)(2,1)S(1)} collective-permute-done((bf16[64,16,256]{2,1,0:T(8,128)(2,1)S(1)}, bf16[64,16,256]{2,1,0:T(8,128)(2,1)S(1)}, u32[]{:S(2)}, u32[]{:S(2)}) %collective-permute-start.12) | collective-permute-done | bytes 524320 | tf_op jit(solution)/shard_map/ppermute | solution.py:38
  145.9 6.5 %collective-permute-done.16 = bf16[64,16,256]{2,1,0:T(8,128)(2,1)S(1)} collective-permute-done((bf16[64,16,256]{2,1,0:T(8,128)(2,1)S(1)}, bf16[64,16,256]{2,1,0:T(8,128)(2,1)S(1)}, u32[]{:S(2)}, u32[]{:S(2)}) %collective-permute-start.16) | collective-permute-done | bytes 524320 | tf_op jit(solution)/shard_map/ppermute | solution.py:38
  154.7 9.3 %collective-permute-done.19.refs_0_ = bf16[64,16,256]{2,1,0:T(8,128)(2,1)S(1)} collective-permute-done((bf16[64,16,256]{2,1,0:T(8,128)(2,1)S(1)}, bf16[64,16,256]{2,1,0:T(8,128)(2,1)S(1)}, u32[]{:S(2)}, u32[]{:S(2)}) %collective-permute-start.19) | collective-permute-done | bytes 524320 | tf_op jit(solution)/shard_map/ppermute | solution.py:38
  164.0 2.0 %shard_map.79 = bf16[16,8192]{1,0:T(8,128)(2,1)S(1)} custom-call(f32[64,16,256]{2,1,0:T(8,128)S(1)} %shard_map.75.own_ref, bf16[64,16,256]{2,1,0:T(8,128)(2,1)S(1)} %collective-permute-done.19.refs_0_, bf16[8192,256]{1,0:T(8,128)(2,1)S(1)} %copy-done.1), custom_call_target="tpu_custom_call" | custom-call | tf_op jit(solution)/shard_map/pallas_call | solution.py:270
  166.1 7.2 %collective-permute-done.18.refs_1_ = bf16[64,16,256]{2,1,0:T(8,128)(2,1)S(1)} collective-permute-done((bf16[64,16,256]{2,1,0:T(8,128)(2,1)S(1)}, bf16[64,16,256]{2,1,0:T(8,128)(2,1)S(1)}, u32[]{:S(2)}, u32[]{:S(2)}) %collective-permute-start.18) | collective-permute-done | bytes 524320 | tf_op jit(solution)/shard_map/ppermute | solution.py:38
  173.3 2.1 %shard_map.80 = bf16[16,8192]{1,0:T(8,128)(2,1)S(1)} custom-call(f32[64,16,256]{2,1,0:T(8,128)S(1)} %shard_map.77.own_ref, bf16[64,16,256]{2,1,0:T(8,128)(2,1)S(1)} %collective-permute-done.17.refs_0_, bf16[64,16,256]{2,1,0:T(8,128)(2,1)S(1)} %collective-permute-done.18.refs_1_, bf16[8192,256]{1,0:T(8,128)(2,1)S(1)} %copy-done.1), custom_call_target="tpu_custom_call" | custom-call | tf_op jit(solution)/shard_map/pallas_call | solution.py:270
  178.6 6.1 %collective-permute-done.23.other_ref = bf16[16,8192]{1,0:T(8,128)(2,1)S(1)} collective-permute-done((bf16[16,8192]{1,0:T(8,128)(2,1)S(1)}, bf16[16,8192]{1,0:T(8,128)(2,1)S(1)}, u32[]{:S(2)}, u32[]{:S(2)}) %collective-permute-start.23) | collective-permute-done | bytes 262176 | tf_op jit(solution)/shard_map/ppermute | solution.py:38
  185.6 4.3 %collective-permute-done.22.other_ref = bf16[16,8192]{1,0:T(8,128)(2,1)S(1)} collective-permute-done((bf16[16,8192]{1,0:T(8,128)(2,1)S(1)}, bf16[16,8192]{1,0:T(8,128)(2,1)S(1)}, u32[]{:S(2)}, u32[]{:S(2)}) %collective-permute-start.22) | collective-permute-done | bytes 262176 | tf_op jit(solution)/shard_map/ppermute | solution.py:38
  (81 shorter events, 37.1 us)
Async XLA Ops:
  3.6 53.3 %collective-permute-start.1 = (bf16[64,16,256]{2,1,0:T(8,128)(2,1)S(1)}, bf16[64,16,256]{2,1,0:T(8,128)(2,1)S(1)}, u32[]{:S(2)}, u32[]{:S(2)}) collective-permute-start(bf16[64,16,256]{2,1,0:T(8,128)(2,1)S(1)} %shard_map.59.refs_0_), channel_id=1, source_target_pairs={{0,4},{4,0},{8,12},{12,8},{16,20},{20,16},{24,28},{28,24},{1,5},{5... | collective-permute-start | bytes 1572872 | tf_op jit(solution)/shard_map/ppermute | solution.py:38
  6.7 50.3 %collective-permute-start = (bf16[64,16,256]{2,1,0:T(8,128)(2,1)S(1)}, bf16[64,16,256]{2,1,0:T(8,128)(2,1)S(1)}, u32[]{:S(2)}, u32[]{:S(2)}) collective-permute-start(bf16[64,16,256]{2,1,0:T(8,128)(2,1)S(1)} %shard_map.59.refs_0_), channel_id=1, source_target_pairs={{0,8},{4,12},{8,0},{12,4},{16,24},{20,28},{24,16},{28,20},{1,9},{5... | collective-permute-start | bytes 1572872 | tf_op jit(solution)/shard_map/ppermute | solution.py:38
  9.8 48.4 %collective-permute-start.2 = (bf16[64,16,256]{2,1,0:T(8,128)(2,1)S(1)}, bf16[64,16,256]{2,1,0:T(8,128)(2,1)}, u32[]{:S(2)}, u32[]{:S(2)}) collective-permute-start(bf16[64,16,256]{2,1,0:T(8,128)(2,1)S(1)} %shard_map.60.refs_0_), channel_id=1, source_target_pairs={{0,16},{4,20},{8,24},{12,28},{16,0},{20,4},{24,8},{28,12},{1,17},{... | collective-permute-start | bytes 1572872 | tf_op jit(solution)/shard_map/ppermute | solution.py:38
  57.0 12.8 %collective-permute-start.3 = (bf16[64,16,256]{2,1,0:T(8,128)(2,1)S(1)}, bf16[64,16,256]{2,1,0:T(8,128)(2,1)}, u32[]{:S(2)}, u32[]{:S(2)}) collective-permute-start(bf16[64,16,256]{2,1,0:T(8,128)(2,1)S(1)} %collective-permute-done.refs_1_), channel_id=1, source_target_pairs={{0,4},{4,0},{8,12},{12,8},{16,20},{20,16},{24,28},{28,24},{1,5},{5... | collective-permute-start | bytes 1572872 | tf_op jit(solution)/shard_map/ppermute | solution.py:38
  60.0 20.0 %collective-permute-start.4 = (bf16[64,16,256]{2,1,0:T(8,128)(2,1)S(1)}, bf16[64,16,256]{2,1,0:T(8,128)(2,1)S(1)}, u32[]{:S(2)}, u32[]{:S(2)}) collective-permute-start(bf16[64,16,256]{2,1,0:T(8,128)(2,1)S(1)} %get-tuple-element.92), channel_id=1, source_target_pairs={{0,4},{4,0},{8,12},{12,8},{16,20},{20,16},{24,28},{28,24},{1,5},{5... | collective-permute-start | bytes 1572872 | tf_op jit(solution)/shard_map/ppermute | solution.py:38
  71.7 15.0 %collective-permute-start.7 = (bf16[64,16,256]{2,1,0:T(8,128)(2,1)S(1)}, bf16[64,16,256]{2,1,0:T(8,128)(2,1)S(1)}, u32[]{:S(2)}, u32[]{:S(2)}) collective-permute-start(bf16[64,16,256]{2,1,0:T(8,128)(2,1)S(1)} %get-tuple-element.97), channel_id=1, source_target_pairs={{0,16},{4,20},{8,24},{12,28},{16,0},{20,4},{24,8},{28,12},{1,17},{... | collective-permute-start | bytes 1572872 | tf_op jit(solution)/shard_map/ppermute | solution.py:38
  80.1 12.1 %collective-permute-start.6 = (bf16[64,16,256]{2,1,0:T(8,128)(2,1)S(1)}, bf16[64,16,256]{2,1,0:T(8,128)(2,1)S(1)}, u32[]{:S(2)}, u32[]{:S(2)}) collective-permute-start(bf16[64,16,256]{2,1,0:T(8,128)(2,1)S(1)} %add_convert_fusion.1), channel_id=1, source_target_pairs={{0,8},{4,12},{8,0},{12,4},{16,24},{20,28},{24,16},{28,20},{1,9},{5... | collective-permute-start | bytes 1572872 | tf_op jit(solution)/shard_map/ppermute | solution.py:38
  80.2 12.1 %collective-permute-start.5 = (bf16[64,16,256]{2,1,0:T(8,128)(2,1)S(1)}, bf16[64,16,256]{2,1,0:T(8,128)(2,1)S(1)}, u32[]{:S(2)}, u32[]{:S(2)}) collective-permute-start(bf16[64,16,256]{2,1,0:T(8,128)(2,1)S(1)} %shard_map.63), channel_id=1, source_target_pairs={{0,4},{4,0},{8,12},{12,8},{16,20},{20,16},{24,28},{28,24},{1,5},{5... | collective-permute-start | bytes 1572872 | tf_op jit(solution)/shard_map/ppermute | solution.py:38
  88.8 5.6 %collective-permute-start.9 = (bf16[16,8192]{1,0:T(8,128)(2,1)S(1)}, bf16[16,8192]{1,0:T(8,128)(2,1)S(1)}, u32[]{:S(2)}, u32[]{:S(2)}) collective-permute-start(bf16[16,8192]{1,0:T(8,128)(2,1)S(1)} %shard_map.67), channel_id=1, source_target_pairs={{0,1},{1,0},{2,3},{3,2},{4,5},{5,4},{6,7},{7,6},{8,9},{9,8},{10,11... | collective-permute-start | bytes 786440 | tf_op jit(solution)/shard_map/ppermute | solution.py:38
  94.3 1.7 collective-permute-start.8
  94.4 9.2 %collective-permute-start.11 = (bf16[16,8192]{1,0:T(8,128)(2,1)S(1)}, bf16[16,8192]{1,0:T(8,128)(2,1)S(1)}, u32[]{:S(2)}, u32[]{:S(2)}) collective-permute-start(bf16[16,8192]{1,0:T(8,128)(2,1)S(1)} %add_convert_fusion.5.mine_ref.refs_0_), channel_id=1, source_target_pairs={{0,2},{1,3},{2,0},{3,1},{4,6},{5,7},{6,4},{7,5},{8,10},{9,11},{10,... | collective-permute-start | bytes 786440 | tf_op jit(solution)/shard_map/ppermute | solution.py:38
  96.1 12.7 %collective-permute-start.10 = (bf16[16,8192]{1,0:T(8,128)(2,1)S(1)}, bf16[16,8192]{1,0:T(8,128)(2,1)S(1)}, u32[]{:S(2)}, u32[]{:S(2)}) collective-permute-start(bf16[16,8192]{1,0:T(8,128)(2,1)S(1)} %add_convert_fusion.4.mine_ref.refs_0_), channel_id=1, source_target_pairs={{0,2},{1,3},{2,0},{3,1},{4,6},{5,7},{6,4},{7,5},{8,10},{9,11},{10,... | collective-permute-start | bytes 786440 | tf_op jit(solution)/shard_map/ppermute | solution.py:38
  105.1 13.2 %collective-permute-start.14 = (bf16[64,16,256]{2,1,0:T(8,128)(2,1)S(1)}, bf16[64,16,256]{2,1,0:T(8,128)(2,1)S(1)}, u32[]{:S(2)}, u32[]{:S(2)}) collective-permute-start(bf16[64,16,256]{2,1,0:T(8,128)(2,1)S(1)} %shard_map.69.refs_0_), channel_id=1, source_target_pairs={{0,4},{4,0},{8,12},{12,8},{16,20},{20,16},{24,28},{28,24},{1,5},{5... | collective-permute-start | bytes 1572872 | tf_op jit(solution)/shard_map/ppermute | solution.py:38
  106.2 18.5 %collective-permute-start.13 = (bf16[64,16,256]{2,1,0:T(8,128)(2,1)S(1)}, bf16[64,16,256]{2,1,0:T(8,128)(2,1)S(1)}, u32[]{:S(2)}, u32[]{:S(2)}) collective-permute-start(bf16[64,16,256]{2,1,0:T(8,128)(2,1)S(1)} %shard_map.69.refs_0_), channel_id=1, source_target_pairs={{0,8},{4,12},{8,0},{12,4},{16,24},{20,28},{24,16},{28,20},{1,9},{5... | collective-permute-start | bytes 1572872 | tf_op jit(solution)/shard_map/ppermute | solution.py:38
  110.3 25.8 %collective-permute-start.12 = (bf16[64,16,256]{2,1,0:T(8,128)(2,1)S(1)}, bf16[64,16,256]{2,1,0:T(8,128)(2,1)S(1)}, u32[]{:S(2)}, u32[]{:S(2)}) collective-permute-start(bf16[64,16,256]{2,1,0:T(8,128)(2,1)S(1)} %shard_map.70.refs_0_), channel_id=1, source_target_pairs={{0,16},{4,20},{8,24},{12,28},{16,0},{20,4},{24,8},{28,12},{1,17},{... | collective-permute-start | bytes 1572872 | tf_op jit(solution)/shard_map/ppermute | solution.py:38
  124.7 13.8 %collective-permute-start.15 = (bf16[64,16,256]{2,1,0:T(8,128)(2,1)S(1)}, bf16[64,16,256]{2,1,0:T(8,128)(2,1)S(1)}, u32[]{:S(2)}, u32[]{:S(2)}) collective-permute-start(bf16[64,16,256]{2,1,0:T(8,128)(2,1)S(1)} %collective-permute-done.13.refs_1_), channel_id=1, source_target_pairs={{0,4},{4,0},{8,12},{12,8},{16,20},{20,16},{24,28},{28,24},{1,5},{5... | collective-permute-start | bytes 1572872 | tf_op jit(solution)/shard_map/ppermute | solution.py:38
  137.5 14.9 %collective-permute-start.16 = (bf16[64,16,256]{2,1,0:T(8,128)(2,1)S(1)}, bf16[64,16,256]{2,1,0:T(8,128)(2,1)S(1)}, u32[]{:S(2)}, u32[]{:S(2)}) collective-permute-start(bf16[64,16,256]{2,1,0:T(8,128)(2,1)S(1)} %get-tuple-element.124), channel_id=1, source_target_pairs={{0,4},{4,0},{8,12},{12,8},{16,20},{20,16},{24,28},{28,24},{1,5},{5... | collective-permute-start | bytes 1572872 | tf_op jit(solution)/shard_map/ppermute | solution.py:38
  140.0 24.0 %collective-permute-start.19 = (bf16[64,16,256]{2,1,0:T(8,128)(2,1)S(1)}, bf16[64,16,256]{2,1,0:T(8,128)(2,1)S(1)}, u32[]{:S(2)}, u32[]{:S(2)}) collective-permute-start(bf16[64,16,256]{2,1,0:T(8,128)(2,1)S(1)} %get-tuple-element.130), channel_id=1, source_target_pairs={{0,16},{4,20},{8,24},{12,28},{16,0},{20,4},{24,8},{28,12},{1,17},{... | collective-permute-start | bytes 1572872 | tf_op jit(solution)/shard_map/ppermute | solution.py:38
  141.4 24.7 %collective-permute-start.17 = (bf16[64,16,256]{2,1,0:T(8,128)(2,1)S(1)}, bf16[64,16,256]{2,1,0:T(8,128)(2,1)S(1)}, u32[]{:S(2)}, u32[]{:S(2)}) collective-permute-start(bf16[64,16,256]{2,1,0:T(8,128)(2,1)S(1)} %shard_map.73), channel_id=1, source_target_pairs={{0,4},{4,0},{8,12},{12,8},{16,20},{20,16},{24,28},{28,24},{1,5},{5... | collective-permute-start | bytes 1572872 | tf_op jit(solution)/shard_map/ppermute | solution.py:38
  152.5 20.8 %collective-permute-start.18 = (bf16[64,16,256]{2,1,0:T(8,128)(2,1)S(1)}, bf16[64,16,256]{2,1,0:T(8,128)(2,1)S(1)}, u32[]{:S(2)}, u32[]{:S(2)}) collective-permute-start(bf16[64,16,256]{2,1,0:T(8,128)(2,1)S(1)} %add_convert_fusion), channel_id=1, source_target_pairs={{0,8},{4,12},{8,0},{12,4},{16,24},{20,28},{24,16},{28,20},{1,9},{5... | collective-permute-start | bytes 1572872 | tf_op jit(solution)/shard_map/ppermute | solution.py:38
  166.0 9.4 %collective-permute-start.21 = (bf16[16,8192]{1,0:T(8,128)(2,1)S(1)}, bf16[16,8192]{1,0:T(8,128)(2,1)S(1)}, u32[]{:S(2)}, u32[]{:S(2)}) collective-permute-start(bf16[16,8192]{1,0:T(8,128)(2,1)S(1)} %shard_map.79), channel_id=1, source_target_pairs={{0,1},{1,0},{2,3},{3,2},{4,5},{5,4},{6,7},{7,6},{8,9},{9,8},{10,11... | collective-permute-start | bytes 786440 | tf_op jit(solution)/shard_map/ppermute | solution.py:38
  175.4 1.7 collective-permute-start.20
  175.5 9.2 %collective-permute-start.23 = (bf16[16,8192]{1,0:T(8,128)(2,1)S(1)}, bf16[16,8192]{1,0:T(8,128)(2,1)S(1)}, u32[]{:S(2)}, u32[]{:S(2)}) collective-permute-start(bf16[16,8192]{1,0:T(8,128)(2,1)S(1)} %add_convert_fusion.3.mine_ref), channel_id=1, source_target_pairs={{0,2},{1,3},{2,0},{3,1},{4,6},{5,7},{6,4},{7,5},{8,10},{9,11},{10,... | collective-permute-start | bytes 786440 | tf_op jit(solution)/shard_map/ppermute | solution.py:38
  177.2 12.8 %collective-permute-start.22 = (bf16[16,8192]{1,0:T(8,128)(2,1)S(1)}, bf16[16,8192]{1,0:T(8,128)(2,1)S(1)}, u32[]{:S(2)}, u32[]{:S(2)}) collective-permute-start(bf16[16,8192]{1,0:T(8,128)(2,1)S(1)} %add_convert_fusion.2.mine_ref), channel_id=1, source_target_pairs={{0,2},{1,3},{2,0},{3,1},{4,6},{5,7},{6,4},{7,5},{8,10},{9,11},{10,... | collective-permute-start | bytes 786440 | tf_op jit(solution)/shard_map/ppermute | solution.py:38
  (5 other events, 44.0 us)

commit v6 on v4

--- a/solution.py
+++ b/solution.py
@@ -15,15 +15,15 @@
 
 ORDER = (
     "As Al Af1 Af2",
-    "Ao1 Bs Ao2 Az1",
-    "Aw Bg1 Ae Bo1",
-    "Bg2 Ac Bo2 Bw",
-    "Bz1 As Be Ag1",
-    "Ag2 Bc Ao1 Bs",
-    "Ao2 Az1 Bf1 Aw",
-    "Ae Bo1 Bg2 Ac",
-    "Ap Bo2 Bp Bw",
-    "Bz1 Ar Be Bc",
+    "Bs Ao1 Ao2 Aw",
+    "Ae1 Bf1 Bg2 Ae2",
+    "Bo1 Ac As Bo2",
+    "Bw Be1 Ag1 Be2",
+    "Ag2 Ao1 Bc Bs",
+    "Ao2 Aw Ae1 Ap",
+    "Bg1 Ae2 Bg2 Bo1",
+    "Bo2 Bp Ac Bw",
+    "Be1 Ar Be2 Bc",
     "Br",
 )
 
@@ -162,23 +162,25 @@
     lookup(ids_ref, refs[:count], refs[count:], ids_ref.shape[0] // refs[count].shape[0])
 
 
-def expand_kernel(count, *refs):
+def expand_kernel(part, own_ref, *refs):
     *refs, emb_ref, out_ref = refs
-    blocks = refs[0].shape[0]
+    blocks, _, width = own_ref.shape
     block_len = emb_ref.shape[0] // blocks
+    held = refs.pop() if part else None
+    features = pl.ds(part * width, width)
 
     def step(b, carry):
         docs = pl.ds(pl.multiple_of(b * block_len, block_len), block_len)
-        parts = []
-        for at in range(0, len(refs), count):
-            total = refs[at][b]
-            for ref in refs[at + 1:at + count]:
-                total = total + ref[b].astype(jnp.float32)
-            parts.append(total.astype(jnp.bfloat16))
-        out_ref[:, docs] = lax.dot_general(
-            jnp.concatenate(parts, axis=1), emb_ref[docs], (((1,), (1,)), ((), ())),
+        total = own_ref[b]
+        for ref in refs:
+            total = total + ref[b].astype(jnp.float32)
+        products = lax.dot_general(
+            total.astype(jnp.bfloat16), emb_ref[docs, features], (((1,), (1,)), ((), ())),
             preferred_element_type=jnp.float32,
-        ).astype(jnp.bfloat16)
+        )
+        if part:
+            products = products + held[:, docs]
+        out_ref[:, docs] = products.astype(out_ref.dtype)
         return carry
 
     lax.fori_loop(0, blocks, step, 0, unroll=TILE_BLOCKS)
@@ -278,13 +280,13 @@
             compiler_params=params(),
         )(ids, *tables)
 
-    def expand(parts):
-        values = [v for values in parts for v in values]
-        return pl.pallas_call(
-            functools.partial(expand_kernel, len(parts[0])),
+    def expand(p, own, arrived, held):
+        values = [own, *arrived] + ([held] if p else [])
+        return pl.pallas_call(
+            functools.partial(expand_kernel, p),
             in_specs=[VMEM] * (len(values) + 1),
             out_specs=VMEM,
-            out_shape=jax.ShapeDtypeStruct((group, docs), jnp.bfloat16),
+            out_shape=jax.ShapeDtypeStruct((group, docs), jnp.bfloat16 if p + 1 == PARTS else jnp.float32),
             compiler_params=params(),
         )(*values, embeddings)
 
@@ -323,6 +325,9 @@
         elif step == "s":
             if products[c] is None:
                 sums = first_sums(c, *take(qrow))
+                if c == 0:
+                    *sums, tied = lax.optimization_barrier((*sums, tuple(lists.values())))
+                    lists = dict(zip(lists, tied))
             else:
                 sums = next_sums(c, take(*products[c]))
                 halves[c] = products[c]
@@ -357,11 +362,12 @@
             arrived[c][p] = take(*arrived[c][p])
             token.append(arrived[c][p][-1])
         elif step == "e":
-            flat = take(*own[c], *(v for values in arrived[c] for v in values))
-            later = [flat[PARTS + i * len(reduce_bits):PARTS + (i + 1) * len(reduce_bits)] for i in range(PARTS)]
-            value = expand([(flat[i], *later[i]) for i in range(PARTS)])
-            products[c] = [value, swap(value, "col", ncol, 1)]
+            here, *later = take(own[c][p], *arrived[c][p])
+            value = expand(p, here, later, products[c])
+            products[c] = value
             token.append(value)
+            if p + 1 == PARTS:
+                products[c] = [value, swap(value, "col", ncol, 1)]
         elif step == "c":
             pair = take(*products[c])
             for i in range(1, ncol.bit_length() - 1):

time: 167 us -> 163 us (0.976)
  starting transfers between devices: 55.6 us -> 41.4 us
  Pallas kernels: 35.5 us -> 43.6 us
  waiting for transfers between devices: 71.6 us -> 74.5 us
    ppermute x41, starting transfers between devices: 55.6 us -> 41.4 us  [swap(): return lax.ppermute(value, axis, [(i, i ^ mask) for i in range(size)])]
    pallas_call x4 -> x8, Pallas kernels: 8.16 us -> 16.2 us  [expand(): pl.pallas_call(functools.partial(expand_kernel, p), in_specs=[VMEM] * (le...]
    ppermute x41, waiting for transfers between devices: 71.6 us -> 74.5 us  [swap(): return lax.ppermute(value, axis, [(i, i ^ mask) for i in range(size)])]
  transfers between devices with their start and end apart: 41 -> 41, of which waited for: 21 -> 22; matrix products, arithmetic and copies ran while one was open for 0% -> 0% of each run, Pallas kernels for 18% -> 25%
where the time goes in v6:
time: 163 us
  waiting for transfers between devices  74.5 us (46%)
  Pallas kernels  43.6 us (27%)
  starting transfers between devices  41.4 us (25%)
  local copies, waits for them, and re-layouts  2.56 us (2%)
    ppermute x41, waiting for transfers between devices, swap(): return lax.ppermute(value, axis, [(i, i ^ mask) for i in range(size)])  74.5 us
    ppermute x41, starting transfers between devices, swap(): return lax.ppermute(value, axis, [(i, i ^ mask) for i in range(size)])  41.4 us
    pallas_call x8, Pallas kernels, expand(): pl.pallas_call(functools.partial(expand_kernel, p), in_specs=[VMEM] * (le...  16.2 us
    pallas_call x8, Pallas kernels, combine_far(): pl.pallas_call(table_kernel, in_specs=[SMEM] + [VMEM] * len(shards), out_...  10.6 us
    pallas_call x4, Pallas kernels, combine(): pl.pallas_call(lookup_kernel, in_specs=[SMEM] + [VMEM] * len(tables), out...  5.8 us
    pallas_call x4, Pallas kernels, fill(): pl.pallas_call(functools.partial(fill_kernel, rows(c), bool(others)), in_...  3.53 us
  transfers between devices with their start and end apart: 41, of which 22 were waited for; matrix products, arithmetic and copies ran while one was open for 0% of the time, Pallas kernels for 25%

profile of v6, /device:TPU:0, one launch (start us, length us, event | category | flops | bytes accessed | tf_op | source)
XLA Modules:
  0.0 163.3 jit_solution(17871854983287830830)
XLA Ops:
  0.6 4.1 %collective-permute-start = (s32[64,8]{0,1:T(8,128)}, s32[64,8]{0,1:T(8,128)S(1)}, u32[]{:S(2)}, u32[]{:S(2)}) collective-permute-start(s32[64,8]{0,1:T(8,128)} %param.7), channel_id=1, source_target_pairs={{0,16},{4,20},{8,24},{12,28},{16,0},{20,4},{24,8},{28,12},{1,17},{... | collective-permute-start | bytes 6152 | tf_op jit(solution)/shard_map/ppermute | solution.py:41
  4.7 2.9 %shard_map.59 = (bf16[64,16,128]{2,1,0:T(8,128)(2,1)S(1)}, bf16[64,16,128]{2,1,0:T(8,128)(2,1)S(1)}) custom-call(f32[32,8192]{1,0:T(8,128)} %vec_ref.11, f32[1,8192]{1,0:T(1,128)} %bitcast.1, bf16[8192,256]{1,0:T(8,128)(2,1)} %refs_2_.11), custom_call_target="tpu_custom_call" | custom-call | tf_op jit(solution)/shard_map/pallas_call | solution.py:228
  11.7 5.3 %collective-permute-done.2.refs_1_ = bf16[64,16,128]{2,1,0:T(8,128)(2,1)S(1)} collective-permute-done((bf16[64,16,128]{2,1,0:T(8,128)(2,1)S(1)}, bf16[64,16,128]{2,1,0:T(8,128)(2,1)S(1)}, u32[]{:S(2)}, u32[]{:S(2)}) %collective-permute-start.2) | collective-permute-done | bytes 262176 | tf_op jit(solution)/shard_map/ppermute | solution.py:41
  19.0 2.1 %collective-permute-done.1.refs_1_ = bf16[64,16,128]{2,1,0:T(8,128)(2,1)S(1)} collective-permute-done((bf16[64,16,128]{2,1,0:T(8,128)(2,1)S(1)}, bf16[64,16,128]{2,1,0:T(8,128)(2,1)S(1)}, u32[]{:S(2)}, u32[]{:S(2)}) %collective-permute-start.1) | collective-permute-done | bytes 262176 | tf_op jit(solution)/shard_map/ppermute | solution.py:41
  22.6 2.2 %copy-done = bf16[8192,256]{1,0:T(8,128)(2,1)S(1)} copy-done((bf16[8192,256]{1,0:T(8,128)(2,1)S(1)}, bf16[8192,256]{1,0:T(8,128)(2,1)}, u32[]{:S(2)}) %copy-start) | copy-done | bytes 4194328
  33.3 3.3 %collective-permute-done.7.refs_3_ = bf16[64,16,128]{2,1,0:T(8,128)(2,1)S(1)} collective-permute-done((bf16[64,16,128]{2,1,0:T(8,128)(2,1)S(1)}, bf16[64,16,128]{2,1,0:T(8,128)(2,1)S(1)}, u32[]{:S(2)}, u32[]{:S(2)}) %collective-permute-start.7) | collective-permute-done | bytes 262176 | tf_op jit(solution)/shard_map/ppermute | solution.py:41
  39.5 2.6 %collective-permute-done.8.refs_0_ = bf16[64,16,128]{2,1,0:T(8,128)(2,1)S(1)} collective-permute-done((bf16[64,16,128]{2,1,0:T(8,128)(2,1)S(1)}, bf16[64,16,128]{2,1,0:T(8,128)(2,1)S(1)}, u32[]{:S(2)}, u32[]{:S(2)}) %collective-permute-start.8) | collective-permute-done | bytes 262176 | tf_op jit(solution)/shard_map/ppermute | solution.py:41
  44.6 3.9 %collective-permute-done.3.refs_1_ = bf16[64,16,128]{2,1,0:T(8,128)(2,1)S(1)} collective-permute-done((bf16[64,16,128]{2,1,0:T(8,128)(2,1)S(1)}, bf16[64,16,128]{2,1,0:T(8,128)(2,1)S(1)}, u32[]{:S(2)}, u32[]{:S(2)}) %collective-permute-start.3) | collective-permute-done | bytes 262176 | tf_op jit(solution)/shard_map/ppermute | solution.py:41
  48.5 2.8 %collective-permute-done.12.refs_1_ = bf16[64,16,128]{2,1,0:T(8,128)(2,1)S(1)} collective-permute-done((bf16[64,16,128]{2,1,0:T(8,128)(2,1)S(1)}, bf16[64,16,128]{2,1,0:T(8,128)(2,1)S(1)}, u32[]{:S(2)}, u32[]{:S(2)}) %collective-permute-start.12) | collective-permute-done | bytes 262176 | tf_op jit(solution)/shard_map/ppermute | solution.py:41
  51.3 2.0 %shard_map.65 = bf16[16,8192]{1,0:T(8,128)(2,1)S(1)} custom-call(f32[64,16,128]{2,1,0:T(8,128)S(1)} %get-tuple-element.167.own_ref, bf16[64,16,128]{2,1,0:T(8,128)(2,1)S(1)} %collective-permute-done.11.refs_0_, f32[16,8192]{1,0:T(8,128)S(1)} %shard_map.64.refs_1_, bf16[8192,256]{1,0:T(8,128)(2,1)S(1)} %copy-done.1), custom_call_target="tpu_custom_call" | custom-call | tf_op jit(solution)/shard_map/pallas_call | solution.py:285
  58.6 5.0 %collective-permute-done.16.other_ref.refs_1_ = bf16[16,8192]{1,0:T(8,128)(2,1)S(1)} collective-permute-done((bf16[16,8192]{1,0:T(8,128)(2,1)S(1)}, bf16[16,8192]{1,0:T(8,128)(2,1)S(1)}, u32[]{:S(2)}, u32[]{:S(2)}) %collective-permute-start.16) | collective-permute-done | bytes 262176 | tf_op jit(solution)/shard_map/ppermute | solution.py:41
  65.1 2.5 %collective-permute-start.18 = (bf16[64,16,128]{2,1,0:T(8,128)(2,1)S(1)}, bf16[64,16,128]{2,1,0:T(8,128)(2,1)S(1)}, u32[]{:S(2)}, u32[]{:S(2)}) collective-permute-start(bf16[64,16,128]{2,1,0:T(8,128)(2,1)S(1)} %get-tuple-element.199.refs_0_), channel_id=1, source_target_pairs={{0,8},{4,12},{8,0},{12,4},{16,24},{20,28},{24,16},{28,20},{1,9},{5... | collective-permute-start | bytes 786440 | tf_op jit(solution)/shard_map/ppermute | solution.py:41
  76.3 4.5 %collective-permute-done.18.refs_1_ = bf16[64,16,128]{2,1,0:T(8,128)(2,1)S(1)} collective-permute-done((bf16[64,16,128]{2,1,0:T(8,128)(2,1)S(1)}, bf16[64,16,128]{2,1,0:T(8,128)(2,1)S(1)}, u32[]{:S(2)}, u32[]{:S(2)}) %collective-permute-start.18) | collective-permute-done | bytes 262176 | tf_op jit(solution)/shard_map/ppermute | solution.py:41
  85.5 2.9 %collective-permute-done.23.refs_1_ = bf16[64,16,128]{2,1,0:T(8,128)(2,1)S(1)} collective-permute-done((bf16[64,16,128]{2,1,0:T(8,128)(2,1)S(1)}, bf16[64,16,128]{2,1,0:T(8,128)(2,1)S(1)}, u32[]{:S(2)}, u32[]{:S(2)}) %collective-permute-start.23) | collective-permute-done | bytes 262176 | tf_op jit(solution)/shard_map/ppermute | solution.py:41
  93.2 5.0 %collective-permute-done.25.other_ref.refs_1_ = bf16[16,8192]{1,0:T(8,128)(2,1)S(1)} collective-permute-done((bf16[16,8192]{1,0:T(8,128)(2,1)S(1)}, bf16[16,8192]{1,0:T(8,128)(2,1)S(1)}, u32[]{:S(2)}, u32[]{:S(2)}) %collective-permute-start.25) | collective-permute-done | bytes 262176 | tf_op jit(solution)/shard_map/ppermute | solution.py:41
  101.5 4.2 %collective-permute-start.29 = (bf16[64,16,128]{2,1,0:T(8,128)(2,1)S(1)}, bf16[64,16,128]{2,1,0:T(8,128)(2,1)S(1)}, u32[]{:S(2)}, u32[]{:S(2)}) collective-permute-start(bf16[64,16,128]{2,1,0:T(8,128)(2,1)S(1)} %get-tuple-element.217), channel_id=1, source_target_pairs={{0,16},{4,20},{8,24},{12,28},{16,0},{20,4},{24,8},{28,12},{1,17},{... | collective-permute-start | bytes 786440 | tf_op jit(solution)/shard_map/ppermute | solution.py:41
  112.7 2.4 %collective-permute-done.30.refs_1_ = bf16[64,16,128]{2,1,0:T(8,128)(2,1)S(1)} collective-permute-done((bf16[64,16,128]{2,1,0:T(8,128)(2,1)S(1)}, bf16[64,16,128]{2,1,0:T(8,128)(2,1)S(1)}, u32[]{:S(2)}, u32[]{:S(2)}) %collective-permute-start.30) | collective-permute-done | bytes 262176 | tf_op jit(solution)/shard_map/ppermute | solution.py:41
  115.1 3.0 %collective-permute-start.34 = (bf16[64,16,128]{2,1,0:T(8,128)(2,1)S(1)}, bf16[64,16,128]{2,1,0:T(8,128)(2,1)S(1)}, u32[]{:S(2)}, u32[]{:S(2)}) collective-permute-start(bf16[64,16,128]{2,1,0:T(8,128)(2,1)S(1)} %collective-permute-done.30.refs_1_), channel_id=1, source_target_pairs={{0,4},{4,0},{8,12},{12,8},{16,20},{20,16},{24,28},{28,24},{1,5},{5... | collective-permute-start | bytes 786440 | tf_op jit(solution)/shard_map/ppermute | solution.py:41
  118.1 2.0 %shard_map.78 = bf16[16,8192]{1,0:T(8,128)(2,1)S(1)} custom-call(f32[64,16,128]{2,1,0:T(8,128)S(1)} %get-tuple-element.227.own_ref, bf16[64,16,128]{2,1,0:T(8,128)(2,1)S(1)} %collective-permute-done.29.refs_0_, f32[16,8192]{1,0:T(8,128)S(1)} %shard_map.76.refs_1_, bf16[8192,256]{1,0:T(8,128)(2,1)S(1)} %copy-done.1), custom_call_target="tpu_custom_call" | custom-call | tf_op jit(solution)/shard_map/pallas_call | solution.py:285
  120.1 2.7 %collective-permute-done.26.refs_1_ = bf16[64,16,128]{2,1,0:T(8,128)(2,1)S(1)} collective-permute-done((bf16[64,16,128]{2,1,0:T(8,128)(2,1)S(1)}, bf16[64,16,128]{2,1,0:T(8,128)(2,1)S(1)}, u32[]{:S(2)}, u32[]{:S(2)}) %collective-permute-start.26) | collective-permute-done | bytes 262176 | tf_op jit(solution)/shard_map/ppermute | solution.py:41
  124.6 6.4 %collective-permute-done.33.refs_3_ = bf16[64,16,128]{2,1,0:T(8,128)(2,1)S(1)} collective-permute-done((bf16[64,16,128]{2,1,0:T(8,128)(2,1)S(1)}, bf16[64,16,128]{2,1,0:T(8,128)(2,1)S(1)}, u32[]{:S(2)}, u32[]{:S(2)}) %collective-permute-start.33) | collective-permute-done | bytes 262176 | tf_op jit(solution)/shard_map/ppermute | solution.py:41
  136.0 8.7 %collective-permute-done.38.refs_0_ = bf16[64,16,128]{2,1,0:T(8,128)(2,1)S(1)} collective-permute-done((bf16[64,16,128]{2,1,0:T(8,128)(2,1)S(1)}, bf16[64,16,128]{2,1,0:T(8,128)(2,1)S(1)}, u32[]{:S(2)}, u32[]{:S(2)}) %collective-permute-start.38) | collective-permute-done | bytes 262176 | tf_op jit(solution)/shard_map/ppermute | solution.py:41
  147.7 2.6 %collective-permute-done.36.refs_0_ = bf16[64,16,128]{2,1,0:T(8,128)(2,1)S(1)} collective-permute-done((bf16[64,16,128]{2,1,0:T(8,128)(2,1)S(1)}, bf16[64,16,128]{2,1,0:T(8,128)(2,1)S(1)}, u32[]{:S(2)}, u32[]{:S(2)}) %collective-permute-start.36) | collective-permute-done | bytes 262176 | tf_op jit(solution)/shard_map/ppermute | solution.py:41
  155.6 6.8 %collective-permute-done.40.other_ref = bf16[16,8192]{1,0:T(8,128)(2,1)S(1)} collective-permute-done((bf16[16,8192]{1,0:T(8,128)(2,1)S(1)}, bf16[16,8192]{1,0:T(8,128)(2,1)S(1)}, u32[]{:S(2)}, u32[]{:S(2)}) %collective-permute-start.40) | collective-permute-done | bytes 262176 | tf_op jit(solution)/shard_map/ppermute | solution.py:41
  (105 shorter events, 72.3 us)
Async XLA Ops:
  9.3 11.8 %collective-permute-start.1 = (bf16[64,16,128]{2,1,0:T(8,128)(2,1)S(1)}, bf16[64,16,128]{2,1,0:T(8,128)(2,1)S(1)}, u32[]{:S(2)}, u32[]{:S(2)}) collective-permute-start(bf16[64,16,128]{2,1,0:T(8,128)(2,1)S(1)} %get-tuple-element.152.refs_0_), channel_id=1, source_target_pairs={{0,8},{4,12},{8,0},{12,4},{16,24},{20,28},{24,16},{28,20},{1,9},{5... | collective-permute-start | bytes 786440 | tf_op jit(solution)/shard_map/ppermute | solution.py:41
  9.7 16.6 %collective-permute-start.4 = (bf16[64,16,128]{2,1,0:T(8,128)(2,1)S(1)}, bf16[64,16,128]{2,1,0:T(8,128)(2,1)S(1)}, u32[]{:S(2)}, u32[]{:S(2)}) collective-permute-start(bf16[64,16,128]{2,1,0:T(8,128)(2,1)S(1)} %get-tuple-element.146.refs_0_), channel_id=1, source_target_pairs={{0,4},{4,0},{8,12},{12,8},{16,20},{20,16},{24,28},{28,24},{1,5},{5... | collective-permute-start | bytes 786440 | tf_op jit(solution)/shard_map/ppermute | solution.py:41
  18.5 13.2 %collective-permute-start.6 = (bf16[64,16,128]{2,1,0:T(8,128)(2,1)S(1)}, bf16[64,16,128]{2,1,0:T(8,128)(2,1)S(1)}, u32[]{:S(2)}, u32[]{:S(2)}) collective-permute-start(bf16[64,16,128]{2,1,0:T(8,128)(2,1)S(1)} %get-tuple-element.152.refs_0_), channel_id=1, source_target_pairs={{0,4},{4,0},{8,12},{12,8},{16,20},{20,16},{24,28},{28,24},{1,5},{5... | collective-permute-start | bytes 786440 | tf_op jit(solution)/shard_map/ppermute | solution.py:41
  21.1 15.5 %collective-permute-start.7 = (bf16[64,16,128]{2,1,0:T(8,128)(2,1)S(1)}, bf16[64,16,128]{2,1,0:T(8,128)(2,1)S(1)}, u32[]{:S(2)}, u32[]{:S(2)}) collective-permute-start(bf16[64,16,128]{2,1,0:T(8,128)(2,1)S(1)} %collective-permute-done.1.refs_1_), channel_id=1, source_target_pairs={{0,4},{4,0},{8,12},{12,8},{16,20},{20,16},{24,28},{28,24},{1,5},{5... | collective-permute-start | bytes 786440 | tf_op jit(solution)/shard_map/ppermute | solution.py:41
  27.7 14.4 %collective-permute-start.8 = (bf16[64,16,128]{2,1,0:T(8,128)(2,1)S(1)}, bf16[64,16,128]{2,1,0:T(8,128)(2,1)S(1)}, u32[]{:S(2)}, u32[]{:S(2)}) collective-permute-start(bf16[64,16,128]{2,1,0:T(8,128)(2,1)S(1)} %get-tuple-element.151), channel_id=1, source_target_pairs={{0,16},{4,20},{8,24},{12,28},{16,0},{20,4},{24,8},{28,12},{1,17},{... | collective-permute-start | bytes 786440 | tf_op jit(solution)/shard_map/ppermute | solution.py:41
  29.3 19.1 %collective-permute-start.3 = (bf16[64,16,128]{2,1,0:T(8,128)(2,1)S(1)}, bf16[64,16,128]{2,1,0:T(8,128)(2,1)S(1)}, u32[]{:S(2)}, u32[]{:S(2)}) collective-permute-start(bf16[64,16,128]{2,1,0:T(8,128)(2,1)S(1)} %get-tuple-element.169.refs_0_), channel_id=1, source_target_pairs={{0,8},{4,12},{8,0},{12,4},{16,24},{20,28},{24,16},{28,20},{1,9},{5... | collective-permute-start | bytes 786440 | tf_op jit(solution)/shard_map/ppermute | solution.py:41
  30.9 20.4 %collective-permute-start.12 = (bf16[64,16,128]{2,1,0:T(8,128)(2,1)S(1)}, bf16[64,16,128]{2,1,0:T(8,128)(2,1)S(1)}, u32[]{:S(2)}, u32[]{:S(2)}) collective-permute-start(bf16[64,16,128]{2,1,0:T(8,128)(2,1)S(1)} %get-tuple-element.181.refs_0_), channel_id=1, source_target_pairs={{0,8},{4,12},{8,0},{12,4},{16,24},{20,28},{24,16},{28,20},{1,9},{5... | collective-permute-start | bytes 786440 | tf_op jit(solution)/shard_map/ppermute | solution.py:41
  31.6 19.6 %collective-permute-start.13 = (bf16[64,16,128]{2,1,0:T(8,128)(2,1)S(1)}, bf16[64,16,128]{2,1,0:T(8,128)(2,1)S(1)}, u32[]{:S(2)}, u32[]{:S(2)}) collective-permute-start(bf16[64,16,128]{2,1,0:T(8,128)(2,1)S(1)} %get-tuple-element.181.refs_0_), channel_id=1, source_target_pairs={{0,4},{4,0},{8,12},{12,8},{16,20},{20,16},{24,28},{28,24},{1,5},{5... | collective-permute-start | bytes 786440 | tf_op jit(solution)/shard_map/ppermute | solution.py:41
  38.0 13.3 %collective-permute-start.11 = (bf16[64,16,128]{2,1,0:T(8,128)(2,1)S(1)}, bf16[64,16,128]{2,1,0:T(8,128)(2,1)S(1)}, u32[]{:S(2)}, u32[]{:S(2)}) collective-permute-start(bf16[64,16,128]{2,1,0:T(8,128)(2,1)S(1)} %get-tuple-element.157), channel_id=1, source_target_pairs={{0,16},{4,20},{8,24},{12,28},{16,0},{20,4},{24,8},{28,12},{1,17},{... | collective-permute-start | bytes 786440 | tf_op jit(solution)/shard_map/ppermute | solution.py:41
  57.8 14.9 %collective-permute-start.20 = (bf16[64,16,128]{2,1,0:T(8,128)(2,1)S(1)}, bf16[64,16,128]{2,1,0:T(8,128)(2,1)S(1)}, u32[]{:S(2)}, u32[]{:S(2)}) collective-permute-start(bf16[64,16,128]{2,1,0:T(8,128)(2,1)S(1)} %get-tuple-element.175), channel_id=1, source_target_pairs={{0,16},{4,20},{8,24},{12,28},{16,0},{20,4},{24,8},{28,12},{1,17},{... | collective-permute-start | bytes 786440 | tf_op jit(solution)/shard_map/ppermute | solution.py:41
  65.1 15.7 %collective-permute-start.18 = (bf16[64,16,128]{2,1,0:T(8,128)(2,1)S(1)}, bf16[64,16,128]{2,1,0:T(8,128)(2,1)S(1)}, u32[]{:S(2)}, u32[]{:S(2)}) collective-permute-start(bf16[64,16,128]{2,1,0:T(8,128)(2,1)S(1)} %get-tuple-element.199.refs_0_), channel_id=1, source_target_pairs={{0,8},{4,12},{8,0},{12,4},{16,24},{20,28},{24,16},{28,20},{1,9},{5... | collective-permute-start | bytes 786440 | tf_op jit(solution)/shard_map/ppermute | solution.py:41
  67.6 13.2 %collective-permute-start.19 = (bf16[64,16,128]{2,1,0:T(8,128)(2,1)S(1)}, bf16[64,16,128]{2,1,0:T(8,128)(2,1)S(1)}, u32[]{:S(2)}, u32[]{:S(2)}) collective-permute-start(bf16[64,16,128]{2,1,0:T(8,128)(2,1)S(1)} %get-tuple-element.199.refs_0_), channel_id=1, source_target_pairs={{0,4},{4,0},{8,12},{12,8},{16,20},{20,16},{24,28},{28,24},{1,5},{5... | collective-permute-start | bytes 786440 | tf_op jit(solution)/shard_map/ppermute | solution.py:41
  69.5 13.9 %collective-permute-start.17 = (bf16[64,16,128]{2,1,0:T(8,128)(2,1)S(1)}, bf16[64,16,128]{2,1,0:T(8,128)(2,1)S(1)}, u32[]{:S(2)}, u32[]{:S(2)}) collective-permute-start(bf16[64,16,128]{2,1,0:T(8,128)(2,1)S(1)} %get-tuple-element.186), channel_id=1, source_target_pairs={{0,16},{4,20},{8,24},{12,28},{16,0},{20,4},{24,8},{28,12},{1,17},{... | collective-permute-start | bytes 786440 | tf_op jit(solution)/shard_map/ppermute | solution.py:41
  71.2 17.3 %collective-permute-start.23 = (bf16[64,16,128]{2,1,0:T(8,128)(2,1)S(1)}, bf16[64,16,128]{2,1,0:T(8,128)(2,1)S(1)}, u32[]{:S(2)}, u32[]{:S(2)}) collective-permute-start(bf16[64,16,128]{2,1,0:T(8,128)(2,1)S(1)} %get-tuple-element.212.refs_0_), channel_id=1, source_target_pairs={{0,8},{4,12},{8,0},{12,4},{16,24},{20,28},{24,16},{28,20},{1,9},{5... | collective-permute-start | bytes 786440 | tf_op jit(solution)/shard_map/ppermute | solution.py:41
  72.7 15.7 %collective-permute-start.24 = (bf16[64,16,128]{2,1,0:T(8,128)(2,1)S(1)}, bf16[64,16,128]{2,1,0:T(8,128)(2,1)S(1)}, u32[]{:S(2)}, u32[]{:S(2)}) collective-permute-start(bf16[64,16,128]{2,1,0:T(8,128)(2,1)S(1)} %get-tuple-element.212.refs_0_), channel_id=1, source_target_pairs={{0,4},{4,0},{8,12},{12,8},{16,20},{20,16},{24,28},{28,24},{1,5},{5... | collective-permute-start | bytes 786440 | tf_op jit(solution)/shard_map/ppermute | solution.py:41
  92.0 15.6 %collective-permute-start.32 = (bf16[64,16,128]{2,1,0:T(8,128)(2,1)S(1)}, bf16[64,16,128]{2,1,0:T(8,128)(2,1)S(1)}, u32[]{:S(2)}, u32[]{:S(2)}) collective-permute-start(bf16[64,16,128]{2,1,0:T(8,128)(2,1)S(1)} %get-tuple-element.203), channel_id=1, source_target_pairs={{0,16},{4,20},{8,24},{12,28},{16,0},{20,4},{24,8},{28,12},{1,17},{... | collective-permute-start | bytes 786440 | tf_op jit(solution)/shard_map/ppermute | solution.py:41
  99.7 15.4 %collective-permute-start.30 = (bf16[64,16,128]{2,1,0:T(8,128)(2,1)S(1)}, bf16[64,16,128]{2,1,0:T(8,128)(2,1)S(1)}, u32[]{:S(2)}, u32[]{:S(2)}) collective-permute-start(bf16[64,16,128]{2,1,0:T(8,128)(2,1)S(1)} %get-tuple-element.232.refs_0_), channel_id=1, source_target_pairs={{0,8},{4,12},{8,0},{12,4},{16,24},{20,28},{24,16},{28,20},{1,9},{5... | collective-permute-start | bytes 786440 | tf_op jit(solution)/shard_map/ppermute | solution.py:41
  99.7 15.3 %collective-permute-start.31 = (bf16[64,16,128]{2,1,0:T(8,128)(2,1)S(1)}, bf16[64,16,128]{2,1,0:T(8,128)(2,1)S(1)}, u32[]{:S(2)}, u32[]{:S(2)}) collective-permute-start(bf16[64,16,128]{2,1,0:T(8,128)(2,1)S(1)} %get-tuple-element.232.refs_0_), channel_id=1, source_target_pairs={{0,4},{4,0},{8,12},{12,8},{16,20},{20,16},{24,28},{28,24},{1,5},{5... | collective-permute-start | bytes 786440 | tf_op jit(solution)/shard_map/ppermute | solution.py:41
  101.5 16.6 %collective-permute-start.29 = (bf16[64,16,128]{2,1,0:T(8,128)(2,1)S(1)}, bf16[64,16,128]{2,1,0:T(8,128)(2,1)S(1)}, u32[]{:S(2)}, u32[]{:S(2)}) collective-permute-start(bf16[64,16,128]{2,1,0:T(8,128)(2,1)S(1)} %get-tuple-element.217), channel_id=1, source_target_pairs={{0,16},{4,20},{8,24},{12,28},{16,0},{20,4},{24,8},{28,12},{1,17},{... | collective-permute-start | bytes 786440 | tf_op jit(solution)/shard_map/ppermute | solution.py:41
  105.7 17.1 %collective-permute-start.26 = (bf16[64,16,128]{2,1,0:T(8,128)(2,1)S(1)}, bf16[64,16,128]{2,1,0:T(8,128)(2,1)S(1)}, u32[]{:S(2)}, u32[]{:S(2)}) collective-permute-start(bf16[64,16,128]{2,1,0:T(8,128)(2,1)S(1)} %get-tuple-element.237.refs_0_), channel_id=1, source_target_pairs={{0,8},{4,12},{8,0},{12,4},{16,24},{20,28},{24,16},{28,20},{1,9},{5... | collective-permute-start | bytes 786440 | tf_op jit(solution)/shard_map/ppermute | solution.py:41
  107.6 15.2 %collective-permute-start.27 = (bf16[64,16,128]{2,1,0:T(8,128)(2,1)S(1)}, bf16[64,16,128]{2,1,0:T(8,128)(2,1)S(1)}, u32[]{:S(2)}, u32[]{:S(2)}) collective-permute-start(bf16[64,16,128]{2,1,0:T(8,128)(2,1)S(1)} %get-tuple-element.237.refs_0_), channel_id=1, source_target_pairs={{0,4},{4,0},{8,12},{12,8},{16,20},{20,16},{24,28},{28,24},{1,5},{5... | collective-permute-start | bytes 786440 | tf_op jit(solution)/shard_map/ppermute | solution.py:41
  124.5 20.2 %collective-permute-start.38 = (bf16[64,16,128]{2,1,0:T(8,128)(2,1)S(1)}, bf16[64,16,128]{2,1,0:T(8,128)(2,1)S(1)}, u32[]{:S(2)}, u32[]{:S(2)}) collective-permute-start(bf16[64,16,128]{2,1,0:T(8,128)(2,1)S(1)} %get-tuple-element.236), channel_id=1, source_target_pairs={{0,16},{4,20},{8,24},{12,28},{16,0},{20,4},{24,8},{28,12},{1,17},{... | collective-permute-start | bytes 786440 | tf_op jit(solution)/shard_map/ppermute | solution.py:41
  133.3 13.5 %collective-permute-start.37 = (bf16[16,8192]{1,0:T(8,128)(2,1)S(1)}, bf16[16,8192]{1,0:T(8,128)(2,1)S(1)}, u32[]{:S(2)}, u32[]{:S(2)}) collective-permute-start(bf16[16,8192]{1,0:T(8,128)(2,1)S(1)} %add_convert_fusion.1.mine_ref), channel_id=1, source_target_pairs={{0,2},{1,3},{2,0},{3,1},{4,6},{5,7},{6,4},{7,5},{8,10},{9,11},{10,... | collective-permute-start | bytes 786440 | tf_op jit(solution)/shard_map/ppermute | solution.py:41
  133.9 16.4 %collective-permute-start.36 = (bf16[64,16,128]{2,1,0:T(8,128)(2,1)S(1)}, bf16[64,16,128]{2,1,0:T(8,128)(2,1)S(1)}, u32[]{:S(2)}, u32[]{:S(2)}) collective-permute-start(bf16[64,16,128]{2,1,0:T(8,128)(2,1)S(1)} %get-tuple-element.241), channel_id=1, source_target_pairs={{0,16},{4,20},{8,24},{12,28},{16,0},{20,4},{24,8},{28,12},{1,17},{... | collective-permute-start | bytes 786440 | tf_op jit(solution)/shard_map/ppermute | solution.py:41
  (22 other events, 191.5 us)

commit v7 on v4

--- a/solution.py
+++ b/solution.py
@@ -10,19 +10,20 @@
 GROUPS = 2
 PARTS = 2
 TILE_BLOCKS = 8
+UNROLL = 16
 VMEM_LIMIT = 8 * 1024 * 1024
 SIDE, NEXT = 1, 2
 
 ORDER = (
     "As Al Af1 Af2",
-    "Ao1 Bs Ao2 Az1",
-    "Aw Bg1 Ae Bo1",
-    "Bg2 Ac Bo2 Bw",
-    "Bz1 As Be Ag1",
-    "Ag2 Bc Ao1 Bs",
-    "Ao2 Az1 Bf1 Aw",
-    "Ae Bo1 Bg2 Ac",
-    "Ap Bo2 Bp Bw",
+    "Ao1 Ao2 Aw Az1",
+    "Bg1 Az2 Bg2 Ae",
+    "Bo1 Ac As Bo2",
+    "Bw Bz1 Ag1 Be",
+    "Ag2 Ao1 Bc Ao2",
+    "Bs Aw Az1 Ap",
+    "Bg1 Ae Bf2 Bo1",
+    "Bo2 Bp Ac Bw",
     "Bz1 Ar Be Bc",
     "Br",
 )
@@ -51,19 +52,20 @@
 
 def store_sums(b, scaled, emb, sums_refs):
     sums = jnp.dot(scaled, emb, preferred_element_type=jnp.float32).astype(jnp.bfloat16)
-    part = sums.shape[1] // len(sums_refs)
+    _, group, part = sums_refs[0].shape
     for i, ref in enumerate(sums_refs):
-        ref[b] = sums[:, i * part:(i + 1) * part]
-
-
-def first_sums_kernel(rows, vec_ref, quality_ref, emb_ref, *refs):
+        c, p = divmod(i, sums.shape[1] // part)
+        ref[b] = sums[c * group:(c + 1) * group, p * part:(p + 1) * part]
+
+
+def first_sums_kernel(vec_ref, quality_ref, emb_ref, *refs):
     *sums_refs, vec, quality, emb, sems = refs
     tiles, tile_docs = emb.shape[:2]
     blocks = sums_refs[0].shape[0]
     block_len = tiles * tile_docs // blocks
     here = [
         pltpu.make_async_copy(quality_ref, quality, sems.at[tiles]),
-        pltpu.make_async_copy(vec_ref.at[rows], vec, sems.at[tiles + 1]),
+        pltpu.make_async_copy(vec_ref, vec, sems.at[tiles + 1]),
     ]
 
     def tile_copy(j):
@@ -88,24 +90,18 @@
     lax.fori_loop(0, tiles, step, 0)
 
 
-def next_sums_kernel(rows, pair, vec_ref, quality_ref, emb_ref, *sums_refs):
+def next_sums_kernel(rows, mine_ref, other_ref, vec_ref, quality_ref, emb_ref, *sums_refs):
     blocks = sums_refs[0].shape[0]
     block_len = emb_ref.shape[0] // blocks
 
     def step(b, carry):
         docs = pl.ds(pl.multiple_of(b * block_len, block_len), block_len)
         quality = quality_ref[:, docs]
-        value = vec_ref[rows, docs]
-        if pair:
-            value = add_f32(pair[0][:, docs], pair[1][:, docs]) * quality - value
+        value = add_f32(mine_ref[:, docs], other_ref[:, docs]) * quality - vec_ref[rows, docs]
         store_sums(b, (value * quality).astype(jnp.bfloat16), emb_ref[docs], sums_refs)
         return carry
 
-    lax.fori_loop(0, blocks, step, 0, unroll=TILE_BLOCKS)
-
-
-def later_sums_kernel(rows, mine_ref, other_ref, *refs):
-    next_sums_kernel(rows, (mine_ref, other_ref), *refs)
+    lax.fori_loop(0, blocks, step, 0, unroll=UNROLL)
 
 
 def fill_kernel(rows, second, mine_ref, other_ref, vec_ref, quality_ref, *refs):
@@ -139,7 +135,7 @@
             ref[b] = total.astype(ref.dtype)
         return carry
 
-    lax.fori_loop(0, outs[0].shape[0], step, 0, unroll=4)
+    lax.fori_loop(0, outs[0].shape[0], step, 0, unroll=UNROLL)
 
 
 def table_kernel(ids_ref, *refs):
@@ -181,7 +177,7 @@
         ).astype(jnp.bfloat16)
         return carry
 
-    lax.fori_loop(0, blocks, step, 0, unroll=TILE_BLOCKS)
+    lax.fori_loop(0, blocks, step, 0, unroll=UNROLL)
 
 
 def body(embeddings, quality, probes, neighbors):
@@ -214,22 +210,14 @@
     def rows(c):
         return pl.ds(c * group, group)
 
-    def first_sums(c, qrow):
-        if c:
-            return pl.pallas_call(
-                functools.partial(next_sums_kernel, rows(c), ()),
-                in_specs=[VMEM] * 3,
-                out_specs=[VMEM] * PARTS,
-                out_shape=[shard_out] * PARTS,
-                compiler_params=params(),
-            )(probes, qrow, embeddings)
-        return pl.pallas_call(
-            functools.partial(first_sums_kernel, rows(c)),
+    def first_sums():
+        return pl.pallas_call(
+            first_sums_kernel,
             in_specs=[HBM] * 3,
-            out_specs=[VMEM] * PARTS,
-            out_shape=[shard_out] * PARTS,
+            out_specs=[VMEM] * (GROUPS * PARTS),
+            out_shape=[shard_out] * (GROUPS * PARTS),
             scratch_shapes=[
-                pltpu.VMEM((group, docs), jnp.float32),
+                pltpu.VMEM((nprobe, docs), jnp.float32),
                 pltpu.VMEM((1, docs), jnp.float32),
                 pltpu.VMEM((tiles, docs // tiles, width), jnp.bfloat16),
                 pltpu.SemaphoreType.DMA((tiles + 2,)),
@@ -239,7 +227,7 @@
 
     def next_sums(c, pair):
         return pl.pallas_call(
-            functools.partial(later_sums_kernel, rows(c)),
+            functools.partial(next_sums_kernel, rows(c)),
             in_specs=[VMEM] * 5,
             out_specs=[VMEM] * PARTS,
             out_shape=[shard_out] * PARTS,
@@ -322,12 +310,15 @@
             token.append(ids[0])
         elif step == "s":
             if products[c] is None:
-                sums = first_sums(c, *take(qrow))
+                *sums, tied = lax.optimization_barrier((*first_sums(), tuple(lists.values())))
+                lists = dict(zip(lists, tied))
+                new = [(i // PARTS, i % PARTS, value) for i, value in enumerate(sums)]
             else:
                 sums = next_sums(c, take(*products[c]))
                 halves[c] = products[c]
+                new = [(c, i, value) for i, value in enumerate(sums)]
             token.append(sums[0])
-            for i, value in enumerate(sums):
+            for c, i, value in new:
                 gathered[c][i] = {0: value}
                 for m in (NEXT, SIDE):
                     gathered[c][i][m] = swap(value, "row", nrow, m)

time: 167 us -> 159 us (0.952)
  Pallas kernels: 35.5 us -> 30.3 us
  starting transfers between devices: 55.6 us -> 51.4 us
  waiting for transfers between devices: 71.6 us -> 75.7 us
  local copies, waits for them, and re-layouts: 2.56 us -> 0.37 us
    ppermute x41, starting transfers between devices: 55.6 us -> 51.4 us  [swap(): return lax.ppermute(value, axis, [(i, i ^ mask) for i in range(size)])]
    ppermute x41, waiting for transfers between devices: 71.6 us -> 75.7 us  [swap(): return lax.ppermute(value, axis, [(i, i ^ mask) for i in range(size)])]
    unnamed x10 -> x8, local copies, waits for them, and re-layouts: 2.21 us -> 0.01 us
    pallas_call x4 -> x3, Pallas kernels: 7.37 us -> 5.26 us  [the longest x1 3.16 us: first_sums(): pl.pallas_call(first_sums_kernel, in_specs=[HBM] * 3, out_specs=[VMEM] *...]
    pallas_call x4, Pallas kernels: 8.16 us -> 6.23 us  [expand(): pl.pallas_call(functools.partial(expand_kernel, len(parts[0])), in_specs=...]
  transfers between devices with their start and end apart: 41 -> 41, of which waited for: 21 -> 23; matrix products, arithmetic and copies ran while one was open for 0% -> 0% of each run, Pallas kernels for 18% -> 18%
where the time goes in v7:
time: 159 us
  waiting for transfers between devices  75.7 us (48%)
  starting transfers between devices  51.4 us (32%)
  Pallas kernels  30.3 us (19%)
    ppermute x41, waiting for transfers between devices, swap(): return lax.ppermute(value, axis, [(i, i ^ mask) for i in range(size)])  75.7 us
    ppermute x41, starting transfers between devices, swap(): return lax.ppermute(value, axis, [(i, i ^ mask) for i in range(size)])  51.4 us
    pallas_call x8, Pallas kernels, combine_far(): pl.pallas_call(table_kernel, in_specs=[SMEM] + [VMEM] * len(shards), out_...  9.98 us
    pallas_call x4, Pallas kernels, expand(): pl.pallas_call(functools.partial(expand_kernel, len(parts[0])), in_specs=...  6.23 us
    pallas_call x4, Pallas kernels, combine(): pl.pallas_call(lookup_kernel, in_specs=[SMEM] + [VMEM] * len(tables), out...  5.37 us
    pallas_call x4, Pallas kernels, fill(): pl.pallas_call(functools.partial(fill_kernel, rows(c), bool(others)), in_...  3.49 us
  transfers between devices with their start and end apart: 41, of which 23 were waited for; matrix products, arithmetic and copies ran while one was open for 0% of the time, Pallas kernels for 18%

profile of v7, /device:TPU:0, one launch (start us, length us, event | category | flops | bytes accessed | tf_op | source)
XLA Modules:
  0.0 159.0 jit_solution(3086583557937520262)
XLA Ops:
  0.6 4.1 %collective-permute-start = (s32[64,8]{0,1:T(8,128)}, s32[64,8]{0,1:T(8,128)S(1)}, u32[]{:S(2)}, u32[]{:S(2)}) collective-permute-start(s32[64,8]{0,1:T(8,128)} %param.7), channel_id=1, source_target_pairs={{0,16},{4,20},{8,24},{12,28},{16,0},{20,4},{24,8},{28,12},{1,17},{... | collective-permute-start | bytes 6152 | tf_op jit(solution)/shard_map/ppermute | solution.py:42
  4.7 3.2 %shard_map.59 = (bf16[64,16,128]{2,1,0:T(8,128)(2,1)S(1)}, bf16[64,16,128]{2,1,0:T(8,128)(2,1)S(1)}, bf16[64,16,128]{2,1,0:T(8,128)(2,1)S(1)}, bf16[64,16,128]{2,1,0:T(8,128)(2,1)S(1)}) custom-call(f32[32,8192]{1,0:T(8,128)} %vec_ref.13, f32[1,8192]{1,0:T(1,128)} %bitcast.1, bf16[8192,256]{1,0:T(8,128)(2,1)} %refs_4_.7), custom_call_target="tpu_custom_call" | custom-call | tf_op jit(solution)/shard_map/pallas_call | solution.py:214
  7.9 1.6 %collective-permute-start.3 = (bf16[64,16,128]{2,1,0:T(8,128)(2,1)S(1)}, bf16[64,16,128]{2,1,0:T(8,128)(2,1)S(1)}, u32[]{:S(2)}, u32[]{:S(2)}) collective-permute-start(bf16[64,16,128]{2,1,0:T(8,128)(2,1)S(1)} %get-tuple-element.153.refs_0_), channel_id=1, source_target_pairs={{0,8},{4,12},{8,0},{12,4},{16,24},{20,28},{24,16},{28,20},{1,9},{5... | collective-permute-start | bytes 786440 | tf_op jit(solution)/shard_map/ppermute | solution.py:42
  12.0 5.2 %collective-permute-done.3.refs_1_ = bf16[64,16,128]{2,1,0:T(8,128)(2,1)S(1)} collective-permute-done((bf16[64,16,128]{2,1,0:T(8,128)(2,1)S(1)}, bf16[64,16,128]{2,1,0:T(8,128)(2,1)S(1)}, u32[]{:S(2)}, u32[]{:S(2)}) %collective-permute-start.3) | collective-permute-done | bytes 262176 | tf_op jit(solution)/shard_map/ppermute | solution.py:42
  19.2 2.1 %collective-permute-done.6.refs_1_ = bf16[64,16,128]{2,1,0:T(8,128)(2,1)S(1)} collective-permute-done((bf16[64,16,128]{2,1,0:T(8,128)(2,1)S(1)}, bf16[64,16,128]{2,1,0:T(8,128)(2,1)S(1)}, u32[]{:S(2)}, u32[]{:S(2)}) %collective-permute-start.6) | collective-permute-done | bytes 262176 | tf_op jit(solution)/shard_map/ppermute | solution.py:42
  22.9 3.6 %collective-permute-done.5.refs_3_ = bf16[64,16,128]{2,1,0:T(8,128)(2,1)S(1)} collective-permute-done((bf16[64,16,128]{2,1,0:T(8,128)(2,1)S(1)}, bf16[64,16,128]{2,1,0:T(8,128)(2,1)S(1)}, u32[]{:S(2)}, u32[]{:S(2)}) %collective-permute-start.5) | collective-permute-done | bytes 262176 | tf_op jit(solution)/shard_map/ppermute | solution.py:42
  32.4 5.3 %collective-permute-done.9.refs_3_ = bf16[64,16,128]{2,1,0:T(8,128)(2,1)S(1)} collective-permute-done((bf16[64,16,128]{2,1,0:T(8,128)(2,1)S(1)}, bf16[64,16,128]{2,1,0:T(8,128)(2,1)S(1)}, u32[]{:S(2)}, u32[]{:S(2)}) %collective-permute-start.9) | collective-permute-done | bytes 262176 | tf_op jit(solution)/shard_map/ppermute | solution.py:42
  45.8 3.4 %collective-permute-done.11.refs_3_ = bf16[64,16,128]{2,1,0:T(8,128)(2,1)S(1)} collective-permute-done((bf16[64,16,128]{2,1,0:T(8,128)(2,1)S(1)}, bf16[64,16,128]{2,1,0:T(8,128)(2,1)S(1)}, u32[]{:S(2)}, u32[]{:S(2)}) %collective-permute-start.11) | collective-permute-done | bytes 262176 | tf_op jit(solution)/shard_map/ppermute | solution.py:42
  57.1 3.8 %collective-permute-done.16.other_ref.refs_1_ = bf16[16,8192]{1,0:T(8,128)(2,1)S(1)} collective-permute-done((bf16[16,8192]{1,0:T(8,128)(2,1)S(1)}, bf16[16,8192]{1,0:T(8,128)(2,1)S(1)}, u32[]{:S(2)}, u32[]{:S(2)}) %collective-permute-start.16) | collective-permute-done | bytes 262176 | tf_op jit(solution)/shard_map/ppermute | solution.py:42
  65.9 3.9 %collective-permute-start.18 = (bf16[64,16,128]{2,1,0:T(8,128)(2,1)S(1)}, bf16[64,16,128]{2,1,0:T(8,128)(2,1)S(1)}, u32[]{:S(2)}, u32[]{:S(2)}) collective-permute-start(bf16[64,16,128]{2,1,0:T(8,128)(2,1)S(1)} %get-tuple-element.196), channel_id=1, source_target_pairs={{0,16},{4,20},{8,24},{12,28},{16,0},{20,4},{24,8},{28,12},{1,17},{... | collective-permute-start | bytes 786440 | tf_op jit(solution)/shard_map/ppermute | solution.py:42
  73.3 5.0 %collective-permute-done.19.refs_1_ = bf16[64,16,128]{2,1,0:T(8,128)(2,1)S(1)} collective-permute-done((bf16[64,16,128]{2,1,0:T(8,128)(2,1)S(1)}, bf16[64,16,128]{2,1,0:T(8,128)(2,1)S(1)}, u32[]{:S(2)}, u32[]{:S(2)}) %collective-permute-start.19) | collective-permute-done | bytes 262176 | tf_op jit(solution)/shard_map/ppermute | solution.py:42
  78.3 3.5 %collective-permute-start.22 = (bf16[64,16,128]{2,1,0:T(8,128)(2,1)S(1)}, bf16[64,16,128]{2,1,0:T(8,128)(2,1)S(1)}, u32[]{:S(2)}, u32[]{:S(2)}) collective-permute-start(bf16[64,16,128]{2,1,0:T(8,128)(2,1)S(1)} %collective-permute-done.19.refs_1_), channel_id=1, source_target_pairs={{0,4},{4,0},{8,12},{12,8},{16,20},{20,16},{24,28},{28,24},{1,5},{5... | collective-permute-start | bytes 786440 | tf_op jit(solution)/shard_map/ppermute | solution.py:42
  84.0 1.7 %collective-permute-start.26 = (bf16[64,16,128]{2,1,0:T(8,128)(2,1)S(1)}, bf16[64,16,128]{2,1,0:T(8,128)(2,1)S(1)}, u32[]{:S(2)}, u32[]{:S(2)}) collective-permute-start(bf16[64,16,128]{2,1,0:T(8,128)(2,1)S(1)} %collective-permute-done.23.refs_1_), channel_id=1, source_target_pairs={{0,4},{4,0},{8,12},{12,8},{16,20},{20,16},{24,28},{28,24},{1,5},{5... | collective-permute-start | bytes 786440 | tf_op jit(solution)/shard_map/ppermute | solution.py:42
  88.3 2.0 %collective-permute-start.25 = (bf16[16,8192]{1,0:T(8,128)(2,1)S(1)}, bf16[16,8192]{1,0:T(8,128)(2,1)S(1)}, u32[]{:S(2)}, u32[]{:S(2)}) collective-permute-start(bf16[16,8192]{1,0:T(8,128)(2,1)S(1)} %add_convert_fusion.2.mine_ref.refs_0_), channel_id=1, source_target_pairs={{0,2},{1,3},{2,0},{3,1},{4,6},{5,7},{6,4},{7,5},{8,10},{9,11},{10,... | collective-permute-start | bytes 786440 | tf_op jit(solution)/shard_map/ppermute | solution.py:42
  90.3 1.8 %collective-permute-done.26.refs_3_ = bf16[64,16,128]{2,1,0:T(8,128)(2,1)S(1)} collective-permute-done((bf16[64,16,128]{2,1,0:T(8,128)(2,1)S(1)}, bf16[64,16,128]{2,1,0:T(8,128)(2,1)S(1)}, u32[]{:S(2)}, u32[]{:S(2)}) %collective-permute-start.26) | collective-permute-done | bytes 262176 | tf_op jit(solution)/shard_map/ppermute | solution.py:42
  95.9 2.5 %collective-permute-start.31 = (bf16[64,16,128]{2,1,0:T(8,128)(2,1)S(1)}, bf16[64,16,128]{2,1,0:T(8,128)(2,1)S(1)}, u32[]{:S(2)}, u32[]{:S(2)}) collective-permute-start(bf16[64,16,128]{2,1,0:T(8,128)(2,1)S(1)} %get-tuple-element.243.refs_0_), channel_id=1, source_target_pairs={{0,4},{4,0},{8,12},{12,8},{16,20},{20,16},{24,28},{28,24},{1,5},{5... | collective-permute-start | bytes 786440 | tf_op jit(solution)/shard_map/ppermute | solution.py:42
  98.4 3.3 %collective-permute-start.29 = (bf16[64,16,128]{2,1,0:T(8,128)(2,1)S(1)}, bf16[64,16,128]{2,1,0:T(8,128)(2,1)S(1)}, u32[]{:S(2)}, u32[]{:S(2)}) collective-permute-start(bf16[64,16,128]{2,1,0:T(8,128)(2,1)S(1)} %get-tuple-element.222), channel_id=1, source_target_pairs={{0,16},{4,20},{8,24},{12,28},{16,0},{20,4},{24,8},{28,12},{1,17},{... | collective-permute-start | bytes 786440 | tf_op jit(solution)/shard_map/ppermute | solution.py:42
  105.4 8.1 %collective-permute-done.30.refs_1_ = bf16[64,16,128]{2,1,0:T(8,128)(2,1)S(1)} collective-permute-done((bf16[64,16,128]{2,1,0:T(8,128)(2,1)S(1)}, bf16[64,16,128]{2,1,0:T(8,128)(2,1)S(1)}, u32[]{:S(2)}, u32[]{:S(2)}) %collective-permute-start.30) | collective-permute-done | bytes 262176 | tf_op jit(solution)/shard_map/ppermute | solution.py:42
  118.0 3.3 %collective-permute-done.34.refs_3_ = bf16[64,16,128]{2,1,0:T(8,128)(2,1)S(1)} collective-permute-done((bf16[64,16,128]{2,1,0:T(8,128)(2,1)S(1)}, bf16[64,16,128]{2,1,0:T(8,128)(2,1)S(1)}, u32[]{:S(2)}, u32[]{:S(2)}) %collective-permute-start.34) | collective-permute-done | bytes 262176 | tf_op jit(solution)/shard_map/ppermute | solution.py:42
  122.7 2.8 %collective-permute-done.33.refs_3_ = bf16[64,16,128]{2,1,0:T(8,128)(2,1)S(1)} collective-permute-done((bf16[64,16,128]{2,1,0:T(8,128)(2,1)S(1)}, bf16[64,16,128]{2,1,0:T(8,128)(2,1)S(1)}, u32[]{:S(2)}, u32[]{:S(2)}) %collective-permute-start.33) | collective-permute-done | bytes 262176 | tf_op jit(solution)/shard_map/ppermute | solution.py:42
  128.5 3.3 %collective-permute-start.37 = (bf16[64,16,128]{2,1,0:T(8,128)(2,1)S(1)}, bf16[64,16,128]{2,1,0:T(8,128)(2,1)S(1)}, u32[]{:S(2)}, u32[]{:S(2)}) collective-permute-start(bf16[64,16,128]{2,1,0:T(8,128)(2,1)S(1)} %get-tuple-element.252), channel_id=1, source_target_pairs={{0,16},{4,20},{8,24},{12,28},{16,0},{20,4},{24,8},{28,12},{1,17},{... | collective-permute-start | bytes 786440 | tf_op jit(solution)/shard_map/ppermute | solution.py:42
  133.1 9.8 %collective-permute-done.36.refs_1_ = bf16[64,16,128]{2,1,0:T(8,128)(2,1)S(1)} collective-permute-done((bf16[64,16,128]{2,1,0:T(8,128)(2,1)S(1)}, bf16[64,16,128]{2,1,0:T(8,128)(2,1)S(1)}, u32[]{:S(2)}, u32[]{:S(2)}) %collective-permute-start.36) | collective-permute-done | bytes 262176 | tf_op jit(solution)/shard_map/ppermute | solution.py:42
  143.8 2.6 %collective-permute-done.37.refs_3_ = bf16[64,16,128]{2,1,0:T(8,128)(2,1)S(1)} collective-permute-done((bf16[64,16,128]{2,1,0:T(8,128)(2,1)S(1)}, bf16[64,16,128]{2,1,0:T(8,128)(2,1)S(1)}, u32[]{:S(2)}, u32[]{:S(2)}) %collective-permute-start.37) | collective-permute-done | bytes 262176 | tf_op jit(solution)/shard_map/ppermute | solution.py:42
  150.6 7.5 %collective-permute-done.40.other_ref = bf16[16,8192]{1,0:T(8,128)(2,1)S(1)} collective-permute-done((bf16[16,8192]{1,0:T(8,128)(2,1)S(1)}, bf16[16,8192]{1,0:T(8,128)(2,1)S(1)}, u32[]{:S(2)}, u32[]{:S(2)}) %collective-permute-start.40) | collective-permute-done | bytes 262176 | tf_op jit(solution)/shard_map/ppermute | solution.py:42
  (98 shorter events, 64.5 us)
Async XLA Ops:
  9.6 13.3 %collective-permute-start.4 = (bf16[64,16,128]{2,1,0:T(8,128)(2,1)S(1)}, bf16[64,16,128]{2,1,0:T(8,128)(2,1)S(1)}, u32[]{:S(2)}, u32[]{:S(2)}) collective-permute-start(bf16[64,16,128]{2,1,0:T(8,128)(2,1)S(1)} %get-tuple-element.153.refs_0_), channel_id=1, source_target_pairs={{0,4},{4,0},{8,12},{12,8},{16,20},{20,16},{24,28},{28,24},{1,5},{5... | collective-permute-start | bytes 786440 | tf_op jit(solution)/shard_map/ppermute | solution.py:42
  18.7 13.6 %collective-permute-start.8 = (bf16[64,16,128]{2,1,0:T(8,128)(2,1)S(1)}, bf16[64,16,128]{2,1,0:T(8,128)(2,1)S(1)}, u32[]{:S(2)}, u32[]{:S(2)}) collective-permute-start(bf16[64,16,128]{2,1,0:T(8,128)(2,1)S(1)} %get-tuple-element.159.refs_0_), channel_id=1, source_target_pairs={{0,4},{4,0},{8,12},{12,8},{16,20},{20,16},{24,28},{28,24},{1,5},{5... | collective-permute-start | bytes 786440 | tf_op jit(solution)/shard_map/ppermute | solution.py:42
  21.4 16.3 %collective-permute-start.9 = (bf16[64,16,128]{2,1,0:T(8,128)(2,1)S(1)}, bf16[64,16,128]{2,1,0:T(8,128)(2,1)S(1)}, u32[]{:S(2)}, u32[]{:S(2)}) collective-permute-start(bf16[64,16,128]{2,1,0:T(8,128)(2,1)S(1)} %collective-permute-done.6.refs_1_), channel_id=1, source_target_pairs={{0,4},{4,0},{8,12},{12,8},{16,20},{20,16},{24,28},{28,24},{1,5},{5... | collective-permute-start | bytes 786440 | tf_op jit(solution)/shard_map/ppermute | solution.py:42
  27.7 14.6 %collective-permute-start.7 = (bf16[64,16,128]{2,1,0:T(8,128)(2,1)S(1)}, bf16[64,16,128]{2,1,0:T(8,128)(2,1)S(1)}, u32[]{:S(2)}, u32[]{:S(2)}) collective-permute-start(bf16[64,16,128]{2,1,0:T(8,128)(2,1)S(1)} %get-tuple-element.157), channel_id=1, source_target_pairs={{0,16},{4,20},{8,24},{12,28},{16,0},{20,4},{24,8},{28,12},{1,17},{... | collective-permute-start | bytes 786440 | tf_op jit(solution)/shard_map/ppermute | solution.py:42
  29.3 15.9 %collective-permute-start.1 = (bf16[64,16,128]{2,1,0:T(8,128)(2,1)S(1)}, bf16[64,16,128]{2,1,0:T(8,128)(2,1)S(1)}, u32[]{:S(2)}, u32[]{:S(2)}) collective-permute-start(bf16[64,16,128]{2,1,0:T(8,128)(2,1)S(1)} %get-tuple-element.179.refs_0_), channel_id=1, source_target_pairs={{0,8},{4,12},{8,0},{12,4},{16,24},{20,28},{24,16},{28,20},{1,9},{5... | collective-permute-start | bytes 786440 | tf_op jit(solution)/shard_map/ppermute | solution.py:42
  30.8 14.4 %collective-permute-start.2 = (bf16[64,16,128]{2,1,0:T(8,128)(2,1)S(1)}, bf16[64,16,128]{2,1,0:T(8,128)(2,1)S(1)}, u32[]{:S(2)}, u32[]{:S(2)}) collective-permute-start(bf16[64,16,128]{2,1,0:T(8,128)(2,1)S(1)} %get-tuple-element.179.refs_0_), channel_id=1, source_target_pairs={{0,4},{4,0},{8,12},{12,8},{16,20},{20,16},{24,28},{28,24},{1,5},{5... | collective-permute-start | bytes 786440 | tf_op jit(solution)/shard_map/ppermute | solution.py:42
  38.9 10.2 %collective-permute-start.11 = (bf16[64,16,128]{2,1,0:T(8,128)(2,1)S(1)}, bf16[64,16,128]{2,1,0:T(8,128)(2,1)S(1)}, u32[]{:S(2)}, u32[]{:S(2)}) collective-permute-start(bf16[64,16,128]{2,1,0:T(8,128)(2,1)S(1)} %get-tuple-element.164), channel_id=1, source_target_pairs={{0,16},{4,20},{8,24},{12,28},{16,0},{20,4},{24,8},{28,12},{1,17},{... | collective-permute-start | bytes 786440 | tf_op jit(solution)/shard_map/ppermute | solution.py:42
  39.0 10.1 %collective-permute-start.12 = (bf16[64,16,128]{2,1,0:T(8,128)(2,1)S(1)}, bf16[64,16,128]{2,1,0:T(8,128)(2,1)S(1)}, u32[]{:S(2)}, u32[]{:S(2)}) collective-permute-start(bf16[64,16,128]{2,1,0:T(8,128)(2,1)S(1)} %get-tuple-element.191.refs_0_), channel_id=1, source_target_pairs={{0,8},{4,12},{8,0},{12,4},{16,24},{20,28},{24,16},{28,20},{1,9},{5... | collective-permute-start | bytes 786440 | tf_op jit(solution)/shard_map/ppermute | solution.py:42
  54.5 10.1 %collective-permute-start.14 = (bf16[64,16,128]{2,1,0:T(8,128)(2,1)S(1)}, bf16[64,16,128]{2,1,0:T(8,128)(2,1)S(1)}, u32[]{:S(2)}, u32[]{:S(2)}) collective-permute-start(bf16[64,16,128]{2,1,0:T(8,128)(2,1)S(1)} %collective-permute-done.12.refs_1_), channel_id=1, source_target_pairs={{0,4},{4,0},{8,12},{12,8},{16,20},{20,16},{24,28},{28,24},{1,5},{5... | collective-permute-start | bytes 786440 | tf_op jit(solution)/shard_map/ppermute | solution.py:42
  55.9 16.9 %collective-permute-start.17 = (bf16[64,16,128]{2,1,0:T(8,128)(2,1)S(1)}, bf16[64,16,128]{2,1,0:T(8,128)(2,1)S(1)}, u32[]{:S(2)}, u32[]{:S(2)}) collective-permute-start(bf16[64,16,128]{2,1,0:T(8,128)(2,1)S(1)} %get-tuple-element.185), channel_id=1, source_target_pairs={{0,16},{4,20},{8,24},{12,28},{16,0},{20,4},{24,8},{28,12},{1,17},{... | collective-permute-start | bytes 786440 | tf_op jit(solution)/shard_map/ppermute | solution.py:42
  62.0 16.3 %collective-permute-start.19 = (bf16[64,16,128]{2,1,0:T(8,128)(2,1)S(1)}, bf16[64,16,128]{2,1,0:T(8,128)(2,1)S(1)}, u32[]{:S(2)}, u32[]{:S(2)}) collective-permute-start(bf16[64,16,128]{2,1,0:T(8,128)(2,1)S(1)} %get-tuple-element.210.refs_0_), channel_id=1, source_target_pairs={{0,8},{4,12},{8,0},{12,4},{16,24},{20,28},{24,16},{28,20},{1,9},{5... | collective-permute-start | bytes 786440 | tf_op jit(solution)/shard_map/ppermute | solution.py:42
  63.1 15.2 %collective-permute-start.20 = (bf16[64,16,128]{2,1,0:T(8,128)(2,1)S(1)}, bf16[64,16,128]{2,1,0:T(8,128)(2,1)S(1)}, u32[]{:S(2)}, u32[]{:S(2)}) collective-permute-start(bf16[64,16,128]{2,1,0:T(8,128)(2,1)S(1)} %get-tuple-element.210.refs_0_), channel_id=1, source_target_pairs={{0,4},{4,0},{8,12},{12,8},{16,20},{20,16},{24,28},{28,24},{1,5},{5... | collective-permute-start | bytes 786440 | tf_op jit(solution)/shard_map/ppermute | solution.py:42
  65.9 15.9 %collective-permute-start.18 = (bf16[64,16,128]{2,1,0:T(8,128)(2,1)S(1)}, bf16[64,16,128]{2,1,0:T(8,128)(2,1)S(1)}, u32[]{:S(2)}, u32[]{:S(2)}) collective-permute-start(bf16[64,16,128]{2,1,0:T(8,128)(2,1)S(1)} %get-tuple-element.196), channel_id=1, source_target_pairs={{0,16},{4,20},{8,24},{12,28},{16,0},{20,4},{24,8},{28,12},{1,17},{... | collective-permute-start | bytes 786440 | tf_op jit(solution)/shard_map/ppermute | solution.py:42
  69.8 14.1 %collective-permute-start.23 = (bf16[64,16,128]{2,1,0:T(8,128)(2,1)S(1)}, bf16[64,16,128]{2,1,0:T(8,128)(2,1)S(1)}, u32[]{:S(2)}, u32[]{:S(2)}) collective-permute-start(bf16[64,16,128]{2,1,0:T(8,128)(2,1)S(1)} %get-tuple-element.218.refs_0_), channel_id=1, source_target_pairs={{0,8},{4,12},{8,0},{12,4},{16,24},{20,28},{24,16},{28,20},{1,9},{5... | collective-permute-start | bytes 786440 | tf_op jit(solution)/shard_map/ppermute | solution.py:42
  72.8 11.2 %collective-permute-start.24 = (bf16[64,16,128]{2,1,0:T(8,128)(2,1)S(1)}, bf16[64,16,128]{2,1,0:T(8,128)(2,1)S(1)}, u32[]{:S(2)}, u32[]{:S(2)}) collective-permute-start(bf16[64,16,128]{2,1,0:T(8,128)(2,1)S(1)} %get-tuple-element.218.refs_0_), channel_id=1, source_target_pairs={{0,4},{4,0},{8,12},{12,8},{16,20},{20,16},{24,28},{28,24},{1,5},{5... | collective-permute-start | bytes 786440 | tf_op jit(solution)/shard_map/ppermute | solution.py:42
  90.3 13.8 %collective-permute-start.28 = (bf16[64,16,128]{2,1,0:T(8,128)(2,1)S(1)}, bf16[64,16,128]{2,1,0:T(8,128)(2,1)S(1)}, u32[]{:S(2)}, u32[]{:S(2)}) collective-permute-start(bf16[64,16,128]{2,1,0:T(8,128)(2,1)S(1)} %get-tuple-element.214), channel_id=1, source_target_pairs={{0,16},{4,20},{8,24},{12,28},{16,0},{20,4},{24,8},{28,12},{1,17},{... | collective-permute-start | bytes 786440 | tf_op jit(solution)/shard_map/ppermute | solution.py:42
  95.8 17.7 %collective-permute-start.30 = (bf16[64,16,128]{2,1,0:T(8,128)(2,1)S(1)}, bf16[64,16,128]{2,1,0:T(8,128)(2,1)S(1)}, u32[]{:S(2)}, u32[]{:S(2)}) collective-permute-start(bf16[64,16,128]{2,1,0:T(8,128)(2,1)S(1)} %get-tuple-element.243.refs_0_), channel_id=1, source_target_pairs={{0,8},{4,12},{8,0},{12,4},{16,24},{20,28},{24,16},{28,20},{1,9},{5... | collective-permute-start | bytes 786440 | tf_op jit(solution)/shard_map/ppermute | solution.py:42
  95.9 17.6 %collective-permute-start.31 = (bf16[64,16,128]{2,1,0:T(8,128)(2,1)S(1)}, bf16[64,16,128]{2,1,0:T(8,128)(2,1)S(1)}, u32[]{:S(2)}, u32[]{:S(2)}) collective-permute-start(bf16[64,16,128]{2,1,0:T(8,128)(2,1)S(1)} %get-tuple-element.243.refs_0_), channel_id=1, source_target_pairs={{0,4},{4,0},{8,12},{12,8},{16,20},{20,16},{24,28},{28,24},{1,5},{5... | collective-permute-start | bytes 786440 | tf_op jit(solution)/shard_map/ppermute | solution.py:42
  98.4 15.8 %collective-permute-start.29 = (bf16[64,16,128]{2,1,0:T(8,128)(2,1)S(1)}, bf16[64,16,128]{2,1,0:T(8,128)(2,1)S(1)}, u32[]{:S(2)}, u32[]{:S(2)}) collective-permute-start(bf16[64,16,128]{2,1,0:T(8,128)(2,1)S(1)} %get-tuple-element.222), channel_id=1, source_target_pairs={{0,16},{4,20},{8,24},{12,28},{16,0},{20,4},{24,8},{28,12},{1,17},{... | collective-permute-start | bytes 786440 | tf_op jit(solution)/shard_map/ppermute | solution.py:42
  101.7 15.7 %collective-permute-start.27 = (bf16[64,16,128]{2,1,0:T(8,128)(2,1)S(1)}, bf16[64,16,128]{2,1,0:T(8,128)(2,1)S(1)}, u32[]{:S(2)}, u32[]{:S(2)}) collective-permute-start(bf16[64,16,128]{2,1,0:T(8,128)(2,1)S(1)} %get-tuple-element.248.refs_0_), channel_id=1, source_target_pairs={{0,8},{4,12},{8,0},{12,4},{16,24},{20,28},{24,16},{28,20},{1,9},{5... | collective-permute-start | bytes 786440 | tf_op jit(solution)/shard_map/ppermute | solution.py:42
  104.1 18.6 %collective-permute-start.32 = (bf16[64,16,128]{2,1,0:T(8,128)(2,1)S(1)}, bf16[64,16,128]{2,1,0:T(8,128)(2,1)S(1)}, u32[]{:S(2)}, u32[]{:S(2)}) collective-permute-start(bf16[64,16,128]{2,1,0:T(8,128)(2,1)S(1)} %get-tuple-element.248.refs_0_), channel_id=1, source_target_pairs={{0,4},{4,0},{8,12},{12,8},{16,20},{20,16},{24,28},{28,24},{1,5},{5... | collective-permute-start | bytes 786440 | tf_op jit(solution)/shard_map/ppermute | solution.py:42
  122.6 20.3 %collective-permute-start.36 = (bf16[64,16,128]{2,1,0:T(8,128)(2,1)S(1)}, bf16[64,16,128]{2,1,0:T(8,128)(2,1)S(1)}, u32[]{:S(2)}, u32[]{:S(2)}) collective-permute-start(bf16[64,16,128]{2,1,0:T(8,128)(2,1)S(1)} %get-tuple-element.247), channel_id=1, source_target_pairs={{0,16},{4,20},{8,24},{12,28},{16,0},{20,4},{24,8},{28,12},{1,17},{... | collective-permute-start | bytes 786440 | tf_op jit(solution)/shard_map/ppermute | solution.py:42
  127.7 15.3 %collective-permute-start.38 = (bf16[16,8192]{1,0:T(8,128)(2,1)S(1)}, bf16[16,8192]{1,0:T(8,128)(2,1)S(1)}, u32[]{:S(2)}, u32[]{:S(2)}) collective-permute-start(bf16[16,8192]{1,0:T(8,128)(2,1)S(1)} %add_convert_fusion.1.mine_ref), channel_id=1, source_target_pairs={{0,2},{1,3},{2,0},{3,1},{4,6},{5,7},{6,4},{7,5},{8,10},{9,11},{10,... | collective-permute-start | bytes 786440 | tf_op jit(solution)/shard_map/ppermute | solution.py:42
  128.5 18.0 %collective-permute-start.37 = (bf16[64,16,128]{2,1,0:T(8,128)(2,1)S(1)}, bf16[64,16,128]{2,1,0:T(8,128)(2,1)S(1)}, u32[]{:S(2)}, u32[]{:S(2)}) collective-permute-start(bf16[64,16,128]{2,1,0:T(8,128)(2,1)S(1)} %get-tuple-element.252), channel_id=1, source_target_pairs={{0,16},{4,20},{8,24},{12,28},{16,0},{20,4},{24,8},{28,12},{1,17},{... | collective-permute-start | bytes 786440 | tf_op jit(solution)/shard_map/ppermute | solution.py:42
  (21 other events, 172.4 us)

commit v8 on v7

v8 whole, which is shorter than its diff:
```python
import functools

import jax
import jax.numpy as jnp
from jax import lax
from jax.experimental import pallas as pl
from jax.experimental.pallas import tpu as pltpu
from jax.sharding import PartitionSpec as P

CORES = 2
GROUPS = 2
PARTS = CORES
TILE_BLOCKS = 8
UNROLL = 32
VMEM_LIMIT = 8 * 1024 * 1024
SIDE, NEXT = 1, 2

ORDER = (
    "As Al Am Bm",
    "Af1 Af2 Ao1 Ao2",
    "Aw Az1 Bg1 Az2",
    "Bg2 Ae Bo1 As",
    "Bo2 Bw Bz1 Ag1",
    "Be Ag2 Ao1 Ao2",
    "Bs Aw Az1 Ap",
    "Bg1 Ae Bf2 Bo1",
    "Bo2 Bp Bw Bz1",
    "Ar Be Au Br",
    "Bu",
)

VMEM = pl.BlockSpec(memory_space=pltpu.VMEM)
SMEM = pl.BlockSpec(memory_space=pltpu.SMEM)
ANY = pl.BlockSpec(memory_space=pl.ANY)
HBM = pl.BlockSpec(memory_space=pltpu.HBM)


def params():
    return pltpu.CompilerParams(vmem_limit_bytes=VMEM_LIMIT)


def swap(value, axis, size, mask):
    return lax.ppermute(value, axis, [(i, i ^ mask) for i in range(size)])


def add_bf16(a, b):
    return (a.astype(jnp.float32) + b.astype(jnp.float32)).astype(jnp.bfloat16)


def add_f32(a, b):
    return a.astype(jnp.float32) + b.astype(jnp.float32)


def block_sum(scaled, emb):
    return jnp.dot(scaled, emb, preferred_element_type=jnp.float32).astype(jnp.bfloat16)


def probe_rows(core, group, size):
    return pl.ds(pl.multiple_of((core * GROUPS + group) * size, size), size)


def first_sums_kernel(core_ref, vec_ref, quality_ref, emb_ref, *refs):
    *sums_refs, vec, quality, emb, sems = refs
    tiles, tile_docs = emb.shape[:2]
    blocks, group, _ = sums_refs[0].shape
    block_len = tiles * tile_docs // blocks
    core = core_ref[0]
    here = [pltpu.make_async_copy(quality_ref, quality, sems.at[tiles])]
    for i in range(CORES * GROUPS):
        rows = probe_rows(core if i < GROUPS else 1 - core, i % GROUPS, group)
        here.append(pltpu.make_async_copy(vec_ref.at[rows], vec.at[pl.ds(i * group, group)], sems.at[tiles + 1 + i]))

    def tile_copy(j):
        docs = pl.ds(pl.multiple_of(j * tile_docs, tile_docs), tile_docs)
        return pltpu.make_async_copy(emb_ref.at[docs], emb.at[j], sems.at[j])

    for copy in here:
        copy.start()
    for j in range(tiles):
        tile_copy(j).start()
    for copy in here:
        copy.wait()

    def step(j, carry):
        tile_copy(j).wait()
        for b in range(blocks // tiles):
            docs = pl.ds(pl.multiple_of(j * tile_docs + b * block_len, block_len), block_len)
            scaled = (vec[:, docs] * quality[:, docs]).astype(jnp.bfloat16)
            sums = block_sum(scaled, emb[j, b * block_len:(b + 1) * block_len])
            for i, ref in enumerate(sums_refs):
                ref[j * (blocks // tiles) + b] = sums[i * group:(i + 1) * group]
        return carry

    lax.fori_loop(0, tiles, step, 0)


def next_sums_kernel(c, core_ref, mine_ref, other_ref, vec_ref, quality_ref, *refs):
    emb_refs, sums_refs = refs[:PARTS], refs[PARTS:]
    blocks, group, _ = sums_refs[0].shape
    block_len = emb_refs[0].shape[0] // blocks
    rows = probe_rows(core_ref[0], c, group)

    def step(b, carry):
        docs = pl.ds(pl.multiple_of(b * block_len, block_len), block_len)
        quality = quality_ref[:, docs]
        value = add_f32(mine_ref[:, docs], other_ref[:, docs]) * quality - vec_ref[rows, docs]
        scaled = (value * quality).astype(jnp.bfloat16)
        for emb_ref, ref in zip(emb_refs, sums_refs):
            ref[b] = block_sum(scaled, emb_ref[docs])
        return carry

    lax.fori_loop(0, blocks, step, 0, unroll=UNROLL)


def fill_kernel(c, second, core_ref, vec_ref, quality_ref, *refs):
    out_ref, out, sems = refs[-3:]
    tiles = sems.shape[1]
    _, group, docs_all = out.shape
    tile_docs = docs_all // tiles
    copies = []
    for i in range(CORES):
        rows = probe_rows(core_ref[0] if i == 0 else 1 - core_ref[0], c, group)
        pair, before = refs[2 * i:2 * i + 2], refs[2 * (CORES + i):2 * (CORES + i) + 2]
        for j in range(tiles):
            docs = pl.ds(j * tile_docs, tile_docs)
            vec, quality = vec_ref[rows, docs], quality_ref[:, docs]
            value = add_f32(pair[0][:, docs], pair[1][:, docs]) * quality
            if second:
                first = add_f32(before[0][:, docs], before[1][:, docs]) * quality - vec
                value = 2.0 * (value - first) - vec
            else:
                value = value - vec
            out[i, :, docs] = value
            copies.append(pltpu.make_async_copy(out.at[i, :, docs], out_ref.at[rows, docs], sems.at[i, j]))
            copies[-1].start()
    for copy in copies:
        copy.wait()


def lookup(ids_ref, tables, outs, entries):
    def step(b, carry):
        places = [ids_ref[b * entries + k] for k in range(entries)]
        for table, ref in zip(tables, outs):
            total = table[places[0]].astype(jnp.float32)
            for place in places[1:]:
                total = total + table[place].astype(jnp.float32)
            ref[b] = total.astype(ref.dtype)
        return carry

    lax.fori_loop(0, outs[0].shape[0], step, 0, unroll=UNROLL)


def table_kernel(ids_ref, *refs):
    *shards, out_ref, table, sems = refs
    blocks = shards[0].shape[0]
    copies = [
        pltpu.make_async_copy(ref, table.at[pl.ds(i * blocks, blocks)], sems.at[i])
        for i, ref in enumerate(shards)
    ]
    for copy in copies:
        copy.start()
    table[len(shards) * blocks] = jnp.zeros(table.shape[1:], table.dtype)
    for copy in copies:
        copy.wait()
    lookup(ids_ref, [table], [out_ref], ids_ref.shape[0] // blocks)


def lookup_kernel(ids_ref, *refs):
    count = len(refs) // 2
    lookup(ids_ref, refs[:count], refs[count:], ids_ref.shape[0] // refs[count].shape[0])


def expand_kernel(count, *refs):
    *refs, out_ref = refs
    values, embs = refs[:-PARTS], refs[-PARTS:]
    blocks = values[0].shape[0]
    block_len = embs[0].shape[0] // blocks

    def step(b, carry):
        docs = pl.ds(pl.multiple_of(b * block_len, block_len), block_len)
        products = None
        for p, emb_ref in enumerate(embs):
            here = values[p * count:(p + 1) * count]
            total = here[0][b]
            for ref in here[1:]:
                total = total + ref[b].astype(jnp.float32)
            product = lax.dot_general(
                total.astype(jnp.bfloat16), emb_ref[docs], (((1,), (1,)), ((), ())),
                preferred_element_type=jnp.float32,
            )
            products = product if products is None else products + product
        out_ref[:, docs] = products.astype(jnp.bfloat16)
        return carry

    lax.fori_loop(0, blocks, step, 0, unroll=UNROLL)


def body(embeddings, quality, probes, neighbors):
    nrow, ncol = lax.axis_size("row"), lax.axis_size("col")
    me = lax.axis_index("row")
    blk_count, list_len = neighbors.shape
    docs, width = embeddings.shape
    nprobe = probes.shape[0]
    group = nprobe // (CORES * GROUPS)
    core = (lax.axis_index("col") % CORES).astype(jnp.int32).reshape(1)
    tiles = blk_count // TILE_BLOCKS
    reduce_bits = [1 << i for i in reversed(range(nrow.bit_length() - 1)) if 1 << i not in (SIDE, NEXT)]
    dests = [0]
    for m in reversed(reduce_bits):
        dests = [d | m for d in dests] + dests
    shards = (0, NEXT, SIDE, NEXT | SIDE)

    def table_ids(lists):
        flat = lists.reshape(-1)
        apart = (flat // blk_count) ^ me
        place = flat % blk_count
        for i, shard in enumerate(shards):
            place = jnp.where(apart == shard, i * blk_count + flat % blk_count, place)
        return jnp.where((apart & ~(NEXT | SIDE)) == 0, place, len(shards) * blk_count)

    qrow = quality[None, :]
    shard_shape = (blk_count, group, width)
    shard_out = jax.ShapeDtypeStruct(shard_shape, jnp.bfloat16)
    vec_out = jax.ShapeDtypeStruct((nprobe, docs), jnp.float32)

    def first_sums():
        return pl.pallas_call(
            first_sums_kernel,
            in_specs=[SMEM] + [HBM] * 3,
            out_specs=[VMEM] * (CORES * GROUPS),
            out_shape=[shard_out] * (CORES * GROUPS),
            scratch_shapes=[
                pltpu.VMEM((nprobe, docs), jnp.float32),
                pltpu.VMEM((1, docs), jnp.float32),
                pltpu.VMEM((tiles, docs // tiles, width), jnp.bfloat16),
                pltpu.SemaphoreType.DMA((tiles + 1 + CORES * GROUPS,)),
            ],
            compiler_params=params(),
        )(core, *(pltpu.with_memory_space_constraint(v, pltpu.HBM) for v in (probes, qrow, embeddings)))

    def next_sums(c, pair):
        return pl.pallas_call(
            functools.partial(next_sums_kernel, c),
            in_specs=[SMEM] + [VMEM] * (4 + PARTS),
            out_specs=[VMEM] * PARTS,
            out_shape=[shard_out] * PARTS,
            compiler_params=params(),
        )(core, *pair, probes, qrow, *embs)

    def fill(c, held, pairs, before=()):
        held = [] if held is None else [held]
        values = [v for pair in (*pairs, *before) for v in pair]
        return pl.pallas_call(
            functools.partial(fill_kernel, c, bool(before)),
            in_specs=[SMEM] + [VMEM] * (2 + len(values)) + [ANY] * len(held),
            out_specs=HBM,
            out_shape=vec_out,
            input_output_aliases={3 + len(values): 0} if held else {},
            scratch_shapes=[pltpu.VMEM((CORES, group, docs), jnp.float32), pltpu.SemaphoreType.DMA((CORES, 4))],
            compiler_params=params(),
        )(core, probes, qrow, *values, *held)

    def combine_far(ids, shards):
        rows_held = len(shards) * blk_count + 1
        return pl.pallas_call(
            table_kernel,
            in_specs=[SMEM] + [VMEM] * len(shards),
            out_specs=[VMEM] * 2,
            out_shape=[shard_out, jax.ShapeDtypeStruct((rows_held, group, width), jnp.bfloat16)],
            scratch_shapes=[pltpu.SemaphoreType.DMA((len(shards),))],
            compiler_params=params(),
        )(ids, *shards)

    def combine(ids, tables, dtype):
        return pl.pallas_call(
            lookup_kernel,
            in_specs=[SMEM] + [VMEM] * len(tables),
            out_specs=[VMEM] * len(tables),
            out_shape=[jax.ShapeDtypeStruct(shard_shape, dtype)] * len(tables),
            compiler_params=params(),
        )(ids, *tables)

    def expand(parts):
        values = [v for values in parts for v in values]
        return pl.pallas_call(
            functools.partial(expand_kernel, len(parts[0])),
            in_specs=[VMEM] * (len(values) + PARTS),
            out_specs=VMEM,
            out_shape=jax.ShapeDtypeStruct((group, docs), jnp.bfloat16),
            compiler_params=params(),
        )(*values, *embs)

    def reduce(outgoing):
        arrived = []
        for m in reduce_bits:
            taken = {d ^ m: swap(outgoing.pop(d), "row", nrow, m) for d in list(outgoing) if d & m}
            for d, value in taken.items():
                if d:
                    outgoing[d] = add_bf16(outgoing[d], value)
                else:
                    arrived.append(value)
        return arrived

    token = []

    def take(*values):
        if token:
            values = lax.optimization_barrier(values + (token.pop(),))[:-1]
        return values

    lists = {d: swap(neighbors, "row", nrow, d) if d else neighbors for d in dests}
    first = second = None
    embs = [embeddings, swap(embeddings, "col", ncol, 1)]
    gathered = [[None] * PARTS for _ in range(GROUPS)]
    tables = [[None] * PARTS for _ in range(GROUPS)]
    own = [[None] * PARTS for _ in range(GROUPS)]
    arrived = [[None] * PARTS for _ in range(GROUPS)]
    pairs = [None] * GROUPS
    before = [None] * GROUPS

    def start_swaps(c, p, value):
        gathered[c][p] = {0: value}
        for m in (NEXT, SIDE):
            gathered[c][p][m] = swap(value, "row", nrow, m)

    def share(c):
        (mine, other), theirs = pairs[c]
        pairs[c] = (take(mine, other), (theirs[0], swap(other, "col", ncol, 1)))

    for word in (word for line in ORDER for word in line.split()):
        c, step, p = ord(word[0]) - ord("A"), word[1], int(word[2:] or 0) - 1
        if step == "l":
            taken = take(*(lists[d] for d in dests))
            ids = dict(zip(dests, lax.optimization_barrier(tuple(table_ids(v) for v in taken))))
            token.append(ids[0])
        elif step == "s":
            if pairs[c] is None:
                *sums, tied = lax.optimization_barrier((*first_sums(), tuple(lists.values())))
                lists = dict(zip(lists, tied))
                token.append(sums[0])
                for i in range(GROUPS):
                    start_swaps(i, 0, sums[i])
                late = [swap(v, "col", ncol, 1) for v in sums[GROUPS:]]
            else:
                share(c)
                before[c] = pairs[c]
                sums = next_sums(c, pairs[c][0])
                token.append(sums[0])
                for i, value in enumerate(sums):
                    start_swaps(c, i, value)
        elif step == "m":
            (value,) = take(late[c])
            token.append(value)
            start_swaps(c, 1, value)
        elif step in "fg":
            held = gathered[c][p]
            if step == "g":
                held[NEXT], held[SIDE] = take(held[NEXT], held[SIDE])
            else:
                (held[NEXT],) = take(held[NEXT])
            held[NEXT | SIDE] = swap(held[NEXT], "row", nrow, SIDE)
            token.append(held[NEXT])
        elif step == "o":
            held = take(*(gathered[c][p][m] for m in shards))
            outgoing = {}
            for d in dests[:-1]:
                if outgoing:
                    outgoing[d] = combine(ids[d], [tables[c][p]], jnp.bfloat16)[0]
                else:
                    outgoing[d], tables[c][p] = combine_far(ids[d], held)
            token.append(outgoing[dests[-2]])
            arrived[c][p] = reduce(outgoing)
        elif step == "w":
            tables[c] = list(take(*tables[c]))
            own[c] = combine(ids[0], tables[c], jnp.float32)
            token.append(own[c][0])
        elif step == "z":
            arrived[c][p] = take(*arrived[c][p])
            token.append(arrived[c][p][-1])
        elif step == "e":
            flat = take(*own[c], *(v for values in arrived[c] for v in values))
            later = [flat[PARTS + i * len(reduce_bits):PARTS + (i + 1) * len(reduce_bits)] for i in range(PARTS)]
            value = expand([(flat[i], *later[i]) for i in range(PARTS)])
            token.append(value)
            other = swap(value, "col", ncol, CORES)
            for i in range(2, ncol.bit_length() - 1):
                value = add_bf16(value, other)
                other = swap(value, "col", ncol, 1 << i)
            pairs[c] = ((value, other), (swap(value, "col", ncol, 1),))
        elif step == "p":
            theirs = take(*before[c][1])
            before[c] = (before[c][0], theirs)
            first = fill(c, first, before[c])
            token.append(first)
        elif step == "r":
            share(c)
            token.append(pairs[c][0][0])
        else:
            theirs = take(*pairs[c][1])
            second = fill(c, second, (pairs[c][0], theirs), before[c])
            token.append(second)
    return first, second


def solution(mesh):
    placed = (P("row", "col"), P("row"), P(None, "row"), P("row", None))
    return jax.shard_map(
        body,
        mesh=mesh,
        in_specs=placed,
        out_specs=(P(None, "row"), P(None, "row")),
        check_vma=False,
    )
```

time: 159 us -> 160 us (level)
  Pallas kernels: 30.3 us -> 47.4 us
  waiting for transfers between devices: 75.7 us -> 62.4 us
  starting transfers between devices: 51.4 us -> 49 us
    ppermute x41 -> x48, waiting for transfers between devices: 75.7 us -> 62.4 us  [swap(): return lax.ppermute(value, axis, [(i, i ^ mask) for i in range(size)])]
    pallas_call x4, Pallas kernels: 6.23 us -> 18.4 us  [expand(): pl.pallas_call(functools.partial(expand_kernel, len(parts[0])), in_specs=...]
    pallas_call x7, Pallas kernels: 8.74 us -> 13.9 us  [the longest x2 7.09 us: next_sums(): pl.pallas_call(functools.partial(next_sums_kernel, c), in_specs=[SMEM] +...]
    ppermute x41 -> x48, starting transfers between devices: 51.4 us -> 49 us  [swap(): return lax.ppermute(value, axis, [(i, i ^ mask) for i in range(size)])]
  transfers between devices with their start and end apart: 41 -> 48, of which waited for: 23 -> 20; matrix products, arithmetic and copies ran while one was open for 0% -> 0% of each run, Pallas kernels for 18% -> 26%
where the time goes in v8:
time: 160 us
  waiting for transfers between devices  62.4 us (39%)
  starting transfers between devices  49 us (31%)
  Pallas kernels  47.4 us (30%)
    ppermute x48, waiting for transfers between devices, swap(): return lax.ppermute(value, axis, [(i, i ^ mask) for i in range(size)])  62.4 us
    ppermute x48, starting transfers between devices, swap(): return lax.ppermute(value, axis, [(i, i ^ mask) for i in range(size)])  49 us
    pallas_call x4, Pallas kernels, expand(): pl.pallas_call(functools.partial(expand_kernel, len(parts[0])), in_specs=...  18.4 us
    pallas_call x8, Pallas kernels, combine_far(): pl.pallas_call(table_kernel, in_specs=[SMEM] + [VMEM] * len(shards), out_...  9.88 us
    pallas_call x2, Pallas kernels, next_sums(): pl.pallas_call(functools.partial(next_sums_kernel, c), in_specs=[SMEM] +...  7.09 us
    pallas_call x4, Pallas kernels, combine(): pl.pallas_call(lookup_kernel, in_specs=[SMEM] + [VMEM] * len(tables), out...  5.3 us
    pallas_call x4, Pallas kernels, fill(): pl.pallas_call(functools.partial(fill_kernel, c, bool(before)), in_specs=...  3.59 us
  transfers between devices with their start and end apart: 48, of which 20 were waited for; matrix products, arithmetic and copies ran while one was open for 0% of the time, Pallas kernels for 26%

profile of v8, /device:TPU:0, one launch (start us, length us, event | category | flops | bytes accessed | tf_op | source)
XLA Modules:
  0.0 160.1 jit_solution(10514449763664472939)
XLA Ops:
  1.1 3.7 %collective-permute-start = (s32[64,8]{0,1:T(8,128)}, s32[64,8]{0,1:T(8,128)S(1)}, u32[]{:S(2)}, u32[]{:S(2)}) collective-permute-start(s32[64,8]{0,1:T(8,128)} %param.7), channel_id=1, source_target_pairs={{0,16},{4,20},{8,24},{12,28},{16,0},{20,4},{24,8},{28,12},{1,17},{... | collective-permute-start | bytes 6152 | tf_op jit(solution)/shard_map/ppermute | solution.py:43
  4.8 3.2 %shard_map.59 = (bf16[64,8,256]{2,1,0:T(8,128)(2,1)S(1)}, bf16[64,8,256]{2,1,0:T(8,128)(2,1)S(1)}, bf16[64,8,256]{2,1,0:T(8,128)(2,1)S(1)}, bf16[64,8,256]{2,1,0:T(8,128)(2,1)S(1)}) custom-call(s32[1]{0:T(128)} %bitcast.core_ref, f32[32,8192]{1,0:T(8,128)} %vec_ref.13, f32[1,8192]{1,0:T(1,128)} %bitcast.2, bf16[8192,256]{1,0:T(8,128)(2,1)} %refs_4_.7), custom_call_target="tpu_custom_call" | custom-call | tf_op jit(solution)/shard_map/pallas_call | solution.py:227
  12.6 5.1 %collective-permute-done.3.refs_1_ = bf16[64,8,256]{2,1,0:T(8,128)(2,1)S(1)} collective-permute-done((bf16[64,8,256]{2,1,0:T(8,128)(2,1)S(1)}, bf16[64,8,256]{2,1,0:T(8,128)(2,1)S(1)}, u32[]{:S(2)}, u32[]{:S(2)}) %collective-permute-start.3) | collective-permute-done | bytes 262176 | tf_op jit(solution)/shard_map/ppermute | solution.py:43
  19.8 2.8 %collective-permute-done.8.refs_1_ = bf16[64,8,256]{2,1,0:T(8,128)(2,1)S(1)} collective-permute-done((bf16[64,8,256]{2,1,0:T(8,128)(2,1)S(1)}, bf16[64,8,256]{2,1,0:T(8,128)(2,1)S(1)}, u32[]{:S(2)}, u32[]{:S(2)}) %collective-permute-start.8) | collective-permute-done | bytes 262176 | tf_op jit(solution)/shard_map/ppermute | solution.py:43
  29.8 2.8 %collective-permute-done.10.refs_2_ = bf16[64,8,256]{2,1,0:T(8,128)(2,1)S(1)} collective-permute-done((bf16[64,8,256]{2,1,0:T(8,128)(2,1)S(1)}, bf16[64,8,256]{2,1,0:T(8,128)(2,1)S(1)}, u32[]{:S(2)}, u32[]{:S(2)}) %collective-permute-start.10) | collective-permute-done | bytes 262176 | tf_op jit(solution)/shard_map/ppermute | solution.py:43
  34.1 4.1 %collective-permute-done.11.refs_3_ = bf16[64,8,256]{2,1,0:T(8,128)(2,1)S(1)} collective-permute-done((bf16[64,8,256]{2,1,0:T(8,128)(2,1)S(1)}, bf16[64,8,256]{2,1,0:T(8,128)(2,1)S(1)}, u32[]{:S(2)}, u32[]{:S(2)}) %collective-permute-start.11) | collective-permute-done | bytes 262176 | tf_op jit(solution)/shard_map/ppermute | solution.py:43
  42.5 5.6 %collective-permute-done.9.refs_1_ = bf16[64,8,256]{2,1,0:T(8,128)(2,1)S(1)} collective-permute-done((bf16[64,8,256]{2,1,0:T(8,128)(2,1)S(1)}, bf16[64,8,256]{2,1,0:T(8,128)(2,1)S(1)}, u32[]{:S(2)}, u32[]{:S(2)}) %collective-permute-start.9) | collective-permute-done | bytes 262176 | tf_op jit(solution)/shard_map/ppermute | solution.py:43
  51.7 5.0 %collective-permute-done.15.refs_2_ = bf16[64,8,256]{2,1,0:T(8,128)(2,1)S(1)} collective-permute-done((bf16[64,8,256]{2,1,0:T(8,128)(2,1)S(1)}, bf16[64,8,256]{2,1,0:T(8,128)(2,1)S(1)}, u32[]{:S(2)}, u32[]{:S(2)}) %collective-permute-start.15) | collective-permute-done | bytes 262176 | tf_op jit(solution)/shard_map/ppermute | solution.py:43
  56.8 4.6 %shard_map.63.mine_ref.refs_0_.refs_4_ = bf16[8,8192]{1,0:T(8,128)(2,1)S(1)} custom-call(f32[64,8,256]{2,1,0:T(8,128)S(1)} %get-tuple-element.175.refs_0_, bf16[64,8,256]{2,1,0:T(8,128)(2,1)S(1)} %collective-permute-done.9.refs_1_, f32[64,8,256]{2,1,0:T(8,128)S(1)} %get-tuple-element.177.refs_2_, bf16[64,8,256]{2,1,0:T(8,128)(2,1)S(1)} %collective-permute-done.13.refs_3_, ...), custom_call_target="tpu_custom_call" | custom-call | tf_op jit(solution)/shard_map/pallas_call | solution.py:285
  64.2 2.2 %collective-permute-done.18.other_ref.refs_1_.refs_5_ = bf16[8,8192]{1,0:T(8,128)(2,1)S(1)} collective-permute-done((bf16[8,8192]{1,0:T(8,128)(2,1)S(1)}, bf16[8,8192]{1,0:T(8,128)(2,1)S(1)}, u32[]{:S(2)}, u32[]{:S(2)}) %collective-permute-start.18) | collective-permute-done | bytes 131104 | tf_op jit(solution)/shard_map/ppermute | solution.py:43
  66.4 3.5 %shard_map.65 = (bf16[64,8,256]{2,1,0:T(8,128)(2,1)S(1)}, bf16[64,8,256]{2,1,0:T(8,128)(2,1)S(1)}) custom-call(s32[1]{0:T(128)} %bitcast.core_ref, bf16[8,8192]{1,0:T(8,128)(2,1)S(1)} %shard_map.63.mine_ref.refs_0_.refs_4_, bf16[8,8192]{1,0:T(8,128)(2,1)S(1)} %collective-permute-done.18.other_ref.refs_1_.refs_5_, f32[32,8192]{1,0:T(8,128)S(1)} %copy-done.1, ...), custom_call_target="tpu_custom_call" | custom-call | tf_op jit(solution)/shard_map/pallas_call | solution.py:242
  76.1 3.7 %collective-permute-done.19.refs_1_ = bf16[64,8,256]{2,1,0:T(8,128)(2,1)S(1)} collective-permute-done((bf16[64,8,256]{2,1,0:T(8,128)(2,1)S(1)}, bf16[64,8,256]{2,1,0:T(8,128)(2,1)S(1)}, u32[]{:S(2)}, u32[]{:S(2)}) %collective-permute-start.19) | collective-permute-done | bytes 262176 | tf_op jit(solution)/shard_map/ppermute | solution.py:43
  85.6 4.6 %shard_map.68.mine_ref.refs_0_.refs_4_ = bf16[8,8192]{1,0:T(8,128)(2,1)S(1)} custom-call(f32[64,8,256]{2,1,0:T(8,128)S(1)} %get-tuple-element.201.refs_0_, bf16[64,8,256]{2,1,0:T(8,128)(2,1)S(1)} %collective-permute-done.19.refs_1_, f32[64,8,256]{2,1,0:T(8,128)S(1)} %get-tuple-element.203.refs_2_, bf16[64,8,256]{2,1,0:T(8,128)(2,1)S(1)} %collective-permute-done.20.refs_3_, ...), custom_call_target="tpu_custom_call" | custom-call | tf_op jit(solution)/shard_map/pallas_call | solution.py:285
  93.9 2.8 %collective-permute-done.26.refs_3_ = bf16[64,8,256]{2,1,0:T(8,128)(2,1)S(1)} collective-permute-done((bf16[64,8,256]{2,1,0:T(8,128)(2,1)S(1)}, bf16[64,8,256]{2,1,0:T(8,128)(2,1)S(1)}, u32[]{:S(2)}, u32[]{:S(2)}) %collective-permute-start.26) | collective-permute-done | bytes 262176 | tf_op jit(solution)/shard_map/ppermute | solution.py:43
  98.1 3.5 %shard_map.71 = (bf16[64,8,256]{2,1,0:T(8,128)(2,1)S(1)}, bf16[64,8,256]{2,1,0:T(8,128)(2,1)S(1)}) custom-call(s32[1]{0:T(128)} %bitcast.core_ref, bf16[8,8192]{1,0:T(8,128)(2,1)S(1)} %shard_map.68.mine_ref.refs_0_.refs_4_, bf16[8,8192]{1,0:T(8,128)(2,1)S(1)} %collective-permute-done.23.other_ref.refs_1_.refs_5_, f32[32,8192]{1,0:T(8,128)S(1)} %copy-done.1, ...), custom_call_target="tpu_custom_call" | custom-call | tf_op jit(solution)/shard_map/pallas_call | solution.py:242
  101.7 2.7 %collective-permute-start.33 = (bf16[64,8,256]{2,1,0:T(8,128)(2,1)S(1)}, bf16[64,8,256]{2,1,0:T(8,128)(2,1)S(1)}, u32[]{:S(2)}, u32[]{:S(2)}) collective-permute-start(bf16[64,8,256]{2,1,0:T(8,128)(2,1)S(1)} %get-tuple-element.239.refs_0_), channel_id=1, source_target_pairs={{0,8},{4,12},{8,0},{12,4},{16,24},{20,28},{24,16},{28,20},{1,9},{5... | collective-permute-start | bytes 786440 | tf_op jit(solution)/shard_map/ppermute | solution.py:43
  110.5 6.4 %collective-permute-done.33.refs_1_ = bf16[64,8,256]{2,1,0:T(8,128)(2,1)S(1)} collective-permute-done((bf16[64,8,256]{2,1,0:T(8,128)(2,1)S(1)}, bf16[64,8,256]{2,1,0:T(8,128)(2,1)S(1)}, u32[]{:S(2)}, u32[]{:S(2)}) %collective-permute-start.33) | collective-permute-done | bytes 262176 | tf_op jit(solution)/shard_map/ppermute | solution.py:43
  117.5 4.6 %shard_map.74.refs_0_ = bf16[8,8192]{1,0:T(8,128)(2,1)S(1)} custom-call(f32[64,8,256]{2,1,0:T(8,128)S(1)} %get-tuple-element.233.refs_0_, bf16[64,8,256]{2,1,0:T(8,128)(2,1)S(1)} %collective-permute-done.31.refs_1_, f32[64,8,256]{2,1,0:T(8,128)S(1)} %get-tuple-element.235.refs_2_, bf16[64,8,256]{2,1,0:T(8,128)(2,1)S(1)} %collective-permute-done.32.refs_3_, ...), custom_call_target="tpu_custom_call" | custom-call | tf_op jit(solution)/shard_map/pallas_call | solution.py:285
  123.6 2.4 %collective-permute-done.39.refs_3_ = bf16[64,8,256]{2,1,0:T(8,128)(2,1)S(1)} collective-permute-done((bf16[64,8,256]{2,1,0:T(8,128)(2,1)S(1)}, bf16[64,8,256]{2,1,0:T(8,128)(2,1)S(1)}, u32[]{:S(2)}, u32[]{:S(2)}) %collective-permute-start.39) | collective-permute-done | bytes 262176 | tf_op jit(solution)/shard_map/ppermute | solution.py:43
  135.8 8.6 %collective-permute-done.40.refs_1_ = bf16[64,8,256]{2,1,0:T(8,128)(2,1)S(1)} collective-permute-done((bf16[64,8,256]{2,1,0:T(8,128)(2,1)S(1)}, bf16[64,8,256]{2,1,0:T(8,128)(2,1)S(1)}, u32[]{:S(2)}, u32[]{:S(2)}) %collective-permute-start.40) | collective-permute-done | bytes 262176 | tf_op jit(solution)/shard_map/ppermute | solution.py:43
  144.4 3.1 %collective-permute-done.41.refs_3_ = bf16[64,8,256]{2,1,0:T(8,128)(2,1)S(1)} collective-permute-done((bf16[64,8,256]{2,1,0:T(8,128)(2,1)S(1)}, bf16[64,8,256]{2,1,0:T(8,128)(2,1)S(1)}, u32[]{:S(2)}, u32[]{:S(2)}) %collective-permute-start.41) | collective-permute-done | bytes 262176 | tf_op jit(solution)/shard_map/ppermute | solution.py:43
  147.5 4.6 %shard_map.79.refs_0_ = bf16[8,8192]{1,0:T(8,128)(2,1)S(1)} custom-call(f32[64,8,256]{2,1,0:T(8,128)S(1)} %get-tuple-element.259.refs_0_, bf16[64,8,256]{2,1,0:T(8,128)(2,1)S(1)} %collective-permute-done.40.refs_1_, f32[64,8,256]{2,1,0:T(8,128)S(1)} %get-tuple-element.261.refs_2_, bf16[64,8,256]{2,1,0:T(8,128)(2,1)S(1)} %collective-permute-done.41.refs_3_, ...), custom_call_target="tpu_custom_call" | custom-call | tf_op jit(solution)/shard_map/pallas_call | solution.py:285
  152.0 2.9 %collective-permute-start.43 = (bf16[8,8192]{1,0:T(8,128)(2,1)S(1)}, bf16[8,8192]{1,0:T(8,128)(2,1)S(1)}, u32[]{:S(2)}, u32[]{:S(2)}) collective-permute-start(bf16[8,8192]{1,0:T(8,128)(2,1)S(1)} %shard_map.79.refs_0_), channel_id=1, source_target_pairs={{0,2},{1,3},{2,0},{3,1},{4,6},{5,7},{6,4},{7,5},{8,10},{9,11},{10,... | collective-permute-start | bytes 393224 | tf_op jit(solution)/shard_map/ppermute | solution.py:43
  155.4 2.4 %collective-permute-done.43.refs_1_ = bf16[8,8192]{1,0:T(8,128)(2,1)S(1)} collective-permute-done((bf16[8,8192]{1,0:T(8,128)(2,1)S(1)}, bf16[8,8192]{1,0:T(8,128)(2,1)S(1)}, u32[]{:S(2)}, u32[]{:S(2)}) %collective-permute-start.43) | collective-permute-done | bytes 131104 | tf_op jit(solution)/shard_map/ppermute | solution.py:43
  (108 shorter events, 64.2 us)
Async XLA Ops:
  0.6 56.1 %collective-permute-start.16 = (bf16[8192,256]{1,0:T(8,128)(2,1)}, bf16[8192,256]{1,0:T(8,128)(2,1)}, u32[]{:S(2)}, u32[]{:S(2)}) collective-permute-start(bf16[8192,256]{1,0:T(8,128)(2,1)} %refs_4_.7), channel_id=1, source_target_pairs={{0,1},{1,0},{2,3},{3,2},{4,5},{5,4},{6,7},{7,6},{8,9},{9,8},{10,11... | collective-permute-start | bytes 12582920 | tf_op jit(solution)/shard_map/ppermute | solution.py:43
  10.2 13.9 %collective-permute-start.6 = (bf16[64,8,256]{2,1,0:T(8,128)(2,1)S(1)}, bf16[64,8,256]{2,1,0:T(8,128)(2,1)S(1)}, u32[]{:S(2)}, u32[]{:S(2)}) collective-permute-start(bf16[64,8,256]{2,1,0:T(8,128)(2,1)S(1)} %get-tuple-element.154.refs_0_), channel_id=1, source_target_pairs={{0,4},{4,0},{8,12},{12,8},{16,20},{20,16},{24,28},{28,24},{1,5},{5... | collective-permute-start | bytes 786440 | tf_op jit(solution)/shard_map/ppermute | solution.py:43
  19.3 13.3 %collective-permute-start.10 = (bf16[64,8,256]{2,1,0:T(8,128)(2,1)S(1)}, bf16[64,8,256]{2,1,0:T(8,128)(2,1)S(1)}, u32[]{:S(2)}, u32[]{:S(2)}) collective-permute-start(bf16[64,8,256]{2,1,0:T(8,128)(2,1)S(1)} %collective-permute-done.5.refs_0_), channel_id=1, source_target_pairs={{0,4},{4,0},{8,12},{12,8},{16,20},{20,16},{24,28},{28,24},{1,5},{5... | collective-permute-start | bytes 786440 | tf_op jit(solution)/shard_map/ppermute | solution.py:43
  22.6 15.6 %collective-permute-start.11 = (bf16[64,8,256]{2,1,0:T(8,128)(2,1)S(1)}, bf16[64,8,256]{2,1,0:T(8,128)(2,1)S(1)}, u32[]{:S(2)}, u32[]{:S(2)}) collective-permute-start(bf16[64,8,256]{2,1,0:T(8,128)(2,1)S(1)} %collective-permute-done.8.refs_1_), channel_id=1, source_target_pairs={{0,4},{4,0},{8,12},{12,8},{16,20},{20,16},{24,28},{28,24},{1,5},{5... | collective-permute-start | bytes 786440 | tf_op jit(solution)/shard_map/ppermute | solution.py:43
  24.1 16.9 %collective-permute-start.1 = (bf16[64,8,256]{2,1,0:T(8,128)(2,1)S(1)}, bf16[64,8,256]{2,1,0:T(8,128)(2,1)S(1)}, u32[]{:S(2)}, u32[]{:S(2)}) collective-permute-start(bf16[64,8,256]{2,1,0:T(8,128)(2,1)S(1)} %get-tuple-element.179.refs_0_), channel_id=1, source_target_pairs={{0,8},{4,12},{8,0},{12,4},{16,24},{20,28},{24,16},{28,20},{1,9},{5... | collective-permute-start | bytes 786440 | tf_op jit(solution)/shard_map/ppermute | solution.py:43
  28.2 19.9 %collective-permute-start.9 = (bf16[64,8,256]{2,1,0:T(8,128)(2,1)S(1)}, bf16[64,8,256]{2,1,0:T(8,128)(2,1)S(1)}, u32[]{:S(2)}, u32[]{:S(2)}) collective-permute-start(bf16[64,8,256]{2,1,0:T(8,128)(2,1)S(1)} %get-tuple-element.158), channel_id=1, source_target_pairs={{0,16},{4,20},{8,24},{12,28},{16,0},{20,4},{24,8},{28,12},{1,17},{... | collective-permute-start | bytes 786440 | tf_op jit(solution)/shard_map/ppermute | solution.py:43
  32.6 16.9 %collective-permute-start.2 = (bf16[64,8,256]{2,1,0:T(8,128)(2,1)S(1)}, bf16[64,8,256]{2,1,0:T(8,128)(2,1)S(1)}, u32[]{:S(2)}, u32[]{:S(2)}) collective-permute-start(bf16[64,8,256]{2,1,0:T(8,128)(2,1)S(1)} %get-tuple-element.179.refs_0_), channel_id=1, source_target_pairs={{0,4},{4,0},{8,12},{12,8},{16,20},{20,16},{24,28},{28,24},{1,5},{5... | collective-permute-start | bytes 786440 | tf_op jit(solution)/shard_map/ppermute | solution.py:43
  39.5 12.3 %collective-permute-start.13 = (bf16[64,8,256]{2,1,0:T(8,128)(2,1)S(1)}, bf16[64,8,256]{2,1,0:T(8,128)(2,1)S(1)}, u32[]{:S(2)}, u32[]{:S(2)}) collective-permute-start(bf16[64,8,256]{2,1,0:T(8,128)(2,1)S(1)} %get-tuple-element.165), channel_id=1, source_target_pairs={{0,16},{4,20},{8,24},{12,28},{16,0},{20,4},{24,8},{28,12},{1,17},{... | collective-permute-start | bytes 786440 | tf_op jit(solution)/shard_map/ppermute | solution.py:43
  49.5 13.4 %collective-permute-start.12 = (bf16[64,8,256]{2,1,0:T(8,128)(2,1)S(1)}, bf16[64,8,256]{2,1,0:T(8,128)(2,1)S(1)}, u32[]{:S(2)}, u32[]{:S(2)}) collective-permute-start(bf16[64,8,256]{2,1,0:T(8,128)(2,1)S(1)} %collective-permute-done.1.refs_1_), channel_id=1, source_target_pairs={{0,4},{4,0},{8,12},{12,8},{16,20},{20,16},{24,28},{28,24},{1,5},{5... | collective-permute-start | bytes 786440 | tf_op jit(solution)/shard_map/ppermute | solution.py:43
  56.8 15.3 %collective-permute-start.17 = (bf16[64,8,256]{2,1,0:T(8,128)(2,1)S(1)}, bf16[64,8,256]{2,1,0:T(8,128)(2,1)S(1)}, u32[]{:S(2)}, u32[]{:S(2)}) collective-permute-start(bf16[64,8,256]{2,1,0:T(8,128)(2,1)S(1)} %collective-permute-done.14.refs_1_), channel_id=1, source_target_pairs={{0,4},{4,0},{8,12},{12,8},{16,20},{20,16},{24,28},{28,24},{1,5},{5... | collective-permute-start | bytes 786440 | tf_op jit(solution)/shard_map/ppermute | solution.py:43
  64.1 15.7 %collective-permute-start.19 = (bf16[64,8,256]{2,1,0:T(8,128)(2,1)S(1)}, bf16[64,8,256]{2,1,0:T(8,128)(2,1)S(1)}, u32[]{:S(2)}, u32[]{:S(2)}) collective-permute-start(bf16[64,8,256]{2,1,0:T(8,128)(2,1)S(1)} %get-tuple-element.185), channel_id=1, source_target_pairs={{0,16},{4,20},{8,24},{12,28},{16,0},{20,4},{24,8},{28,12},{1,17},{... | collective-permute-start | bytes 786440 | tf_op jit(solution)/shard_map/ppermute | solution.py:43
  69.9 12.4 %collective-permute-start.21 = (bf16[64,8,256]{2,1,0:T(8,128)(2,1)S(1)}, bf16[64,8,256]{2,1,0:T(8,128)(2,1)S(1)}, u32[]{:S(2)}, u32[]{:S(2)}) collective-permute-start(bf16[64,8,256]{2,1,0:T(8,128)(2,1)S(1)} %get-tuple-element.209.refs_0_), channel_id=1, source_target_pairs={{0,8},{4,12},{8,0},{12,4},{16,24},{20,28},{24,16},{28,20},{1,9},{5... | collective-permute-start | bytes 786440 | tf_op jit(solution)/shard_map/ppermute | solution.py:43
  73.3 12.3 %collective-permute-start.20 = (bf16[64,8,256]{2,1,0:T(8,128)(2,1)S(1)}, bf16[64,8,256]{2,1,0:T(8,128)(2,1)S(1)}, u32[]{:S(2)}, u32[]{:S(2)}) collective-permute-start(bf16[64,8,256]{2,1,0:T(8,128)(2,1)S(1)} %get-tuple-element.194), channel_id=1, source_target_pairs={{0,16},{4,20},{8,24},{12,28},{16,0},{20,4},{24,8},{28,12},{1,17},{... | collective-permute-start | bytes 786440 | tf_op jit(solution)/shard_map/ppermute | solution.py:43
  75.5 14.8 %collective-permute-start.24 = (bf16[64,8,256]{2,1,0:T(8,128)(2,1)S(1)}, bf16[64,8,256]{2,1,0:T(8,128)(2,1)S(1)}, u32[]{:S(2)}, u32[]{:S(2)}) collective-permute-start(bf16[64,8,256]{2,1,0:T(8,128)(2,1)S(1)} %get-tuple-element.214.refs_0_), channel_id=1, source_target_pairs={{0,8},{4,12},{8,0},{12,4},{16,24},{20,28},{24,16},{28,20},{1,9},{5... | collective-permute-start | bytes 786440 | tf_op jit(solution)/shard_map/ppermute | solution.py:43
  92.6 14.8 %collective-permute-start.31 = (bf16[64,8,256]{2,1,0:T(8,128)(2,1)S(1)}, bf16[64,8,256]{2,1,0:T(8,128)(2,1)S(1)}, u32[]{:S(2)}, u32[]{:S(2)}) collective-permute-start(bf16[64,8,256]{2,1,0:T(8,128)(2,1)S(1)} %get-tuple-element.213), channel_id=1, source_target_pairs={{0,16},{4,20},{8,24},{12,28},{16,0},{20,4},{24,8},{28,12},{1,17},{... | collective-permute-start | bytes 786440 | tf_op jit(solution)/shard_map/ppermute | solution.py:43
  93.9 11.5 %collective-permute-start.35 = (bf16[8,8192]{1,0:T(8,128)(2,1)S(1)}, bf16[8,8192]{1,0:T(8,128)(2,1)S(1)}, u32[]{:S(2)}, u32[]{:S(2)}) collective-permute-start(bf16[8,8192]{1,0:T(8,128)(2,1)S(1)} %shard_map.63.mine_ref.refs_0_.refs_4_), channel_id=1, source_target_pairs={{0,1},{1,0},{2,3},{3,2},{4,5},{5,4},{6,7},{7,6},{8,9},{9,8},{10,11... | collective-permute-start | bytes 393224 | tf_op jit(solution)/shard_map/ppermute | solution.py:43
  101.7 15.3 %collective-permute-start.33 = (bf16[64,8,256]{2,1,0:T(8,128)(2,1)S(1)}, bf16[64,8,256]{2,1,0:T(8,128)(2,1)S(1)}, u32[]{:S(2)}, u32[]{:S(2)}) collective-permute-start(bf16[64,8,256]{2,1,0:T(8,128)(2,1)S(1)} %get-tuple-element.239.refs_0_), channel_id=1, source_target_pairs={{0,8},{4,12},{8,0},{12,4},{16,24},{20,28},{24,16},{28,20},{1,9},{5... | collective-permute-start | bytes 786440 | tf_op jit(solution)/shard_map/ppermute | solution.py:43
  104.4 12.6 %collective-permute-start.34 = (bf16[64,8,256]{2,1,0:T(8,128)(2,1)S(1)}, bf16[64,8,256]{2,1,0:T(8,128)(2,1)S(1)}, u32[]{:S(2)}, u32[]{:S(2)}) collective-permute-start(bf16[64,8,256]{2,1,0:T(8,128)(2,1)S(1)} %get-tuple-element.239.refs_0_), channel_id=1, source_target_pairs={{0,4},{4,0},{8,12},{12,8},{16,20},{20,16},{24,28},{28,24},{1,5},{5... | collective-permute-start | bytes 786440 | tf_op jit(solution)/shard_map/ppermute | solution.py:43
  104.7 12.8 %collective-permute-start.32 = (bf16[64,8,256]{2,1,0:T(8,128)(2,1)S(1)}, bf16[64,8,256]{2,1,0:T(8,128)(2,1)S(1)}, u32[]{:S(2)}, u32[]{:S(2)}) collective-permute-start(bf16[64,8,256]{2,1,0:T(8,128)(2,1)S(1)} %get-tuple-element.218), channel_id=1, source_target_pairs={{0,16},{4,20},{8,24},{12,28},{16,0},{20,4},{24,8},{28,12},{1,17},{... | collective-permute-start | bytes 786440 | tf_op jit(solution)/shard_map/ppermute | solution.py:43
  105.5 16.6 %collective-permute-start.30 = (bf16[64,8,256]{2,1,0:T(8,128)(2,1)S(1)}, bf16[64,8,256]{2,1,0:T(8,128)(2,1)S(1)}, u32[]{:S(2)}, u32[]{:S(2)}) collective-permute-start(bf16[64,8,256]{2,1,0:T(8,128)(2,1)S(1)} %get-tuple-element.244.refs_0_), channel_id=1, source_target_pairs={{0,8},{4,12},{8,0},{12,4},{16,24},{20,28},{24,16},{28,20},{1,9},{5... | collective-permute-start | bytes 786440 | tf_op jit(solution)/shard_map/ppermute | solution.py:43
  108.8 18.5 %collective-permute-start.37 = (bf16[64,8,256]{2,1,0:T(8,128)(2,1)S(1)}, bf16[64,8,256]{2,1,0:T(8,128)(2,1)S(1)}, u32[]{:S(2)}, u32[]{:S(2)}) collective-permute-start(bf16[64,8,256]{2,1,0:T(8,128)(2,1)S(1)} %get-tuple-element.244.refs_0_), channel_id=1, source_target_pairs={{0,4},{4,0},{8,12},{12,8},{16,20},{20,16},{24,28},{28,24},{1,5},{5... | collective-permute-start | bytes 786440 | tf_op jit(solution)/shard_map/ppermute | solution.py:43
  127.2 17.1 %collective-permute-start.40 = (bf16[64,8,256]{2,1,0:T(8,128)(2,1)S(1)}, bf16[64,8,256]{2,1,0:T(8,128)(2,1)S(1)}, u32[]{:S(2)}, u32[]{:S(2)}) collective-permute-start(bf16[64,8,256]{2,1,0:T(8,128)(2,1)S(1)} %get-tuple-element.243), channel_id=1, source_target_pairs={{0,16},{4,20},{8,24},{12,28},{16,0},{20,4},{24,8},{28,12},{1,17},{... | collective-permute-start | bytes 786440 | tf_op jit(solution)/shard_map/ppermute | solution.py:43
  130.0 17.4 %collective-permute-start.41 = (bf16[64,8,256]{2,1,0:T(8,128)(2,1)S(1)}, bf16[64,8,256]{2,1,0:T(8,128)(2,1)S(1)}, u32[]{:S(2)}, u32[]{:S(2)}) collective-permute-start(bf16[64,8,256]{2,1,0:T(8,128)(2,1)S(1)} %get-tuple-element.248), channel_id=1, source_target_pairs={{0,16},{4,20},{8,24},{12,28},{16,0},{20,4},{24,8},{28,12},{1,17},{... | collective-permute-start | bytes 786440 | tf_op jit(solution)/shard_map/ppermute | solution.py:43
  132.2 12.2 %collective-permute-start.42 = (bf16[8,8192]{1,0:T(8,128)(2,1)S(1)}, bf16[8,8192]{1,0:T(8,128)(2,1)S(1)}, u32[]{:S(2)}, u32[]{:S(2)}) collective-permute-start(bf16[8,8192]{1,0:T(8,128)(2,1)S(1)} %shard_map.74.refs_0_), channel_id=1, source_target_pairs={{0,2},{1,3},{2,0},{3,1},{4,6},{5,7},{6,4},{7,5},{8,10},{9,11},{10,... | collective-permute-start | bytes 393224 | tf_op jit(solution)/shard_map/ppermute | solution.py:43
  (28 other events, 199.1 us)

commit v9 on v8

--- a/solution.py
+++ b/solution.py
@@ -11,7 +11,7 @@
 GROUPS = 2
 PARTS = CORES
 TILE_BLOCKS = 8
-UNROLL = 32
+UNROLL = 16
 VMEM_LIMIT = 8 * 1024 * 1024
 SIDE, NEXT = 1, 2
 
@@ -25,7 +25,7 @@
     "Bs Aw Az1 Ap",
     "Bg1 Ae Bf2 Bo1",
     "Bo2 Bp Bw Bz1",
-    "Ar Be Au Br",
+    "Ar Au Be Br",
     "Bu",
 )
 

time: 160 us -> 161 us (level)
  starting transfers between devices: 49 us -> 43 us
  waiting for transfers between devices: 62.4 us -> 67 us
    ppermute x48, starting transfers between devices: 49 us -> 43 us  [swap(): return lax.ppermute(value, axis, [(i, i ^ mask) for i in range(size)])]
    ppermute x48, waiting for transfers between devices: 62.4 us -> 67 us  [swap(): return lax.ppermute(value, axis, [(i, i ^ mask) for i in range(size)])]
  transfers between devices with their start and end apart: 48 -> 48, of which waited for: 20 -> 21; matrix products, arithmetic and copies ran while one was open for 0% -> 0% of each run, Pallas kernels for 26% -> 27%
where the time goes in v9:
time: 161 us; the launch traced here: 160 us
  waiting for transfers between devices  67 us (42%)
  Pallas kernels  49 us (30%)
  starting transfers between devices  43 us (27%)
    ppermute x48, waiting for transfers between devices, swap(): return lax.ppermute(value, axis, [(i, i ^ mask) for i in range(size)])  67 us
    ppermute x48, starting transfers between devices, swap(): return lax.ppermute(value, axis, [(i, i ^ mask) for i in range(size)])  43 us
    pallas_call x4, Pallas kernels, expand(): pl.pallas_call(functools.partial(expand_kernel, len(parts[0])), in_specs=...  19.3 us
    pallas_call x8, Pallas kernels, combine_far(): pl.pallas_call(table_kernel, in_specs=[SMEM] + [VMEM] * len(shards), out_...  9.98 us
    pallas_call x2, Pallas kernels, next_sums(): pl.pallas_call(functools.partial(next_sums_kernel, c), in_specs=[SMEM] +...  7.59 us
    pallas_call x4, Pallas kernels, combine(): pl.pallas_call(lookup_kernel, in_specs=[SMEM] + [VMEM] * len(tables), out...  5.37 us
    pallas_call x4, Pallas kernels, fill(): pl.pallas_call(functools.partial(fill_kernel, c, bool(before)), in_specs=...  3.59 us
  transfers between devices with their start and end apart: 48, of which 21 were waited for; matrix products, arithmetic and copies ran while one was open for 0% of the time, Pallas kernels for 27%

profile of v9, /device:TPU:0, one launch (start us, length us, event | category | flops | bytes accessed | tf_op | source)
XLA Modules:
  0.0 160.3 jit_solution(9340353286551503551)
XLA Ops:
  1.1 3.7 %collective-permute-start = (s32[64,8]{0,1:T(8,128)}, s32[64,8]{0,1:T(8,128)S(1)}, u32[]{:S(2)}, u32[]{:S(2)}) collective-permute-start(s32[64,8]{0,1:T(8,128)} %param.7), channel_id=1, source_target_pairs={{0,16},{4,20},{8,24},{12,28},{16,0},{20,4},{24,8},{28,12},{1,17},{... | collective-permute-start | bytes 6152 | tf_op jit(solution)/shard_map/ppermute | solution.py:43
  4.8 3.2 %shard_map.59 = (bf16[64,8,256]{2,1,0:T(8,128)(2,1)S(1)}, bf16[64,8,256]{2,1,0:T(8,128)(2,1)S(1)}, bf16[64,8,256]{2,1,0:T(8,128)(2,1)S(1)}, bf16[64,8,256]{2,1,0:T(8,128)(2,1)S(1)}) custom-call(s32[1]{0:T(128)} %bitcast.core_ref, f32[32,8192]{1,0:T(8,128)} %vec_ref.13, f32[1,8192]{1,0:T(1,128)} %bitcast.2, bf16[8192,256]{1,0:T(8,128)(2,1)} %refs_4_.7), custom_call_target="tpu_custom_call" | custom-call | tf_op jit(solution)/shard_map/pallas_call | solution.py:227
  12.6 5.1 %collective-permute-done.3.refs_1_ = bf16[64,8,256]{2,1,0:T(8,128)(2,1)S(1)} collective-permute-done((bf16[64,8,256]{2,1,0:T(8,128)(2,1)S(1)}, bf16[64,8,256]{2,1,0:T(8,128)(2,1)S(1)}, u32[]{:S(2)}, u32[]{:S(2)}) %collective-permute-start.3) | collective-permute-done | bytes 262176 | tf_op jit(solution)/shard_map/ppermute | solution.py:43
  19.8 2.8 %collective-permute-done.8.refs_1_ = bf16[64,8,256]{2,1,0:T(8,128)(2,1)S(1)} collective-permute-done((bf16[64,8,256]{2,1,0:T(8,128)(2,1)S(1)}, bf16[64,8,256]{2,1,0:T(8,128)(2,1)S(1)}, u32[]{:S(2)}, u32[]{:S(2)}) %collective-permute-start.8) | collective-permute-done | bytes 262176 | tf_op jit(solution)/shard_map/ppermute | solution.py:43
  29.8 2.8 %collective-permute-done.10.refs_2_ = bf16[64,8,256]{2,1,0:T(8,128)(2,1)S(1)} collective-permute-done((bf16[64,8,256]{2,1,0:T(8,128)(2,1)S(1)}, bf16[64,8,256]{2,1,0:T(8,128)(2,1)S(1)}, u32[]{:S(2)}, u32[]{:S(2)}) %collective-permute-start.10) | collective-permute-done | bytes 262176 | tf_op jit(solution)/shard_map/ppermute | solution.py:43
  34.1 4.1 %collective-permute-done.11.refs_3_ = bf16[64,8,256]{2,1,0:T(8,128)(2,1)S(1)} collective-permute-done((bf16[64,8,256]{2,1,0:T(8,128)(2,1)S(1)}, bf16[64,8,256]{2,1,0:T(8,128)(2,1)S(1)}, u32[]{:S(2)}, u32[]{:S(2)}) %collective-permute-start.11) | collective-permute-done | bytes 262176 | tf_op jit(solution)/shard_map/ppermute | solution.py:43
  42.6 5.6 %collective-permute-done.9.refs_1_ = bf16[64,8,256]{2,1,0:T(8,128)(2,1)S(1)} collective-permute-done((bf16[64,8,256]{2,1,0:T(8,128)(2,1)S(1)}, bf16[64,8,256]{2,1,0:T(8,128)(2,1)S(1)}, u32[]{:S(2)}, u32[]{:S(2)}) %collective-permute-start.9) | collective-permute-done | bytes 262176 | tf_op jit(solution)/shard_map/ppermute | solution.py:43
  51.7 5.0 %collective-permute-done.15.refs_2_ = bf16[64,8,256]{2,1,0:T(8,128)(2,1)S(1)} collective-permute-done((bf16[64,8,256]{2,1,0:T(8,128)(2,1)S(1)}, bf16[64,8,256]{2,1,0:T(8,128)(2,1)S(1)}, u32[]{:S(2)}, u32[]{:S(2)}) %collective-permute-start.15) | collective-permute-done | bytes 262176 | tf_op jit(solution)/shard_map/ppermute | solution.py:43
  56.8 4.8 %shard_map.63.mine_ref.refs_0_.refs_4_ = bf16[8,8192]{1,0:T(8,128)(2,1)S(1)} custom-call(f32[64,8,256]{2,1,0:T(8,128)S(1)} %get-tuple-element.175.refs_0_, bf16[64,8,256]{2,1,0:T(8,128)(2,1)S(1)} %collective-permute-done.9.refs_1_, f32[64,8,256]{2,1,0:T(8,128)S(1)} %get-tuple-element.177.refs_2_, bf16[64,8,256]{2,1,0:T(8,128)(2,1)S(1)} %collective-permute-done.13.refs_3_, ...), custom_call_target="tpu_custom_call" | custom-call | tf_op jit(solution)/shard_map/pallas_call | solution.py:285
  66.6 3.8 %shard_map.65 = (bf16[64,8,256]{2,1,0:T(8,128)(2,1)S(1)}, bf16[64,8,256]{2,1,0:T(8,128)(2,1)S(1)}) custom-call(s32[1]{0:T(128)} %bitcast.core_ref, bf16[8,8192]{1,0:T(8,128)(2,1)S(1)} %shard_map.63.mine_ref.refs_0_.refs_4_, bf16[8,8192]{1,0:T(8,128)(2,1)S(1)} %collective-permute-done.18.other_ref.refs_1_.refs_5_, f32[32,8192]{1,0:T(8,128)S(1)} %copy-done.1, ...), custom_call_target="tpu_custom_call" | custom-call | tf_op jit(solution)/shard_map/pallas_call | solution.py:242
  73.8 2.2 %collective-permute-start.20 = (bf16[64,8,256]{2,1,0:T(8,128)(2,1)S(1)}, bf16[64,8,256]{2,1,0:T(8,128)(2,1)S(1)}, u32[]{:S(2)}, u32[]{:S(2)}) collective-permute-start(bf16[64,8,256]{2,1,0:T(8,128)(2,1)S(1)} %get-tuple-element.194), channel_id=1, source_target_pairs={{0,16},{4,20},{8,24},{12,28},{16,0},{20,4},{24,8},{28,12},{1,17},{... | collective-permute-start | bytes 786440 | tf_op jit(solution)/shard_map/ppermute | solution.py:43
  76.6 3.4 %collective-permute-done.19.refs_1_ = bf16[64,8,256]{2,1,0:T(8,128)(2,1)S(1)} collective-permute-done((bf16[64,8,256]{2,1,0:T(8,128)(2,1)S(1)}, bf16[64,8,256]{2,1,0:T(8,128)(2,1)S(1)}, u32[]{:S(2)}, u32[]{:S(2)}) %collective-permute-start.19) | collective-permute-done | bytes 262176 | tf_op jit(solution)/shard_map/ppermute | solution.py:43
  85.9 4.8 %shard_map.68.mine_ref.refs_0_.refs_4_ = bf16[8,8192]{1,0:T(8,128)(2,1)S(1)} custom-call(f32[64,8,256]{2,1,0:T(8,128)S(1)} %get-tuple-element.201.refs_0_, bf16[64,8,256]{2,1,0:T(8,128)(2,1)S(1)} %collective-permute-done.19.refs_1_, f32[64,8,256]{2,1,0:T(8,128)S(1)} %get-tuple-element.203.refs_2_, bf16[64,8,256]{2,1,0:T(8,128)(2,1)S(1)} %collective-permute-done.20.refs_3_, ...), custom_call_target="tpu_custom_call" | custom-call | tf_op jit(solution)/shard_map/pallas_call | solution.py:285
  94.1 3.1 %collective-permute-done.26.refs_3_ = bf16[64,8,256]{2,1,0:T(8,128)(2,1)S(1)} collective-permute-done((bf16[64,8,256]{2,1,0:T(8,128)(2,1)S(1)}, bf16[64,8,256]{2,1,0:T(8,128)(2,1)S(1)}, u32[]{:S(2)}, u32[]{:S(2)}) %collective-permute-start.26) | collective-permute-done | bytes 262176 | tf_op jit(solution)/shard_map/ppermute | solution.py:43
  98.4 3.8 %shard_map.71 = (bf16[64,8,256]{2,1,0:T(8,128)(2,1)S(1)}, bf16[64,8,256]{2,1,0:T(8,128)(2,1)S(1)}) custom-call(s32[1]{0:T(128)} %bitcast.core_ref, bf16[8,8192]{1,0:T(8,128)(2,1)S(1)} %shard_map.68.mine_ref.refs_0_.refs_4_, bf16[8,8192]{1,0:T(8,128)(2,1)S(1)} %collective-permute-done.23.other_ref.refs_1_.refs_5_, f32[32,8192]{1,0:T(8,128)S(1)} %copy-done.1, ...), custom_call_target="tpu_custom_call" | custom-call | tf_op jit(solution)/shard_map/pallas_call | solution.py:242
  103.6 2.4 %collective-permute-start.32 = (bf16[64,8,256]{2,1,0:T(8,128)(2,1)S(1)}, bf16[64,8,256]{2,1,0:T(8,128)(2,1)S(1)}, u32[]{:S(2)}, u32[]{:S(2)}) collective-permute-start(bf16[64,8,256]{2,1,0:T(8,128)(2,1)S(1)} %get-tuple-element.218), channel_id=1, source_target_pairs={{0,16},{4,20},{8,24},{12,28},{16,0},{20,4},{24,8},{28,12},{1,17},{... | collective-permute-start | bytes 786440 | tf_op jit(solution)/shard_map/ppermute | solution.py:43
  108.3 8.5 %collective-permute-done.33.refs_1_ = bf16[64,8,256]{2,1,0:T(8,128)(2,1)S(1)} collective-permute-done((bf16[64,8,256]{2,1,0:T(8,128)(2,1)S(1)}, bf16[64,8,256]{2,1,0:T(8,128)(2,1)S(1)}, u32[]{:S(2)}, u32[]{:S(2)}) %collective-permute-start.33) | collective-permute-done | bytes 262176 | tf_op jit(solution)/shard_map/ppermute | solution.py:43
  118.8 4.8 %shard_map.74.refs_0_ = bf16[8,8192]{1,0:T(8,128)(2,1)S(1)} custom-call(f32[64,8,256]{2,1,0:T(8,128)S(1)} %get-tuple-element.233.refs_0_, bf16[64,8,256]{2,1,0:T(8,128)(2,1)S(1)} %collective-permute-done.31.refs_1_, f32[64,8,256]{2,1,0:T(8,128)S(1)} %get-tuple-element.235.refs_2_, bf16[64,8,256]{2,1,0:T(8,128)(2,1)S(1)} %collective-permute-done.32.refs_3_, ...), custom_call_target="tpu_custom_call" | custom-call | tf_op jit(solution)/shard_map/pallas_call | solution.py:285
  128.8 2.8 %collective-permute-done.38.refs_3_ = bf16[64,8,256]{2,1,0:T(8,128)(2,1)S(1)} collective-permute-done((bf16[64,8,256]{2,1,0:T(8,128)(2,1)S(1)}, bf16[64,8,256]{2,1,0:T(8,128)(2,1)S(1)}, u32[]{:S(2)}, u32[]{:S(2)}) %collective-permute-start.38) | collective-permute-done | bytes 262176 | tf_op jit(solution)/shard_map/ppermute | solution.py:43
  136.5 7.5 %collective-permute-done.40.refs_1_ = bf16[64,8,256]{2,1,0:T(8,128)(2,1)S(1)} collective-permute-done((bf16[64,8,256]{2,1,0:T(8,128)(2,1)S(1)}, bf16[64,8,256]{2,1,0:T(8,128)(2,1)S(1)}, u32[]{:S(2)}, u32[]{:S(2)}) %collective-permute-start.40) | collective-permute-done | bytes 262176 | tf_op jit(solution)/shard_map/ppermute | solution.py:43
  144.9 2.2 %collective-permute-done.41.refs_3_ = bf16[64,8,256]{2,1,0:T(8,128)(2,1)S(1)} collective-permute-done((bf16[64,8,256]{2,1,0:T(8,128)(2,1)S(1)}, bf16[64,8,256]{2,1,0:T(8,128)(2,1)S(1)}, u32[]{:S(2)}, u32[]{:S(2)}) %collective-permute-start.41) | collective-permute-done | bytes 262176 | tf_op jit(solution)/shard_map/ppermute | solution.py:43
  147.2 4.8 %shard_map.80.refs_0_ = bf16[8,8192]{1,0:T(8,128)(2,1)S(1)} custom-call(f32[64,8,256]{2,1,0:T(8,128)S(1)} %get-tuple-element.262.refs_0_, bf16[64,8,256]{2,1,0:T(8,128)(2,1)S(1)} %collective-permute-done.40.refs_1_, f32[64,8,256]{2,1,0:T(8,128)S(1)} %get-tuple-element.264.refs_2_, bf16[64,8,256]{2,1,0:T(8,128)(2,1)S(1)} %collective-permute-done.41.refs_3_, ...), custom_call_target="tpu_custom_call" | custom-call | tf_op jit(solution)/shard_map/pallas_call | solution.py:285
  152.0 2.4 %collective-permute-start.45 = (bf16[8,8192]{1,0:T(8,128)(2,1)S(1)}, bf16[8,8192]{1,0:T(8,128)(2,1)S(1)}, u32[]{:S(2)}, u32[]{:S(2)}) collective-permute-start(bf16[8,8192]{1,0:T(8,128)(2,1)S(1)} %shard_map.80.refs_0_), channel_id=1, source_target_pairs={{0,2},{1,3},{2,0},{3,1},{4,6},{5,7},{6,4},{7,5},{8,10},{9,11},{10,... | collective-permute-start | bytes 393224 | tf_op jit(solution)/shard_map/ppermute | solution.py:43
  154.4 3.7 %collective-permute-done.45.refs_1_ = bf16[8,8192]{1,0:T(8,128)(2,1)S(1)} collective-permute-done((bf16[8,8192]{1,0:T(8,128)(2,1)S(1)}, bf16[8,8192]{1,0:T(8,128)(2,1)S(1)}, u32[]{:S(2)}, u32[]{:S(2)}) %collective-permute-start.45) | collective-permute-done | bytes 131104 | tf_op jit(solution)/shard_map/ppermute | solution.py:43
  (108 shorter events, 62.0 us)
Async XLA Ops:
  0.6 56.1 %collective-permute-start.16 = (bf16[8192,256]{1,0:T(8,128)(2,1)}, bf16[8192,256]{1,0:T(8,128)(2,1)}, u32[]{:S(2)}, u32[]{:S(2)}) collective-permute-start(bf16[8192,256]{1,0:T(8,128)(2,1)} %refs_4_.7), channel_id=1, source_target_pairs={{0,1},{1,0},{2,3},{3,2},{4,5},{5,4},{6,7},{7,6},{8,9},{9,8},{10,11... | collective-permute-start | bytes 12582920 | tf_op jit(solution)/shard_map/ppermute | solution.py:43
  10.2 13.9 %collective-permute-start.6 = (bf16[64,8,256]{2,1,0:T(8,128)(2,1)S(1)}, bf16[64,8,256]{2,1,0:T(8,128)(2,1)S(1)}, u32[]{:S(2)}, u32[]{:S(2)}) collective-permute-start(bf16[64,8,256]{2,1,0:T(8,128)(2,1)S(1)} %get-tuple-element.154.refs_0_), channel_id=1, source_target_pairs={{0,4},{4,0},{8,12},{12,8},{16,20},{20,16},{24,28},{28,24},{1,5},{5... | collective-permute-start | bytes 786440 | tf_op jit(solution)/shard_map/ppermute | solution.py:43
  19.3 13.3 %collective-permute-start.10 = (bf16[64,8,256]{2,1,0:T(8,128)(2,1)S(1)}, bf16[64,8,256]{2,1,0:T(8,128)(2,1)S(1)}, u32[]{:S(2)}, u32[]{:S(2)}) collective-permute-start(bf16[64,8,256]{2,1,0:T(8,128)(2,1)S(1)} %collective-permute-done.5.refs_0_), channel_id=1, source_target_pairs={{0,4},{4,0},{8,12},{12,8},{16,20},{20,16},{24,28},{28,24},{1,5},{5... | collective-permute-start | bytes 786440 | tf_op jit(solution)/shard_map/ppermute | solution.py:43
  22.6 15.6 %collective-permute-start.11 = (bf16[64,8,256]{2,1,0:T(8,128)(2,1)S(1)}, bf16[64,8,256]{2,1,0:T(8,128)(2,1)S(1)}, u32[]{:S(2)}, u32[]{:S(2)}) collective-permute-start(bf16[64,8,256]{2,1,0:T(8,128)(2,1)S(1)} %collective-permute-done.8.refs_1_), channel_id=1, source_target_pairs={{0,4},{4,0},{8,12},{12,8},{16,20},{20,16},{24,28},{28,24},{1,5},{5... | collective-permute-start | bytes 786440 | tf_op jit(solution)/shard_map/ppermute | solution.py:43
  24.1 16.9 %collective-permute-start.1 = (bf16[64,8,256]{2,1,0:T(8,128)(2,1)S(1)}, bf16[64,8,256]{2,1,0:T(8,128)(2,1)S(1)}, u32[]{:S(2)}, u32[]{:S(2)}) collective-permute-start(bf16[64,8,256]{2,1,0:T(8,128)(2,1)S(1)} %get-tuple-element.179.refs_0_), channel_id=1, source_target_pairs={{0,8},{4,12},{8,0},{12,4},{16,24},{20,28},{24,16},{28,20},{1,9},{5... | collective-permute-start | bytes 786440 | tf_op jit(solution)/shard_map/ppermute | solution.py:43
  28.3 19.9 %collective-permute-start.9 = (bf16[64,8,256]{2,1,0:T(8,128)(2,1)S(1)}, bf16[64,8,256]{2,1,0:T(8,128)(2,1)S(1)}, u32[]{:S(2)}, u32[]{:S(2)}) collective-permute-start(bf16[64,8,256]{2,1,0:T(8,128)(2,1)S(1)} %get-tuple-element.158), channel_id=1, source_target_pairs={{0,16},{4,20},{8,24},{12,28},{16,0},{20,4},{24,8},{28,12},{1,17},{... | collective-permute-start | bytes 786440 | tf_op jit(solution)/shard_map/ppermute | solution.py:43
  32.6 16.9 %collective-permute-start.2 = (bf16[64,8,256]{2,1,0:T(8,128)(2,1)S(1)}, bf16[64,8,256]{2,1,0:T(8,128)(2,1)S(1)}, u32[]{:S(2)}, u32[]{:S(2)}) collective-permute-start(bf16[64,8,256]{2,1,0:T(8,128)(2,1)S(1)} %get-tuple-element.179.refs_0_), channel_id=1, source_target_pairs={{0,4},{4,0},{8,12},{12,8},{16,20},{20,16},{24,28},{28,24},{1,5},{5... | collective-permute-start | bytes 786440 | tf_op jit(solution)/shard_map/ppermute | solution.py:43
  39.5 12.3 %collective-permute-start.13 = (bf16[64,8,256]{2,1,0:T(8,128)(2,1)S(1)}, bf16[64,8,256]{2,1,0:T(8,128)(2,1)S(1)}, u32[]{:S(2)}, u32[]{:S(2)}) collective-permute-start(bf16[64,8,256]{2,1,0:T(8,128)(2,1)S(1)} %get-tuple-element.165), channel_id=1, source_target_pairs={{0,16},{4,20},{8,24},{12,28},{16,0},{20,4},{24,8},{28,12},{1,17},{... | collective-permute-start | bytes 786440 | tf_op jit(solution)/shard_map/ppermute | solution.py:43
  49.5 13.6 %collective-permute-start.12 = (bf16[64,8,256]{2,1,0:T(8,128)(2,1)S(1)}, bf16[64,8,256]{2,1,0:T(8,128)(2,1)S(1)}, u32[]{:S(2)}, u32[]{:S(2)}) collective-permute-start(bf16[64,8,256]{2,1,0:T(8,128)(2,1)S(1)} %collective-permute-done.1.refs_1_), channel_id=1, source_target_pairs={{0,4},{4,0},{8,12},{12,8},{16,20},{20,16},{24,28},{28,24},{1,5},{5... | collective-permute-start | bytes 786440 | tf_op jit(solution)/shard_map/ppermute | solution.py:43
  56.8 15.8 %collective-permute-start.17 = (bf16[64,8,256]{2,1,0:T(8,128)(2,1)S(1)}, bf16[64,8,256]{2,1,0:T(8,128)(2,1)S(1)}, u32[]{:S(2)}, u32[]{:S(2)}) collective-permute-start(bf16[64,8,256]{2,1,0:T(8,128)(2,1)S(1)} %collective-permute-done.14.refs_1_), channel_id=1, source_target_pairs={{0,4},{4,0},{8,12},{12,8},{16,20},{20,16},{24,28},{28,24},{1,5},{5... | collective-permute-start | bytes 786440 | tf_op jit(solution)/shard_map/ppermute | solution.py:43
  64.4 15.6 %collective-permute-start.19 = (bf16[64,8,256]{2,1,0:T(8,128)(2,1)S(1)}, bf16[64,8,256]{2,1,0:T(8,128)(2,1)S(1)}, u32[]{:S(2)}, u32[]{:S(2)}) collective-permute-start(bf16[64,8,256]{2,1,0:T(8,128)(2,1)S(1)} %get-tuple-element.185), channel_id=1, source_target_pairs={{0,16},{4,20},{8,24},{12,28},{16,0},{20,4},{24,8},{28,12},{1,17},{... | collective-permute-start | bytes 786440 | tf_op jit(solution)/shard_map/ppermute | solution.py:43
  70.4 12.4 %collective-permute-start.21 = (bf16[64,8,256]{2,1,0:T(8,128)(2,1)S(1)}, bf16[64,8,256]{2,1,0:T(8,128)(2,1)S(1)}, u32[]{:S(2)}, u32[]{:S(2)}) collective-permute-start(bf16[64,8,256]{2,1,0:T(8,128)(2,1)S(1)} %get-tuple-element.209.refs_0_), channel_id=1, source_target_pairs={{0,8},{4,12},{8,0},{12,4},{16,24},{20,28},{24,16},{28,20},{1,9},{5... | collective-permute-start | bytes 786440 | tf_op jit(solution)/shard_map/ppermute | solution.py:43
  73.8 12.1 %collective-permute-start.20 = (bf16[64,8,256]{2,1,0:T(8,128)(2,1)S(1)}, bf16[64,8,256]{2,1,0:T(8,128)(2,1)S(1)}, u32[]{:S(2)}, u32[]{:S(2)}) collective-permute-start(bf16[64,8,256]{2,1,0:T(8,128)(2,1)S(1)} %get-tuple-element.194), channel_id=1, source_target_pairs={{0,16},{4,20},{8,24},{12,28},{16,0},{20,4},{24,8},{28,12},{1,17},{... | collective-permute-start | bytes 786440 | tf_op jit(solution)/shard_map/ppermute | solution.py:43
  76.0 14.7 %collective-permute-start.24 = (bf16[64,8,256]{2,1,0:T(8,128)(2,1)S(1)}, bf16[64,8,256]{2,1,0:T(8,128)(2,1)S(1)}, u32[]{:S(2)}, u32[]{:S(2)}) collective-permute-start(bf16[64,8,256]{2,1,0:T(8,128)(2,1)S(1)} %get-tuple-element.214.refs_0_), channel_id=1, source_target_pairs={{0,8},{4,12},{8,0},{12,4},{16,24},{20,28},{24,16},{28,20},{1,9},{5... | collective-permute-start | bytes 786440 | tf_op jit(solution)/shard_map/ppermute | solution.py:43
  93.9 12.1 %collective-permute-start.31 = (bf16[64,8,256]{2,1,0:T(8,128)(2,1)S(1)}, bf16[64,8,256]{2,1,0:T(8,128)(2,1)S(1)}, u32[]{:S(2)}, u32[]{:S(2)}) collective-permute-start(bf16[64,8,256]{2,1,0:T(8,128)(2,1)S(1)} %get-tuple-element.213), channel_id=1, source_target_pairs={{0,16},{4,20},{8,24},{12,28},{16,0},{20,4},{24,8},{28,12},{1,17},{... | collective-permute-start | bytes 786440 | tf_op jit(solution)/shard_map/ppermute | solution.py:43
  94.0 11.9 %collective-permute-start.35 = (bf16[8,8192]{1,0:T(8,128)(2,1)S(1)}, bf16[8,8192]{1,0:T(8,128)(2,1)S(1)}, u32[]{:S(2)}, u32[]{:S(2)}) collective-permute-start(bf16[8,8192]{1,0:T(8,128)(2,1)S(1)} %shard_map.63.mine_ref.refs_0_.refs_4_), channel_id=1, source_target_pairs={{0,1},{1,0},{2,3},{3,2},{4,5},{5,4},{6,7},{7,6},{8,9},{9,8},{10,11... | collective-permute-start | bytes 393224 | tf_op jit(solution)/shard_map/ppermute | solution.py:43
  102.3 14.5 %collective-permute-start.33 = (bf16[64,8,256]{2,1,0:T(8,128)(2,1)S(1)}, bf16[64,8,256]{2,1,0:T(8,128)(2,1)S(1)}, u32[]{:S(2)}, u32[]{:S(2)}) collective-permute-start(bf16[64,8,256]{2,1,0:T(8,128)(2,1)S(1)} %get-tuple-element.239.refs_0_), channel_id=1, source_target_pairs={{0,8},{4,12},{8,0},{12,4},{16,24},{20,28},{24,16},{28,20},{1,9},{5... | collective-permute-start | bytes 786440 | tf_op jit(solution)/shard_map/ppermute | solution.py:43
  102.3 14.4 %collective-permute-start.34 = (bf16[64,8,256]{2,1,0:T(8,128)(2,1)S(1)}, bf16[64,8,256]{2,1,0:T(8,128)(2,1)S(1)}, u32[]{:S(2)}, u32[]{:S(2)}) collective-permute-start(bf16[64,8,256]{2,1,0:T(8,128)(2,1)S(1)} %get-tuple-element.239.refs_0_), channel_id=1, source_target_pairs={{0,4},{4,0},{8,12},{12,8},{16,20},{20,16},{24,28},{28,24},{1,5},{5... | collective-permute-start | bytes 786440 | tf_op jit(solution)/shard_map/ppermute | solution.py:43
  103.6 15.2 %collective-permute-start.32 = (bf16[64,8,256]{2,1,0:T(8,128)(2,1)S(1)}, bf16[64,8,256]{2,1,0:T(8,128)(2,1)S(1)}, u32[]{:S(2)}, u32[]{:S(2)}) collective-permute-start(bf16[64,8,256]{2,1,0:T(8,128)(2,1)S(1)} %get-tuple-element.218), channel_id=1, source_target_pairs={{0,16},{4,20},{8,24},{12,28},{16,0},{20,4},{24,8},{28,12},{1,17},{... | collective-permute-start | bytes 786440 | tf_op jit(solution)/shard_map/ppermute | solution.py:43
  105.9 17.7 %collective-permute-start.30 = (bf16[64,8,256]{2,1,0:T(8,128)(2,1)S(1)}, bf16[64,8,256]{2,1,0:T(8,128)(2,1)S(1)}, u32[]{:S(2)}, u32[]{:S(2)}) collective-permute-start(bf16[64,8,256]{2,1,0:T(8,128)(2,1)S(1)} %get-tuple-element.244.refs_0_), channel_id=1, source_target_pairs={{0,8},{4,12},{8,0},{12,4},{16,24},{20,28},{24,16},{28,20},{1,9},{5... | collective-permute-start | bytes 786440 | tf_op jit(solution)/shard_map/ppermute | solution.py:43
  117.2 11.5 %collective-permute-start.37 = (bf16[64,8,256]{2,1,0:T(8,128)(2,1)S(1)}, bf16[64,8,256]{2,1,0:T(8,128)(2,1)S(1)}, u32[]{:S(2)}, u32[]{:S(2)}) collective-permute-start(bf16[64,8,256]{2,1,0:T(8,128)(2,1)S(1)} %get-tuple-element.244.refs_0_), channel_id=1, source_target_pairs={{0,4},{4,0},{8,12},{12,8},{16,20},{20,16},{24,28},{28,24},{1,5},{5... | collective-permute-start | bytes 786440 | tf_op jit(solution)/shard_map/ppermute | solution.py:43
  126.6 17.4 %collective-permute-start.40 = (bf16[64,8,256]{2,1,0:T(8,128)(2,1)S(1)}, bf16[64,8,256]{2,1,0:T(8,128)(2,1)S(1)}, u32[]{:S(2)}, u32[]{:S(2)}) collective-permute-start(bf16[64,8,256]{2,1,0:T(8,128)(2,1)S(1)} %get-tuple-element.243), channel_id=1, source_target_pairs={{0,16},{4,20},{8,24},{12,28},{16,0},{20,4},{24,8},{28,12},{1,17},{... | collective-permute-start | bytes 786440 | tf_op jit(solution)/shard_map/ppermute | solution.py:43
  132.8 14.3 %collective-permute-start.41 = (bf16[64,8,256]{2,1,0:T(8,128)(2,1)S(1)}, bf16[64,8,256]{2,1,0:T(8,128)(2,1)S(1)}, u32[]{:S(2)}, u32[]{:S(2)}) collective-permute-start(bf16[64,8,256]{2,1,0:T(8,128)(2,1)S(1)} %get-tuple-element.248), channel_id=1, source_target_pairs={{0,16},{4,20},{8,24},{12,28},{16,0},{20,4},{24,8},{28,12},{1,17},{... | collective-permute-start | bytes 786440 | tf_op jit(solution)/shard_map/ppermute | solution.py:43
  133.0 11.0 %collective-permute-start.43 = (bf16[8,8192]{1,0:T(8,128)(2,1)S(1)}, bf16[8,8192]{1,0:T(8,128)(2,1)S(1)}, u32[]{:S(2)}, u32[]{:S(2)}) collective-permute-start(bf16[8,8192]{1,0:T(8,128)(2,1)S(1)} %shard_map.74.refs_0_), channel_id=1, source_target_pairs={{0,1},{1,0},{2,3},{3,2},{4,5},{5,4},{6,7},{7,6},{8,9},{9,8},{10,11... | collective-permute-start | bytes 393224 | tf_op jit(solution)/shard_map/ppermute | solution.py:43
  (28 other events, 218.6 us)

commit v10 on v8

--- a/solution.py
+++ b/solution.py
@@ -18,15 +18,15 @@
 ORDER = (
     "As Al Am Bm",
     "Af1 Af2 Ao1 Ao2",
-    "Aw Az1 Bg1 Az2",
-    "Bg2 Ae Bo1 As",
-    "Bo2 Bw Bz1 Ag1",
-    "Be Ag2 Ao1 Ao2",
-    "Bs Aw Az1 Ap",
-    "Bg1 Ae Bf2 Bo1",
-    "Bo2 Bp Bw Bz1",
-    "Ar Be Au Br",
-    "Bu",
+    "Aw Ak Az1 Bg1",
+    "Az2 Bg2 Ae Bo1",
+    "As Bo2 Bw Bz1",
+    "Ag1 Be Ag2 Ao1",
+    "Ao2 Bs Aw Az1",
+    "Ap Bg1 Ae Bf2",
+    "Bo1 Bo2 Bp Bw",
+    "Bz1 Ar Au Be",
+    "Br Bu",
 )
 
 VMEM = pl.BlockSpec(memory_space=pltpu.VMEM)
@@ -92,6 +92,12 @@
         return carry
 
     lax.fori_loop(0, tiles, step, 0)
+
+
+def hold_kernel(src_ref, out_ref, sem):
+    copy = pltpu.make_async_copy(src_ref, out_ref, sem)
+    copy.start()
+    copy.wait()
 
 
 def next_sums_kernel(c, core_ref, mine_ref, other_ref, vec_ref, quality_ref, *refs):
@@ -237,6 +243,16 @@
             ],
             compiler_params=params(),
         )(core, *(pltpu.with_memory_space_constraint(v, pltpu.HBM) for v in (probes, qrow, embeddings)))
+
+    def hold(value):
+        return pl.pallas_call(
+            hold_kernel,
+            in_specs=[ANY],
+            out_specs=VMEM,
+            out_shape=jax.ShapeDtypeStruct(value.shape, value.dtype),
+            scratch_shapes=[pltpu.SemaphoreType.DMA],
+            compiler_params=params(),
+        )(value)
 
     def next_sums(c, pair):
         return pl.pallas_call(
@@ -352,6 +368,9 @@
             (value,) = take(late[c])
             token.append(value)
             start_swaps(c, 1, value)
+        elif step == "k":
+            embs[1] = hold(*take(embs[1]))
+            token.append(embs[1])
         elif step in "fg":
             held = gathered[c][p]
             if step == "g":

time: 160 us -> 152 us (0.950)
  waiting for transfers between devices: 62.4 us -> 73.5 us
  Pallas kernels: 47.4 us -> 36.5 us
  starting transfers between devices: 49 us -> 40.4 us
    ppermute x48, waiting for transfers between devices: 62.4 us -> 73.5 us  [swap(): return lax.ppermute(value, axis, [(i, i ^ mask) for i in range(size)])]
    pallas_call x4, Pallas kernels: 18.4 us -> 9.59 us  [expand(): pl.pallas_call(functools.partial(expand_kernel, len(parts[0])), in_specs=...]
    ppermute x48, starting transfers between devices: 49 us -> 40.4 us  [swap(): return lax.ppermute(value, axis, [(i, i ^ mask) for i in range(size)])]
    pallas_call x2, Pallas kernels: 7.09 us -> 2.65 us  [next_sums(): pl.pallas_call(functools.partial(next_sums_kernel, c), in_specs=[SMEM] +...]
    pallas_call x0 -> x1, Pallas kernels: none -> 2.35 us  [hold(): pl.pallas_call(hold_kernel, in_specs=[ANY], out_specs=VMEM, out_shape=jax...]
  transfers between devices with their start and end apart: 48 -> 48, of which waited for: 20 -> 22; matrix products, arithmetic and copies ran while one was open for 0% -> 0% of each run, Pallas kernels for 26% -> 22%
where the time goes in v10:
time: 152 us
  waiting for transfers between devices  73.5 us (48%)
  starting transfers between devices  40.4 us (27%)
  Pallas kernels  36.5 us (24%)
    ppermute x48, waiting for transfers between devices, swap(): return lax.ppermute(value, axis, [(i, i ^ mask) for i in range(size)])  73.5 us
    ppermute x48, starting transfers between devices, swap(): return lax.ppermute(value, axis, [(i, i ^ mask) for i in range(size)])  40.4 us
    pallas_call x8, Pallas kernels, combine_far(): pl.pallas_call(table_kernel, in_specs=[SMEM] + [VMEM] * len(shards), out_...  9.87 us
    pallas_call x4, Pallas kernels, expand(): pl.pallas_call(functools.partial(expand_kernel, len(parts[0])), in_specs=...  9.59 us
    pallas_call x4, Pallas kernels, combine(): pl.pallas_call(lookup_kernel, in_specs=[SMEM] + [VMEM] * len(tables), out...  5.3 us
    pallas_call x4, Pallas kernels, fill(): pl.pallas_call(functools.partial(fill_kernel, c, bool(before)), in_specs=...  3.59 us
    pallas_call x1, Pallas kernels, first_sums(): pl.pallas_call(first_sums_kernel, in_specs=[SMEM] + [HBM] * 3, out_specs=...  3.19 us
  transfers between devices with their start and end apart: 48, of which 22 were waited for; matrix products, arithmetic and copies ran while one was open for 0% of the time, Pallas kernels for 22%

profile of v10, /device:TPU:0, one launch (start us, length us, event | category | flops | bytes accessed | tf_op | source)
XLA Modules:
  0.0 151.7 jit_solution(15294194364825067908)
XLA Ops:
  1.1 3.7 %collective-permute-start = (s32[64,8]{0,1:T(8,128)}, s32[64,8]{0,1:T(8,128)S(1)}, u32[]{:S(2)}, u32[]{:S(2)}) collective-permute-start(s32[64,8]{0,1:T(8,128)} %param.7), channel_id=1, source_target_pairs={{0,16},{4,20},{8,24},{12,28},{16,0},{20,4},{24,8},{28,12},{1,17},{... | collective-permute-start | bytes 6152 | tf_op jit(solution)/shard_map/ppermute | solution.py:43
  4.8 3.2 %shard_map.59 = (bf16[64,8,256]{2,1,0:T(8,128)(2,1)S(1)}, bf16[64,8,256]{2,1,0:T(8,128)(2,1)S(1)}, bf16[64,8,256]{2,1,0:T(8,128)(2,1)S(1)}, bf16[64,8,256]{2,1,0:T(8,128)(2,1)S(1)}) custom-call(s32[1]{0:T(128)} %bitcast.core_ref, f32[32,8192]{1,0:T(8,128)} %vec_ref.13, f32[1,8192]{1,0:T(1,128)} %bitcast.2, bf16[8192,256]{1,0:T(8,128)(2,1)} %refs_4_.7), custom_call_target="tpu_custom_call" | custom-call | tf_op jit(solution)/shard_map/pallas_call | solution.py:233
  12.6 5.1 %collective-permute-done.3.refs_1_ = bf16[64,8,256]{2,1,0:T(8,128)(2,1)S(1)} collective-permute-done((bf16[64,8,256]{2,1,0:T(8,128)(2,1)S(1)}, bf16[64,8,256]{2,1,0:T(8,128)(2,1)S(1)}, u32[]{:S(2)}, u32[]{:S(2)}) %collective-permute-start.3) | collective-permute-done | bytes 262176 | tf_op jit(solution)/shard_map/ppermute | solution.py:43
  19.8 2.8 %collective-permute-done.8.refs_1_ = bf16[64,8,256]{2,1,0:T(8,128)(2,1)S(1)} collective-permute-done((bf16[64,8,256]{2,1,0:T(8,128)(2,1)S(1)}, bf16[64,8,256]{2,1,0:T(8,128)(2,1)S(1)}, u32[]{:S(2)}, u32[]{:S(2)}) %collective-permute-start.8) | collective-permute-done | bytes 262176 | tf_op jit(solution)/shard_map/ppermute | solution.py:43
  24.1 2.9 %collective-permute-done.7.refs_3_ = bf16[64,8,256]{2,1,0:T(8,128)(2,1)S(1)} collective-permute-done((bf16[64,8,256]{2,1,0:T(8,128)(2,1)S(1)}, bf16[64,8,256]{2,1,0:T(8,128)(2,1)S(1)}, u32[]{:S(2)}, u32[]{:S(2)}) %collective-permute-start.7) | collective-permute-done | bytes 262176 | tf_op jit(solution)/shard_map/ppermute | solution.py:43
  34.1 4.1 %collective-permute-done.12.refs_3_ = bf16[64,8,256]{2,1,0:T(8,128)(2,1)S(1)} collective-permute-done((bf16[64,8,256]{2,1,0:T(8,128)(2,1)S(1)}, bf16[64,8,256]{2,1,0:T(8,128)(2,1)S(1)}, u32[]{:S(2)}, u32[]{:S(2)}) %collective-permute-start.12) | collective-permute-done | bytes 262176 | tf_op jit(solution)/shard_map/ppermute | solution.py:43
  45.4 2.3 %shard_map.63.refs_5_.refs_1_ = bf16[8192,256]{1,0:T(8,128)(2,1)S(1)} custom-call(bf16[8192,256]{1,0:T(8,128)(2,1)} %collective-permute-done.10.src_ref), custom_call_target="tpu_custom_call" | custom-call | tf_op jit(solution)/shard_map/pallas_call | solution.py:248
  48.4 3.8 %collective-permute-done.14.refs_3_ = bf16[64,8,256]{2,1,0:T(8,128)(2,1)S(1)} collective-permute-done((bf16[64,8,256]{2,1,0:T(8,128)(2,1)S(1)}, bf16[64,8,256]{2,1,0:T(8,128)(2,1)S(1)}, u32[]{:S(2)}, u32[]{:S(2)}) %collective-permute-start.14) | collective-permute-done | bytes 262176 | tf_op jit(solution)/shard_map/ppermute | solution.py:43
  53.7 2.4 %shard_map.64.mine_ref.refs_0_.refs_4_ = bf16[8,8192]{1,0:T(8,128)(2,1)S(1)} custom-call(f32[64,8,256]{2,1,0:T(8,128)S(1)} %get-tuple-element.177.refs_0_, bf16[64,8,256]{2,1,0:T(8,128)(2,1)S(1)} %collective-permute-done.9.refs_1_, f32[64,8,256]{2,1,0:T(8,128)S(1)} %get-tuple-element.179.refs_2_, bf16[64,8,256]{2,1,0:T(8,128)(2,1)S(1)} %collective-permute-done.14.refs_3_, ...), custom_call_target="tpu_custom_call" | custom-call | tf_op jit(solution)/shard_map/pallas_call | solution.py:301
  58.9 2.2 %collective-permute-done.18.other_ref.refs_1_.refs_5_ = bf16[8,8192]{1,0:T(8,128)(2,1)S(1)} collective-permute-done((bf16[8,8192]{1,0:T(8,128)(2,1)S(1)}, bf16[8,8192]{1,0:T(8,128)(2,1)S(1)}, u32[]{:S(2)}, u32[]{:S(2)}) %collective-permute-start.18) | collective-permute-done | bytes 131104 | tf_op jit(solution)/shard_map/ppermute | solution.py:43
  67.1 7.3 %collective-permute-done.19.refs_1_ = bf16[64,8,256]{2,1,0:T(8,128)(2,1)S(1)} collective-permute-done((bf16[64,8,256]{2,1,0:T(8,128)(2,1)S(1)}, bf16[64,8,256]{2,1,0:T(8,128)(2,1)S(1)}, u32[]{:S(2)}, u32[]{:S(2)}) %collective-permute-start.19) | collective-permute-done | bytes 262176 | tf_op jit(solution)/shard_map/ppermute | solution.py:43
  77.9 2.2 %collective-permute-done.20.refs_3_ = bf16[64,8,256]{2,1,0:T(8,128)(2,1)S(1)} collective-permute-done((bf16[64,8,256]{2,1,0:T(8,128)(2,1)S(1)}, bf16[64,8,256]{2,1,0:T(8,128)(2,1)S(1)}, u32[]{:S(2)}, u32[]{:S(2)}) %collective-permute-start.20) | collective-permute-done | bytes 262176 | tf_op jit(solution)/shard_map/ppermute | solution.py:43
  80.1 2.4 %shard_map.69.mine_ref.refs_0_.refs_4_ = bf16[8,8192]{1,0:T(8,128)(2,1)S(1)} custom-call(f32[64,8,256]{2,1,0:T(8,128)S(1)} %get-tuple-element.203.refs_0_, bf16[64,8,256]{2,1,0:T(8,128)(2,1)S(1)} %collective-permute-done.19.refs_1_, f32[64,8,256]{2,1,0:T(8,128)S(1)} %get-tuple-element.205.refs_2_, bf16[64,8,256]{2,1,0:T(8,128)(2,1)S(1)} %collective-permute-done.20.refs_3_, ...), custom_call_target="tpu_custom_call" | custom-call | tf_op jit(solution)/shard_map/pallas_call | solution.py:301
  86.7 2.5 %collective-permute-done.26.refs_3_ = bf16[64,8,256]{2,1,0:T(8,128)(2,1)S(1)} collective-permute-done((bf16[64,8,256]{2,1,0:T(8,128)(2,1)S(1)}, bf16[64,8,256]{2,1,0:T(8,128)(2,1)S(1)}, u32[]{:S(2)}, u32[]{:S(2)}) %collective-permute-start.26) | collective-permute-done | bytes 262176 | tf_op jit(solution)/shard_map/ppermute | solution.py:43
  92.6 2.9 %collective-permute-start.32 = (bf16[64,8,256]{2,1,0:T(8,128)(2,1)S(1)}, bf16[64,8,256]{2,1,0:T(8,128)(2,1)S(1)}, u32[]{:S(2)}, u32[]{:S(2)}) collective-permute-start(bf16[64,8,256]{2,1,0:T(8,128)(2,1)S(1)} %get-tuple-element.220), channel_id=1, source_target_pairs={{0,16},{4,20},{8,24},{12,28},{16,0},{20,4},{24,8},{28,12},{1,17},{... | collective-permute-start | bytes 786440 | tf_op jit(solution)/shard_map/ppermute | solution.py:43
  99.7 7.9 %collective-permute-done.33.refs_1_ = bf16[64,8,256]{2,1,0:T(8,128)(2,1)S(1)} collective-permute-done((bf16[64,8,256]{2,1,0:T(8,128)(2,1)S(1)}, bf16[64,8,256]{2,1,0:T(8,128)(2,1)S(1)}, u32[]{:S(2)}, u32[]{:S(2)}) %collective-permute-start.33) | collective-permute-done | bytes 262176 | tf_op jit(solution)/shard_map/ppermute | solution.py:43
  109.6 2.4 %shard_map.75.refs_0_ = bf16[8,8192]{1,0:T(8,128)(2,1)S(1)} custom-call(f32[64,8,256]{2,1,0:T(8,128)S(1)} %get-tuple-element.235.refs_0_, bf16[64,8,256]{2,1,0:T(8,128)(2,1)S(1)} %collective-permute-done.31.refs_1_, f32[64,8,256]{2,1,0:T(8,128)S(1)} %get-tuple-element.237.refs_2_, bf16[64,8,256]{2,1,0:T(8,128)(2,1)S(1)} %collective-permute-done.32.refs_3_, ...), custom_call_target="tpu_custom_call" | custom-call | tf_op jit(solution)/shard_map/pallas_call | solution.py:301
  114.0 2.8 %collective-permute-done.39.refs_3_ = bf16[64,8,256]{2,1,0:T(8,128)(2,1)S(1)} collective-permute-done((bf16[64,8,256]{2,1,0:T(8,128)(2,1)S(1)}, bf16[64,8,256]{2,1,0:T(8,128)(2,1)S(1)}, u32[]{:S(2)}, u32[]{:S(2)}) %collective-permute-start.39) | collective-permute-done | bytes 262176 | tf_op jit(solution)/shard_map/ppermute | solution.py:43
  118.8 3.6 %collective-permute-done.37.refs_2_ = bf16[64,8,256]{2,1,0:T(8,128)(2,1)S(1)} collective-permute-done((bf16[64,8,256]{2,1,0:T(8,128)(2,1)S(1)}, bf16[64,8,256]{2,1,0:T(8,128)(2,1)S(1)}, u32[]{:S(2)}, u32[]{:S(2)}) %collective-permute-start.37) | collective-permute-done | bytes 262176 | tf_op jit(solution)/shard_map/ppermute | solution.py:43
  122.4 4.4 %collective-permute-done.38.refs_3_ = bf16[64,8,256]{2,1,0:T(8,128)(2,1)S(1)} collective-permute-done((bf16[64,8,256]{2,1,0:T(8,128)(2,1)S(1)}, bf16[64,8,256]{2,1,0:T(8,128)(2,1)S(1)}, u32[]{:S(2)}, u32[]{:S(2)}) %collective-permute-start.38) | collective-permute-done | bytes 262176 | tf_op jit(solution)/shard_map/ppermute | solution.py:43
  131.7 4.6 %collective-permute-done.40.refs_1_ = bf16[64,8,256]{2,1,0:T(8,128)(2,1)S(1)} collective-permute-done((bf16[64,8,256]{2,1,0:T(8,128)(2,1)S(1)}, bf16[64,8,256]{2,1,0:T(8,128)(2,1)S(1)}, u32[]{:S(2)}, u32[]{:S(2)}) %collective-permute-start.40) | collective-permute-done | bytes 262176 | tf_op jit(solution)/shard_map/ppermute | solution.py:43
  137.3 4.5 %collective-permute-done.41.refs_3_ = bf16[64,8,256]{2,1,0:T(8,128)(2,1)S(1)} collective-permute-done((bf16[64,8,256]{2,1,0:T(8,128)(2,1)S(1)}, bf16[64,8,256]{2,1,0:T(8,128)(2,1)S(1)}, u32[]{:S(2)}, u32[]{:S(2)}) %collective-permute-start.41) | collective-permute-done | bytes 262176 | tf_op jit(solution)/shard_map/ppermute | solution.py:43
  141.7 2.4 %shard_map.81.refs_0_ = bf16[8,8192]{1,0:T(8,128)(2,1)S(1)} custom-call(f32[64,8,256]{2,1,0:T(8,128)S(1)} %get-tuple-element.264.refs_0_, bf16[64,8,256]{2,1,0:T(8,128)(2,1)S(1)} %collective-permute-done.40.refs_1_, f32[64,8,256]{2,1,0:T(8,128)S(1)} %get-tuple-element.266.refs_2_, bf16[64,8,256]{2,1,0:T(8,128)(2,1)S(1)} %collective-permute-done.41.refs_3_, ...), custom_call_target="tpu_custom_call" | custom-call | tf_op jit(solution)/shard_map/pallas_call | solution.py:301
  145.1 4.4 %collective-permute-done.45.refs_1_ = bf16[8,8192]{1,0:T(8,128)(2,1)S(1)} collective-permute-done((bf16[8,8192]{1,0:T(8,128)(2,1)S(1)}, bf16[8,8192]{1,0:T(8,128)(2,1)S(1)}, u32[]{:S(2)}, u32[]{:S(2)}) %collective-permute-start.45) | collective-permute-done | bytes 131104 | tf_op jit(solution)/shard_map/ppermute | solution.py:43
  (109 shorter events, 63.9 us)
Async XLA Ops:
  0.6 41.9 %collective-permute-start.10 = (bf16[8192,256]{1,0:T(8,128)(2,1)}, bf16[8192,256]{1,0:T(8,128)(2,1)}, u32[]{:S(2)}, u32[]{:S(2)}) collective-permute-start(bf16[8192,256]{1,0:T(8,128)(2,1)} %refs_4_.7), channel_id=1, source_target_pairs={{0,1},{1,0},{2,3},{3,2},{4,5},{5,4},{6,7},{7,6},{8,9},{9,8},{10,11... | collective-permute-start | bytes 12582920 | tf_op jit(solution)/shard_map/ppermute | solution.py:43
  10.2 13.9 %collective-permute-start.6 = (bf16[64,8,256]{2,1,0:T(8,128)(2,1)S(1)}, bf16[64,8,256]{2,1,0:T(8,128)(2,1)S(1)}, u32[]{:S(2)}, u32[]{:S(2)}) collective-permute-start(bf16[64,8,256]{2,1,0:T(8,128)(2,1)S(1)} %get-tuple-element.155.refs_0_), channel_id=1, source_target_pairs={{0,4},{4,0},{8,12},{12,8},{16,20},{20,16},{24,28},{28,24},{1,5},{5... | collective-permute-start | bytes 786440 | tf_op jit(solution)/shard_map/ppermute | solution.py:43
  19.3 13.3 %collective-permute-start.11 = (bf16[64,8,256]{2,1,0:T(8,128)(2,1)S(1)}, bf16[64,8,256]{2,1,0:T(8,128)(2,1)S(1)}, u32[]{:S(2)}, u32[]{:S(2)}) collective-permute-start(bf16[64,8,256]{2,1,0:T(8,128)(2,1)S(1)} %collective-permute-done.5.refs_0_), channel_id=1, source_target_pairs={{0,4},{4,0},{8,12},{12,8},{16,20},{20,16},{24,28},{28,24},{1,5},{5... | collective-permute-start | bytes 786440 | tf_op jit(solution)/shard_map/ppermute | solution.py:43
  22.6 15.6 %collective-permute-start.12 = (bf16[64,8,256]{2,1,0:T(8,128)(2,1)S(1)}, bf16[64,8,256]{2,1,0:T(8,128)(2,1)S(1)}, u32[]{:S(2)}, u32[]{:S(2)}) collective-permute-start(bf16[64,8,256]{2,1,0:T(8,128)(2,1)S(1)} %collective-permute-done.8.refs_1_), channel_id=1, source_target_pairs={{0,4},{4,0},{8,12},{12,8},{16,20},{20,16},{24,28},{28,24},{1,5},{5... | collective-permute-start | bytes 786440 | tf_op jit(solution)/shard_map/ppermute | solution.py:43
  28.2 12.8 %collective-permute-start.9 = (bf16[64,8,256]{2,1,0:T(8,128)(2,1)S(1)}, bf16[64,8,256]{2,1,0:T(8,128)(2,1)S(1)}, u32[]{:S(2)}, u32[]{:S(2)}) collective-permute-start(bf16[64,8,256]{2,1,0:T(8,128)(2,1)S(1)} %get-tuple-element.159), channel_id=1, source_target_pairs={{0,16},{4,20},{8,24},{12,28},{16,0},{20,4},{24,8},{28,12},{1,17},{... | collective-permute-start | bytes 786440 | tf_op jit(solution)/shard_map/ppermute | solution.py:43
  29.8 18.0 %collective-permute-start.1 = (bf16[64,8,256]{2,1,0:T(8,128)(2,1)S(1)}, bf16[64,8,256]{2,1,0:T(8,128)(2,1)S(1)}, u32[]{:S(2)}, u32[]{:S(2)}) collective-permute-start(bf16[64,8,256]{2,1,0:T(8,128)(2,1)S(1)} %get-tuple-element.181.refs_0_), channel_id=1, source_target_pairs={{0,8},{4,12},{8,0},{12,4},{16,24},{20,28},{24,16},{28,20},{1,9},{5... | collective-permute-start | bytes 786440 | tf_op jit(solution)/shard_map/ppermute | solution.py:43
  32.6 15.2 %collective-permute-start.2 = (bf16[64,8,256]{2,1,0:T(8,128)(2,1)S(1)}, bf16[64,8,256]{2,1,0:T(8,128)(2,1)S(1)}, u32[]{:S(2)}, u32[]{:S(2)}) collective-permute-start(bf16[64,8,256]{2,1,0:T(8,128)(2,1)S(1)} %get-tuple-element.181.refs_0_), channel_id=1, source_target_pairs={{0,4},{4,0},{8,12},{12,8},{16,20},{20,16},{24,28},{28,24},{1,5},{5... | collective-permute-start | bytes 786440 | tf_op jit(solution)/shard_map/ppermute | solution.py:43
  38.2 13.9 %collective-permute-start.15 = (bf16[64,8,256]{2,1,0:T(8,128)(2,1)S(1)}, bf16[64,8,256]{2,1,0:T(8,128)(2,1)S(1)}, u32[]{:S(2)}, u32[]{:S(2)}) collective-permute-start(bf16[64,8,256]{2,1,0:T(8,128)(2,1)S(1)} %collective-permute-done.4.refs_0_), channel_id=1, source_target_pairs={{0,8},{4,12},{8,0},{12,4},{16,24},{20,28},{24,16},{28,20},{1,9},{5... | collective-permute-start | bytes 786440 | tf_op jit(solution)/shard_map/ppermute | solution.py:43
  41.1 11.1 %collective-permute-start.14 = (bf16[64,8,256]{2,1,0:T(8,128)(2,1)S(1)}, bf16[64,8,256]{2,1,0:T(8,128)(2,1)S(1)}, u32[]{:S(2)}, u32[]{:S(2)}) collective-permute-start(bf16[64,8,256]{2,1,0:T(8,128)(2,1)S(1)} %get-tuple-element.166), channel_id=1, source_target_pairs={{0,16},{4,20},{8,24},{12,28},{16,0},{20,4},{24,8},{28,12},{1,17},{... | collective-permute-start | bytes 786440 | tf_op jit(solution)/shard_map/ppermute | solution.py:43
  52.2 10.9 %collective-permute-start.17 = (bf16[64,8,256]{2,1,0:T(8,128)(2,1)S(1)}, bf16[64,8,256]{2,1,0:T(8,128)(2,1)S(1)}, u32[]{:S(2)}, u32[]{:S(2)}) collective-permute-start(bf16[64,8,256]{2,1,0:T(8,128)(2,1)S(1)} %collective-permute-done.15.refs_1_), channel_id=1, source_target_pairs={{0,4},{4,0},{8,12},{12,8},{16,20},{20,16},{24,28},{28,24},{1,5},{5... | collective-permute-start | bytes 786440 | tf_op jit(solution)/shard_map/ppermute | solution.py:43
  58.8 15.6 %collective-permute-start.19 = (bf16[64,8,256]{2,1,0:T(8,128)(2,1)S(1)}, bf16[64,8,256]{2,1,0:T(8,128)(2,1)S(1)}, u32[]{:S(2)}, u32[]{:S(2)}) collective-permute-start(bf16[64,8,256]{2,1,0:T(8,128)(2,1)S(1)} %get-tuple-element.187), channel_id=1, source_target_pairs={{0,16},{4,20},{8,24},{12,28},{16,0},{20,4},{24,8},{28,12},{1,17},{... | collective-permute-start | bytes 786440 | tf_op jit(solution)/shard_map/ppermute | solution.py:43
  62.4 13.7 %collective-permute-start.21 = (bf16[64,8,256]{2,1,0:T(8,128)(2,1)S(1)}, bf16[64,8,256]{2,1,0:T(8,128)(2,1)S(1)}, u32[]{:S(2)}, u32[]{:S(2)}) collective-permute-start(bf16[64,8,256]{2,1,0:T(8,128)(2,1)S(1)} %get-tuple-element.211.refs_0_), channel_id=1, source_target_pairs={{0,8},{4,12},{8,0},{12,4},{16,24},{20,28},{24,16},{28,20},{1,9},{5... | collective-permute-start | bytes 786440 | tf_op jit(solution)/shard_map/ppermute | solution.py:43
  62.4 13.6 %collective-permute-start.22 = (bf16[64,8,256]{2,1,0:T(8,128)(2,1)S(1)}, bf16[64,8,256]{2,1,0:T(8,128)(2,1)S(1)}, u32[]{:S(2)}, u32[]{:S(2)}) collective-permute-start(bf16[64,8,256]{2,1,0:T(8,128)(2,1)S(1)} %get-tuple-element.211.refs_0_), channel_id=1, source_target_pairs={{0,4},{4,0},{8,12},{12,8},{16,20},{20,16},{24,28},{28,24},{1,5},{5... | collective-permute-start | bytes 786440 | tf_op jit(solution)/shard_map/ppermute | solution.py:43
  64.3 15.8 %collective-permute-start.20 = (bf16[64,8,256]{2,1,0:T(8,128)(2,1)S(1)}, bf16[64,8,256]{2,1,0:T(8,128)(2,1)S(1)}, u32[]{:S(2)}, u32[]{:S(2)}) collective-permute-start(bf16[64,8,256]{2,1,0:T(8,128)(2,1)S(1)} %get-tuple-element.196), channel_id=1, source_target_pairs={{0,16},{4,20},{8,24},{12,28},{16,0},{20,4},{24,8},{28,12},{1,17},{... | collective-permute-start | bytes 786440 | tf_op jit(solution)/shard_map/ppermute | solution.py:43
  66.4 16.1 %collective-permute-start.24 = (bf16[64,8,256]{2,1,0:T(8,128)(2,1)S(1)}, bf16[64,8,256]{2,1,0:T(8,128)(2,1)S(1)}, u32[]{:S(2)}, u32[]{:S(2)}) collective-permute-start(bf16[64,8,256]{2,1,0:T(8,128)(2,1)S(1)} %get-tuple-element.216.refs_0_), channel_id=1, source_target_pairs={{0,8},{4,12},{8,0},{12,4},{16,24},{20,28},{24,16},{28,20},{1,9},{5... | collective-permute-start | bytes 786440 | tf_op jit(solution)/shard_map/ppermute | solution.py:43
  86.5 11.0 %collective-permute-start.31 = (bf16[64,8,256]{2,1,0:T(8,128)(2,1)S(1)}, bf16[64,8,256]{2,1,0:T(8,128)(2,1)S(1)}, u32[]{:S(2)}, u32[]{:S(2)}) collective-permute-start(bf16[64,8,256]{2,1,0:T(8,128)(2,1)S(1)} %get-tuple-element.215), channel_id=1, source_target_pairs={{0,16},{4,20},{8,24},{12,28},{16,0},{20,4},{24,8},{28,12},{1,17},{... | collective-permute-start | bytes 786440 | tf_op jit(solution)/shard_map/ppermute | solution.py:43
  91.8 15.8 %collective-permute-start.33 = (bf16[64,8,256]{2,1,0:T(8,128)(2,1)S(1)}, bf16[64,8,256]{2,1,0:T(8,128)(2,1)S(1)}, u32[]{:S(2)}, u32[]{:S(2)}) collective-permute-start(bf16[64,8,256]{2,1,0:T(8,128)(2,1)S(1)} %get-tuple-element.241.refs_0_), channel_id=1, source_target_pairs={{0,8},{4,12},{8,0},{12,4},{16,24},{20,28},{24,16},{28,20},{1,9},{5... | collective-permute-start | bytes 786440 | tf_op jit(solution)/shard_map/ppermute | solution.py:43
  91.9 15.7 %collective-permute-start.34 = (bf16[64,8,256]{2,1,0:T(8,128)(2,1)S(1)}, bf16[64,8,256]{2,1,0:T(8,128)(2,1)S(1)}, u32[]{:S(2)}, u32[]{:S(2)}) collective-permute-start(bf16[64,8,256]{2,1,0:T(8,128)(2,1)S(1)} %get-tuple-element.241.refs_0_), channel_id=1, source_target_pairs={{0,4},{4,0},{8,12},{12,8},{16,20},{20,16},{24,28},{28,24},{1,5},{5... | collective-permute-start | bytes 786440 | tf_op jit(solution)/shard_map/ppermute | solution.py:43
  92.6 17.0 %collective-permute-start.32 = (bf16[64,8,256]{2,1,0:T(8,128)(2,1)S(1)}, bf16[64,8,256]{2,1,0:T(8,128)(2,1)S(1)}, u32[]{:S(2)}, u32[]{:S(2)}) collective-permute-start(bf16[64,8,256]{2,1,0:T(8,128)(2,1)S(1)} %get-tuple-element.220), channel_id=1, source_target_pairs={{0,16},{4,20},{8,24},{12,28},{16,0},{20,4},{24,8},{28,12},{1,17},{... | collective-permute-start | bytes 786440 | tf_op jit(solution)/shard_map/ppermute | solution.py:43
  95.5 18.1 %collective-permute-start.30 = (bf16[64,8,256]{2,1,0:T(8,128)(2,1)S(1)}, bf16[64,8,256]{2,1,0:T(8,128)(2,1)S(1)}, u32[]{:S(2)}, u32[]{:S(2)}) collective-permute-start(bf16[64,8,256]{2,1,0:T(8,128)(2,1)S(1)} %get-tuple-element.246.refs_0_), channel_id=1, source_target_pairs={{0,8},{4,12},{8,0},{12,4},{16,24},{20,28},{24,16},{28,20},{1,9},{5... | collective-permute-start | bytes 786440 | tf_op jit(solution)/shard_map/ppermute | solution.py:43
  107.9 14.5 %collective-permute-start.37 = (bf16[64,8,256]{2,1,0:T(8,128)(2,1)S(1)}, bf16[64,8,256]{2,1,0:T(8,128)(2,1)S(1)}, u32[]{:S(2)}, u32[]{:S(2)}) collective-permute-start(bf16[64,8,256]{2,1,0:T(8,128)(2,1)S(1)} %get-tuple-element.246.refs_0_), channel_id=1, source_target_pairs={{0,4},{4,0},{8,12},{12,8},{16,20},{20,16},{24,28},{28,24},{1,5},{5... | collective-permute-start | bytes 786440 | tf_op jit(solution)/shard_map/ppermute | solution.py:43
  113.6 13.2 %collective-permute-start.38 = (bf16[64,8,256]{2,1,0:T(8,128)(2,1)S(1)}, bf16[64,8,256]{2,1,0:T(8,128)(2,1)S(1)}, u32[]{:S(2)}, u32[]{:S(2)}) collective-permute-start(bf16[64,8,256]{2,1,0:T(8,128)(2,1)S(1)} %collective-permute-done.30.refs_1_), channel_id=1, source_target_pairs={{0,4},{4,0},{8,12},{12,8},{16,20},{20,16},{24,28},{28,24},{1,5},{5... | collective-permute-start | bytes 786440 | tf_op jit(solution)/shard_map/ppermute | solution.py:43
  118.0 18.3 %collective-permute-start.40 = (bf16[64,8,256]{2,1,0:T(8,128)(2,1)S(1)}, bf16[64,8,256]{2,1,0:T(8,128)(2,1)S(1)}, u32[]{:S(2)}, u32[]{:S(2)}) collective-permute-start(bf16[64,8,256]{2,1,0:T(8,128)(2,1)S(1)} %get-tuple-element.245), channel_id=1, source_target_pairs={{0,16},{4,20},{8,24},{12,28},{16,0},{20,4},{24,8},{28,12},{1,17},{... | collective-permute-start | bytes 786440 | tf_op jit(solution)/shard_map/ppermute | solution.py:43
  128.0 13.7 %collective-permute-start.41 = (bf16[64,8,256]{2,1,0:T(8,128)(2,1)S(1)}, bf16[64,8,256]{2,1,0:T(8,128)(2,1)S(1)}, u32[]{:S(2)}, u32[]{:S(2)}) collective-permute-start(bf16[64,8,256]{2,1,0:T(8,128)(2,1)S(1)} %get-tuple-element.250), channel_id=1, source_target_pairs={{0,16},{4,20},{8,24},{12,28},{16,0},{20,4},{24,8},{28,12},{1,17},{... | collective-permute-start | bytes 786440 | tf_op jit(solution)/shard_map/ppermute | solution.py:43
  (28 other events, 195.5 us)

commit v11 on v10

--- a/solution.py
+++ b/solution.py
@@ -17,16 +17,17 @@
 
 ORDER = (
     "As Al Am Bm",
-    "Af1 Af2 Ao1 Ao2",
-    "Aw Ak Az1 Bg1",
-    "Az2 Bg2 Ae Bo1",
-    "As Bo2 Bw Bz1",
-    "Ag1 Be Ag2 Ao1",
-    "Ao2 Bs Aw Az1",
-    "Ap Bg1 Ae Bf2",
-    "Bo1 Bo2 Bp Bw",
-    "Bz1 Ar Au Be",
-    "Br Bu",
+    "Af1 Af2 Ao1 Ak",
+    "Ao2 Aw Ae1 Bg1",
+    "Az2 Bg2 Ae2 Bo1",
+    "As1 As2 Bo2 Bw",
+    "Be1 Ag1 Bz2 Be2",
+    "Ag2 Ao1 Bs1 Ap",
+    "Ao2 Bs2 Aw Ae1",
+    "Bg1 Bf2 Bo1 Ae2",
+    "Bo2 Bp Bw Be1",
+    "Ar Au Be2 Br",
+    "Bu",
 )
 
 VMEM = pl.BlockSpec(memory_space=pltpu.VMEM)
@@ -100,19 +101,16 @@
     copy.wait()
 
 
-def next_sums_kernel(c, core_ref, mine_ref, other_ref, vec_ref, quality_ref, *refs):
-    emb_refs, sums_refs = refs[:PARTS], refs[PARTS:]
-    blocks, group, _ = sums_refs[0].shape
-    block_len = emb_refs[0].shape[0] // blocks
+def next_sums_kernel(c, core_ref, mine_ref, other_ref, vec_ref, quality_ref, emb_ref, sums_ref):
+    blocks, group, _ = sums_ref.shape
+    block_len = emb_ref.shape[0] // blocks
     rows = probe_rows(core_ref[0], c, group)
 
     def step(b, carry):
         docs = pl.ds(pl.multiple_of(b * block_len, block_len), block_len)
         quality = quality_ref[:, docs]
         value = add_f32(mine_ref[:, docs], other_ref[:, docs]) * quality - vec_ref[rows, docs]
-        scaled = (value * quality).astype(jnp.bfloat16)
-        for emb_ref, ref in zip(emb_refs, sums_refs):
-            ref[b] = block_sum(scaled, emb_ref[docs])
+        sums_ref[b] = block_sum((value * quality).astype(jnp.bfloat16), emb_ref[docs])
         return carry
 
     lax.fori_loop(0, blocks, step, 0, unroll=UNROLL)
@@ -176,26 +174,24 @@
     lookup(ids_ref, refs[:count], refs[count:], ids_ref.shape[0] // refs[count].shape[0])
 
 
-def expand_kernel(count, *refs):
-    *refs, out_ref = refs
-    values, embs = refs[:-PARTS], refs[-PARTS:]
-    blocks = values[0].shape[0]
-    block_len = embs[0].shape[0] // blocks
+def expand_kernel(*refs):
+    own_ref, *arrived_refs, emb_ref, out_ref = refs
+    held = arrived_refs.pop() if len(arrived_refs[-1].shape) == 2 else None
+    blocks = own_ref.shape[0]
+    block_len = emb_ref.shape[0] // blocks
 
     def step(b, carry):
         docs = pl.ds(pl.multiple_of(b * block_len, block_len), block_len)
-        products = None
-        for p, emb_ref in enumerate(embs):
-            here = values[p * count:(p + 1) * count]
-            total = here[0][b]
-            for ref in here[1:]:
-                total = total + ref[b].astype(jnp.float32)
-            product = lax.dot_general(
-                total.astype(jnp.bfloat16), emb_ref[docs], (((1,), (1,)), ((), ())),
-                preferred_element_type=jnp.float32,
-            )
-            products = product if products is None else products + product
-        out_ref[:, docs] = products.astype(jnp.bfloat16)
+        total = own_ref[b]
+        for ref in arrived_refs:
+            total = total + ref[b].astype(jnp.float32)
+        products = lax.dot_general(
+            total.astype(jnp.bfloat16), emb_ref[docs], (((1,), (1,)), ((), ())),
+            preferred_element_type=jnp.float32,
+        )
+        if held is not None:
+            products = products + held[:, docs]
+        out_ref[:, docs] = products.astype(out_ref.dtype)
         return carry
 
     lax.fori_loop(0, blocks, step, 0, unroll=UNROLL)
@@ -254,14 +250,14 @@
             compiler_params=params(),
         )(value)
 
-    def next_sums(c, pair):
+    def next_sums(c, p, pair):
         return pl.pallas_call(
             functools.partial(next_sums_kernel, c),
-            in_specs=[SMEM] + [VMEM] * (4 + PARTS),
-            out_specs=[VMEM] * PARTS,
-            out_shape=[shard_out] * PARTS,
-            compiler_params=params(),
-        )(core, *pair, probes, qrow, *embs)
+            in_specs=[SMEM] + [VMEM] * 5,
+            out_specs=VMEM,
+            out_shape=shard_out,
+            compiler_params=params(),
+        )(core, *pair, probes, qrow, embs[p])
 
     def fill(c, held, pairs, before=()):
         held = [] if held is None else [held]
@@ -296,15 +292,15 @@
             compiler_params=params(),
         )(ids, *tables)
 
-    def expand(parts):
-        values = [v for values in parts for v in values]
-        return pl.pallas_call(
-            functools.partial(expand_kernel, len(parts[0])),
-            in_specs=[VMEM] * (len(values) + PARTS),
+    def expand(p, own, arrived, held):
+        values = [own, *arrived] + ([held] if p else [])
+        return pl.pallas_call(
+            expand_kernel,
+            in_specs=[VMEM] * (len(values) + 1),
             out_specs=VMEM,
-            out_shape=jax.ShapeDtypeStruct((group, docs), jnp.bfloat16),
-            compiler_params=params(),
-        )(*values, *embs)
+            out_shape=jax.ShapeDtypeStruct((group, docs), jnp.bfloat16 if p + 1 == PARTS else jnp.float32),
+            compiler_params=params(),
+        )(*values, embs[p])
 
     def reduce(outgoing):
         arrived = []
@@ -331,6 +327,7 @@
     tables = [[None] * PARTS for _ in range(GROUPS)]
     own = [[None] * PARTS for _ in range(GROUPS)]
     arrived = [[None] * PARTS for _ in range(GROUPS)]
+    products = [None] * GROUPS
     pairs = [None] * GROUPS
     before = [None] * GROUPS
 
@@ -358,12 +355,15 @@
                     start_swaps(i, 0, sums[i])
                 late = [swap(v, "col", ncol, 1) for v in sums[GROUPS:]]
             else:
-                share(c)
-                before[c] = pairs[c]
-                sums = next_sums(c, pairs[c][0])
-                token.append(sums[0])
-                for i, value in enumerate(sums):
-                    start_swaps(c, i, value)
+                if p == 0:
+                    share(c)
+                    before[c] = pairs[c]
+                    pair = pairs[c][0]
+                else:
+                    pair = take(*pairs[c][0])
+                value = next_sums(c, p, pair)
+                token.append(value)
+                start_swaps(c, p, value)
         elif step == "m":
             (value,) = take(late[c])
             token.append(value)
@@ -397,15 +397,16 @@
             arrived[c][p] = take(*arrived[c][p])
             token.append(arrived[c][p][-1])
         elif step == "e":
-            flat = take(*own[c], *(v for values in arrived[c] for v in values))
-            later = [flat[PARTS + i * len(reduce_bits):PARTS + (i + 1) * len(reduce_bits)] for i in range(PARTS)]
-            value = expand([(flat[i], *later[i]) for i in range(PARTS)])
+            here, *later = take(own[c][p], *arrived[c][p])
+            value = expand(p, here, later, products[c])
+            products[c] = value
             token.append(value)
-            other = swap(value, "col", ncol, CORES)
-            for i in range(2, ncol.bit_length() - 1):
-                value = add_bf16(value, other)
-                other = swap(value, "col", ncol, 1 << i)
-            pairs[c] = ((value, other), (swap(value, "col", ncol, 1),))
+            if p + 1 == PARTS:
+                other = swap(value, "col", ncol, CORES)
+                for i in range(2, ncol.bit_length() - 1):
+                    value = add_bf16(value, other)
+                    other = swap(value, "col", ncol, 1 << i)
+                pairs[c] = ((value, other), (swap(value, "col", ncol, 1),))
         elif step == "p":
             theirs = take(*before[c][1])
             before[c] = (before[c][0], theirs)

time: 152 us -> 148 us (0.974)
  waiting for transfers between devices: 73.5 us -> 66.4 us
  Pallas kernels: 36.5 us -> 38.1 us
    ppermute x48, waiting for transfers between devices: 73.5 us -> 66.4 us  [swap(): return lax.ppermute(value, axis, [(i, i ^ mask) for i in range(size)])]
    pallas_call x4 -> x8, Pallas kernels: 9.59 us -> 10.5 us  [expand(): pl.pallas_call(expand_kernel, in_specs=[VMEM] * (len(values) + 1), out_sp...]
    pallas_call x2 -> x4, Pallas kernels: 2.65 us -> 3.12 us  [next_sums(): pl.pallas_call(functools.partial(next_sums_kernel, c), in_specs=[SMEM] +...]
  transfers between devices with their start and end apart: 48 -> 48, of which waited for: 22 -> 21; matrix products, arithmetic and copies ran while one was open for 0% -> 0% of each run, Pallas kernels for 22% -> 24%
where the time goes in v11:
time: 148 us; the launch traced here: 147 us
  waiting for transfers between devices  66.4 us (45%)
  starting transfers between devices  41.5 us (28%)
  Pallas kernels  38.1 us (26%)
    ppermute x48, waiting for transfers between devices, swap(): return lax.ppermute(value, axis, [(i, i ^ mask) for i in range(size)])  66.4 us
    ppermute x48, starting transfers between devices, swap(): return lax.ppermute(value, axis, [(i, i ^ mask) for i in range(size)])  41.5 us
    pallas_call x8, Pallas kernels, expand(): pl.pallas_call(expand_kernel, in_specs=[VMEM] * (len(values) + 1), out_sp...  10.5 us
    pallas_call x8, Pallas kernels, combine_far(): pl.pallas_call(table_kernel, in_specs=[SMEM] + [VMEM] * len(shards), out_...  10.1 us
    pallas_call x4, Pallas kernels, combine(): pl.pallas_call(lookup_kernel, in_specs=[SMEM] + [VMEM] * len(tables), out...  5.3 us
    pallas_call x4, Pallas kernels, fill(): pl.pallas_call(functools.partial(fill_kernel, c, bool(before)), in_specs=...  3.6 us
    pallas_call x1, Pallas kernels, first_sums(): pl.pallas_call(first_sums_kernel, in_specs=[SMEM] + [HBM] * 3, out_specs=...  3.19 us
    pallas_call x4, Pallas kernels, next_sums(): pl.pallas_call(functools.partial(next_sums_kernel, c), in_specs=[SMEM] +...  3.12 us
  transfers between devices with their start and end apart: 48, of which 21 were waited for; matrix products, arithmetic and copies ran while one was open for 0% of the time, Pallas kernels for 24%

profile of v11, /device:TPU:0, one launch (start us, length us, event | category | flops | bytes accessed | tf_op | source)
XLA Modules:
  0.0 147.5 jit_solution(11044393317820042315)
XLA Ops:
  1.1 3.7 %collective-permute-start = (s32[64,8]{0,1:T(8,128)}, s32[64,8]{0,1:T(8,128)S(1)}, u32[]{:S(2)}, u32[]{:S(2)}) collective-permute-start(s32[64,8]{0,1:T(8,128)} %param.7), channel_id=1, source_target_pairs={{0,16},{4,20},{8,24},{12,28},{16,0},{20,4},{24,8},{28,12},{1,17},{... | collective-permute-start | bytes 6152 | tf_op jit(solution)/shard_map/ppermute | solution.py:44
  4.8 3.2 %shard_map.59 = (bf16[64,8,256]{2,1,0:T(8,128)(2,1)S(1)}, bf16[64,8,256]{2,1,0:T(8,128)(2,1)S(1)}, bf16[64,8,256]{2,1,0:T(8,128)(2,1)S(1)}, bf16[64,8,256]{2,1,0:T(8,128)(2,1)S(1)}) custom-call(s32[1]{0:T(128)} %bitcast.core_ref, f32[32,8192]{1,0:T(8,128)} %vec_ref.17, f32[1,8192]{1,0:T(1,128)} %bitcast.2, bf16[8192,256]{1,0:T(8,128)(2,1)} %refs_2_.7), custom_call_target="tpu_custom_call" | custom-call | tf_op jit(solution)/shard_map/pallas_call | solution.py:229
  12.6 5.1 %collective-permute-done.3.refs_1_ = bf16[64,8,256]{2,1,0:T(8,128)(2,1)S(1)} collective-permute-done((bf16[64,8,256]{2,1,0:T(8,128)(2,1)S(1)}, bf16[64,8,256]{2,1,0:T(8,128)(2,1)S(1)}, u32[]{:S(2)}, u32[]{:S(2)}) %collective-permute-start.3) | collective-permute-done | bytes 262176 | tf_op jit(solution)/shard_map/ppermute | solution.py:44
  19.8 2.8 %collective-permute-done.8.refs_1_ = bf16[64,8,256]{2,1,0:T(8,128)(2,1)S(1)} collective-permute-done((bf16[64,8,256]{2,1,0:T(8,128)(2,1)S(1)}, bf16[64,8,256]{2,1,0:T(8,128)(2,1)S(1)}, u32[]{:S(2)}, u32[]{:S(2)}) %collective-permute-start.8) | collective-permute-done | bytes 262176 | tf_op jit(solution)/shard_map/ppermute | solution.py:44
  24.1 2.9 %collective-permute-done.7.refs_3_ = bf16[64,8,256]{2,1,0:T(8,128)(2,1)S(1)} collective-permute-done((bf16[64,8,256]{2,1,0:T(8,128)(2,1)S(1)}, bf16[64,8,256]{2,1,0:T(8,128)(2,1)S(1)}, u32[]{:S(2)}, u32[]{:S(2)}) %collective-permute-start.7) | collective-permute-done | bytes 262176 | tf_op jit(solution)/shard_map/ppermute | solution.py:44
  32.9 2.3 %shard_map.61.refs_3_.emb_ref = bf16[8192,256]{1,0:T(8,128)(2,1)S(1)} custom-call(bf16[8192,256]{1,0:T(8,128)(2,1)} %collective-permute-done.11.src_ref), custom_call_target="tpu_custom_call" | custom-call | tf_op jit(solution)/shard_map/pallas_call | solution.py:244
  35.7 2.5 %collective-permute-done.10.refs_3_ = bf16[64,8,256]{2,1,0:T(8,128)(2,1)S(1)} collective-permute-done((bf16[64,8,256]{2,1,0:T(8,128)(2,1)S(1)}, bf16[64,8,256]{2,1,0:T(8,128)(2,1)S(1)}, u32[]{:S(2)}, u32[]{:S(2)}) %collective-permute-start.10) | collective-permute-done | bytes 262176 | tf_op jit(solution)/shard_map/ppermute | solution.py:44
  45.8 2.5 %collective-permute-done.14.refs_1_ = bf16[64,8,256]{2,1,0:T(8,128)(2,1)S(1)} collective-permute-done((bf16[64,8,256]{2,1,0:T(8,128)(2,1)S(1)}, bf16[64,8,256]{2,1,0:T(8,128)(2,1)S(1)}, u32[]{:S(2)}, u32[]{:S(2)}) %collective-permute-start.14) | collective-permute-done | bytes 262176 | tf_op jit(solution)/shard_map/ppermute | solution.py:44
  48.3 2.2 %collective-permute-done.15.refs_1_ = bf16[64,8,256]{2,1,0:T(8,128)(2,1)S(1)} collective-permute-done((bf16[64,8,256]{2,1,0:T(8,128)(2,1)S(1)}, bf16[64,8,256]{2,1,0:T(8,128)(2,1)S(1)}, u32[]{:S(2)}, u32[]{:S(2)}) %collective-permute-start.15) | collective-permute-done | bytes 262176 | tf_op jit(solution)/shard_map/ppermute | solution.py:44
  53.1 2.4 %collective-permute-done.13.refs_3_ = bf16[64,8,256]{2,1,0:T(8,128)(2,1)S(1)} collective-permute-done((bf16[64,8,256]{2,1,0:T(8,128)(2,1)S(1)}, bf16[64,8,256]{2,1,0:T(8,128)(2,1)S(1)}, u32[]{:S(2)}, u32[]{:S(2)}) %collective-permute-start.13) | collective-permute-done | bytes 262176 | tf_op jit(solution)/shard_map/ppermute | solution.py:44
  58.7 3.5 %collective-permute-done.18.other_ref.refs_1_.refs_5_ = bf16[8,8192]{1,0:T(8,128)(2,1)S(1)} collective-permute-done((bf16[8,8192]{1,0:T(8,128)(2,1)S(1)}, bf16[8,8192]{1,0:T(8,128)(2,1)S(1)}, u32[]{:S(2)}, u32[]{:S(2)}) %collective-permute-start.18) | collective-permute-done | bytes 131104 | tf_op jit(solution)/shard_map/ppermute | solution.py:44
  63.0 3.7 %collective-permute-start.20 = (bf16[64,8,256]{2,1,0:T(8,128)(2,1)S(1)}, bf16[64,8,256]{2,1,0:T(8,128)(2,1)S(1)}, u32[]{:S(2)}, u32[]{:S(2)}) collective-permute-start(bf16[64,8,256]{2,1,0:T(8,128)(2,1)S(1)} %shard_map.67.refs_0_), channel_id=1, source_target_pairs={{0,8},{4,12},{8,0},{12,4},{16,24},{20,28},{24,16},{28,20},{1,9},{5... | collective-permute-start | bytes 786440 | tf_op jit(solution)/shard_map/ppermute | solution.py:44
  68.9 1.7 %collective-permute-start.19 = (bf16[64,8,256]{2,1,0:T(8,128)(2,1)S(1)}, bf16[64,8,256]{2,1,0:T(8,128)(2,1)S(1)}, u32[]{:S(2)}, u32[]{:S(2)}) collective-permute-start(bf16[64,8,256]{2,1,0:T(8,128)(2,1)S(1)} %get-tuple-element.193), channel_id=1, source_target_pairs={{0,16},{4,20},{8,24},{12,28},{16,0},{20,4},{24,8},{28,12},{1,17},{... | collective-permute-start | bytes 786440 | tf_op jit(solution)/shard_map/ppermute | solution.py:44
  76.1 3.1 %collective-permute-done.19.refs_1_ = bf16[64,8,256]{2,1,0:T(8,128)(2,1)S(1)} collective-permute-done((bf16[64,8,256]{2,1,0:T(8,128)(2,1)S(1)}, bf16[64,8,256]{2,1,0:T(8,128)(2,1)S(1)}, u32[]{:S(2)}, u32[]{:S(2)}) %collective-permute-start.19) | collective-permute-done | bytes 262176 | tf_op jit(solution)/shard_map/ppermute | solution.py:44
  80.5 1.8 %collective-permute-start.29 = (bf16[64,8,256]{2,1,0:T(8,128)(2,1)S(1)}, bf16[64,8,256]{2,1,0:T(8,128)(2,1)S(1)}, u32[]{:S(2)}, u32[]{:S(2)}) collective-permute-start(bf16[64,8,256]{2,1,0:T(8,128)(2,1)S(1)} %collective-permute-done.25.refs_1_), channel_id=1, source_target_pairs={{0,4},{4,0},{8,12},{12,8},{16,20},{20,16},{24,28},{28,24},{1,5},{5... | collective-permute-start | bytes 786440 | tf_op jit(solution)/shard_map/ppermute | solution.py:44
  85.7 1.7 %collective-permute-done.23.other_ref.refs_1_.refs_5_ = bf16[8,8192]{1,0:T(8,128)(2,1)S(1)} collective-permute-done((bf16[8,8192]{1,0:T(8,128)(2,1)S(1)}, bf16[8,8192]{1,0:T(8,128)(2,1)S(1)}, u32[]{:S(2)}, u32[]{:S(2)}) %collective-permute-start.23) | collective-permute-done | bytes 131104 | tf_op jit(solution)/shard_map/ppermute | solution.py:44
  94.8 5.5 %collective-permute-done.35.refs_1_ = bf16[64,8,256]{2,1,0:T(8,128)(2,1)S(1)} collective-permute-done((bf16[64,8,256]{2,1,0:T(8,128)(2,1)S(1)}, bf16[64,8,256]{2,1,0:T(8,128)(2,1)S(1)}, u32[]{:S(2)}, u32[]{:S(2)}) %collective-permute-start.35) | collective-permute-done | bytes 262176 | tf_op jit(solution)/shard_map/ppermute | solution.py:44
  103.8 3.0 %collective-permute-done.32.refs_1_ = bf16[64,8,256]{2,1,0:T(8,128)(2,1)S(1)} collective-permute-done((bf16[64,8,256]{2,1,0:T(8,128)(2,1)S(1)}, bf16[64,8,256]{2,1,0:T(8,128)(2,1)S(1)}, u32[]{:S(2)}, u32[]{:S(2)}) %collective-permute-start.32) | collective-permute-done | bytes 262176 | tf_op jit(solution)/shard_map/ppermute | solution.py:44
  106.8 4.0 %collective-permute-done.39.refs_3_ = bf16[64,8,256]{2,1,0:T(8,128)(2,1)S(1)} collective-permute-done((bf16[64,8,256]{2,1,0:T(8,128)(2,1)S(1)}, bf16[64,8,256]{2,1,0:T(8,128)(2,1)S(1)}, u32[]{:S(2)}, u32[]{:S(2)}) %collective-permute-start.39) | collective-permute-done | bytes 262176 | tf_op jit(solution)/shard_map/ppermute | solution.py:44
  112.3 10.5 %collective-permute-done.38.refs_1_ = bf16[64,8,256]{2,1,0:T(8,128)(2,1)S(1)} collective-permute-done((bf16[64,8,256]{2,1,0:T(8,128)(2,1)S(1)}, bf16[64,8,256]{2,1,0:T(8,128)(2,1)S(1)}, u32[]{:S(2)}, u32[]{:S(2)}) %collective-permute-start.38) | collective-permute-done | bytes 262176 | tf_op jit(solution)/shard_map/ppermute | solution.py:44
  126.7 2.5 %collective-permute-done.41.refs_1_ = bf16[8,8192]{1,0:T(8,128)(2,1)S(1)} collective-permute-done((bf16[8,8192]{1,0:T(8,128)(2,1)S(1)}, bf16[8,8192]{1,0:T(8,128)(2,1)S(1)}, u32[]{:S(2)}, u32[]{:S(2)}) %collective-permute-start.41) | collective-permute-done | bytes 131104 | tf_op jit(solution)/shard_map/ppermute | solution.py:44
  131.4 2.7 %collective-permute-done.42.refs_1_ = bf16[64,8,256]{2,1,0:T(8,128)(2,1)S(1)} collective-permute-done((bf16[64,8,256]{2,1,0:T(8,128)(2,1)S(1)}, bf16[64,8,256]{2,1,0:T(8,128)(2,1)S(1)}, u32[]{:S(2)}, u32[]{:S(2)}) %collective-permute-start.42) | collective-permute-done | bytes 262176 | tf_op jit(solution)/shard_map/ppermute | solution.py:44
  136.3 2.4 %collective-permute-done.40.refs_1_ = bf16[64,8,256]{2,1,0:T(8,128)(2,1)S(1)} collective-permute-done((bf16[64,8,256]{2,1,0:T(8,128)(2,1)S(1)}, bf16[64,8,256]{2,1,0:T(8,128)(2,1)S(1)}, u32[]{:S(2)}, u32[]{:S(2)}) %collective-permute-start.40) | collective-permute-done | bytes 262176 | tf_op jit(solution)/shard_map/ppermute | solution.py:44
  140.7 4.4 %collective-permute-done.45.refs_1_ = bf16[8,8192]{1,0:T(8,128)(2,1)S(1)} collective-permute-done((bf16[8,8192]{1,0:T(8,128)(2,1)S(1)}, bf16[8,8192]{1,0:T(8,128)(2,1)S(1)}, u32[]{:S(2)}, u32[]{:S(2)}) %collective-permute-start.45) | collective-permute-done | bytes 131104 | tf_op jit(solution)/shard_map/ppermute | solution.py:44
  (115 shorter events, 66.5 us)
Async XLA Ops:
  0.6 30.7 %collective-permute-start.11 = (bf16[8192,256]{1,0:T(8,128)(2,1)}, bf16[8192,256]{1,0:T(8,128)(2,1)}, u32[]{:S(2)}, u32[]{:S(2)}) collective-permute-start(bf16[8192,256]{1,0:T(8,128)(2,1)} %refs_2_.7), channel_id=1, source_target_pairs={{0,1},{1,0},{2,3},{3,2},{4,5},{5,4},{6,7},{7,6},{8,9},{9,8},{10,11... | collective-permute-start | bytes 12582920 | tf_op jit(solution)/shard_map/ppermute | solution.py:44
  10.2 13.9 %collective-permute-start.6 = (bf16[64,8,256]{2,1,0:T(8,128)(2,1)S(1)}, bf16[64,8,256]{2,1,0:T(8,128)(2,1)S(1)}, u32[]{:S(2)}, u32[]{:S(2)}) collective-permute-start(bf16[64,8,256]{2,1,0:T(8,128)(2,1)S(1)} %get-tuple-element.152.refs_0_), channel_id=1, source_target_pairs={{0,4},{4,0},{8,12},{12,8},{16,20},{20,16},{24,28},{28,24},{1,5},{5... | collective-permute-start | bytes 786440 | tf_op jit(solution)/shard_map/ppermute | solution.py:44
  12.1 10.5 %collective-permute-start.8 = (bf16[64,8,256]{2,1,0:T(8,128)(2,1)S(1)}, bf16[64,8,256]{2,1,0:T(8,128)(2,1)S(1)}, u32[]{:S(2)}, u32[]{:S(2)}) collective-permute-start(bf16[64,8,256]{2,1,0:T(8,128)(2,1)S(1)} %collective-permute-done.5.refs_0_), channel_id=1, source_target_pairs={{0,8},{4,12},{8,0},{12,4},{16,24},{20,28},{24,16},{28,20},{1,9},{5... | collective-permute-start | bytes 786440 | tf_op jit(solution)/shard_map/ppermute | solution.py:44
  19.3 16.0 %collective-permute-start.9 = (bf16[64,8,256]{2,1,0:T(8,128)(2,1)S(1)}, bf16[64,8,256]{2,1,0:T(8,128)(2,1)S(1)}, u32[]{:S(2)}, u32[]{:S(2)}) collective-permute-start(bf16[64,8,256]{2,1,0:T(8,128)(2,1)S(1)} %collective-permute-done.5.refs_0_), channel_id=1, source_target_pairs={{0,4},{4,0},{8,12},{12,8},{16,20},{20,16},{24,28},{28,24},{1,5},{5... | collective-permute-start | bytes 786440 | tf_op jit(solution)/shard_map/ppermute | solution.py:44
  22.6 15.6 %collective-permute-start.10 = (bf16[64,8,256]{2,1,0:T(8,128)(2,1)S(1)}, bf16[64,8,256]{2,1,0:T(8,128)(2,1)S(1)}, u32[]{:S(2)}, u32[]{:S(2)}) collective-permute-start(bf16[64,8,256]{2,1,0:T(8,128)(2,1)S(1)} %collective-permute-done.8.refs_1_), channel_id=1, source_target_pairs={{0,4},{4,0},{8,12},{12,8},{16,20},{20,16},{24,28},{28,24},{1,5},{5... | collective-permute-start | bytes 786440 | tf_op jit(solution)/shard_map/ppermute | solution.py:44
  28.2 12.7 %collective-permute-start.12 = (bf16[64,8,256]{2,1,0:T(8,128)(2,1)S(1)}, bf16[64,8,256]{2,1,0:T(8,128)(2,1)S(1)}, u32[]{:S(2)}, u32[]{:S(2)}) collective-permute-start(bf16[64,8,256]{2,1,0:T(8,128)(2,1)S(1)} %get-tuple-element.157), channel_id=1, source_target_pairs={{0,16},{4,20},{8,24},{12,28},{16,0},{20,4},{24,8},{28,12},{1,17},{... | collective-permute-start | bytes 786440 | tf_op jit(solution)/shard_map/ppermute | solution.py:44
  29.8 15.9 %collective-permute-start.1 = (bf16[64,8,256]{2,1,0:T(8,128)(2,1)S(1)}, bf16[64,8,256]{2,1,0:T(8,128)(2,1)S(1)}, u32[]{:S(2)}, u32[]{:S(2)}) collective-permute-start(bf16[64,8,256]{2,1,0:T(8,128)(2,1)S(1)} %get-tuple-element.177.refs_0_), channel_id=1, source_target_pairs={{0,8},{4,12},{8,0},{12,4},{16,24},{20,28},{24,16},{28,20},{1,9},{5... | collective-permute-start | bytes 786440 | tf_op jit(solution)/shard_map/ppermute | solution.py:44
  31.3 14.3 %collective-permute-start.2 = (bf16[64,8,256]{2,1,0:T(8,128)(2,1)S(1)}, bf16[64,8,256]{2,1,0:T(8,128)(2,1)S(1)}, u32[]{:S(2)}, u32[]{:S(2)}) collective-permute-start(bf16[64,8,256]{2,1,0:T(8,128)(2,1)S(1)} %get-tuple-element.177.refs_0_), channel_id=1, source_target_pairs={{0,4},{4,0},{8,12},{12,8},{16,20},{20,16},{24,28},{28,24},{1,5},{5... | collective-permute-start | bytes 786440 | tf_op jit(solution)/shard_map/ppermute | solution.py:44
  35.2 15.2 %collective-permute-start.15 = (bf16[64,8,256]{2,1,0:T(8,128)(2,1)S(1)}, bf16[64,8,256]{2,1,0:T(8,128)(2,1)S(1)}, u32[]{:S(2)}, u32[]{:S(2)}) collective-permute-start(bf16[64,8,256]{2,1,0:T(8,128)(2,1)S(1)} %collective-permute-done.4.refs_0_), channel_id=1, source_target_pairs={{0,8},{4,12},{8,0},{12,4},{16,24},{20,28},{24,16},{28,20},{1,9},{5... | collective-permute-start | bytes 786440 | tf_op jit(solution)/shard_map/ppermute | solution.py:44
  50.4 17.2 %collective-permute-start.17 = (bf16[64,8,256]{2,1,0:T(8,128)(2,1)S(1)}, bf16[64,8,256]{2,1,0:T(8,128)(2,1)S(1)}, u32[]{:S(2)}, u32[]{:S(2)}) collective-permute-start(bf16[64,8,256]{2,1,0:T(8,128)(2,1)S(1)} %collective-permute-done.15.refs_1_), channel_id=1, source_target_pairs={{0,4},{4,0},{8,12},{12,8},{16,20},{20,16},{24,28},{28,24},{1,5},{5... | collective-permute-start | bytes 786440 | tf_op jit(solution)/shard_map/ppermute | solution.py:44
  56.7 14.5 %collective-permute-start.22 = (bf16[64,8,256]{2,1,0:T(8,128)(2,1)S(1)}, bf16[64,8,256]{2,1,0:T(8,128)(2,1)S(1)}, u32[]{:S(2)}, u32[]{:S(2)}) collective-permute-start(bf16[64,8,256]{2,1,0:T(8,128)(2,1)S(1)} %get-tuple-element.183), channel_id=1, source_target_pairs={{0,16},{4,20},{8,24},{12,28},{16,0},{20,4},{24,8},{28,12},{1,17},{... | collective-permute-start | bytes 786440 | tf_op jit(solution)/shard_map/ppermute | solution.py:44
  63.0 12.7 %collective-permute-start.20 = (bf16[64,8,256]{2,1,0:T(8,128)(2,1)S(1)}, bf16[64,8,256]{2,1,0:T(8,128)(2,1)S(1)}, u32[]{:S(2)}, u32[]{:S(2)}) collective-permute-start(bf16[64,8,256]{2,1,0:T(8,128)(2,1)S(1)} %shard_map.67.refs_0_), channel_id=1, source_target_pairs={{0,8},{4,12},{8,0},{12,4},{16,24},{20,28},{24,16},{28,20},{1,9},{5... | collective-permute-start | bytes 786440 | tf_op jit(solution)/shard_map/ppermute | solution.py:44
  68.9 10.3 %collective-permute-start.19 = (bf16[64,8,256]{2,1,0:T(8,128)(2,1)S(1)}, bf16[64,8,256]{2,1,0:T(8,128)(2,1)S(1)}, u32[]{:S(2)}, u32[]{:S(2)}) collective-permute-start(bf16[64,8,256]{2,1,0:T(8,128)(2,1)S(1)} %get-tuple-element.193), channel_id=1, source_target_pairs={{0,16},{4,20},{8,24},{12,28},{16,0},{20,4},{24,8},{28,12},{1,17},{... | collective-permute-start | bytes 786440 | tf_op jit(solution)/shard_map/ppermute | solution.py:44
  80.5 10.2 %collective-permute-start.29 = (bf16[64,8,256]{2,1,0:T(8,128)(2,1)S(1)}, bf16[64,8,256]{2,1,0:T(8,128)(2,1)S(1)}, u32[]{:S(2)}, u32[]{:S(2)}) collective-permute-start(bf16[64,8,256]{2,1,0:T(8,128)(2,1)S(1)} %collective-permute-done.25.refs_1_), channel_id=1, source_target_pairs={{0,4},{4,0},{8,12},{12,8},{16,20},{20,16},{24,28},{28,24},{1,5},{5... | collective-permute-start | bytes 786440 | tf_op jit(solution)/shard_map/ppermute | solution.py:44
  85.6 14.6 %collective-permute-start.35 = (bf16[64,8,256]{2,1,0:T(8,128)(2,1)S(1)}, bf16[64,8,256]{2,1,0:T(8,128)(2,1)S(1)}, u32[]{:S(2)}, u32[]{:S(2)}) collective-permute-start(bf16[64,8,256]{2,1,0:T(8,128)(2,1)S(1)} %get-tuple-element.210), channel_id=1, source_target_pairs={{0,16},{4,20},{8,24},{12,28},{16,0},{20,4},{24,8},{28,12},{1,17},{... | collective-permute-start | bytes 786440 | tf_op jit(solution)/shard_map/ppermute | solution.py:44
  88.1 13.4 %collective-permute-start.33 = (bf16[64,8,256]{2,1,0:T(8,128)(2,1)S(1)}, bf16[64,8,256]{2,1,0:T(8,128)(2,1)S(1)}, u32[]{:S(2)}, u32[]{:S(2)}) collective-permute-start(bf16[64,8,256]{2,1,0:T(8,128)(2,1)S(1)} %shard_map.74.refs_0_), channel_id=1, source_target_pairs={{0,8},{4,12},{8,0},{12,4},{16,24},{20,28},{24,16},{28,20},{1,9},{5... | collective-permute-start | bytes 786440 | tf_op jit(solution)/shard_map/ppermute | solution.py:44
  88.6 13.0 %collective-permute-start.34 = (bf16[64,8,256]{2,1,0:T(8,128)(2,1)S(1)}, bf16[64,8,256]{2,1,0:T(8,128)(2,1)S(1)}, u32[]{:S(2)}, u32[]{:S(2)}) collective-permute-start(bf16[64,8,256]{2,1,0:T(8,128)(2,1)S(1)} %shard_map.74.refs_0_), channel_id=1, source_target_pairs={{0,4},{4,0},{8,12},{12,8},{16,20},{20,16},{24,28},{28,24},{1,5},{5... | collective-permute-start | bytes 786440 | tf_op jit(solution)/shard_map/ppermute | solution.py:44
  92.8 14.0 %collective-permute-start.32 = (bf16[64,8,256]{2,1,0:T(8,128)(2,1)S(1)}, bf16[64,8,256]{2,1,0:T(8,128)(2,1)S(1)}, u32[]{:S(2)}, u32[]{:S(2)}) collective-permute-start(bf16[64,8,256]{2,1,0:T(8,128)(2,1)S(1)} %shard_map.77.refs_0_), channel_id=1, source_target_pairs={{0,8},{4,12},{8,0},{12,4},{16,24},{20,28},{24,16},{28,20},{1,9},{5... | collective-permute-start | bytes 786440 | tf_op jit(solution)/shard_map/ppermute | solution.py:44
  103.2 19.6 %collective-permute-start.38 = (bf16[64,8,256]{2,1,0:T(8,128)(2,1)S(1)}, bf16[64,8,256]{2,1,0:T(8,128)(2,1)S(1)}, u32[]{:S(2)}, u32[]{:S(2)}) collective-permute-start(bf16[64,8,256]{2,1,0:T(8,128)(2,1)S(1)} %get-tuple-element.220), channel_id=1, source_target_pairs={{0,16},{4,20},{8,24},{12,28},{16,0},{20,4},{24,8},{28,12},{1,17},{... | collective-permute-start | bytes 786440 | tf_op jit(solution)/shard_map/ppermute | solution.py:44
  103.3 21.3 %collective-permute-start.36 = (bf16[64,8,256]{2,1,0:T(8,128)(2,1)S(1)}, bf16[64,8,256]{2,1,0:T(8,128)(2,1)S(1)}, u32[]{:S(2)}, u32[]{:S(2)}) collective-permute-start(bf16[64,8,256]{2,1,0:T(8,128)(2,1)S(1)} %shard_map.77.refs_0_), channel_id=1, source_target_pairs={{0,4},{4,0},{8,12},{12,8},{16,20},{20,16},{24,28},{28,24},{1,5},{5... | collective-permute-start | bytes 786440 | tf_op jit(solution)/shard_map/ppermute | solution.py:44
  106.8 17.8 %collective-permute-start.37 = (bf16[64,8,256]{2,1,0:T(8,128)(2,1)S(1)}, bf16[64,8,256]{2,1,0:T(8,128)(2,1)S(1)}, u32[]{:S(2)}, u32[]{:S(2)}) collective-permute-start(bf16[64,8,256]{2,1,0:T(8,128)(2,1)S(1)} %collective-permute-done.32.refs_1_), channel_id=1, source_target_pairs={{0,4},{4,0},{8,12},{12,8},{16,20},{20,16},{24,28},{28,24},{1,5},{5... | collective-permute-start | bytes 786440 | tf_op jit(solution)/shard_map/ppermute | solution.py:44
  106.8 19.4 %collective-permute-start.27 = (bf16[8,8192]{1,0:T(8,128)(2,1)S(1)}, bf16[8,8192]{1,0:T(8,128)(2,1)S(1)}, u32[]{:S(2)}, u32[]{:S(2)}) collective-permute-start(bf16[8,8192]{1,0:T(8,128)(2,1)S(1)} %shard_map.72.mine_ref.refs_0_.refs_4_), channel_id=1, source_target_pairs={{0,1},{1,0},{2,3},{3,2},{4,5},{5,4},{6,7},{7,6},{8,9},{9,8},{10,11... | collective-permute-start | bytes 393224 | tf_op jit(solution)/shard_map/ppermute | solution.py:44
  112.1 22.0 %collective-permute-start.42 = (bf16[64,8,256]{2,1,0:T(8,128)(2,1)S(1)}, bf16[64,8,256]{2,1,0:T(8,128)(2,1)S(1)}, u32[]{:S(2)}, u32[]{:S(2)}) collective-permute-start(bf16[64,8,256]{2,1,0:T(8,128)(2,1)S(1)} %get-tuple-element.238), channel_id=1, source_target_pairs={{0,16},{4,20},{8,24},{12,28},{16,0},{20,4},{24,8},{28,12},{1,17},{... | collective-permute-start | bytes 786440 | tf_op jit(solution)/shard_map/ppermute | solution.py:44
  126.0 12.7 %collective-permute-start.40 = (bf16[64,8,256]{2,1,0:T(8,128)(2,1)S(1)}, bf16[64,8,256]{2,1,0:T(8,128)(2,1)S(1)}, u32[]{:S(2)}, u32[]{:S(2)}) collective-permute-start(bf16[64,8,256]{2,1,0:T(8,128)(2,1)S(1)} %get-tuple-element.245), channel_id=1, source_target_pairs={{0,16},{4,20},{8,24},{12,28},{16,0},{20,4},{24,8},{28,12},{1,17},{... | collective-permute-start | bytes 786440 | tf_op jit(solution)/shard_map/ppermute | solution.py:44
  (28 other events, 200.5 us)

commit v12 on v11

--- a/solution.py
+++ b/solution.py
@@ -21,13 +21,12 @@
     "Ao2 Aw Ae1 Bg1",
     "Az2 Bg2 Ae2 Bo1",
     "As1 As2 Bo2 Bw",
-    "Be1 Ag1 Bz2 Be2",
-    "Ag2 Ao1 Bs1 Ap",
-    "Ao2 Bs2 Aw Ae1",
-    "Bg1 Bf2 Bo1 Ae2",
-    "Bo2 Bp Bw Be1",
-    "Ar Au Be2 Br",
-    "Bu",
+    "Be1 Af1 Be2 Ag2",
+    "Ao1 Bs1 Ap Bs2",
+    "Ao2 Aw Ae1 Bf1",
+    "Ae2 Bf2 Bo1 Bo2",
+    "Bw Ar Bp Be1",
+    "Au Be2 Br Bu",
 )
 
 VMEM = pl.BlockSpec(memory_space=pltpu.VMEM)

time: 148 us -> 146 us (0.986)
  waiting for transfers between devices: 66.4 us -> 57.3 us
  starting transfers between devices: 41.5 us -> 49 us
    ppermute x48, waiting for transfers between devices: 66.4 us -> 57.3 us  [swap(): return lax.ppermute(value, axis, [(i, i ^ mask) for i in range(size)])]
    ppermute x48, starting transfers between devices: 41.5 us -> 49 us  [swap(): return lax.ppermute(value, axis, [(i, i ^ mask) for i in range(size)])]
  transfers between devices with their start and end apart: 48 -> 48, of which waited for: 21 -> 19; matrix products, arithmetic and copies ran while one was open for 0% -> 0% of each run, Pallas kernels for 24% -> 25%
where the time goes in v12:
time: 146 us
  waiting for transfers between devices  57.3 us (39%)
  starting transfers between devices  49 us (34%)
  Pallas kernels  37.9 us (26%)
    ppermute x48, waiting for transfers between devices, swap(): return lax.ppermute(value, axis, [(i, i ^ mask) for i in range(size)])  57.3 us
    ppermute x48, starting transfers between devices, swap(): return lax.ppermute(value, axis, [(i, i ^ mask) for i in range(size)])  49 us
    pallas_call x8, Pallas kernels, expand(): pl.pallas_call(expand_kernel, in_specs=[VMEM] * (len(values) + 1), out_sp...  10.5 us
    pallas_call x8, Pallas kernels, combine_far(): pl.pallas_call(table_kernel, in_specs=[SMEM] + [VMEM] * len(shards), out_...  9.9 us
    pallas_call x4, Pallas kernels, combine(): pl.pallas_call(lookup_kernel, in_specs=[SMEM] + [VMEM] * len(tables), out...  5.3 us
    pallas_call x4, Pallas kernels, fill(): pl.pallas_call(functools.partial(fill_kernel, c, bool(before)), in_specs=...  3.6 us
    pallas_call x1, Pallas kernels, first_sums(): pl.pallas_call(first_sums_kernel, in_specs=[SMEM] + [HBM] * 3, out_specs=...  3.19 us
    pallas_call x4, Pallas kernels, next_sums(): pl.pallas_call(functools.partial(next_sums_kernel, c), in_specs=[SMEM] +...  3.12 us
  transfers between devices with their start and end apart: 48, of which 19 were waited for; matrix products, arithmetic and copies ran while one was open for 0% of the time, Pallas kernels for 25%

profile of v12, /device:TPU:0, one launch (start us, length us, event | category | flops | bytes accessed | tf_op | source)
XLA Modules:
  0.0 145.6 jit_solution(5044761793728197998)
XLA Ops:
  1.1 3.7 %collective-permute-start = (s32[64,8]{0,1:T(8,128)}, s32[64,8]{0,1:T(8,128)S(1)}, u32[]{:S(2)}, u32[]{:S(2)}) collective-permute-start(s32[64,8]{0,1:T(8,128)} %param.7), channel_id=1, source_target_pairs={{0,16},{4,20},{8,24},{12,28},{16,0},{20,4},{24,8},{28,12},{1,17},{... | collective-permute-start | bytes 6152 | tf_op jit(solution)/shard_map/ppermute | solution.py:43
  4.8 3.2 %shard_map.59 = (bf16[64,8,256]{2,1,0:T(8,128)(2,1)S(1)}, bf16[64,8,256]{2,1,0:T(8,128)(2,1)S(1)}, bf16[64,8,256]{2,1,0:T(8,128)(2,1)S(1)}, bf16[64,8,256]{2,1,0:T(8,128)(2,1)S(1)}) custom-call(s32[1]{0:T(128)} %bitcast.core_ref, f32[32,8192]{1,0:T(8,128)} %vec_ref.17, f32[1,8192]{1,0:T(1,128)} %bitcast.2, bf16[8192,256]{1,0:T(8,128)(2,1)} %refs_2_.7), custom_call_target="tpu_custom_call" | custom-call | tf_op jit(solution)/shard_map/pallas_call | solution.py:228
  12.6 5.1 %collective-permute-done.3.refs_1_ = bf16[64,8,256]{2,1,0:T(8,128)(2,1)S(1)} collective-permute-done((bf16[64,8,256]{2,1,0:T(8,128)(2,1)S(1)}, bf16[64,8,256]{2,1,0:T(8,128)(2,1)S(1)}, u32[]{:S(2)}, u32[]{:S(2)}) %collective-permute-start.3) | collective-permute-done | bytes 262176 | tf_op jit(solution)/shard_map/ppermute | solution.py:43
  19.8 2.8 %collective-permute-done.8.refs_1_ = bf16[64,8,256]{2,1,0:T(8,128)(2,1)S(1)} collective-permute-done((bf16[64,8,256]{2,1,0:T(8,128)(2,1)S(1)}, bf16[64,8,256]{2,1,0:T(8,128)(2,1)S(1)}, u32[]{:S(2)}, u32[]{:S(2)}) %collective-permute-start.8) | collective-permute-done | bytes 262176 | tf_op jit(solution)/shard_map/ppermute | solution.py:43
  24.1 2.9 %collective-permute-done.7.refs_3_ = bf16[64,8,256]{2,1,0:T(8,128)(2,1)S(1)} collective-permute-done((bf16[64,8,256]{2,1,0:T(8,128)(2,1)S(1)}, bf16[64,8,256]{2,1,0:T(8,128)(2,1)S(1)}, u32[]{:S(2)}, u32[]{:S(2)}) %collective-permute-start.7) | collective-permute-done | bytes 262176 | tf_op jit(solution)/shard_map/ppermute | solution.py:43
  32.9 2.3 %shard_map.61.refs_3_.emb_ref = bf16[8192,256]{1,0:T(8,128)(2,1)S(1)} custom-call(bf16[8192,256]{1,0:T(8,128)(2,1)} %collective-permute-done.11.src_ref), custom_call_target="tpu_custom_call" | custom-call | tf_op jit(solution)/shard_map/pallas_call | solution.py:243
  35.2 3.0 %collective-permute-done.10.refs_3_ = bf16[64,8,256]{2,1,0:T(8,128)(2,1)S(1)} collective-permute-done((bf16[64,8,256]{2,1,0:T(8,128)(2,1)S(1)}, bf16[64,8,256]{2,1,0:T(8,128)(2,1)S(1)}, u32[]{:S(2)}, u32[]{:S(2)}) %collective-permute-start.10) | collective-permute-done | bytes 262176 | tf_op jit(solution)/shard_map/ppermute | solution.py:43
  47.3 3.1 %collective-permute-done.14.refs_1_ = bf16[64,8,256]{2,1,0:T(8,128)(2,1)S(1)} collective-permute-done((bf16[64,8,256]{2,1,0:T(8,128)(2,1)S(1)}, bf16[64,8,256]{2,1,0:T(8,128)(2,1)S(1)}, u32[]{:S(2)}, u32[]{:S(2)}) %collective-permute-start.14) | collective-permute-done | bytes 262176 | tf_op jit(solution)/shard_map/ppermute | solution.py:43
  50.8 2.5 %collective-permute-start.17 = (bf16[64,8,256]{2,1,0:T(8,128)(2,1)S(1)}, bf16[64,8,256]{2,1,0:T(8,128)(2,1)S(1)}, u32[]{:S(2)}, u32[]{:S(2)}) collective-permute-start(bf16[64,8,256]{2,1,0:T(8,128)(2,1)S(1)} %collective-permute-done.15.refs_1_), channel_id=1, source_target_pairs={{0,4},{4,0},{8,12},{12,8},{16,20},{20,16},{24,28},{28,24},{1,5},{5... | collective-permute-start | bytes 786440 | tf_op jit(solution)/shard_map/ppermute | solution.py:43
  66.1 5.9 %collective-permute-done.21.refs_1_ = bf16[64,8,256]{2,1,0:T(8,128)(2,1)S(1)} collective-permute-done((bf16[64,8,256]{2,1,0:T(8,128)(2,1)S(1)}, bf16[64,8,256]{2,1,0:T(8,128)(2,1)S(1)}, u32[]{:S(2)}, u32[]{:S(2)}) %collective-permute-start.21) | collective-permute-done | bytes 262176 | tf_op jit(solution)/shard_map/ppermute | solution.py:43
  72.1 1.7 %collective-permute-start.23 = (bf16[64,8,256]{2,1,0:T(8,128)(2,1)S(1)}, bf16[64,8,256]{2,1,0:T(8,128)(2,1)S(1)}, u32[]{:S(2)}, u32[]{:S(2)}) collective-permute-start(bf16[64,8,256]{2,1,0:T(8,128)(2,1)S(1)} %shard_map.67.refs_0_), channel_id=1, source_target_pairs={{0,4},{4,0},{8,12},{12,8},{16,20},{20,16},{24,28},{28,24},{1,5},{5... | collective-permute-start | bytes 786440 | tf_op jit(solution)/shard_map/ppermute | solution.py:43
  79.1 1.8 %collective-permute-start.29 = (bf16[64,8,256]{2,1,0:T(8,128)(2,1)S(1)}, bf16[64,8,256]{2,1,0:T(8,128)(2,1)S(1)}, u32[]{:S(2)}, u32[]{:S(2)}) collective-permute-start(bf16[64,8,256]{2,1,0:T(8,128)(2,1)S(1)} %collective-permute-done.25.refs_1_), channel_id=1, source_target_pairs={{0,4},{4,0},{8,12},{12,8},{16,20},{20,16},{24,28},{28,24},{1,5},{5... | collective-permute-start | bytes 786440 | tf_op jit(solution)/shard_map/ppermute | solution.py:43
  82.1 2.0 %collective-permute-done.24.refs_3_ = bf16[64,8,256]{2,1,0:T(8,128)(2,1)S(1)} collective-permute-done((bf16[64,8,256]{2,1,0:T(8,128)(2,1)S(1)}, bf16[64,8,256]{2,1,0:T(8,128)(2,1)S(1)}, u32[]{:S(2)}, u32[]{:S(2)}) %collective-permute-start.24) | collective-permute-done | bytes 262176 | tf_op jit(solution)/shard_map/ppermute | solution.py:43
  86.6 2.4 %collective-permute-start.33 = (bf16[64,8,256]{2,1,0:T(8,128)(2,1)S(1)}, bf16[64,8,256]{2,1,0:T(8,128)(2,1)S(1)}, u32[]{:S(2)}, u32[]{:S(2)}) collective-permute-start(bf16[64,8,256]{2,1,0:T(8,128)(2,1)S(1)} %shard_map.74.refs_0_), channel_id=1, source_target_pairs={{0,8},{4,12},{8,0},{12,4},{16,24},{20,28},{24,16},{28,20},{1,9},{5... | collective-permute-start | bytes 786440 | tf_op jit(solution)/shard_map/ppermute | solution.py:43
  92.2 1.9 %collective-permute-start.38 = (bf16[64,8,256]{2,1,0:T(8,128)(2,1)S(1)}, bf16[64,8,256]{2,1,0:T(8,128)(2,1)S(1)}, u32[]{:S(2)}, u32[]{:S(2)}) collective-permute-start(bf16[64,8,256]{2,1,0:T(8,128)(2,1)S(1)} %shard_map.76.refs_0_), channel_id=1, source_target_pairs={{0,8},{4,12},{8,0},{12,4},{16,24},{20,28},{24,16},{28,20},{1,9},{5... | collective-permute-start | bytes 786440 | tf_op jit(solution)/shard_map/ppermute | solution.py:43
  94.2 1.7 %collective-permute-start.36 = (bf16[64,8,256]{2,1,0:T(8,128)(2,1)S(1)}, bf16[64,8,256]{2,1,0:T(8,128)(2,1)S(1)}, u32[]{:S(2)}, u32[]{:S(2)}) collective-permute-start(bf16[64,8,256]{2,1,0:T(8,128)(2,1)S(1)} %shard_map.74.refs_0_), channel_id=1, source_target_pairs={{0,4},{4,0},{8,12},{12,8},{16,20},{20,16},{24,28},{28,24},{1,5},{5... | collective-permute-start | bytes 786440 | tf_op jit(solution)/shard_map/ppermute | solution.py:43
  97.2 3.3 %collective-permute-done.34.refs_1_ = bf16[64,8,256]{2,1,0:T(8,128)(2,1)S(1)} collective-permute-done((bf16[64,8,256]{2,1,0:T(8,128)(2,1)S(1)}, bf16[64,8,256]{2,1,0:T(8,128)(2,1)S(1)}, u32[]{:S(2)}, u32[]{:S(2)}) %collective-permute-start.34) | collective-permute-done | bytes 262176 | tf_op jit(solution)/shard_map/ppermute | solution.py:43
  101.8 2.5 %collective-permute-start.37 = (bf16[64,8,256]{2,1,0:T(8,128)(2,1)S(1)}, bf16[64,8,256]{2,1,0:T(8,128)(2,1)S(1)}, u32[]{:S(2)}, u32[]{:S(2)}) collective-permute-start(bf16[64,8,256]{2,1,0:T(8,128)(2,1)S(1)} %collective-permute-done.33.refs_1_), channel_id=1, source_target_pairs={{0,4},{4,0},{8,12},{12,8},{16,20},{20,16},{24,28},{28,24},{1,5},{5... | collective-permute-start | bytes 786440 | tf_op jit(solution)/shard_map/ppermute | solution.py:43
  104.4 4.9 %collective-permute-done.32.refs_1_ = bf16[64,8,256]{2,1,0:T(8,128)(2,1)S(1)} collective-permute-done((bf16[64,8,256]{2,1,0:T(8,128)(2,1)S(1)}, bf16[64,8,256]{2,1,0:T(8,128)(2,1)S(1)}, u32[]{:S(2)}, u32[]{:S(2)}) %collective-permute-start.32) | collective-permute-done | bytes 262176 | tf_op jit(solution)/shard_map/ppermute | solution.py:43
  114.5 2.6 %collective-permute-done.39.refs_2_ = bf16[64,8,256]{2,1,0:T(8,128)(2,1)S(1)} collective-permute-done((bf16[64,8,256]{2,1,0:T(8,128)(2,1)S(1)}, bf16[64,8,256]{2,1,0:T(8,128)(2,1)S(1)}, u32[]{:S(2)}, u32[]{:S(2)}) %collective-permute-start.39) | collective-permute-done | bytes 262176 | tf_op jit(solution)/shard_map/ppermute | solution.py:43
  117.1 3.9 %collective-permute-done.40.refs_3_ = bf16[64,8,256]{2,1,0:T(8,128)(2,1)S(1)} collective-permute-done((bf16[64,8,256]{2,1,0:T(8,128)(2,1)S(1)}, bf16[64,8,256]{2,1,0:T(8,128)(2,1)S(1)}, u32[]{:S(2)}, u32[]{:S(2)}) %collective-permute-start.40) | collective-permute-done | bytes 262176 | tf_op jit(solution)/shard_map/ppermute | solution.py:43
  125.3 5.7 %collective-permute-done.44.refs_1_ = bf16[64,8,256]{2,1,0:T(8,128)(2,1)S(1)} collective-permute-done((bf16[64,8,256]{2,1,0:T(8,128)(2,1)S(1)}, bf16[64,8,256]{2,1,0:T(8,128)(2,1)S(1)}, u32[]{:S(2)}, u32[]{:S(2)}) %collective-permute-start.44) | collective-permute-done | bytes 262176 | tf_op jit(solution)/shard_map/ppermute | solution.py:43
  133.3 3.2 %collective-permute-done.41.refs_1_ = bf16[64,8,256]{2,1,0:T(8,128)(2,1)S(1)} collective-permute-done((bf16[64,8,256]{2,1,0:T(8,128)(2,1)S(1)}, bf16[64,8,256]{2,1,0:T(8,128)(2,1)S(1)}, u32[]{:S(2)}, u32[]{:S(2)}) %collective-permute-start.41) | collective-permute-done | bytes 262176 | tf_op jit(solution)/shard_map/ppermute | solution.py:43
  138.9 4.4 %collective-permute-done.45.refs_1_ = bf16[8,8192]{1,0:T(8,128)(2,1)S(1)} collective-permute-done((bf16[8,8192]{1,0:T(8,128)(2,1)S(1)}, bf16[8,8192]{1,0:T(8,128)(2,1)S(1)}, u32[]{:S(2)}, u32[]{:S(2)}) %collective-permute-start.45) | collective-permute-done | bytes 131104 | tf_op jit(solution)/shard_map/ppermute | solution.py:43
  (115 shorter events, 67.9 us)
Async XLA Ops:
  0.6 30.7 %collective-permute-start.11 = (bf16[8192,256]{1,0:T(8,128)(2,1)}, bf16[8192,256]{1,0:T(8,128)(2,1)}, u32[]{:S(2)}, u32[]{:S(2)}) collective-permute-start(bf16[8192,256]{1,0:T(8,128)(2,1)} %refs_2_.7), channel_id=1, source_target_pairs={{0,1},{1,0},{2,3},{3,2},{4,5},{5,4},{6,7},{7,6},{8,9},{9,8},{10,11... | collective-permute-start | bytes 12582920 | tf_op jit(solution)/shard_map/ppermute | solution.py:43
  10.2 13.9 %collective-permute-start.6 = (bf16[64,8,256]{2,1,0:T(8,128)(2,1)S(1)}, bf16[64,8,256]{2,1,0:T(8,128)(2,1)S(1)}, u32[]{:S(2)}, u32[]{:S(2)}) collective-permute-start(bf16[64,8,256]{2,1,0:T(8,128)(2,1)S(1)} %get-tuple-element.149.refs_0_), channel_id=1, source_target_pairs={{0,4},{4,0},{8,12},{12,8},{16,20},{20,16},{24,28},{28,24},{1,5},{5... | collective-permute-start | bytes 786440 | tf_op jit(solution)/shard_map/ppermute | solution.py:43
  19.3 16.0 %collective-permute-start.9 = (bf16[64,8,256]{2,1,0:T(8,128)(2,1)S(1)}, bf16[64,8,256]{2,1,0:T(8,128)(2,1)S(1)}, u32[]{:S(2)}, u32[]{:S(2)}) collective-permute-start(bf16[64,8,256]{2,1,0:T(8,128)(2,1)S(1)} %collective-permute-done.5.refs_0_), channel_id=1, source_target_pairs={{0,4},{4,0},{8,12},{12,8},{16,20},{20,16},{24,28},{28,24},{1,5},{5... | collective-permute-start | bytes 786440 | tf_op jit(solution)/shard_map/ppermute | solution.py:43
  22.6 15.6 %collective-permute-start.10 = (bf16[64,8,256]{2,1,0:T(8,128)(2,1)S(1)}, bf16[64,8,256]{2,1,0:T(8,128)(2,1)S(1)}, u32[]{:S(2)}, u32[]{:S(2)}) collective-permute-start(bf16[64,8,256]{2,1,0:T(8,128)(2,1)S(1)} %collective-permute-done.8.refs_1_), channel_id=1, source_target_pairs={{0,4},{4,0},{8,12},{12,8},{16,20},{20,16},{24,28},{28,24},{1,5},{5... | collective-permute-start | bytes 786440 | tf_op jit(solution)/shard_map/ppermute | solution.py:43
  28.2 14.3 %collective-permute-start.12 = (bf16[64,8,256]{2,1,0:T(8,128)(2,1)S(1)}, bf16[64,8,256]{2,1,0:T(8,128)(2,1)S(1)}, u32[]{:S(2)}, u32[]{:S(2)}) collective-permute-start(bf16[64,8,256]{2,1,0:T(8,128)(2,1)S(1)} %get-tuple-element.154), channel_id=1, source_target_pairs={{0,16},{4,20},{8,24},{12,28},{16,0},{20,4},{24,8},{28,12},{1,17},{... | collective-permute-start | bytes 786440 | tf_op jit(solution)/shard_map/ppermute | solution.py:43
  29.8 17.0 %collective-permute-start.1 = (bf16[64,8,256]{2,1,0:T(8,128)(2,1)S(1)}, bf16[64,8,256]{2,1,0:T(8,128)(2,1)S(1)}, u32[]{:S(2)}, u32[]{:S(2)}) collective-permute-start(bf16[64,8,256]{2,1,0:T(8,128)(2,1)S(1)} %get-tuple-element.174.refs_0_), channel_id=1, source_target_pairs={{0,8},{4,12},{8,0},{12,4},{16,24},{20,28},{24,16},{28,20},{1,9},{5... | collective-permute-start | bytes 786440 | tf_op jit(solution)/shard_map/ppermute | solution.py:43
  31.3 15.4 %collective-permute-start.2 = (bf16[64,8,256]{2,1,0:T(8,128)(2,1)S(1)}, bf16[64,8,256]{2,1,0:T(8,128)(2,1)S(1)}, u32[]{:S(2)}, u32[]{:S(2)}) collective-permute-start(bf16[64,8,256]{2,1,0:T(8,128)(2,1)S(1)} %get-tuple-element.174.refs_0_), channel_id=1, source_target_pairs={{0,4},{4,0},{8,12},{12,8},{16,20},{20,16},{24,28},{28,24},{1,5},{5... | collective-permute-start | bytes 786440 | tf_op jit(solution)/shard_map/ppermute | solution.py:43
  39.5 11.0 %collective-permute-start.14 = (bf16[64,8,256]{2,1,0:T(8,128)(2,1)S(1)}, bf16[64,8,256]{2,1,0:T(8,128)(2,1)S(1)}, u32[]{:S(2)}, u32[]{:S(2)}) collective-permute-start(bf16[64,8,256]{2,1,0:T(8,128)(2,1)S(1)} %get-tuple-element.161), channel_id=1, source_target_pairs={{0,16},{4,20},{8,24},{12,28},{16,0},{20,4},{24,8},{28,12},{1,17},{... | collective-permute-start | bytes 786440 | tf_op jit(solution)/shard_map/ppermute | solution.py:43
  50.8 10.9 %collective-permute-start.17 = (bf16[64,8,256]{2,1,0:T(8,128)(2,1)S(1)}, bf16[64,8,256]{2,1,0:T(8,128)(2,1)S(1)}, u32[]{:S(2)}, u32[]{:S(2)}) collective-permute-start(bf16[64,8,256]{2,1,0:T(8,128)(2,1)S(1)} %collective-permute-done.15.refs_1_), channel_id=1, source_target_pairs={{0,4},{4,0},{8,12},{12,8},{16,20},{20,16},{24,28},{28,24},{1,5},{5... | collective-permute-start | bytes 786440 | tf_op jit(solution)/shard_map/ppermute | solution.py:43
  57.4 14.6 %collective-permute-start.21 = (bf16[64,8,256]{2,1,0:T(8,128)(2,1)S(1)}, bf16[64,8,256]{2,1,0:T(8,128)(2,1)S(1)}, u32[]{:S(2)}, u32[]{:S(2)}) collective-permute-start(bf16[64,8,256]{2,1,0:T(8,128)(2,1)S(1)} %get-tuple-element.180), channel_id=1, source_target_pairs={{0,16},{4,20},{8,24},{12,28},{16,0},{20,4},{24,8},{28,12},{1,17},{... | collective-permute-start | bytes 786440 | tf_op jit(solution)/shard_map/ppermute | solution.py:43
  60.4 16.0 %collective-permute-start.20 = (bf16[64,8,256]{2,1,0:T(8,128)(2,1)S(1)}, bf16[64,8,256]{2,1,0:T(8,128)(2,1)S(1)}, u32[]{:S(2)}, u32[]{:S(2)}) collective-permute-start(bf16[64,8,256]{2,1,0:T(8,128)(2,1)S(1)} %shard_map.67.refs_0_), channel_id=1, source_target_pairs={{0,8},{4,12},{8,0},{12,4},{16,24},{20,28},{24,16},{28,20},{1,9},{5... | collective-permute-start | bytes 786440 | tf_op jit(solution)/shard_map/ppermute | solution.py:43
  63.0 14.7 %collective-permute-start.19 = (bf16[64,8,256]{2,1,0:T(8,128)(2,1)S(1)}, bf16[64,8,256]{2,1,0:T(8,128)(2,1)S(1)}, u32[]{:S(2)}, u32[]{:S(2)}) collective-permute-start(bf16[64,8,256]{2,1,0:T(8,128)(2,1)S(1)} %get-tuple-element.190), channel_id=1, source_target_pairs={{0,16},{4,20},{8,24},{12,28},{16,0},{20,4},{24,8},{28,12},{1,17},{... | collective-permute-start | bytes 786440 | tf_op jit(solution)/shard_map/ppermute | solution.py:43
  64.2 14.9 %collective-permute-start.25 = (bf16[64,8,256]{2,1,0:T(8,128)(2,1)S(1)}, bf16[64,8,256]{2,1,0:T(8,128)(2,1)S(1)}, u32[]{:S(2)}, u32[]{:S(2)}) collective-permute-start(bf16[64,8,256]{2,1,0:T(8,128)(2,1)S(1)} %shard_map.68.refs_0_), channel_id=1, source_target_pairs={{0,8},{4,12},{8,0},{12,4},{16,24},{20,28},{24,16},{28,20},{1,9},{5... | collective-permute-start | bytes 786440 | tf_op jit(solution)/shard_map/ppermute | solution.py:43
  65.7 13.4 %collective-permute-start.26 = (bf16[64,8,256]{2,1,0:T(8,128)(2,1)S(1)}, bf16[64,8,256]{2,1,0:T(8,128)(2,1)S(1)}, u32[]{:S(2)}, u32[]{:S(2)}) collective-permute-start(bf16[64,8,256]{2,1,0:T(8,128)(2,1)S(1)} %shard_map.68.refs_0_), channel_id=1, source_target_pairs={{0,4},{4,0},{8,12},{12,8},{16,20},{20,16},{24,28},{28,24},{1,5},{5... | collective-permute-start | bytes 786440 | tf_op jit(solution)/shard_map/ppermute | solution.py:43
  79.1 11.6 %collective-permute-start.29 = (bf16[64,8,256]{2,1,0:T(8,128)(2,1)S(1)}, bf16[64,8,256]{2,1,0:T(8,128)(2,1)S(1)}, u32[]{:S(2)}, u32[]{:S(2)}) collective-permute-start(bf16[64,8,256]{2,1,0:T(8,128)(2,1)S(1)} %collective-permute-done.25.refs_1_), channel_id=1, source_target_pairs={{0,4},{4,0},{8,12},{12,8},{16,20},{20,16},{24,28},{28,24},{1,5},{5... | collective-permute-start | bytes 786440 | tf_op jit(solution)/shard_map/ppermute | solution.py:43
  85.3 15.2 %collective-permute-start.34 = (bf16[64,8,256]{2,1,0:T(8,128)(2,1)S(1)}, bf16[64,8,256]{2,1,0:T(8,128)(2,1)S(1)}, u32[]{:S(2)}, u32[]{:S(2)}) collective-permute-start(bf16[64,8,256]{2,1,0:T(8,128)(2,1)S(1)} %get-tuple-element.205), channel_id=1, source_target_pairs={{0,16},{4,20},{8,24},{12,28},{16,0},{20,4},{24,8},{28,12},{1,17},{... | collective-permute-start | bytes 786440 | tf_op jit(solution)/shard_map/ppermute | solution.py:43
  86.6 15.2 %collective-permute-start.33 = (bf16[64,8,256]{2,1,0:T(8,128)(2,1)S(1)}, bf16[64,8,256]{2,1,0:T(8,128)(2,1)S(1)}, u32[]{:S(2)}, u32[]{:S(2)}) collective-permute-start(bf16[64,8,256]{2,1,0:T(8,128)(2,1)S(1)} %shard_map.74.refs_0_), channel_id=1, source_target_pairs={{0,8},{4,12},{8,0},{12,4},{16,24},{20,28},{24,16},{28,20},{1,9},{5... | collective-permute-start | bytes 786440 | tf_op jit(solution)/shard_map/ppermute | solution.py:43
  91.9 17.3 %collective-permute-start.32 = (bf16[64,8,256]{2,1,0:T(8,128)(2,1)S(1)}, bf16[64,8,256]{2,1,0:T(8,128)(2,1)S(1)}, u32[]{:S(2)}, u32[]{:S(2)}) collective-permute-start(bf16[64,8,256]{2,1,0:T(8,128)(2,1)S(1)} %get-tuple-element.219), channel_id=1, source_target_pairs={{0,16},{4,20},{8,24},{12,28},{16,0},{20,4},{24,8},{28,12},{1,17},{... | collective-permute-start | bytes 786440 | tf_op jit(solution)/shard_map/ppermute | solution.py:43
  92.2 18.3 %collective-permute-start.38 = (bf16[64,8,256]{2,1,0:T(8,128)(2,1)S(1)}, bf16[64,8,256]{2,1,0:T(8,128)(2,1)S(1)}, u32[]{:S(2)}, u32[]{:S(2)}) collective-permute-start(bf16[64,8,256]{2,1,0:T(8,128)(2,1)S(1)} %shard_map.76.refs_0_), channel_id=1, source_target_pairs={{0,8},{4,12},{8,0},{12,4},{16,24},{20,28},{24,16},{28,20},{1,9},{5... | collective-permute-start | bytes 786440 | tf_op jit(solution)/shard_map/ppermute | solution.py:43
  94.2 17.5 %collective-permute-start.36 = (bf16[64,8,256]{2,1,0:T(8,128)(2,1)S(1)}, bf16[64,8,256]{2,1,0:T(8,128)(2,1)S(1)}, u32[]{:S(2)}, u32[]{:S(2)}) collective-permute-start(bf16[64,8,256]{2,1,0:T(8,128)(2,1)S(1)} %shard_map.74.refs_0_), channel_id=1, source_target_pairs={{0,4},{4,0},{8,12},{12,8},{16,20},{20,16},{24,28},{28,24},{1,5},{5... | collective-permute-start | bytes 786440 | tf_op jit(solution)/shard_map/ppermute | solution.py:43
  104.3 12.8 %collective-permute-start.39 = (bf16[64,8,256]{2,1,0:T(8,128)(2,1)S(1)}, bf16[64,8,256]{2,1,0:T(8,128)(2,1)S(1)}, u32[]{:S(2)}, u32[]{:S(2)}) collective-permute-start(bf16[64,8,256]{2,1,0:T(8,128)(2,1)S(1)} %shard_map.76.refs_0_), channel_id=1, source_target_pairs={{0,4},{4,0},{8,12},{12,8},{16,20},{20,16},{24,28},{28,24},{1,5},{5... | collective-permute-start | bytes 786440 | tf_op jit(solution)/shard_map/ppermute | solution.py:43
  110.5 10.5 %collective-permute-start.40 = (bf16[64,8,256]{2,1,0:T(8,128)(2,1)S(1)}, bf16[64,8,256]{2,1,0:T(8,128)(2,1)S(1)}, u32[]{:S(2)}, u32[]{:S(2)}) collective-permute-start(bf16[64,8,256]{2,1,0:T(8,128)(2,1)S(1)} %collective-permute-done.38.refs_1_), channel_id=1, source_target_pairs={{0,4},{4,0},{8,12},{12,8},{16,20},{20,16},{24,28},{28,24},{1,5},{5... | collective-permute-start | bytes 786440 | tf_op jit(solution)/shard_map/ppermute | solution.py:43
  113.0 18.0 %collective-permute-start.44 = (bf16[64,8,256]{2,1,0:T(8,128)(2,1)S(1)}, bf16[64,8,256]{2,1,0:T(8,128)(2,1)S(1)}, u32[]{:S(2)}, u32[]{:S(2)}) collective-permute-start(bf16[64,8,256]{2,1,0:T(8,128)(2,1)S(1)} %get-tuple-element.235), channel_id=1, source_target_pairs={{0,16},{4,20},{8,24},{12,28},{16,0},{20,4},{24,8},{28,12},{1,17},{... | collective-permute-start | bytes 786440 | tf_op jit(solution)/shard_map/ppermute | solution.py:43
  122.3 14.2 %collective-permute-start.41 = (bf16[64,8,256]{2,1,0:T(8,128)(2,1)S(1)}, bf16[64,8,256]{2,1,0:T(8,128)(2,1)S(1)}, u32[]{:S(2)}, u32[]{:S(2)}) collective-permute-start(bf16[64,8,256]{2,1,0:T(8,128)(2,1)S(1)} %get-tuple-element.241), channel_id=1, source_target_pairs={{0,16},{4,20},{8,24},{12,28},{16,0},{20,4},{24,8},{28,12},{1,17},{... | collective-permute-start | bytes 786440 | tf_op jit(solution)/shard_map/ppermute | solution.py:43
  (28 other events, 206.0 us)

commit v13 on v12

--- a/solution.py
+++ b/solution.py
@@ -10,14 +10,14 @@
 CORES = 2
 GROUPS = 2
 PARTS = CORES
-TILE_BLOCKS = 8
+TILE_DOCS = 1024
 UNROLL = 32
 VMEM_LIMIT = 8 * 1024 * 1024
 SIDE, NEXT = 1, 2
 
 ORDER = (
-    "As Al Am Bm",
-    "Af1 Af2 Ao1 Ak",
+    "As Am Bm Af1",
+    "Al Af2 Ao1 Ak",
     "Ao2 Aw Ae1 Bg1",
     "Az2 Bg2 Ae2 Bo1",
     "As1 As2 Bo2 Bw",
@@ -60,8 +60,9 @@
 
 
 def first_sums_kernel(core_ref, vec_ref, quality_ref, emb_ref, *refs):
-    *sums_refs, vec, quality, emb, sems = refs
-    tiles, tile_docs = emb.shape[:2]
+    *sums_refs, emb, vec, quality, sems = refs
+    tiles = emb_ref.shape[0] // TILE_DOCS
+    tile_docs = TILE_DOCS
     blocks, group, _ = sums_refs[0].shape
     block_len = tiles * tile_docs // blocks
     core = core_ref[0]
@@ -72,7 +73,7 @@
 
     def tile_copy(j):
         docs = pl.ds(pl.multiple_of(j * tile_docs, tile_docs), tile_docs)
-        return pltpu.make_async_copy(emb_ref.at[docs], emb.at[j], sems.at[j])
+        return pltpu.make_async_copy(emb_ref.at[docs], emb.at[docs], sems.at[j])
 
     for copy in here:
         copy.start()
@@ -86,7 +87,7 @@
         for b in range(blocks // tiles):
             docs = pl.ds(pl.multiple_of(j * tile_docs + b * block_len, block_len), block_len)
             scaled = (vec[:, docs] * quality[:, docs]).astype(jnp.bfloat16)
-            sums = block_sum(scaled, emb[j, b * block_len:(b + 1) * block_len])
+            sums = block_sum(scaled, emb[docs])
             for i, ref in enumerate(sums_refs):
                 ref[j * (blocks // tiles) + b] = sums[i * group:(i + 1) * group]
         return carry
@@ -204,7 +205,7 @@
     nprobe = probes.shape[0]
     group = nprobe // (CORES * GROUPS)
     core = (lax.axis_index("col") % CORES).astype(jnp.int32).reshape(1)
-    tiles = blk_count // TILE_BLOCKS
+    tiles = docs // TILE_DOCS
     reduce_bits = [1 << i for i in reversed(range(nrow.bit_length() - 1)) if 1 << i not in (SIDE, NEXT)]
     dests = [0]
     for m in reversed(reduce_bits):
@@ -228,12 +229,11 @@
         return pl.pallas_call(
             first_sums_kernel,
             in_specs=[SMEM] + [HBM] * 3,
-            out_specs=[VMEM] * (CORES * GROUPS),
-            out_shape=[shard_out] * (CORES * GROUPS),
+            out_specs=[VMEM] * (CORES * GROUPS + 1),
+            out_shape=[shard_out] * (CORES * GROUPS) + [jax.ShapeDtypeStruct((docs, width), jnp.bfloat16)],
             scratch_shapes=[
                 pltpu.VMEM((nprobe, docs), jnp.float32),
                 pltpu.VMEM((1, docs), jnp.float32),
-                pltpu.VMEM((tiles, docs // tiles, width), jnp.bfloat16),
                 pltpu.SemaphoreType.DMA((tiles + 1 + CORES * GROUPS,)),
             ],
             compiler_params=params(),
@@ -321,7 +321,7 @@
 
     lists = {d: swap(neighbors, "row", nrow, d) if d else neighbors for d in dests}
     first = second = None
-    embs = [embeddings, swap(embeddings, "col", ncol, 1)]
+    embs = None
     gathered = [[None] * PARTS for _ in range(GROUPS)]
     tables = [[None] * PARTS for _ in range(GROUPS)]
     own = [[None] * PARTS for _ in range(GROUPS)]
@@ -347,8 +347,8 @@
             token.append(ids[0])
         elif step == "s":
             if pairs[c] is None:
-                *sums, tied = lax.optimization_barrier((*first_sums(), tuple(lists.values())))
-                lists = dict(zip(lists, tied))
+                *sums, emb = first_sums()
+                embs = [emb, swap(emb, "col", ncol, 1)]
                 token.append(sums[0])
                 for i in range(GROUPS):
                     start_swaps(i, 0, sums[i])

time: 146 us -> 151 us (1.034)
  waiting for transfers between devices: 57.3 us -> 39.5 us
  Pallas kernels: 37.9 us -> 52.9 us
  starting transfers between devices: 49 us -> 56.3 us
    ppermute x48, waiting for transfers between devices: 57.3 us -> 39.5 us  [swap(): return lax.ppermute(value, axis, [(i, i ^ mask) for i in range(size)])]
    pallas_call x8, Pallas kernels: 10.5 us -> 19.2 us  [expand(): pl.pallas_call(expand_kernel, in_specs=[VMEM] * (len(values) + 1), out_sp...]
    ppermute x48, starting transfers between devices: 49 us -> 56.3 us  [swap(): return lax.ppermute(value, axis, [(i, i ^ mask) for i in range(size)])]
    pallas_call x4, Pallas kernels: 3.12 us -> 7.51 us  [next_sums(): pl.pallas_call(functools.partial(next_sums_kernel, c), in_specs=[SMEM] +...]
    pallas_call x1, Pallas kernels: 3.19 us -> 4.97 us  [first_sums(): pl.pallas_call(first_sums_kernel, in_specs=[SMEM] + [HBM] * 3, out_specs=...]
  transfers between devices with their start and end apart: 48 -> 48, of which waited for: 19 -> 20; matrix products, arithmetic and copies ran while one was open for 0% -> 0% of each run, Pallas kernels for 25% -> 30%
where the time goes in v13:
time: 151 us; the launch traced here: 150 us
  starting transfers between devices  56.3 us (37%)
  Pallas kernels  52.9 us (35%)
  waiting for transfers between devices  39.5 us (26%)
    ppermute x48, starting transfers between devices, swap(): return lax.ppermute(value, axis, [(i, i ^ mask) for i in range(size)])  56.3 us
    ppermute x48, waiting for transfers between devices, swap(): return lax.ppermute(value, axis, [(i, i ^ mask) for i in range(size)])  39.5 us
    pallas_call x8, Pallas kernels, expand(): pl.pallas_call(expand_kernel, in_specs=[VMEM] * (len(values) + 1), out_sp...  19.2 us
    pallas_call x8, Pallas kernels, combine_far(): pl.pallas_call(table_kernel, in_specs=[SMEM] + [VMEM] * len(shards), out_...  10.1 us
    pallas_call x4, Pallas kernels, next_sums(): pl.pallas_call(functools.partial(next_sums_kernel, c), in_specs=[SMEM] +...  7.51 us
    pallas_call x4, Pallas kernels, combine(): pl.pallas_call(lookup_kernel, in_specs=[SMEM] + [VMEM] * len(tables), out...  5.3 us
    pallas_call x1, Pallas kernels, first_sums(): pl.pallas_call(first_sums_kernel, in_specs=[SMEM] + [HBM] * 3, out_specs=...  4.97 us
    pallas_call x4, Pallas kernels, fill(): pl.pallas_call(functools.partial(fill_kernel, c, bool(before)), in_specs=...  3.6 us
  transfers between devices with their start and end apart: 48, of which 20 were waited for; matrix products, arithmetic and copies ran while one was open for 0% of the time, Pallas kernels for 30%

profile of v13, /device:TPU:0, one launch (start us, length us, event | category | flops | bytes accessed | tf_op | source)
XLA Modules:
  0.0 150.2 jit_solution(8091004717532534184)
XLA Ops:
  0.7 5.0 %shard_map.59 = (bf16[64,8,256]{2,1,0:T(8,128)(2,1)S(1)}, bf16[64,8,256]{2,1,0:T(8,128)(2,1)S(1)}, bf16[64,8,256]{2,1,0:T(8,128)(2,1)S(1)}, bf16[64,8,256]{2,1,0:T(8,128)(2,1)S(1)}, bf16[8192,256]{1,0:T(8,128)(2,1)}) custom-call(s32[1]{0:T(128)} %bitcast.core_ref, f32[32,8192]{1,0:T(8,128)} %vec_ref.17, f32[1,8192]{1,0:T(1,128)} %bitcast.2, ...), custom_call_target="tpu_custom_call" | custom-call | tf_op jit(solution)/shard_map/pallas_call | solution.py:229
  6.7 2.7 %collective-permute-start.1 = (bf16[64,8,256]{2,1,0:T(8,128)(2,1)S(1)}, bf16[64,8,256]{2,1,0:T(8,128)(2,1)S(1)}, u32[]{:S(2)}, u32[]{:S(2)}) collective-permute-start(bf16[64,8,256]{2,1,0:T(8,128)(2,1)S(1)} %get-tuple-element.138.refs_0_), channel_id=1, source_target_pairs={{0,8},{4,12},{8,0},{12,4},{16,24},{20,28},{24,16},{28,20},{1,9},{5... | collective-permute-start | bytes 786440 | tf_op jit(solution)/shard_map/ppermute | solution.py:43
  12.1 3.2 %collective-permute-start.8 = (bf16[64,8,256]{2,1,0:T(8,128)(2,1)S(1)}, bf16[64,8,256]{2,1,0:T(8,128)(2,1)S(1)}, u32[]{:S(2)}, u32[]{:S(2)}) collective-permute-start(bf16[64,8,256]{2,1,0:T(8,128)(2,1)S(1)} %collective-permute-done.3.refs_0_), channel_id=1, source_target_pairs={{0,8},{4,12},{8,0},{12,4},{16,24},{20,28},{24,16},{28,20},{1,9},{5... | collective-permute-start | bytes 786440 | tf_op jit(solution)/shard_map/ppermute | solution.py:43
  17.9 2.6 %collective-permute-start = (s32[64,8]{0,1:T(8,128)S(1)}, s32[64,8]{0,1:T(8,128)S(1)}, u32[]{:S(2)}, u32[]{:S(2)}) collective-permute-start(s32[64,8]{0,1:T(8,128)S(1)} %copy-done.2), channel_id=1, source_target_pairs={{0,16},{4,20},{8,24},{12,28},{16,0},{20,4},{24,8},{28,12},{1,17},{... | collective-permute-start | bytes 6152 | tf_op jit(solution)/shard_map/ppermute | solution.py:43
  20.5 1.9 %collective-permute-done = s32[64,8]{0,1:T(8,128)S(1)} collective-permute-done((s32[64,8]{0,1:T(8,128)S(1)}, s32[64,8]{0,1:T(8,128)S(1)}, u32[]{:S(2)}, u32[]{:S(2)}) %collective-permute-start) | collective-permute-done | bytes 2080 | tf_op jit(solution)/shard_map/ppermute | solution.py:43
  26.1 2.7 %collective-permute-start.12 = (bf16[64,8,256]{2,1,0:T(8,128)(2,1)S(1)}, bf16[64,8,256]{2,1,0:T(8,128)(2,1)S(1)}, u32[]{:S(2)}, u32[]{:S(2)}) collective-permute-start(bf16[64,8,256]{2,1,0:T(8,128)(2,1)S(1)} %get-tuple-element.144), channel_id=1, source_target_pairs={{0,16},{4,20},{8,24},{12,28},{16,0},{20,4},{24,8},{28,12},{1,17},{... | collective-permute-start | bytes 786440 | tf_op jit(solution)/shard_map/ppermute | solution.py:43
  30.6 2.0 %collective-permute-start.5 = (bf16[64,8,256]{2,1,0:T(8,128)(2,1)S(1)}, bf16[64,8,256]{2,1,0:T(8,128)(2,1)S(1)}, u32[]{:S(2)}, u32[]{:S(2)}) collective-permute-start(bf16[64,8,256]{2,1,0:T(8,128)(2,1)S(1)} %get-tuple-element.164.refs_0_), channel_id=1, source_target_pairs={{0,4},{4,0},{8,12},{12,8},{16,20},{20,16},{24,28},{28,24},{1,5},{5... | collective-permute-start | bytes 786440 | tf_op jit(solution)/shard_map/ppermute | solution.py:43
  32.6 2.2 %shard_map.61.refs_3_.emb_ref = bf16[8192,256]{1,0:T(8,128)(2,1)S(1)} custom-call(bf16[8192,256]{1,0:T(8,128)(2,1)} %collective-permute-done.11.src_ref), custom_call_target="tpu_custom_call" | custom-call | tf_op jit(solution)/shard_map/pallas_call | solution.py:243
  34.8 2.5 %collective-permute-done.10.refs_3_ = bf16[64,8,256]{2,1,0:T(8,128)(2,1)S(1)} collective-permute-done((bf16[64,8,256]{2,1,0:T(8,128)(2,1)S(1)}, bf16[64,8,256]{2,1,0:T(8,128)(2,1)S(1)}, u32[]{:S(2)}, u32[]{:S(2)}) %collective-permute-start.10) | collective-permute-done | bytes 262176 | tf_op jit(solution)/shard_map/ppermute | solution.py:43
  38.5 2.7 %collective-permute-start.14 = (bf16[64,8,256]{2,1,0:T(8,128)(2,1)S(1)}, bf16[64,8,256]{2,1,0:T(8,128)(2,1)S(1)}, u32[]{:S(2)}, u32[]{:S(2)}) collective-permute-start(bf16[64,8,256]{2,1,0:T(8,128)(2,1)S(1)} %get-tuple-element.151), channel_id=1, source_target_pairs={{0,16},{4,20},{8,24},{12,28},{16,0},{20,4},{24,8},{28,12},{1,17},{... | collective-permute-start | bytes 786440 | tf_op jit(solution)/shard_map/ppermute | solution.py:43
  45.2 3.5 %shard_map.64.refs_2_ = f32[8,8192]{1,0:T(8,128)S(1)} custom-call(f32[64,8,256]{2,1,0:T(8,128)S(1)} %get-tuple-element.155.refs_0_, bf16[64,8,256]{2,1,0:T(8,128)(2,1)S(1)} %collective-permute-done.12.refs_1_, bf16[8192,256]{1,0:T(8,128)(2,1)} %get-tuple-element.143.refs_2_.emb_ref), custom_call_target="tpu_custom_call" | custom-call | tf_op jit(solution)/shard_map/pallas_call | solution.py:296
  55.2 2.4 %collective-permute-done.13.refs_3_ = bf16[64,8,256]{2,1,0:T(8,128)(2,1)S(1)} collective-permute-done((bf16[64,8,256]{2,1,0:T(8,128)(2,1)S(1)}, bf16[64,8,256]{2,1,0:T(8,128)(2,1)S(1)}, u32[]{:S(2)}, u32[]{:S(2)}) %collective-permute-start.13) | collective-permute-done | bytes 262176 | tf_op jit(solution)/shard_map/ppermute | solution.py:43
  60.2 3.0 %shard_map.67.refs_0_ = bf16[64,8,256]{2,1,0:T(8,128)(2,1)S(1)} custom-call(s32[1]{0:T(128)} %bitcast.core_ref, bf16[8,8192]{1,0:T(8,128)(2,1)S(1)} %shard_map.65.mine_ref.refs_0_.refs_4_, bf16[8,8192]{1,0:T(8,128)(2,1)S(1)} %collective-permute-done.18.other_ref.refs_1_.refs_5_, f32[32,8192]{1,0:T(8,128)S(1)} %copy-done, f32[1,8192]{1,0:T(1,128)S(1)} %bitcast.3, ...), custom_call_target="tpu_custom_call" | custom-call | tf_op jit(solution)/shard_map/pallas_call | solution.py:253
  65.6 2.5 %collective-permute-start.19 = (bf16[64,8,256]{2,1,0:T(8,128)(2,1)S(1)}, bf16[64,8,256]{2,1,0:T(8,128)(2,1)S(1)}, u32[]{:S(2)}, u32[]{:S(2)}) collective-permute-start(bf16[64,8,256]{2,1,0:T(8,128)(2,1)S(1)} %get-tuple-element.180), channel_id=1, source_target_pairs={{0,16},{4,20},{8,24},{12,28},{16,0},{20,4},{24,8},{28,12},{1,17},{... | collective-permute-start | bytes 786440 | tf_op jit(solution)/shard_map/ppermute | solution.py:43
  72.6 3.5 %shard_map.71.refs_2_ = f32[8,8192]{1,0:T(8,128)S(1)} custom-call(f32[64,8,256]{2,1,0:T(8,128)S(1)} %get-tuple-element.185.refs_0_, bf16[64,8,256]{2,1,0:T(8,128)(2,1)S(1)} %collective-permute-done.21.refs_1_, bf16[8192,256]{1,0:T(8,128)(2,1)} %get-tuple-element.143.refs_2_.emb_ref), custom_call_target="tpu_custom_call" | custom-call | tf_op jit(solution)/shard_map/pallas_call | solution.py:296
  76.1 2.1 %collective-permute-done.20.refs_1_ = bf16[64,8,256]{2,1,0:T(8,128)(2,1)S(1)} collective-permute-done((bf16[64,8,256]{2,1,0:T(8,128)(2,1)S(1)}, bf16[64,8,256]{2,1,0:T(8,128)(2,1)S(1)}, u32[]{:S(2)}, u32[]{:S(2)}) %collective-permute-start.20) | collective-permute-done | bytes 262176 | tf_op jit(solution)/shard_map/ppermute | solution.py:43
  88.7 3.0 %shard_map.74.refs_0_ = bf16[64,8,256]{2,1,0:T(8,128)(2,1)S(1)} custom-call(s32[1]{0:T(128)} %bitcast.core_ref, bf16[8,8192]{1,0:T(8,128)(2,1)S(1)} %shard_map.72.mine_ref.refs_0_.refs_4_, bf16[8,8192]{1,0:T(8,128)(2,1)S(1)} %collective-permute-done.22.other_ref.refs_1_.refs_5_, f32[32,8192]{1,0:T(8,128)S(1)} %copy-done, f32[1,8192]{1,0:T(1,128)S(1)} %bitcast.5, ...), custom_call_target="tpu_custom_call" | custom-call | tf_op jit(solution)/shard_map/pallas_call | solution.py:253
  96.1 3.0 %collective-permute-start.32 = (bf16[64,8,256]{2,1,0:T(8,128)(2,1)S(1)}, bf16[64,8,256]{2,1,0:T(8,128)(2,1)S(1)}, u32[]{:S(2)}, u32[]{:S(2)}) collective-permute-start(bf16[64,8,256]{2,1,0:T(8,128)(2,1)S(1)} %get-tuple-element.209), channel_id=1, source_target_pairs={{0,16},{4,20},{8,24},{12,28},{16,0},{20,4},{24,8},{28,12},{1,17},{... | collective-permute-start | bytes 786440 | tf_op jit(solution)/shard_map/ppermute | solution.py:43
  103.5 3.5 %shard_map.79.refs_2_ = f32[8,8192]{1,0:T(8,128)S(1)} custom-call(f32[64,8,256]{2,1,0:T(8,128)S(1)} %get-tuple-element.214.refs_0_, bf16[64,8,256]{2,1,0:T(8,128)(2,1)S(1)} %collective-permute-done.34.refs_1_, bf16[8192,256]{1,0:T(8,128)(2,1)} %get-tuple-element.143.refs_2_.emb_ref), custom_call_target="tpu_custom_call" | custom-call | tf_op jit(solution)/shard_map/pallas_call | solution.py:296
  109.1 3.4 %collective-permute-done.32.refs_1_ = bf16[64,8,256]{2,1,0:T(8,128)(2,1)S(1)} collective-permute-done((bf16[64,8,256]{2,1,0:T(8,128)(2,1)S(1)}, bf16[64,8,256]{2,1,0:T(8,128)(2,1)S(1)}, u32[]{:S(2)}, u32[]{:S(2)}) %collective-permute-start.32) | collective-permute-done | bytes 262176 | tf_op jit(solution)/shard_map/ppermute | solution.py:43
  120.9 3.8 %collective-permute-done.40.refs_3_ = bf16[64,8,256]{2,1,0:T(8,128)(2,1)S(1)} collective-permute-done((bf16[64,8,256]{2,1,0:T(8,128)(2,1)S(1)}, bf16[64,8,256]{2,1,0:T(8,128)(2,1)S(1)}, u32[]{:S(2)}, u32[]{:S(2)}) %collective-permute-start.40) | collective-permute-done | bytes 262176 | tf_op jit(solution)/shard_map/ppermute | solution.py:43
  129.1 7.1 %collective-permute-done.44.refs_1_ = bf16[64,8,256]{2,1,0:T(8,128)(2,1)S(1)} collective-permute-done((bf16[64,8,256]{2,1,0:T(8,128)(2,1)S(1)}, bf16[64,8,256]{2,1,0:T(8,128)(2,1)S(1)}, u32[]{:S(2)}, u32[]{:S(2)}) %collective-permute-start.44) | collective-permute-done | bytes 262176 | tf_op jit(solution)/shard_map/ppermute | solution.py:43
  136.1 3.5 %shard_map.85.refs_2_ = f32[8,8192]{1,0:T(8,128)S(1)} custom-call(f32[64,8,256]{2,1,0:T(8,128)S(1)} %get-tuple-element.240.refs_0_, bf16[64,8,256]{2,1,0:T(8,128)(2,1)S(1)} %collective-permute-done.44.refs_1_, bf16[8192,256]{1,0:T(8,128)(2,1)} %get-tuple-element.143.refs_2_.emb_ref), custom_call_target="tpu_custom_call" | custom-call | tf_op jit(solution)/shard_map/pallas_call | solution.py:296
  144.0 3.7 %collective-permute-done.45.refs_1_ = bf16[8,8192]{1,0:T(8,128)(2,1)S(1)} collective-permute-done((bf16[8,8192]{1,0:T(8,128)(2,1)S(1)}, bf16[8,8192]{1,0:T(8,128)(2,1)S(1)}, u32[]{:S(2)}, u32[]{:S(2)}) %collective-permute-start.45) | collective-permute-done | bytes 131104 | tf_op jit(solution)/shard_map/ppermute | solution.py:43
  (113 shorter events, 74.1 us)
Async XLA Ops:
  5.6 25.0 %collective-permute-start.11 = (bf16[8192,256]{1,0:T(8,128)(2,1)}, bf16[8192,256]{1,0:T(8,128)(2,1)}, u32[]{:S(2)}, u32[]{:S(2)}) collective-permute-start(bf16[8192,256]{1,0:T(8,128)(2,1)} %get-tuple-element.143.refs_2_.emb_ref), channel_id=1, source_target_pairs={{0,1},{1,0},{2,3},{3,2},{4,5},{5,4},{6,7},{7,6},{8,9},{9,8},{10,11... | collective-permute-start | bytes 12582920 | tf_op jit(solution)/shard_map/ppermute | solution.py:43
  9.3 15.6 %collective-permute-start.6 = (bf16[64,8,256]{2,1,0:T(8,128)(2,1)S(1)}, bf16[64,8,256]{2,1,0:T(8,128)(2,1)S(1)}, u32[]{:S(2)}, u32[]{:S(2)}) collective-permute-start(bf16[64,8,256]{2,1,0:T(8,128)(2,1)S(1)} %get-tuple-element.138.refs_0_), channel_id=1, source_target_pairs={{0,4},{4,0},{8,12},{12,8},{16,20},{20,16},{24,28},{28,24},{1,5},{5... | collective-permute-start | bytes 786440 | tf_op jit(solution)/shard_map/ppermute | solution.py:43
  22.4 12.4 %collective-permute-start.9 = (bf16[64,8,256]{2,1,0:T(8,128)(2,1)S(1)}, bf16[64,8,256]{2,1,0:T(8,128)(2,1)S(1)}, u32[]{:S(2)}, u32[]{:S(2)}) collective-permute-start(bf16[64,8,256]{2,1,0:T(8,128)(2,1)S(1)} %collective-permute-done.3.refs_0_), channel_id=1, source_target_pairs={{0,4},{4,0},{8,12},{12,8},{16,20},{20,16},{24,28},{28,24},{1,5},{5... | collective-permute-start | bytes 786440 | tf_op jit(solution)/shard_map/ppermute | solution.py:43
  23.4 13.9 %collective-permute-start.10 = (bf16[64,8,256]{2,1,0:T(8,128)(2,1)S(1)}, bf16[64,8,256]{2,1,0:T(8,128)(2,1)S(1)}, u32[]{:S(2)}, u32[]{:S(2)}) collective-permute-start(bf16[64,8,256]{2,1,0:T(8,128)(2,1)S(1)} %collective-permute-done.8.refs_1_), channel_id=1, source_target_pairs={{0,4},{4,0},{8,12},{12,8},{16,20},{20,16},{24,28},{28,24},{1,5},{5... | collective-permute-start | bytes 786440 | tf_op jit(solution)/shard_map/ppermute | solution.py:43
  26.1 16.6 %collective-permute-start.12 = (bf16[64,8,256]{2,1,0:T(8,128)(2,1)S(1)}, bf16[64,8,256]{2,1,0:T(8,128)(2,1)S(1)}, u32[]{:S(2)}, u32[]{:S(2)}) collective-permute-start(bf16[64,8,256]{2,1,0:T(8,128)(2,1)S(1)} %get-tuple-element.144), channel_id=1, source_target_pairs={{0,16},{4,20},{8,24},{12,28},{16,0},{20,4},{24,8},{28,12},{1,17},{... | collective-permute-start | bytes 786440 | tf_op jit(solution)/shard_map/ppermute | solution.py:43
  28.8 19.9 %collective-permute-start.4 = (bf16[64,8,256]{2,1,0:T(8,128)(2,1)S(1)}, bf16[64,8,256]{2,1,0:T(8,128)(2,1)S(1)}, u32[]{:S(2)}, u32[]{:S(2)}) collective-permute-start(bf16[64,8,256]{2,1,0:T(8,128)(2,1)S(1)} %get-tuple-element.164.refs_0_), channel_id=1, source_target_pairs={{0,8},{4,12},{8,0},{12,4},{16,24},{20,28},{24,16},{28,20},{1,9},{5... | collective-permute-start | bytes 786440 | tf_op jit(solution)/shard_map/ppermute | solution.py:43
  30.6 18.1 %collective-permute-start.5 = (bf16[64,8,256]{2,1,0:T(8,128)(2,1)S(1)}, bf16[64,8,256]{2,1,0:T(8,128)(2,1)S(1)}, u32[]{:S(2)}, u32[]{:S(2)}) collective-permute-start(bf16[64,8,256]{2,1,0:T(8,128)(2,1)S(1)} %get-tuple-element.164.refs_0_), channel_id=1, source_target_pairs={{0,4},{4,0},{8,12},{12,8},{16,20},{20,16},{24,28},{28,24},{1,5},{5... | collective-permute-start | bytes 786440 | tf_op jit(solution)/shard_map/ppermute | solution.py:43
  38.5 12.2 %collective-permute-start.14 = (bf16[64,8,256]{2,1,0:T(8,128)(2,1)S(1)}, bf16[64,8,256]{2,1,0:T(8,128)(2,1)S(1)}, u32[]{:S(2)}, u32[]{:S(2)}) collective-permute-start(bf16[64,8,256]{2,1,0:T(8,128)(2,1)S(1)} %get-tuple-element.151), channel_id=1, source_target_pairs={{0,16},{4,20},{8,24},{12,28},{16,0},{20,4},{24,8},{28,12},{1,17},{... | collective-permute-start | bytes 786440 | tf_op jit(solution)/shard_map/ppermute | solution.py:43
  50.7 13.7 %collective-permute-start.17 = (bf16[64,8,256]{2,1,0:T(8,128)(2,1)S(1)}, bf16[64,8,256]{2,1,0:T(8,128)(2,1)S(1)}, u32[]{:S(2)}, u32[]{:S(2)}) collective-permute-start(bf16[64,8,256]{2,1,0:T(8,128)(2,1)S(1)} %collective-permute-done.15.refs_1_), channel_id=1, source_target_pairs={{0,4},{4,0},{8,12},{12,8},{16,20},{20,16},{24,28},{28,24},{1,5},{5... | collective-permute-start | bytes 786440 | tf_op jit(solution)/shard_map/ppermute | solution.py:43
  63.2 15.0 %collective-permute-start.20 = (bf16[64,8,256]{2,1,0:T(8,128)(2,1)S(1)}, bf16[64,8,256]{2,1,0:T(8,128)(2,1)S(1)}, u32[]{:S(2)}, u32[]{:S(2)}) collective-permute-start(bf16[64,8,256]{2,1,0:T(8,128)(2,1)S(1)} %shard_map.67.refs_0_), channel_id=1, source_target_pairs={{0,8},{4,12},{8,0},{12,4},{16,24},{20,28},{24,16},{28,20},{1,9},{5... | collective-permute-start | bytes 786440 | tf_op jit(solution)/shard_map/ppermute | solution.py:43
  65.6 14.1 %collective-permute-start.19 = (bf16[64,8,256]{2,1,0:T(8,128)(2,1)S(1)}, bf16[64,8,256]{2,1,0:T(8,128)(2,1)S(1)}, u32[]{:S(2)}, u32[]{:S(2)}) collective-permute-start(bf16[64,8,256]{2,1,0:T(8,128)(2,1)S(1)} %get-tuple-element.180), channel_id=1, source_target_pairs={{0,16},{4,20},{8,24},{12,28},{16,0},{20,4},{24,8},{28,12},{1,17},{... | collective-permute-start | bytes 786440 | tf_op jit(solution)/shard_map/ppermute | solution.py:43
  68.1 14.3 %collective-permute-start.25 = (bf16[64,8,256]{2,1,0:T(8,128)(2,1)S(1)}, bf16[64,8,256]{2,1,0:T(8,128)(2,1)S(1)}, u32[]{:S(2)}, u32[]{:S(2)}) collective-permute-start(bf16[64,8,256]{2,1,0:T(8,128)(2,1)S(1)} %shard_map.68.refs_0_), channel_id=1, source_target_pairs={{0,8},{4,12},{8,0},{12,4},{16,24},{20,28},{24,16},{28,20},{1,9},{5... | collective-permute-start | bytes 786440 | tf_op jit(solution)/shard_map/ppermute | solution.py:43
  69.0 13.4 %collective-permute-start.26 = (bf16[64,8,256]{2,1,0:T(8,128)(2,1)S(1)}, bf16[64,8,256]{2,1,0:T(8,128)(2,1)S(1)}, u32[]{:S(2)}, u32[]{:S(2)}) collective-permute-start(bf16[64,8,256]{2,1,0:T(8,128)(2,1)S(1)} %shard_map.68.refs_0_), channel_id=1, source_target_pairs={{0,4},{4,0},{8,12},{12,8},{16,20},{20,16},{24,28},{28,24},{1,5},{5... | collective-permute-start | bytes 786440 | tf_op jit(solution)/shard_map/ppermute | solution.py:43
  70.1 14.5 %collective-permute-start.23 = (bf16[64,8,256]{2,1,0:T(8,128)(2,1)S(1)}, bf16[64,8,256]{2,1,0:T(8,128)(2,1)S(1)}, u32[]{:S(2)}, u32[]{:S(2)}) collective-permute-start(bf16[64,8,256]{2,1,0:T(8,128)(2,1)S(1)} %shard_map.67.refs_0_), channel_id=1, source_target_pairs={{0,4},{4,0},{8,12},{12,8},{16,20},{20,16},{24,28},{28,24},{1,5},{5... | collective-permute-start | bytes 786440 | tf_op jit(solution)/shard_map/ppermute | solution.py:43
  82.3 12.5 %collective-permute-start.29 = (bf16[64,8,256]{2,1,0:T(8,128)(2,1)S(1)}, bf16[64,8,256]{2,1,0:T(8,128)(2,1)S(1)}, u32[]{:S(2)}, u32[]{:S(2)}) collective-permute-start(bf16[64,8,256]{2,1,0:T(8,128)(2,1)S(1)} %collective-permute-done.25.refs_1_), channel_id=1, source_target_pairs={{0,4},{4,0},{8,12},{12,8},{16,20},{20,16},{24,28},{28,24},{1,5},{5... | collective-permute-start | bytes 786440 | tf_op jit(solution)/shard_map/ppermute | solution.py:43
  87.7 15.8 %collective-permute-start.34 = (bf16[64,8,256]{2,1,0:T(8,128)(2,1)S(1)}, bf16[64,8,256]{2,1,0:T(8,128)(2,1)S(1)}, u32[]{:S(2)}, u32[]{:S(2)}) collective-permute-start(bf16[64,8,256]{2,1,0:T(8,128)(2,1)S(1)} %get-tuple-element.195), channel_id=1, source_target_pairs={{0,16},{4,20},{8,24},{12,28},{16,0},{20,4},{24,8},{28,12},{1,17},{... | collective-permute-start | bytes 786440 | tf_op jit(solution)/shard_map/ppermute | solution.py:43
  91.6 15.4 %collective-permute-start.33 = (bf16[64,8,256]{2,1,0:T(8,128)(2,1)S(1)}, bf16[64,8,256]{2,1,0:T(8,128)(2,1)S(1)}, u32[]{:S(2)}, u32[]{:S(2)}) collective-permute-start(bf16[64,8,256]{2,1,0:T(8,128)(2,1)S(1)} %shard_map.74.refs_0_), channel_id=1, source_target_pairs={{0,8},{4,12},{8,0},{12,4},{16,24},{20,28},{24,16},{28,20},{1,9},{5... | collective-permute-start | bytes 786440 | tf_op jit(solution)/shard_map/ppermute | solution.py:43
  96.1 16.4 %collective-permute-start.32 = (bf16[64,8,256]{2,1,0:T(8,128)(2,1)S(1)}, bf16[64,8,256]{2,1,0:T(8,128)(2,1)S(1)}, u32[]{:S(2)}, u32[]{:S(2)}) collective-permute-start(bf16[64,8,256]{2,1,0:T(8,128)(2,1)S(1)} %get-tuple-element.209), channel_id=1, source_target_pairs={{0,16},{4,20},{8,24},{12,28},{16,0},{20,4},{24,8},{28,12},{1,17},{... | collective-permute-start | bytes 786440 | tf_op jit(solution)/shard_map/ppermute | solution.py:43
  99.1 16.1 %collective-permute-start.38 = (bf16[64,8,256]{2,1,0:T(8,128)(2,1)S(1)}, bf16[64,8,256]{2,1,0:T(8,128)(2,1)S(1)}, u32[]{:S(2)}, u32[]{:S(2)}) collective-permute-start(bf16[64,8,256]{2,1,0:T(8,128)(2,1)S(1)} %shard_map.76.refs_0_), channel_id=1, source_target_pairs={{0,8},{4,12},{8,0},{12,4},{16,24},{20,28},{24,16},{28,20},{1,9},{5... | collective-permute-start | bytes 786440 | tf_op jit(solution)/shard_map/ppermute | solution.py:43
  99.1 17.1 %collective-permute-start.36 = (bf16[64,8,256]{2,1,0:T(8,128)(2,1)S(1)}, bf16[64,8,256]{2,1,0:T(8,128)(2,1)S(1)}, u32[]{:S(2)}, u32[]{:S(2)}) collective-permute-start(bf16[64,8,256]{2,1,0:T(8,128)(2,1)S(1)} %shard_map.74.refs_0_), channel_id=1, source_target_pairs={{0,4},{4,0},{8,12},{12,8},{16,20},{20,16},{24,28},{28,24},{1,5},{5... | collective-permute-start | bytes 786440 | tf_op jit(solution)/shard_map/ppermute | solution.py:43
  117.5 18.6 %collective-permute-start.44 = (bf16[64,8,256]{2,1,0:T(8,128)(2,1)S(1)}, bf16[64,8,256]{2,1,0:T(8,128)(2,1)S(1)}, u32[]{:S(2)}, u32[]{:S(2)}) collective-permute-start(bf16[64,8,256]{2,1,0:T(8,128)(2,1)S(1)} %get-tuple-element.225), channel_id=1, source_target_pairs={{0,16},{4,20},{8,24},{12,28},{16,0},{20,4},{24,8},{28,12},{1,17},{... | collective-permute-start | bytes 786440 | tf_op jit(solution)/shard_map/ppermute | solution.py:43
  126.1 15.1 %collective-permute-start.41 = (bf16[64,8,256]{2,1,0:T(8,128)(2,1)S(1)}, bf16[64,8,256]{2,1,0:T(8,128)(2,1)S(1)}, u32[]{:S(2)}, u32[]{:S(2)}) collective-permute-start(bf16[64,8,256]{2,1,0:T(8,128)(2,1)S(1)} %get-tuple-element.231), channel_id=1, source_target_pairs={{0,16},{4,20},{8,24},{12,28},{16,0},{20,4},{24,8},{28,12},{1,17},{... | collective-permute-start | bytes 786440 | tf_op jit(solution)/shard_map/ppermute | solution.py:43
  126.3 13.4 %collective-permute-start.42 = (bf16[8,8192]{1,0:T(8,128)(2,1)S(1)}, bf16[8,8192]{1,0:T(8,128)(2,1)S(1)}, u32[]{:S(2)}, u32[]{:S(2)}) collective-permute-start(bf16[8,8192]{1,0:T(8,128)(2,1)S(1)} %shard_map.80.refs_0_), channel_id=1, source_target_pairs={{0,1},{1,0},{2,3},{3,2},{4,5},{5,4},{6,7},{7,6},{8,9},{9,8},{10,11... | collective-permute-start | bytes 393224 | tf_op jit(solution)/shard_map/ppermute | solution.py:43
  126.8 12.9 %collective-permute-start.43 = (bf16[8,8192]{1,0:T(8,128)(2,1)S(1)}, bf16[8,8192]{1,0:T(8,128)(2,1)S(1)}, u32[]{:S(2)}, u32[]{:S(2)}) collective-permute-start(bf16[8,8192]{1,0:T(8,128)(2,1)S(1)} %collective-permute-done.35.refs_1_), channel_id=1, source_target_pairs={{0,1},{1,0},{2,3},{3,2},{4,5},{5,4},{6,7},{7,6},{8,9},{9,8},{10,11... | collective-permute-start | bytes 393224 | tf_op jit(solution)/shard_map/ppermute | solution.py:43
  (27 other events, 216.7 us)

commit v14 on v12

--- a/solution.py
+++ b/solution.py
@@ -16,8 +16,8 @@
 SIDE, NEXT = 1, 2
 
 ORDER = (
-    "As Al Am Bm",
-    "Af1 Af2 Ao1 Ak",
+    "As Am Bm Af1",
+    "Al Af2 Ao1 Ak",
     "Ao2 Aw Ae1 Bg1",
     "Az2 Bg2 Ae2 Bo1",
     "As1 As2 Bo2 Bw",
@@ -347,8 +347,7 @@
             token.append(ids[0])
         elif step == "s":
             if pairs[c] is None:
-                *sums, tied = lax.optimization_barrier((*first_sums(), tuple(lists.values())))
-                lists = dict(zip(lists, tied))
+                sums = first_sums()
                 token.append(sums[0])
                 for i in range(GROUPS):
                     start_swaps(i, 0, sums[i])

time: 146 us -> 147 us (level)
  starting transfers between devices: 49 us -> 51.2 us
    ppermute x48, starting transfers between devices: 49 us -> 51.2 us  [swap(): return lax.ppermute(value, axis, [(i, i ^ mask) for i in range(size)])]
  transfers between devices with their start and end apart: 48 -> 48, of which waited for: 19 -> 19; matrix products, arithmetic and copies ran while one was open for 0% -> 0% of each run, Pallas kernels for 25% -> 24%
where the time goes in v14:
time: 147 us
  waiting for transfers between devices  56 us (38%)
  starting transfers between devices  51.2 us (35%)
  Pallas kernels  37.9 us (26%)
    ppermute x48, waiting for transfers between devices, swap(): return lax.ppermute(value, axis, [(i, i ^ mask) for i in range(size)])  56 us
    ppermute x48, starting transfers between devices, swap(): return lax.ppermute(value, axis, [(i, i ^ mask) for i in range(size)])  51.2 us
    pallas_call x8, Pallas kernels, expand(): pl.pallas_call(expand_kernel, in_specs=[VMEM] * (len(values) + 1), out_sp...  10.5 us
    pallas_call x8, Pallas kernels, combine_far(): pl.pallas_call(table_kernel, in_specs=[SMEM] + [VMEM] * len(shards), out_...  9.9 us
    pallas_call x4, Pallas kernels, combine(): pl.pallas_call(lookup_kernel, in_specs=[SMEM] + [VMEM] * len(tables), out...  5.3 us
    pallas_call x4, Pallas kernels, fill(): pl.pallas_call(functools.partial(fill_kernel, c, bool(before)), in_specs=...  3.6 us
    pallas_call x1, Pallas kernels, first_sums(): pl.pallas_call(first_sums_kernel, in_specs=[SMEM] + [HBM] * 3, out_specs=...  3.18 us
    pallas_call x4, Pallas kernels, next_sums(): pl.pallas_call(functools.partial(next_sums_kernel, c), in_specs=[SMEM] +...  3.12 us
  transfers between devices with their start and end apart: 48, of which 19 were waited for; matrix products, arithmetic and copies ran while one was open for 0% of the time, Pallas kernels for 24%

profile of v14, /device:TPU:0, one launch (start us, length us, event | category | flops | bytes accessed | tf_op | source)
XLA Modules:
  0.0 146.6 jit_solution(3900095361082387021)
XLA Ops:
  1.1 3.2 %shard_map.59 = (bf16[64,8,256]{2,1,0:T(8,128)(2,1)S(1)}, bf16[64,8,256]{2,1,0:T(8,128)(2,1)S(1)}, bf16[64,8,256]{2,1,0:T(8,128)(2,1)S(1)}, bf16[64,8,256]{2,1,0:T(8,128)(2,1)S(1)}) custom-call(s32[1]{0:T(128)} %bitcast.core_ref, f32[32,8192]{1,0:T(8,128)} %vec_ref.17, f32[1,8192]{1,0:T(1,128)} %bitcast.2, bf16[8192,256]{1,0:T(8,128)(2,1)} %refs_2_.7), custom_call_target="tpu_custom_call" | custom-call | tf_op jit(solution)/shard_map/pallas_call | solution.py:228
  4.9 2.6 %collective-permute-start.1 = (bf16[64,8,256]{2,1,0:T(8,128)(2,1)S(1)}, bf16[64,8,256]{2,1,0:T(8,128)(2,1)S(1)}, u32[]{:S(2)}, u32[]{:S(2)}) collective-permute-start(bf16[64,8,256]{2,1,0:T(8,128)(2,1)S(1)} %get-tuple-element.137.refs_0_), channel_id=1, source_target_pairs={{0,8},{4,12},{8,0},{12,4},{16,24},{20,28},{24,16},{28,20},{1,9},{5... | collective-permute-start | bytes 786440 | tf_op jit(solution)/shard_map/ppermute | solution.py:43
  9.1 2.2 %collective-permute-start.8 = (bf16[64,8,256]{2,1,0:T(8,128)(2,1)S(1)}, bf16[64,8,256]{2,1,0:T(8,128)(2,1)S(1)}, u32[]{:S(2)}, u32[]{:S(2)}) collective-permute-start(bf16[64,8,256]{2,1,0:T(8,128)(2,1)S(1)} %collective-permute-done.3.refs_0_), channel_id=1, source_target_pairs={{0,8},{4,12},{8,0},{12,4},{16,24},{20,28},{24,16},{28,20},{1,9},{5... | collective-permute-start | bytes 786440 | tf_op jit(solution)/shard_map/ppermute | solution.py:43
  11.3 3.5 %collective-permute-done.1.refs_1_ = bf16[64,8,256]{2,1,0:T(8,128)(2,1)S(1)} collective-permute-done((bf16[64,8,256]{2,1,0:T(8,128)(2,1)S(1)}, bf16[64,8,256]{2,1,0:T(8,128)(2,1)S(1)}, u32[]{:S(2)}, u32[]{:S(2)}) %collective-permute-start.1) | collective-permute-done | bytes 262176 | tf_op jit(solution)/shard_map/ppermute | solution.py:43
  14.7 1.9 %collective-permute-start.7 = (bf16[64,8,256]{2,1,0:T(8,128)(2,1)S(1)}, bf16[64,8,256]{2,1,0:T(8,128)(2,1)S(1)}, u32[]{:S(2)}, u32[]{:S(2)}) collective-permute-start(bf16[64,8,256]{2,1,0:T(8,128)(2,1)S(1)} %collective-permute-done.1.refs_1_), channel_id=1, source_target_pairs={{0,4},{4,0},{8,12},{12,8},{16,20},{20,16},{24,28},{28,24},{1,5},{5... | collective-permute-start | bytes 786440 | tf_op jit(solution)/shard_map/ppermute | solution.py:43
  16.6 2.6 %collective-permute-start = (s32[64,8]{0,1:T(8,128)S(1)}, s32[64,8]{0,1:T(8,128)S(1)}, u32[]{:S(2)}, u32[]{:S(2)}) collective-permute-start(s32[64,8]{0,1:T(8,128)S(1)} %copy-done.3), channel_id=1, source_target_pairs={{0,16},{4,20},{8,24},{12,28},{16,0},{20,4},{24,8},{28,12},{1,17},{... | collective-permute-start | bytes 6152 | tf_op jit(solution)/shard_map/ppermute | solution.py:43
  19.2 1.9 %collective-permute-done = s32[64,8]{0,1:T(8,128)S(1)} collective-permute-done((s32[64,8]{0,1:T(8,128)S(1)}, s32[64,8]{0,1:T(8,128)S(1)}, u32[]{:S(2)}, u32[]{:S(2)}) %collective-permute-start) | collective-permute-done | bytes 2080 | tf_op jit(solution)/shard_map/ppermute | solution.py:43
  24.9 2.7 %collective-permute-start.12 = (bf16[64,8,256]{2,1,0:T(8,128)(2,1)S(1)}, bf16[64,8,256]{2,1,0:T(8,128)(2,1)S(1)}, u32[]{:S(2)}, u32[]{:S(2)}) collective-permute-start(bf16[64,8,256]{2,1,0:T(8,128)(2,1)S(1)} %get-tuple-element.142), channel_id=1, source_target_pairs={{0,16},{4,20},{8,24},{12,28},{16,0},{20,4},{24,8},{28,12},{1,17},{... | collective-permute-start | bytes 786440 | tf_op jit(solution)/shard_map/ppermute | solution.py:43
  29.1 2.2 %collective-permute-start.5 = (bf16[64,8,256]{2,1,0:T(8,128)(2,1)S(1)}, bf16[64,8,256]{2,1,0:T(8,128)(2,1)S(1)}, u32[]{:S(2)}, u32[]{:S(2)}) collective-permute-start(bf16[64,8,256]{2,1,0:T(8,128)(2,1)S(1)} %get-tuple-element.162.refs_0_), channel_id=1, source_target_pairs={{0,4},{4,0},{8,12},{12,8},{16,20},{20,16},{24,28},{28,24},{1,5},{5... | collective-permute-start | bytes 786440 | tf_op jit(solution)/shard_map/ppermute | solution.py:43
  31.3 2.3 %shard_map.61.refs_3_.emb_ref = bf16[8192,256]{1,0:T(8,128)(2,1)S(1)} custom-call(bf16[8192,256]{1,0:T(8,128)(2,1)} %collective-permute-done.11.src_ref), custom_call_target="tpu_custom_call" | custom-call | tf_op jit(solution)/shard_map/pallas_call | solution.py:243
  33.7 2.3 %collective-permute-done.10.refs_3_ = bf16[64,8,256]{2,1,0:T(8,128)(2,1)S(1)} collective-permute-done((bf16[64,8,256]{2,1,0:T(8,128)(2,1)S(1)}, bf16[64,8,256]{2,1,0:T(8,128)(2,1)S(1)}, u32[]{:S(2)}, u32[]{:S(2)}) %collective-permute-start.10) | collective-permute-done | bytes 262176 | tf_op jit(solution)/shard_map/ppermute | solution.py:43
  37.2 2.7 %collective-permute-start.14 = (bf16[64,8,256]{2,1,0:T(8,128)(2,1)S(1)}, bf16[64,8,256]{2,1,0:T(8,128)(2,1)S(1)}, u32[]{:S(2)}, u32[]{:S(2)}) collective-permute-start(bf16[64,8,256]{2,1,0:T(8,128)(2,1)S(1)} %get-tuple-element.149), channel_id=1, source_target_pairs={{0,16},{4,20},{8,24},{12,28},{16,0},{20,4},{24,8},{28,12},{1,17},{... | collective-permute-start | bytes 786440 | tf_op jit(solution)/shard_map/ppermute | solution.py:43
  46.2 2.6 %collective-permute-done.14.refs_1_ = bf16[64,8,256]{2,1,0:T(8,128)(2,1)S(1)} collective-permute-done((bf16[64,8,256]{2,1,0:T(8,128)(2,1)S(1)}, bf16[64,8,256]{2,1,0:T(8,128)(2,1)S(1)}, u32[]{:S(2)}, u32[]{:S(2)}) %collective-permute-start.14) | collective-permute-done | bytes 262176 | tf_op jit(solution)/shard_map/ppermute | solution.py:43
  61.3 2.1 %collective-permute-start.19 = (bf16[64,8,256]{2,1,0:T(8,128)(2,1)S(1)}, bf16[64,8,256]{2,1,0:T(8,128)(2,1)S(1)}, u32[]{:S(2)}, u32[]{:S(2)}) collective-permute-start(bf16[64,8,256]{2,1,0:T(8,128)(2,1)S(1)} %get-tuple-element.178), channel_id=1, source_target_pairs={{0,16},{4,20},{8,24},{12,28},{16,0},{20,4},{24,8},{28,12},{1,17},{... | collective-permute-start | bytes 786440 | tf_op jit(solution)/shard_map/ppermute | solution.py:43
  65.0 5.9 %collective-permute-done.21.refs_1_ = bf16[64,8,256]{2,1,0:T(8,128)(2,1)S(1)} collective-permute-done((bf16[64,8,256]{2,1,0:T(8,128)(2,1)S(1)}, bf16[64,8,256]{2,1,0:T(8,128)(2,1)S(1)}, u32[]{:S(2)}, u32[]{:S(2)}) %collective-permute-start.21) | collective-permute-done | bytes 262176 | tf_op jit(solution)/shard_map/ppermute | solution.py:43
  75.6 1.9 %collective-permute-done.19.refs_1_ = bf16[64,8,256]{2,1,0:T(8,128)(2,1)S(1)} collective-permute-done((bf16[64,8,256]{2,1,0:T(8,128)(2,1)S(1)}, bf16[64,8,256]{2,1,0:T(8,128)(2,1)S(1)}, u32[]{:S(2)}, u32[]{:S(2)}) %collective-permute-start.19) | collective-permute-done | bytes 262176 | tf_op jit(solution)/shard_map/ppermute | solution.py:43
  85.6 2.2 %collective-permute-start.33 = (bf16[64,8,256]{2,1,0:T(8,128)(2,1)S(1)}, bf16[64,8,256]{2,1,0:T(8,128)(2,1)S(1)}, u32[]{:S(2)}, u32[]{:S(2)}) collective-permute-start(bf16[64,8,256]{2,1,0:T(8,128)(2,1)S(1)} %shard_map.74.refs_0_), channel_id=1, source_target_pairs={{0,8},{4,12},{8,0},{12,4},{16,24},{20,28},{24,16},{28,20},{1,9},{5... | collective-permute-start | bytes 786440 | tf_op jit(solution)/shard_map/ppermute | solution.py:43
  90.7 3.0 %collective-permute-start.32 = (bf16[64,8,256]{2,1,0:T(8,128)(2,1)S(1)}, bf16[64,8,256]{2,1,0:T(8,128)(2,1)S(1)}, u32[]{:S(2)}, u32[]{:S(2)}) collective-permute-start(bf16[64,8,256]{2,1,0:T(8,128)(2,1)S(1)} %get-tuple-element.207), channel_id=1, source_target_pairs={{0,16},{4,20},{8,24},{12,28},{16,0},{20,4},{24,8},{28,12},{1,17},{... | collective-permute-start | bytes 786440 | tf_op jit(solution)/shard_map/ppermute | solution.py:43
  96.3 5.0 %collective-permute-done.34.refs_1_ = bf16[64,8,256]{2,1,0:T(8,128)(2,1)S(1)} collective-permute-done((bf16[64,8,256]{2,1,0:T(8,128)(2,1)S(1)}, bf16[64,8,256]{2,1,0:T(8,128)(2,1)S(1)}, u32[]{:S(2)}, u32[]{:S(2)}) %collective-permute-start.34) | collective-permute-done | bytes 262176 | tf_op jit(solution)/shard_map/ppermute | solution.py:43
  104.7 4.1 %collective-permute-done.32.refs_1_ = bf16[64,8,256]{2,1,0:T(8,128)(2,1)S(1)} collective-permute-done((bf16[64,8,256]{2,1,0:T(8,128)(2,1)S(1)}, bf16[64,8,256]{2,1,0:T(8,128)(2,1)S(1)}, u32[]{:S(2)}, u32[]{:S(2)}) %collective-permute-start.32) | collective-permute-done | bytes 262176 | tf_op jit(solution)/shard_map/ppermute | solution.py:43
  115.5 3.8 %collective-permute-done.40.refs_3_ = bf16[64,8,256]{2,1,0:T(8,128)(2,1)S(1)} collective-permute-done((bf16[64,8,256]{2,1,0:T(8,128)(2,1)S(1)}, bf16[64,8,256]{2,1,0:T(8,128)(2,1)S(1)}, u32[]{:S(2)}, u32[]{:S(2)}) %collective-permute-start.40) | collective-permute-done | bytes 262176 | tf_op jit(solution)/shard_map/ppermute | solution.py:43
  123.5 9.5 %collective-permute-done.44.refs_1_ = bf16[64,8,256]{2,1,0:T(8,128)(2,1)S(1)} collective-permute-done((bf16[64,8,256]{2,1,0:T(8,128)(2,1)S(1)}, bf16[64,8,256]{2,1,0:T(8,128)(2,1)S(1)}, u32[]{:S(2)}, u32[]{:S(2)}) %collective-permute-start.44) | collective-permute-done | bytes 262176 | tf_op jit(solution)/shard_map/ppermute | solution.py:43
  135.3 2.7 %collective-permute-done.41.refs_1_ = bf16[64,8,256]{2,1,0:T(8,128)(2,1)S(1)} collective-permute-done((bf16[64,8,256]{2,1,0:T(8,128)(2,1)S(1)}, bf16[64,8,256]{2,1,0:T(8,128)(2,1)S(1)}, u32[]{:S(2)}, u32[]{:S(2)}) %collective-permute-start.41) | collective-permute-done | bytes 262176 | tf_op jit(solution)/shard_map/ppermute | solution.py:43
  139.4 4.9 %collective-permute-done.45.refs_1_ = bf16[8,8192]{1,0:T(8,128)(2,1)S(1)} collective-permute-done((bf16[8,8192]{1,0:T(8,128)(2,1)S(1)}, bf16[8,8192]{1,0:T(8,128)(2,1)S(1)}, u32[]{:S(2)}, u32[]{:S(2)}) %collective-permute-start.45) | collective-permute-done | bytes 131104 | tf_op jit(solution)/shard_map/ppermute | solution.py:43
  (115 shorter events, 68.0 us)
Async XLA Ops:
  0.6 28.5 %collective-permute-start.11 = (bf16[8192,256]{1,0:T(8,128)(2,1)}, bf16[8192,256]{1,0:T(8,128)(2,1)}, u32[]{:S(2)}, u32[]{:S(2)}) collective-permute-start(bf16[8192,256]{1,0:T(8,128)(2,1)} %refs_2_.7), channel_id=1, source_target_pairs={{0,1},{1,0},{2,3},{3,2},{4,5},{5,4},{6,7},{7,6},{8,9},{9,8},{10,11... | collective-permute-start | bytes 12582920 | tf_op jit(solution)/shard_map/ppermute | solution.py:43
  7.6 16.0 %collective-permute-start.6 = (bf16[64,8,256]{2,1,0:T(8,128)(2,1)S(1)}, bf16[64,8,256]{2,1,0:T(8,128)(2,1)S(1)}, u32[]{:S(2)}, u32[]{:S(2)}) collective-permute-start(bf16[64,8,256]{2,1,0:T(8,128)(2,1)S(1)} %get-tuple-element.137.refs_0_), channel_id=1, source_target_pairs={{0,4},{4,0},{8,12},{12,8},{16,20},{20,16},{24,28},{28,24},{1,5},{5... | collective-permute-start | bytes 786440 | tf_op jit(solution)/shard_map/ppermute | solution.py:43
  9.1 12.7 %collective-permute-start.8 = (bf16[64,8,256]{2,1,0:T(8,128)(2,1)S(1)}, bf16[64,8,256]{2,1,0:T(8,128)(2,1)S(1)}, u32[]{:S(2)}, u32[]{:S(2)}) collective-permute-start(bf16[64,8,256]{2,1,0:T(8,128)(2,1)S(1)} %collective-permute-done.3.refs_0_), channel_id=1, source_target_pairs={{0,8},{4,12},{8,0},{12,4},{16,24},{20,28},{24,16},{28,20},{1,9},{5... | collective-permute-start | bytes 786440 | tf_op jit(solution)/shard_map/ppermute | solution.py:43
  21.1 12.6 %collective-permute-start.9 = (bf16[64,8,256]{2,1,0:T(8,128)(2,1)S(1)}, bf16[64,8,256]{2,1,0:T(8,128)(2,1)S(1)}, u32[]{:S(2)}, u32[]{:S(2)}) collective-permute-start(bf16[64,8,256]{2,1,0:T(8,128)(2,1)S(1)} %collective-permute-done.3.refs_0_), channel_id=1, source_target_pairs={{0,4},{4,0},{8,12},{12,8},{16,20},{20,16},{24,28},{28,24},{1,5},{5... | collective-permute-start | bytes 786440 | tf_op jit(solution)/shard_map/ppermute | solution.py:43
  21.8 14.2 %collective-permute-start.10 = (bf16[64,8,256]{2,1,0:T(8,128)(2,1)S(1)}, bf16[64,8,256]{2,1,0:T(8,128)(2,1)S(1)}, u32[]{:S(2)}, u32[]{:S(2)}) collective-permute-start(bf16[64,8,256]{2,1,0:T(8,128)(2,1)S(1)} %collective-permute-done.8.refs_1_), channel_id=1, source_target_pairs={{0,4},{4,0},{8,12},{12,8},{16,20},{20,16},{24,28},{28,24},{1,5},{5... | collective-permute-start | bytes 786440 | tf_op jit(solution)/shard_map/ppermute | solution.py:43
  24.9 16.6 %collective-permute-start.12 = (bf16[64,8,256]{2,1,0:T(8,128)(2,1)S(1)}, bf16[64,8,256]{2,1,0:T(8,128)(2,1)S(1)}, u32[]{:S(2)}, u32[]{:S(2)}) collective-permute-start(bf16[64,8,256]{2,1,0:T(8,128)(2,1)S(1)} %get-tuple-element.142), channel_id=1, source_target_pairs={{0,16},{4,20},{8,24},{12,28},{16,0},{20,4},{24,8},{28,12},{1,17},{... | collective-permute-start | bytes 786440 | tf_op jit(solution)/shard_map/ppermute | solution.py:43
  27.5 17.7 %collective-permute-start.4 = (bf16[64,8,256]{2,1,0:T(8,128)(2,1)S(1)}, bf16[64,8,256]{2,1,0:T(8,128)(2,1)S(1)}, u32[]{:S(2)}, u32[]{:S(2)}) collective-permute-start(bf16[64,8,256]{2,1,0:T(8,128)(2,1)S(1)} %get-tuple-element.162.refs_0_), channel_id=1, source_target_pairs={{0,8},{4,12},{8,0},{12,4},{16,24},{20,28},{24,16},{28,20},{1,9},{5... | collective-permute-start | bytes 786440 | tf_op jit(solution)/shard_map/ppermute | solution.py:43
  29.1 16.2 %collective-permute-start.5 = (bf16[64,8,256]{2,1,0:T(8,128)(2,1)S(1)}, bf16[64,8,256]{2,1,0:T(8,128)(2,1)S(1)}, u32[]{:S(2)}, u32[]{:S(2)}) collective-permute-start(bf16[64,8,256]{2,1,0:T(8,128)(2,1)S(1)} %get-tuple-element.162.refs_0_), channel_id=1, source_target_pairs={{0,4},{4,0},{8,12},{12,8},{16,20},{20,16},{24,28},{28,24},{1,5},{5... | collective-permute-start | bytes 786440 | tf_op jit(solution)/shard_map/ppermute | solution.py:43
  37.2 11.6 %collective-permute-start.14 = (bf16[64,8,256]{2,1,0:T(8,128)(2,1)S(1)}, bf16[64,8,256]{2,1,0:T(8,128)(2,1)S(1)}, u32[]{:S(2)}, u32[]{:S(2)}) collective-permute-start(bf16[64,8,256]{2,1,0:T(8,128)(2,1)S(1)} %get-tuple-element.149), channel_id=1, source_target_pairs={{0,16},{4,20},{8,24},{12,28},{16,0},{20,4},{24,8},{28,12},{1,17},{... | collective-permute-start | bytes 786440 | tf_op jit(solution)/shard_map/ppermute | solution.py:43
  56.0 14.9 %collective-permute-start.21 = (bf16[64,8,256]{2,1,0:T(8,128)(2,1)S(1)}, bf16[64,8,256]{2,1,0:T(8,128)(2,1)S(1)}, u32[]{:S(2)}, u32[]{:S(2)}) collective-permute-start(bf16[64,8,256]{2,1,0:T(8,128)(2,1)S(1)} %get-tuple-element.168), channel_id=1, source_target_pairs={{0,16},{4,20},{8,24},{12,28},{16,0},{20,4},{24,8},{28,12},{1,17},{... | collective-permute-start | bytes 786440 | tf_op jit(solution)/shard_map/ppermute | solution.py:43
  58.1 16.1 %collective-permute-start.20 = (bf16[64,8,256]{2,1,0:T(8,128)(2,1)S(1)}, bf16[64,8,256]{2,1,0:T(8,128)(2,1)S(1)}, u32[]{:S(2)}, u32[]{:S(2)}) collective-permute-start(bf16[64,8,256]{2,1,0:T(8,128)(2,1)S(1)} %shard_map.67.refs_0_), channel_id=1, source_target_pairs={{0,8},{4,12},{8,0},{12,4},{16,24},{20,28},{24,16},{28,20},{1,9},{5... | collective-permute-start | bytes 786440 | tf_op jit(solution)/shard_map/ppermute | solution.py:43
  61.3 16.2 %collective-permute-start.19 = (bf16[64,8,256]{2,1,0:T(8,128)(2,1)S(1)}, bf16[64,8,256]{2,1,0:T(8,128)(2,1)S(1)}, u32[]{:S(2)}, u32[]{:S(2)}) collective-permute-start(bf16[64,8,256]{2,1,0:T(8,128)(2,1)S(1)} %get-tuple-element.178), channel_id=1, source_target_pairs={{0,16},{4,20},{8,24},{12,28},{16,0},{20,4},{24,8},{28,12},{1,17},{... | collective-permute-start | bytes 786440 | tf_op jit(solution)/shard_map/ppermute | solution.py:43
  63.4 15.5 %collective-permute-start.25 = (bf16[64,8,256]{2,1,0:T(8,128)(2,1)S(1)}, bf16[64,8,256]{2,1,0:T(8,128)(2,1)S(1)}, u32[]{:S(2)}, u32[]{:S(2)}) collective-permute-start(bf16[64,8,256]{2,1,0:T(8,128)(2,1)S(1)} %shard_map.68.refs_0_), channel_id=1, source_target_pairs={{0,8},{4,12},{8,0},{12,4},{16,24},{20,28},{24,16},{28,20},{1,9},{5... | collective-permute-start | bytes 786440 | tf_op jit(solution)/shard_map/ppermute | solution.py:43
  64.5 14.4 %collective-permute-start.26 = (bf16[64,8,256]{2,1,0:T(8,128)(2,1)S(1)}, bf16[64,8,256]{2,1,0:T(8,128)(2,1)S(1)}, u32[]{:S(2)}, u32[]{:S(2)}) collective-permute-start(bf16[64,8,256]{2,1,0:T(8,128)(2,1)S(1)} %shard_map.68.refs_0_), channel_id=1, source_target_pairs={{0,4},{4,0},{8,12},{12,8},{16,20},{20,16},{24,28},{28,24},{1,5},{5... | collective-permute-start | bytes 786440 | tf_op jit(solution)/shard_map/ppermute | solution.py:43
  84.3 16.9 %collective-permute-start.34 = (bf16[64,8,256]{2,1,0:T(8,128)(2,1)S(1)}, bf16[64,8,256]{2,1,0:T(8,128)(2,1)S(1)}, u32[]{:S(2)}, u32[]{:S(2)}) collective-permute-start(bf16[64,8,256]{2,1,0:T(8,128)(2,1)S(1)} %get-tuple-element.193), channel_id=1, source_target_pairs={{0,16},{4,20},{8,24},{12,28},{16,0},{20,4},{24,8},{28,12},{1,17},{... | collective-permute-start | bytes 786440 | tf_op jit(solution)/shard_map/ppermute | solution.py:43
  85.6 17.0 %collective-permute-start.33 = (bf16[64,8,256]{2,1,0:T(8,128)(2,1)S(1)}, bf16[64,8,256]{2,1,0:T(8,128)(2,1)S(1)}, u32[]{:S(2)}, u32[]{:S(2)}) collective-permute-start(bf16[64,8,256]{2,1,0:T(8,128)(2,1)S(1)} %shard_map.74.refs_0_), channel_id=1, source_target_pairs={{0,8},{4,12},{8,0},{12,4},{16,24},{20,28},{24,16},{28,20},{1,9},{5... | collective-permute-start | bytes 786440 | tf_op jit(solution)/shard_map/ppermute | solution.py:43
  90.7 18.1 %collective-permute-start.32 = (bf16[64,8,256]{2,1,0:T(8,128)(2,1)S(1)}, bf16[64,8,256]{2,1,0:T(8,128)(2,1)S(1)}, u32[]{:S(2)}, u32[]{:S(2)}) collective-permute-start(bf16[64,8,256]{2,1,0:T(8,128)(2,1)S(1)} %get-tuple-element.207), channel_id=1, source_target_pairs={{0,16},{4,20},{8,24},{12,28},{16,0},{20,4},{24,8},{28,12},{1,17},{... | collective-permute-start | bytes 786440 | tf_op jit(solution)/shard_map/ppermute | solution.py:43
  93.6 16.4 %collective-permute-start.38 = (bf16[64,8,256]{2,1,0:T(8,128)(2,1)S(1)}, bf16[64,8,256]{2,1,0:T(8,128)(2,1)S(1)}, u32[]{:S(2)}, u32[]{:S(2)}) collective-permute-start(bf16[64,8,256]{2,1,0:T(8,128)(2,1)S(1)} %shard_map.76.refs_0_), channel_id=1, source_target_pairs={{0,8},{4,12},{8,0},{12,4},{16,24},{20,28},{24,16},{28,20},{1,9},{5... | collective-permute-start | bytes 786440 | tf_op jit(solution)/shard_map/ppermute | solution.py:43
  93.7 18.1 %collective-permute-start.36 = (bf16[64,8,256]{2,1,0:T(8,128)(2,1)S(1)}, bf16[64,8,256]{2,1,0:T(8,128)(2,1)S(1)}, u32[]{:S(2)}, u32[]{:S(2)}) collective-permute-start(bf16[64,8,256]{2,1,0:T(8,128)(2,1)S(1)} %shard_map.74.refs_0_), channel_id=1, source_target_pairs={{0,4},{4,0},{8,12},{12,8},{16,20},{20,16},{24,28},{28,24},{1,5},{5... | collective-permute-start | bytes 786440 | tf_op jit(solution)/shard_map/ppermute | solution.py:43
  104.2 11.3 %collective-permute-start.39 = (bf16[64,8,256]{2,1,0:T(8,128)(2,1)S(1)}, bf16[64,8,256]{2,1,0:T(8,128)(2,1)S(1)}, u32[]{:S(2)}, u32[]{:S(2)}) collective-permute-start(bf16[64,8,256]{2,1,0:T(8,128)(2,1)S(1)} %shard_map.76.refs_0_), channel_id=1, source_target_pairs={{0,4},{4,0},{8,12},{12,8},{16,20},{20,16},{24,28},{28,24},{1,5},{5... | collective-permute-start | bytes 786440 | tf_op jit(solution)/shard_map/ppermute | solution.py:43
  113.0 19.9 %collective-permute-start.44 = (bf16[64,8,256]{2,1,0:T(8,128)(2,1)S(1)}, bf16[64,8,256]{2,1,0:T(8,128)(2,1)S(1)}, u32[]{:S(2)}, u32[]{:S(2)}) collective-permute-start(bf16[64,8,256]{2,1,0:T(8,128)(2,1)S(1)} %get-tuple-element.223), channel_id=1, source_target_pairs={{0,16},{4,20},{8,24},{12,28},{16,0},{20,4},{24,8},{28,12},{1,17},{... | collective-permute-start | bytes 786440 | tf_op jit(solution)/shard_map/ppermute | solution.py:43
  120.5 17.4 %collective-permute-start.41 = (bf16[64,8,256]{2,1,0:T(8,128)(2,1)S(1)}, bf16[64,8,256]{2,1,0:T(8,128)(2,1)S(1)}, u32[]{:S(2)}, u32[]{:S(2)}) collective-permute-start(bf16[64,8,256]{2,1,0:T(8,128)(2,1)S(1)} %get-tuple-element.229), channel_id=1, source_target_pairs={{0,16},{4,20},{8,24},{12,28},{16,0},{20,4},{24,8},{28,12},{1,17},{... | collective-permute-start | bytes 786440 | tf_op jit(solution)/shard_map/ppermute | solution.py:43
  120.7 13.6 %collective-permute-start.42 = (bf16[8,8192]{1,0:T(8,128)(2,1)S(1)}, bf16[8,8192]{1,0:T(8,128)(2,1)S(1)}, u32[]{:S(2)}, u32[]{:S(2)}) collective-permute-start(bf16[8,8192]{1,0:T(8,128)(2,1)S(1)} %shard_map.80.refs_0_), channel_id=1, source_target_pairs={{0,1},{1,0},{2,3},{3,2},{4,5},{5,4},{6,7},{7,6},{8,9},{9,8},{10,11... | collective-permute-start | bytes 393224 | tf_op jit(solution)/shard_map/ppermute | solution.py:43
  121.2 13.1 %collective-permute-start.43 = (bf16[8,8192]{1,0:T(8,128)(2,1)S(1)}, bf16[8,8192]{1,0:T(8,128)(2,1)S(1)}, u32[]{:S(2)}, u32[]{:S(2)}) collective-permute-start(bf16[8,8192]{1,0:T(8,128)(2,1)S(1)} %collective-permute-done.35.refs_1_), channel_id=1, source_target_pairs={{0,1},{1,0},{2,3},{3,2},{4,5},{5,4},{6,7},{7,6},{8,9},{9,8},{10,11... | collective-permute-start | bytes 393224 | tf_op jit(solution)/shard_map/ppermute | solution.py:43
  (28 other events, 211.2 us)

commit v15 on v12

--- a/solution.py
+++ b/solution.py
@@ -11,7 +11,7 @@
 GROUPS = 2
 PARTS = CORES
 TILE_BLOCKS = 8
-UNROLL = 32
+UNROLL = 64
 VMEM_LIMIT = 8 * 1024 * 1024
 SIDE, NEXT = 1, 2
 

time: 146 us -> 145 us (level)
  Pallas kernels: 37.9 us -> 34.9 us
  waiting for transfers between devices: 57.3 us -> 59.3 us
    ppermute x48, waiting for transfers between devices: 57.3 us -> 59.3 us  [swap(): return lax.ppermute(value, axis, [(i, i ^ mask) for i in range(size)])]
  transfers between devices with their start and end apart: 48 -> 48, of which waited for: 19 -> 19; matrix products, arithmetic and copies ran while one was open for 0% -> 0% of each run, Pallas kernels for 25% -> 23%
where the time goes in v15:
time: 145 us
  waiting for transfers between devices  59.3 us (41%)
  starting transfers between devices  49 us (34%)
  Pallas kernels  34.9 us (24%)
    ppermute x48, waiting for transfers between devices, swap(): return lax.ppermute(value, axis, [(i, i ^ mask) for i in range(size)])  59.3 us
    ppermute x48, starting transfers between devices, swap(): return lax.ppermute(value, axis, [(i, i ^ mask) for i in range(size)])  49 us
    pallas_call x8, Pallas kernels, expand(): pl.pallas_call(expand_kernel, in_specs=[VMEM] * (len(values) + 1), out_sp...  9.51 us
    pallas_call x8, Pallas kernels, combine_far(): pl.pallas_call(table_kernel, in_specs=[SMEM] + [VMEM] * len(shards), out_...  8.94 us
    pallas_call x4, Pallas kernels, combine(): pl.pallas_call(lookup_kernel, in_specs=[SMEM] + [VMEM] * len(tables), out...  4.62 us
    pallas_call x4, Pallas kernels, fill(): pl.pallas_call(functools.partial(fill_kernel, c, bool(before)), in_specs=...  3.62 us
    pallas_call x1, Pallas kernels, first_sums(): pl.pallas_call(first_sums_kernel, in_specs=[SMEM] + [HBM] * 3, out_specs=...  3.19 us
  transfers between devices with their start and end apart: 48, of which 19 were waited for; matrix products, arithmetic and copies ran while one was open for 0% of the time, Pallas kernels for 23%

profile of v15, /device:TPU:0, one launch (start us, length us, event | category | flops | bytes accessed | tf_op | source)
XLA Modules:
  0.0 144.6 jit_solution(5868290500841971290)
XLA Ops:
  1.1 3.7 %collective-permute-start = (s32[64,8]{0,1:T(8,128)}, s32[64,8]{0,1:T(8,128)S(1)}, u32[]{:S(2)}, u32[]{:S(2)}) collective-permute-start(s32[64,8]{0,1:T(8,128)} %param.7), channel_id=1, source_target_pairs={{0,16},{4,20},{8,24},{12,28},{16,0},{20,4},{24,8},{28,12},{1,17},{... | collective-permute-start | bytes 6152 | tf_op jit(solution)/shard_map/ppermute | solution.py:43
  4.8 3.2 %shard_map.59 = (bf16[64,8,256]{2,1,0:T(8,128)(2,1)S(1)}, bf16[64,8,256]{2,1,0:T(8,128)(2,1)S(1)}, bf16[64,8,256]{2,1,0:T(8,128)(2,1)S(1)}, bf16[64,8,256]{2,1,0:T(8,128)(2,1)S(1)}) custom-call(s32[1]{0:T(128)} %bitcast.core_ref, f32[32,8192]{1,0:T(8,128)} %vec_ref.17, f32[1,8192]{1,0:T(1,128)} %bitcast.2, bf16[8192,256]{1,0:T(8,128)(2,1)} %refs_2_.7), custom_call_target="tpu_custom_call" | custom-call | tf_op jit(solution)/shard_map/pallas_call | solution.py:228
  12.6 5.1 %collective-permute-done.3.refs_1_ = bf16[64,8,256]{2,1,0:T(8,128)(2,1)S(1)} collective-permute-done((bf16[64,8,256]{2,1,0:T(8,128)(2,1)S(1)}, bf16[64,8,256]{2,1,0:T(8,128)(2,1)S(1)}, u32[]{:S(2)}, u32[]{:S(2)}) %collective-permute-start.3) | collective-permute-done | bytes 262176 | tf_op jit(solution)/shard_map/ppermute | solution.py:43
  19.8 2.8 %collective-permute-done.8.refs_1_ = bf16[64,8,256]{2,1,0:T(8,128)(2,1)S(1)} collective-permute-done((bf16[64,8,256]{2,1,0:T(8,128)(2,1)S(1)}, bf16[64,8,256]{2,1,0:T(8,128)(2,1)S(1)}, u32[]{:S(2)}, u32[]{:S(2)}) %collective-permute-start.8) | collective-permute-done | bytes 262176 | tf_op jit(solution)/shard_map/ppermute | solution.py:43
  24.1 2.9 %collective-permute-done.7.refs_3_ = bf16[64,8,256]{2,1,0:T(8,128)(2,1)S(1)} collective-permute-done((bf16[64,8,256]{2,1,0:T(8,128)(2,1)S(1)}, bf16[64,8,256]{2,1,0:T(8,128)(2,1)S(1)}, u32[]{:S(2)}, u32[]{:S(2)}) %collective-permute-start.7) | collective-permute-done | bytes 262176 | tf_op jit(solution)/shard_map/ppermute | solution.py:43
  32.7 2.3 %shard_map.61.refs_3_.emb_ref = bf16[8192,256]{1,0:T(8,128)(2,1)S(1)} custom-call(bf16[8192,256]{1,0:T(8,128)(2,1)} %collective-permute-done.11.src_ref), custom_call_target="tpu_custom_call" | custom-call | tf_op jit(solution)/shard_map/pallas_call | solution.py:243
  35.1 3.1 %collective-permute-done.10.refs_3_ = bf16[64,8,256]{2,1,0:T(8,128)(2,1)S(1)} collective-permute-done((bf16[64,8,256]{2,1,0:T(8,128)(2,1)S(1)}, bf16[64,8,256]{2,1,0:T(8,128)(2,1)S(1)}, u32[]{:S(2)}, u32[]{:S(2)}) %collective-permute-start.10) | collective-permute-done | bytes 262176 | tf_op jit(solution)/shard_map/ppermute | solution.py:43
  46.9 3.5 %collective-permute-done.14.refs_1_ = bf16[64,8,256]{2,1,0:T(8,128)(2,1)S(1)} collective-permute-done((bf16[64,8,256]{2,1,0:T(8,128)(2,1)S(1)}, bf16[64,8,256]{2,1,0:T(8,128)(2,1)S(1)}, u32[]{:S(2)}, u32[]{:S(2)}) %collective-permute-start.14) | collective-permute-done | bytes 262176 | tf_op jit(solution)/shard_map/ppermute | solution.py:43
  50.7 2.5 %collective-permute-start.17 = (bf16[64,8,256]{2,1,0:T(8,128)(2,1)S(1)}, bf16[64,8,256]{2,1,0:T(8,128)(2,1)S(1)}, u32[]{:S(2)}, u32[]{:S(2)}) collective-permute-start(bf16[64,8,256]{2,1,0:T(8,128)(2,1)S(1)} %collective-permute-done.15.refs_1_), channel_id=1, source_target_pairs={{0,4},{4,0},{8,12},{12,8},{16,20},{20,16},{24,28},{28,24},{1,5},{5... | collective-permute-start | bytes 786440 | tf_op jit(solution)/shard_map/ppermute | solution.py:43
  63.6 1.7 %collective-permute-start.25 = (bf16[64,8,256]{2,1,0:T(8,128)(2,1)S(1)}, bf16[64,8,256]{2,1,0:T(8,128)(2,1)S(1)}, u32[]{:S(2)}, u32[]{:S(2)}) collective-permute-start(bf16[64,8,256]{2,1,0:T(8,128)(2,1)S(1)} %shard_map.68.refs_0_), channel_id=1, source_target_pairs={{0,8},{4,12},{8,0},{12,4},{16,24},{20,28},{24,16},{28,20},{1,9},{5... | collective-permute-start | bytes 786440 | tf_op jit(solution)/shard_map/ppermute | solution.py:43
  65.6 5.6 %collective-permute-done.21.refs_1_ = bf16[64,8,256]{2,1,0:T(8,128)(2,1)S(1)} collective-permute-done((bf16[64,8,256]{2,1,0:T(8,128)(2,1)S(1)}, bf16[64,8,256]{2,1,0:T(8,128)(2,1)S(1)}, u32[]{:S(2)}, u32[]{:S(2)}) %collective-permute-start.21) | collective-permute-done | bytes 262176 | tf_op jit(solution)/shard_map/ppermute | solution.py:43
  71.3 1.7 %collective-permute-start.23 = (bf16[64,8,256]{2,1,0:T(8,128)(2,1)S(1)}, bf16[64,8,256]{2,1,0:T(8,128)(2,1)S(1)}, u32[]{:S(2)}, u32[]{:S(2)}) collective-permute-start(bf16[64,8,256]{2,1,0:T(8,128)(2,1)S(1)} %shard_map.67.refs_0_), channel_id=1, source_target_pairs={{0,4},{4,0},{8,12},{12,8},{16,20},{20,16},{24,28},{28,24},{1,5},{5... | collective-permute-start | bytes 786440 | tf_op jit(solution)/shard_map/ppermute | solution.py:43
  78.1 1.8 %collective-permute-start.29 = (bf16[64,8,256]{2,1,0:T(8,128)(2,1)S(1)}, bf16[64,8,256]{2,1,0:T(8,128)(2,1)S(1)}, u32[]{:S(2)}, u32[]{:S(2)}) collective-permute-start(bf16[64,8,256]{2,1,0:T(8,128)(2,1)S(1)} %collective-permute-done.25.refs_1_), channel_id=1, source_target_pairs={{0,4},{4,0},{8,12},{12,8},{16,20},{20,16},{24,28},{28,24},{1,5},{5... | collective-permute-start | bytes 786440 | tf_op jit(solution)/shard_map/ppermute | solution.py:43
  81.3 1.8 %collective-permute-done.24.refs_3_ = bf16[64,8,256]{2,1,0:T(8,128)(2,1)S(1)} collective-permute-done((bf16[64,8,256]{2,1,0:T(8,128)(2,1)S(1)}, bf16[64,8,256]{2,1,0:T(8,128)(2,1)S(1)}, u32[]{:S(2)}, u32[]{:S(2)}) %collective-permute-start.24) | collective-permute-done | bytes 262176 | tf_op jit(solution)/shard_map/ppermute | solution.py:43
  85.6 2.0 %collective-permute-start.33 = (bf16[64,8,256]{2,1,0:T(8,128)(2,1)S(1)}, bf16[64,8,256]{2,1,0:T(8,128)(2,1)S(1)}, u32[]{:S(2)}, u32[]{:S(2)}) collective-permute-start(bf16[64,8,256]{2,1,0:T(8,128)(2,1)S(1)} %shard_map.74.refs_0_), channel_id=1, source_target_pairs={{0,8},{4,12},{8,0},{12,4},{16,24},{20,28},{24,16},{28,20},{1,9},{5... | collective-permute-start | bytes 786440 | tf_op jit(solution)/shard_map/ppermute | solution.py:43
  92.8 1.7 %collective-permute-start.36 = (bf16[64,8,256]{2,1,0:T(8,128)(2,1)S(1)}, bf16[64,8,256]{2,1,0:T(8,128)(2,1)S(1)}, u32[]{:S(2)}, u32[]{:S(2)}) collective-permute-start(bf16[64,8,256]{2,1,0:T(8,128)(2,1)S(1)} %shard_map.74.refs_0_), channel_id=1, source_target_pairs={{0,4},{4,0},{8,12},{12,8},{16,20},{20,16},{24,28},{28,24},{1,5},{5... | collective-permute-start | bytes 786440 | tf_op jit(solution)/shard_map/ppermute | solution.py:43
  95.7 3.6 %collective-permute-done.34.refs_1_ = bf16[64,8,256]{2,1,0:T(8,128)(2,1)S(1)} collective-permute-done((bf16[64,8,256]{2,1,0:T(8,128)(2,1)S(1)}, bf16[64,8,256]{2,1,0:T(8,128)(2,1)S(1)}, u32[]{:S(2)}, u32[]{:S(2)}) %collective-permute-start.34) | collective-permute-done | bytes 262176 | tf_op jit(solution)/shard_map/ppermute | solution.py:43
  100.5 2.6 %collective-permute-start.37 = (bf16[64,8,256]{2,1,0:T(8,128)(2,1)S(1)}, bf16[64,8,256]{2,1,0:T(8,128)(2,1)S(1)}, u32[]{:S(2)}, u32[]{:S(2)}) collective-permute-start(bf16[64,8,256]{2,1,0:T(8,128)(2,1)S(1)} %collective-permute-done.33.refs_1_), channel_id=1, source_target_pairs={{0,4},{4,0},{8,12},{12,8},{16,20},{20,16},{24,28},{28,24},{1,5},{5... | collective-permute-start | bytes 786440 | tf_op jit(solution)/shard_map/ppermute | solution.py:43
  103.1 5.4 %collective-permute-done.32.refs_1_ = bf16[64,8,256]{2,1,0:T(8,128)(2,1)S(1)} collective-permute-done((bf16[64,8,256]{2,1,0:T(8,128)(2,1)S(1)}, bf16[64,8,256]{2,1,0:T(8,128)(2,1)S(1)}, u32[]{:S(2)}, u32[]{:S(2)}) %collective-permute-start.32) | collective-permute-done | bytes 262176 | tf_op jit(solution)/shard_map/ppermute | solution.py:43
  112.6 3.2 %collective-permute-done.39.refs_2_ = bf16[64,8,256]{2,1,0:T(8,128)(2,1)S(1)} collective-permute-done((bf16[64,8,256]{2,1,0:T(8,128)(2,1)S(1)}, bf16[64,8,256]{2,1,0:T(8,128)(2,1)S(1)}, u32[]{:S(2)}, u32[]{:S(2)}) %collective-permute-start.39) | collective-permute-done | bytes 262176 | tf_op jit(solution)/shard_map/ppermute | solution.py:43
  115.9 3.9 %collective-permute-done.40.refs_3_ = bf16[64,8,256]{2,1,0:T(8,128)(2,1)S(1)} collective-permute-done((bf16[64,8,256]{2,1,0:T(8,128)(2,1)S(1)}, bf16[64,8,256]{2,1,0:T(8,128)(2,1)S(1)}, u32[]{:S(2)}, u32[]{:S(2)}) %collective-permute-start.40) | collective-permute-done | bytes 262176 | tf_op jit(solution)/shard_map/ppermute | solution.py:43
  123.6 6.4 %collective-permute-done.44.refs_1_ = bf16[64,8,256]{2,1,0:T(8,128)(2,1)S(1)} collective-permute-done((bf16[64,8,256]{2,1,0:T(8,128)(2,1)S(1)}, bf16[64,8,256]{2,1,0:T(8,128)(2,1)S(1)}, u32[]{:S(2)}, u32[]{:S(2)}) %collective-permute-start.44) | collective-permute-done | bytes 262176 | tf_op jit(solution)/shard_map/ppermute | solution.py:43
  132.2 3.4 %collective-permute-done.41.refs_1_ = bf16[64,8,256]{2,1,0:T(8,128)(2,1)S(1)} collective-permute-done((bf16[64,8,256]{2,1,0:T(8,128)(2,1)S(1)}, bf16[64,8,256]{2,1,0:T(8,128)(2,1)S(1)}, u32[]{:S(2)}, u32[]{:S(2)}) %collective-permute-start.41) | collective-permute-done | bytes 262176 | tf_op jit(solution)/shard_map/ppermute | solution.py:43
  138.2 4.0 %collective-permute-done.45.refs_1_ = bf16[8,8192]{1,0:T(8,128)(2,1)S(1)} collective-permute-done((bf16[8,8192]{1,0:T(8,128)(2,1)S(1)}, bf16[8,8192]{1,0:T(8,128)(2,1)S(1)}, u32[]{:S(2)}, u32[]{:S(2)}) %collective-permute-start.45) | collective-permute-done | bytes 131104 | tf_op jit(solution)/shard_map/ppermute | solution.py:43
  (115 shorter events, 65.7 us)
Async XLA Ops:
  0.6 30.6 %collective-permute-start.11 = (bf16[8192,256]{1,0:T(8,128)(2,1)}, bf16[8192,256]{1,0:T(8,128)(2,1)}, u32[]{:S(2)}, u32[]{:S(2)}) collective-permute-start(bf16[8192,256]{1,0:T(8,128)(2,1)} %refs_2_.7), channel_id=1, source_target_pairs={{0,1},{1,0},{2,3},{3,2},{4,5},{5,4},{6,7},{7,6},{8,9},{9,8},{10,11... | collective-permute-start | bytes 12582920 | tf_op jit(solution)/shard_map/ppermute | solution.py:43
  10.2 13.9 %collective-permute-start.6 = (bf16[64,8,256]{2,1,0:T(8,128)(2,1)S(1)}, bf16[64,8,256]{2,1,0:T(8,128)(2,1)S(1)}, u32[]{:S(2)}, u32[]{:S(2)}) collective-permute-start(bf16[64,8,256]{2,1,0:T(8,128)(2,1)S(1)} %get-tuple-element.149.refs_0_), channel_id=1, source_target_pairs={{0,4},{4,0},{8,12},{12,8},{16,20},{20,16},{24,28},{28,24},{1,5},{5... | collective-permute-start | bytes 786440 | tf_op jit(solution)/shard_map/ppermute | solution.py:43
  12.1 10.5 %collective-permute-start.8 = (bf16[64,8,256]{2,1,0:T(8,128)(2,1)S(1)}, bf16[64,8,256]{2,1,0:T(8,128)(2,1)S(1)}, u32[]{:S(2)}, u32[]{:S(2)}) collective-permute-start(bf16[64,8,256]{2,1,0:T(8,128)(2,1)S(1)} %collective-permute-done.5.refs_0_), channel_id=1, source_target_pairs={{0,8},{4,12},{8,0},{12,4},{16,24},{20,28},{24,16},{28,20},{1,9},{5... | collective-permute-start | bytes 786440 | tf_op jit(solution)/shard_map/ppermute | solution.py:43
  19.3 15.8 %collective-permute-start.9 = (bf16[64,8,256]{2,1,0:T(8,128)(2,1)S(1)}, bf16[64,8,256]{2,1,0:T(8,128)(2,1)S(1)}, u32[]{:S(2)}, u32[]{:S(2)}) collective-permute-start(bf16[64,8,256]{2,1,0:T(8,128)(2,1)S(1)} %collective-permute-done.5.refs_0_), channel_id=1, source_target_pairs={{0,4},{4,0},{8,12},{12,8},{16,20},{20,16},{24,28},{28,24},{1,5},{5... | collective-permute-start | bytes 786440 | tf_op jit(solution)/shard_map/ppermute | solution.py:43
  22.6 15.6 %collective-permute-start.10 = (bf16[64,8,256]{2,1,0:T(8,128)(2,1)S(1)}, bf16[64,8,256]{2,1,0:T(8,128)(2,1)S(1)}, u32[]{:S(2)}, u32[]{:S(2)}) collective-permute-start(bf16[64,8,256]{2,1,0:T(8,128)(2,1)S(1)} %collective-permute-done.8.refs_1_), channel_id=1, source_target_pairs={{0,4},{4,0},{8,12},{12,8},{16,20},{20,16},{24,28},{28,24},{1,5},{5... | collective-permute-start | bytes 786440 | tf_op jit(solution)/shard_map/ppermute | solution.py:43
  28.1 14.3 %collective-permute-start.12 = (bf16[64,8,256]{2,1,0:T(8,128)(2,1)S(1)}, bf16[64,8,256]{2,1,0:T(8,128)(2,1)S(1)}, u32[]{:S(2)}, u32[]{:S(2)}) collective-permute-start(bf16[64,8,256]{2,1,0:T(8,128)(2,1)S(1)} %get-tuple-element.154), channel_id=1, source_target_pairs={{0,16},{4,20},{8,24},{12,28},{16,0},{20,4},{24,8},{28,12},{1,17},{... | collective-permute-start | bytes 786440 | tf_op jit(solution)/shard_map/ppermute | solution.py:43
  29.6 16.7 %collective-permute-start.1 = (bf16[64,8,256]{2,1,0:T(8,128)(2,1)S(1)}, bf16[64,8,256]{2,1,0:T(8,128)(2,1)S(1)}, u32[]{:S(2)}, u32[]{:S(2)}) collective-permute-start(bf16[64,8,256]{2,1,0:T(8,128)(2,1)S(1)} %get-tuple-element.174.refs_0_), channel_id=1, source_target_pairs={{0,8},{4,12},{8,0},{12,4},{16,24},{20,28},{24,16},{28,20},{1,9},{5... | collective-permute-start | bytes 786440 | tf_op jit(solution)/shard_map/ppermute | solution.py:43
  31.2 15.1 %collective-permute-start.2 = (bf16[64,8,256]{2,1,0:T(8,128)(2,1)S(1)}, bf16[64,8,256]{2,1,0:T(8,128)(2,1)S(1)}, u32[]{:S(2)}, u32[]{:S(2)}) collective-permute-start(bf16[64,8,256]{2,1,0:T(8,128)(2,1)S(1)} %get-tuple-element.174.refs_0_), channel_id=1, source_target_pairs={{0,4},{4,0},{8,12},{12,8},{16,20},{20,16},{24,28},{28,24},{1,5},{5... | collective-permute-start | bytes 786440 | tf_op jit(solution)/shard_map/ppermute | solution.py:43
  39.3 11.0 %collective-permute-start.14 = (bf16[64,8,256]{2,1,0:T(8,128)(2,1)S(1)}, bf16[64,8,256]{2,1,0:T(8,128)(2,1)S(1)}, u32[]{:S(2)}, u32[]{:S(2)}) collective-permute-start(bf16[64,8,256]{2,1,0:T(8,128)(2,1)S(1)} %get-tuple-element.161), channel_id=1, source_target_pairs={{0,16},{4,20},{8,24},{12,28},{16,0},{20,4},{24,8},{28,12},{1,17},{... | collective-permute-start | bytes 786440 | tf_op jit(solution)/shard_map/ppermute | solution.py:43
  50.7 10.5 %collective-permute-start.17 = (bf16[64,8,256]{2,1,0:T(8,128)(2,1)S(1)}, bf16[64,8,256]{2,1,0:T(8,128)(2,1)S(1)}, u32[]{:S(2)}, u32[]{:S(2)}) collective-permute-start(bf16[64,8,256]{2,1,0:T(8,128)(2,1)S(1)} %collective-permute-done.15.refs_1_), channel_id=1, source_target_pairs={{0,4},{4,0},{8,12},{12,8},{16,20},{20,16},{24,28},{28,24},{1,5},{5... | collective-permute-start | bytes 786440 | tf_op jit(solution)/shard_map/ppermute | solution.py:43
  57.0 14.3 %collective-permute-start.21 = (bf16[64,8,256]{2,1,0:T(8,128)(2,1)S(1)}, bf16[64,8,256]{2,1,0:T(8,128)(2,1)S(1)}, u32[]{:S(2)}, u32[]{:S(2)}) collective-permute-start(bf16[64,8,256]{2,1,0:T(8,128)(2,1)S(1)} %get-tuple-element.180), channel_id=1, source_target_pairs={{0,16},{4,20},{8,24},{12,28},{16,0},{20,4},{24,8},{28,12},{1,17},{... | collective-permute-start | bytes 786440 | tf_op jit(solution)/shard_map/ppermute | solution.py:43
  60.1 15.3 %collective-permute-start.20 = (bf16[64,8,256]{2,1,0:T(8,128)(2,1)S(1)}, bf16[64,8,256]{2,1,0:T(8,128)(2,1)S(1)}, u32[]{:S(2)}, u32[]{:S(2)}) collective-permute-start(bf16[64,8,256]{2,1,0:T(8,128)(2,1)S(1)} %shard_map.67.refs_0_), channel_id=1, source_target_pairs={{0,8},{4,12},{8,0},{12,4},{16,24},{20,28},{24,16},{28,20},{1,9},{5... | collective-permute-start | bytes 786440 | tf_op jit(solution)/shard_map/ppermute | solution.py:43
  62.3 14.6 %collective-permute-start.19 = (bf16[64,8,256]{2,1,0:T(8,128)(2,1)S(1)}, bf16[64,8,256]{2,1,0:T(8,128)(2,1)S(1)}, u32[]{:S(2)}, u32[]{:S(2)}) collective-permute-start(bf16[64,8,256]{2,1,0:T(8,128)(2,1)S(1)} %get-tuple-element.190), channel_id=1, source_target_pairs={{0,16},{4,20},{8,24},{12,28},{16,0},{20,4},{24,8},{28,12},{1,17},{... | collective-permute-start | bytes 786440 | tf_op jit(solution)/shard_map/ppermute | solution.py:43
  63.6 14.5 %collective-permute-start.25 = (bf16[64,8,256]{2,1,0:T(8,128)(2,1)S(1)}, bf16[64,8,256]{2,1,0:T(8,128)(2,1)S(1)}, u32[]{:S(2)}, u32[]{:S(2)}) collective-permute-start(bf16[64,8,256]{2,1,0:T(8,128)(2,1)S(1)} %shard_map.68.refs_0_), channel_id=1, source_target_pairs={{0,8},{4,12},{8,0},{12,4},{16,24},{20,28},{24,16},{28,20},{1,9},{5... | collective-permute-start | bytes 786440 | tf_op jit(solution)/shard_map/ppermute | solution.py:43
  65.3 12.8 %collective-permute-start.26 = (bf16[64,8,256]{2,1,0:T(8,128)(2,1)S(1)}, bf16[64,8,256]{2,1,0:T(8,128)(2,1)S(1)}, u32[]{:S(2)}, u32[]{:S(2)}) collective-permute-start(bf16[64,8,256]{2,1,0:T(8,128)(2,1)S(1)} %shard_map.68.refs_0_), channel_id=1, source_target_pairs={{0,4},{4,0},{8,12},{12,8},{16,20},{20,16},{24,28},{28,24},{1,5},{5... | collective-permute-start | bytes 786440 | tf_op jit(solution)/shard_map/ppermute | solution.py:43
  78.1 11.0 %collective-permute-start.29 = (bf16[64,8,256]{2,1,0:T(8,128)(2,1)S(1)}, bf16[64,8,256]{2,1,0:T(8,128)(2,1)S(1)}, u32[]{:S(2)}, u32[]{:S(2)}) collective-permute-start(bf16[64,8,256]{2,1,0:T(8,128)(2,1)S(1)} %collective-permute-done.25.refs_1_), channel_id=1, source_target_pairs={{0,4},{4,0},{8,12},{12,8},{16,20},{20,16},{24,28},{28,24},{1,5},{5... | collective-permute-start | bytes 786440 | tf_op jit(solution)/shard_map/ppermute | solution.py:43
  84.2 15.1 %collective-permute-start.34 = (bf16[64,8,256]{2,1,0:T(8,128)(2,1)S(1)}, bf16[64,8,256]{2,1,0:T(8,128)(2,1)S(1)}, u32[]{:S(2)}, u32[]{:S(2)}) collective-permute-start(bf16[64,8,256]{2,1,0:T(8,128)(2,1)S(1)} %get-tuple-element.205), channel_id=1, source_target_pairs={{0,16},{4,20},{8,24},{12,28},{16,0},{20,4},{24,8},{28,12},{1,17},{... | collective-permute-start | bytes 786440 | tf_op jit(solution)/shard_map/ppermute | solution.py:43
  85.6 14.9 %collective-permute-start.33 = (bf16[64,8,256]{2,1,0:T(8,128)(2,1)S(1)}, bf16[64,8,256]{2,1,0:T(8,128)(2,1)S(1)}, u32[]{:S(2)}, u32[]{:S(2)}) collective-permute-start(bf16[64,8,256]{2,1,0:T(8,128)(2,1)S(1)} %shard_map.74.refs_0_), channel_id=1, source_target_pairs={{0,8},{4,12},{8,0},{12,4},{16,24},{20,28},{24,16},{28,20},{1,9},{5... | collective-permute-start | bytes 786440 | tf_op jit(solution)/shard_map/ppermute | solution.py:43
  90.4 18.1 %collective-permute-start.32 = (bf16[64,8,256]{2,1,0:T(8,128)(2,1)S(1)}, bf16[64,8,256]{2,1,0:T(8,128)(2,1)S(1)}, u32[]{:S(2)}, u32[]{:S(2)}) collective-permute-start(bf16[64,8,256]{2,1,0:T(8,128)(2,1)S(1)} %get-tuple-element.219), channel_id=1, source_target_pairs={{0,16},{4,20},{8,24},{12,28},{16,0},{20,4},{24,8},{28,12},{1,17},{... | collective-permute-start | bytes 786440 | tf_op jit(solution)/shard_map/ppermute | solution.py:43
  91.6 18.1 %collective-permute-start.38 = (bf16[64,8,256]{2,1,0:T(8,128)(2,1)S(1)}, bf16[64,8,256]{2,1,0:T(8,128)(2,1)S(1)}, u32[]{:S(2)}, u32[]{:S(2)}) collective-permute-start(bf16[64,8,256]{2,1,0:T(8,128)(2,1)S(1)} %shard_map.76.refs_0_), channel_id=1, source_target_pairs={{0,8},{4,12},{8,0},{12,4},{16,24},{20,28},{24,16},{28,20},{1,9},{5... | collective-permute-start | bytes 786440 | tf_op jit(solution)/shard_map/ppermute | solution.py:43
  92.8 17.5 %collective-permute-start.36 = (bf16[64,8,256]{2,1,0:T(8,128)(2,1)S(1)}, bf16[64,8,256]{2,1,0:T(8,128)(2,1)S(1)}, u32[]{:S(2)}, u32[]{:S(2)}) collective-permute-start(bf16[64,8,256]{2,1,0:T(8,128)(2,1)S(1)} %shard_map.74.refs_0_), channel_id=1, source_target_pairs={{0,4},{4,0},{8,12},{12,8},{16,20},{20,16},{24,28},{28,24},{1,5},{5... | collective-permute-start | bytes 786440 | tf_op jit(solution)/shard_map/ppermute | solution.py:43
  103.0 12.8 %collective-permute-start.39 = (bf16[64,8,256]{2,1,0:T(8,128)(2,1)S(1)}, bf16[64,8,256]{2,1,0:T(8,128)(2,1)S(1)}, u32[]{:S(2)}, u32[]{:S(2)}) collective-permute-start(bf16[64,8,256]{2,1,0:T(8,128)(2,1)S(1)} %shard_map.76.refs_0_), channel_id=1, source_target_pairs={{0,4},{4,0},{8,12},{12,8},{16,20},{20,16},{24,28},{28,24},{1,5},{5... | collective-permute-start | bytes 786440 | tf_op jit(solution)/shard_map/ppermute | solution.py:43
  111.4 18.6 %collective-permute-start.44 = (bf16[64,8,256]{2,1,0:T(8,128)(2,1)S(1)}, bf16[64,8,256]{2,1,0:T(8,128)(2,1)S(1)}, u32[]{:S(2)}, u32[]{:S(2)}) collective-permute-start(bf16[64,8,256]{2,1,0:T(8,128)(2,1)S(1)} %get-tuple-element.235), channel_id=1, source_target_pairs={{0,16},{4,20},{8,24},{12,28},{16,0},{20,4},{24,8},{28,12},{1,17},{... | collective-permute-start | bytes 786440 | tf_op jit(solution)/shard_map/ppermute | solution.py:43
  120.8 14.7 %collective-permute-start.41 = (bf16[64,8,256]{2,1,0:T(8,128)(2,1)S(1)}, bf16[64,8,256]{2,1,0:T(8,128)(2,1)S(1)}, u32[]{:S(2)}, u32[]{:S(2)}) collective-permute-start(bf16[64,8,256]{2,1,0:T(8,128)(2,1)S(1)} %get-tuple-element.241), channel_id=1, source_target_pairs={{0,16},{4,20},{8,24},{12,28},{16,0},{20,4},{24,8},{28,12},{1,17},{... | collective-permute-start | bytes 786440 | tf_op jit(solution)/shard_map/ppermute | solution.py:43
  (28 other events, 204.4 us)

commit v16 on v15

--- a/solution.py
+++ b/solution.py
@@ -16,17 +16,17 @@
 SIDE, NEXT = 1, 2
 
 ORDER = (
-    "As Al Am Bm",
+    "As Am Al Bm",
     "Af1 Af2 Ao1 Ak",
     "Ao2 Aw Ae1 Bg1",
-    "Az2 Bg2 Ae2 Bo1",
-    "As1 As2 Bo2 Bw",
-    "Be1 Af1 Be2 Ag2",
-    "Ao1 Bs1 Ap Bs2",
-    "Ao2 Aw Ae1 Bf1",
-    "Ae2 Bf2 Bo1 Bo2",
-    "Bw Ar Bp Be1",
-    "Au Be2 Br Bu",
+    "Ae2 Bg2 Bo1 As1",
+    "As2 Bo2 Bw Be1",
+    "Af1 Be2 Ag2 Ao1",
+    "Bs1 Ap Bs2 Ao2",
+    "Aw Ae1 Bf1 Ae2",
+    "Bf2 Bo1 Bo2 Bw",
+    "Ar Bp Be1 Au",
+    "Be2 Br Bu",
 )
 
 VMEM = pl.BlockSpec(memory_space=pltpu.VMEM)

time: 145 us -> 146 us (level)
  waiting for transfers between devices: 59.3 us -> 62.5 us
  starting transfers between devices: 49 us -> 46.5 us
    ppermute x48, waiting for transfers between devices: 59.3 us -> 62.5 us  [swap(): return lax.ppermute(value, axis, [(i, i ^ mask) for i in range(size)])]
    ppermute x48, starting transfers between devices: 49 us -> 46.5 us  [swap(): return lax.ppermute(value, axis, [(i, i ^ mask) for i in range(size)])]
where the time goes in v16:
time: 146 us; the launch traced here: 145 us
  waiting for transfers between devices  62.5 us (43%)
  starting transfers between devices  46.5 us (32%)
  Pallas kernels  34.9 us (24%)
    ppermute x48, waiting for transfers between devices, swap(): return lax.ppermute(value, axis, [(i, i ^ mask) for i in range(size)])  62.5 us
    ppermute x48, starting transfers between devices, swap(): return lax.ppermute(value, axis, [(i, i ^ mask) for i in range(size)])  46.5 us
    pallas_call x8, Pallas kernels, expand(): pl.pallas_call(expand_kernel, in_specs=[VMEM] * (len(values) + 1), out_sp...  9.51 us
    pallas_call x8, Pallas kernels, combine_far(): pl.pallas_call(table_kernel, in_specs=[SMEM] + [VMEM] * len(shards), out_...  8.94 us
    pallas_call x4, Pallas kernels, combine(): pl.pallas_call(lookup_kernel, in_specs=[SMEM] + [VMEM] * len(tables), out...  4.62 us
    pallas_call x4, Pallas kernels, fill(): pl.pallas_call(functools.partial(fill_kernel, c, bool(before)), in_specs=...  3.62 us
    pallas_call x1, Pallas kernels, first_sums(): pl.pallas_call(first_sums_kernel, in_specs=[SMEM] + [HBM] * 3, out_specs=...  3.19 us
  transfers between devices with their start and end apart: 48, of which 19 were waited for; matrix products, arithmetic and copies ran while one was open for 0% of the time, Pallas kernels for 23%

profile of v16, /device:TPU:0, one launch (start us, length us, event | category | flops | bytes accessed | tf_op | source)
XLA Modules:
  0.0 145.4 jit_solution(7285042528623706982)
XLA Ops:
  1.1 3.7 %collective-permute-start = (s32[64,8]{0,1:T(8,128)}, s32[64,8]{0,1:T(8,128)S(1)}, u32[]{:S(2)}, u32[]{:S(2)}) collective-permute-start(s32[64,8]{0,1:T(8,128)} %param.7), channel_id=1, source_target_pairs={{0,16},{4,20},{8,24},{12,28},{16,0},{20,4},{24,8},{28,12},{1,17},{... | collective-permute-start | bytes 6152 | tf_op jit(solution)/shard_map/ppermute | solution.py:43
  4.8 3.2 %shard_map.59 = (bf16[64,8,256]{2,1,0:T(8,128)(2,1)S(1)}, bf16[64,8,256]{2,1,0:T(8,128)(2,1)S(1)}, bf16[64,8,256]{2,1,0:T(8,128)(2,1)S(1)}, bf16[64,8,256]{2,1,0:T(8,128)(2,1)S(1)}) custom-call(s32[1]{0:T(128)} %bitcast.core_ref, f32[32,8192]{1,0:T(8,128)} %vec_ref.17, f32[1,8192]{1,0:T(1,128)} %bitcast.2, bf16[8192,256]{1,0:T(8,128)(2,1)} %refs_2_.7), custom_call_target="tpu_custom_call" | custom-call | tf_op jit(solution)/shard_map/pallas_call | solution.py:228
  8.6 1.6 %collective-permute-start.4 = (bf16[64,8,256]{2,1,0:T(8,128)(2,1)S(1)}, bf16[64,8,256]{2,1,0:T(8,128)(2,1)S(1)}, u32[]{:S(2)}, u32[]{:S(2)}) collective-permute-start(bf16[64,8,256]{2,1,0:T(8,128)(2,1)S(1)} %get-tuple-element.148.refs_0_), channel_id=1, source_target_pairs={{0,8},{4,12},{8,0},{12,4},{16,24},{20,28},{24,16},{28,20},{1,9},{5... | collective-permute-start | bytes 786440 | tf_op jit(solution)/shard_map/ppermute | solution.py:43
  12.5 5.2 %collective-permute-done.4.refs_1_ = bf16[64,8,256]{2,1,0:T(8,128)(2,1)S(1)} collective-permute-done((bf16[64,8,256]{2,1,0:T(8,128)(2,1)S(1)}, bf16[64,8,256]{2,1,0:T(8,128)(2,1)S(1)}, u32[]{:S(2)}, u32[]{:S(2)}) %collective-permute-start.4) | collective-permute-done | bytes 262176 | tf_op jit(solution)/shard_map/ppermute | solution.py:43
  19.8 2.8 %collective-permute-done.8.refs_1_ = bf16[64,8,256]{2,1,0:T(8,128)(2,1)S(1)} collective-permute-done((bf16[64,8,256]{2,1,0:T(8,128)(2,1)S(1)}, bf16[64,8,256]{2,1,0:T(8,128)(2,1)S(1)}, u32[]{:S(2)}, u32[]{:S(2)}) %collective-permute-start.8) | collective-permute-done | bytes 262176 | tf_op jit(solution)/shard_map/ppermute | solution.py:43
  24.1 2.9 %collective-permute-done.7.refs_3_ = bf16[64,8,256]{2,1,0:T(8,128)(2,1)S(1)} collective-permute-done((bf16[64,8,256]{2,1,0:T(8,128)(2,1)S(1)}, bf16[64,8,256]{2,1,0:T(8,128)(2,1)S(1)}, u32[]{:S(2)}, u32[]{:S(2)}) %collective-permute-start.7) | collective-permute-done | bytes 262176 | tf_op jit(solution)/shard_map/ppermute | solution.py:43
  29.6 1.6 %collective-permute-start.2 = (bf16[64,8,256]{2,1,0:T(8,128)(2,1)S(1)}, bf16[64,8,256]{2,1,0:T(8,128)(2,1)S(1)}, u32[]{:S(2)}, u32[]{:S(2)}) collective-permute-start(bf16[64,8,256]{2,1,0:T(8,128)(2,1)S(1)} %get-tuple-element.172.refs_0_), channel_id=1, source_target_pairs={{0,8},{4,12},{8,0},{12,4},{16,24},{20,28},{24,16},{28,20},{1,9},{5... | collective-permute-start | bytes 786440 | tf_op jit(solution)/shard_map/ppermute | solution.py:43
  32.7 2.3 %shard_map.61.refs_3_.emb_ref = bf16[8192,256]{1,0:T(8,128)(2,1)S(1)} custom-call(bf16[8192,256]{1,0:T(8,128)(2,1)} %collective-permute-done.11.src_ref), custom_call_target="tpu_custom_call" | custom-call | tf_op jit(solution)/shard_map/pallas_call | solution.py:243
  35.1 3.1 %collective-permute-done.10.refs_3_ = bf16[64,8,256]{2,1,0:T(8,128)(2,1)S(1)} collective-permute-done((bf16[64,8,256]{2,1,0:T(8,128)(2,1)S(1)}, bf16[64,8,256]{2,1,0:T(8,128)(2,1)S(1)}, u32[]{:S(2)}, u32[]{:S(2)}) %collective-permute-start.10) | collective-permute-done | bytes 262176 | tf_op jit(solution)/shard_map/ppermute | solution.py:43
  40.8 1.6 %collective-permute-start.14 = (bf16[64,8,256]{2,1,0:T(8,128)(2,1)S(1)}, bf16[64,8,256]{2,1,0:T(8,128)(2,1)S(1)}, u32[]{:S(2)}, u32[]{:S(2)}) collective-permute-start(bf16[64,8,256]{2,1,0:T(8,128)(2,1)S(1)} %collective-permute-done.5.refs_0_), channel_id=1, source_target_pairs={{0,8},{4,12},{8,0},{12,4},{16,24},{20,28},{24,16},{28,20},{1,9},{5... | collective-permute-start | bytes 786440 | tf_op jit(solution)/shard_map/ppermute | solution.py:43
  46.9 3.5 %collective-permute-done.16.refs_1_ = bf16[64,8,256]{2,1,0:T(8,128)(2,1)S(1)} collective-permute-done((bf16[64,8,256]{2,1,0:T(8,128)(2,1)S(1)}, bf16[64,8,256]{2,1,0:T(8,128)(2,1)S(1)}, u32[]{:S(2)}, u32[]{:S(2)}) %collective-permute-start.16) | collective-permute-done | bytes 262176 | tf_op jit(solution)/shard_map/ppermute | solution.py:43
  61.1 2.5 %collective-permute-start.19 = (bf16[64,8,256]{2,1,0:T(8,128)(2,1)S(1)}, bf16[64,8,256]{2,1,0:T(8,128)(2,1)S(1)}, u32[]{:S(2)}, u32[]{:S(2)}) collective-permute-start(bf16[64,8,256]{2,1,0:T(8,128)(2,1)S(1)} %get-tuple-element.188), channel_id=1, source_target_pairs={{0,16},{4,20},{8,24},{12,28},{16,0},{20,4},{24,8},{28,12},{1,17},{... | collective-permute-start | bytes 786440 | tf_op jit(solution)/shard_map/ppermute | solution.py:43
  65.6 6.2 %collective-permute-done.21.refs_1_ = bf16[64,8,256]{2,1,0:T(8,128)(2,1)S(1)} collective-permute-done((bf16[64,8,256]{2,1,0:T(8,128)(2,1)S(1)}, bf16[64,8,256]{2,1,0:T(8,128)(2,1)S(1)}, u32[]{:S(2)}, u32[]{:S(2)}) %collective-permute-start.21) | collective-permute-done | bytes 262176 | tf_op jit(solution)/shard_map/ppermute | solution.py:43
  81.3 2.5 %collective-permute-done.24.refs_3_ = bf16[64,8,256]{2,1,0:T(8,128)(2,1)S(1)} collective-permute-done((bf16[64,8,256]{2,1,0:T(8,128)(2,1)S(1)}, bf16[64,8,256]{2,1,0:T(8,128)(2,1)S(1)}, u32[]{:S(2)}, u32[]{:S(2)}) %collective-permute-start.24) | collective-permute-done | bytes 262176 | tf_op jit(solution)/shard_map/ppermute | solution.py:43
  85.7 1.8 %collective-permute-start.33 = (bf16[64,8,256]{2,1,0:T(8,128)(2,1)S(1)}, bf16[64,8,256]{2,1,0:T(8,128)(2,1)S(1)}, u32[]{:S(2)}, u32[]{:S(2)}) collective-permute-start(bf16[64,8,256]{2,1,0:T(8,128)(2,1)S(1)} %shard_map.74.refs_0_), channel_id=1, source_target_pairs={{0,8},{4,12},{8,0},{12,4},{16,24},{20,28},{24,16},{28,20},{1,9},{5... | collective-permute-start | bytes 786440 | tf_op jit(solution)/shard_map/ppermute | solution.py:43
  91.6 2.0 %collective-permute-start.38 = (bf16[64,8,256]{2,1,0:T(8,128)(2,1)S(1)}, bf16[64,8,256]{2,1,0:T(8,128)(2,1)S(1)}, u32[]{:S(2)}, u32[]{:S(2)}) collective-permute-start(bf16[64,8,256]{2,1,0:T(8,128)(2,1)S(1)} %shard_map.76.refs_0_), channel_id=1, source_target_pairs={{0,8},{4,12},{8,0},{12,4},{16,24},{20,28},{24,16},{28,20},{1,9},{5... | collective-permute-start | bytes 786440 | tf_op jit(solution)/shard_map/ppermute | solution.py:43
  95.7 3.5 %collective-permute-done.34.refs_1_ = bf16[64,8,256]{2,1,0:T(8,128)(2,1)S(1)} collective-permute-done((bf16[64,8,256]{2,1,0:T(8,128)(2,1)S(1)}, bf16[64,8,256]{2,1,0:T(8,128)(2,1)S(1)}, u32[]{:S(2)}, u32[]{:S(2)}) %collective-permute-start.34) | collective-permute-done | bytes 262176 | tf_op jit(solution)/shard_map/ppermute | solution.py:43
  100.4 2.7 %collective-permute-start.37 = (bf16[64,8,256]{2,1,0:T(8,128)(2,1)S(1)}, bf16[64,8,256]{2,1,0:T(8,128)(2,1)S(1)}, u32[]{:S(2)}, u32[]{:S(2)}) collective-permute-start(bf16[64,8,256]{2,1,0:T(8,128)(2,1)S(1)} %collective-permute-done.33.refs_1_), channel_id=1, source_target_pairs={{0,4},{4,0},{8,12},{12,8},{16,20},{20,16},{24,28},{28,24},{1,5},{5... | collective-permute-start | bytes 786440 | tf_op jit(solution)/shard_map/ppermute | solution.py:43
  103.1 5.4 %collective-permute-done.32.refs_1_ = bf16[64,8,256]{2,1,0:T(8,128)(2,1)S(1)} collective-permute-done((bf16[64,8,256]{2,1,0:T(8,128)(2,1)S(1)}, bf16[64,8,256]{2,1,0:T(8,128)(2,1)S(1)}, u32[]{:S(2)}, u32[]{:S(2)}) %collective-permute-start.32) | collective-permute-done | bytes 262176 | tf_op jit(solution)/shard_map/ppermute | solution.py:43
  112.4 3.3 %collective-permute-done.39.refs_2_ = bf16[64,8,256]{2,1,0:T(8,128)(2,1)S(1)} collective-permute-done((bf16[64,8,256]{2,1,0:T(8,128)(2,1)S(1)}, bf16[64,8,256]{2,1,0:T(8,128)(2,1)S(1)}, u32[]{:S(2)}, u32[]{:S(2)}) %collective-permute-start.39) | collective-permute-done | bytes 262176 | tf_op jit(solution)/shard_map/ppermute | solution.py:43
  115.7 4.0 %collective-permute-done.40.refs_3_ = bf16[64,8,256]{2,1,0:T(8,128)(2,1)S(1)} collective-permute-done((bf16[64,8,256]{2,1,0:T(8,128)(2,1)S(1)}, bf16[64,8,256]{2,1,0:T(8,128)(2,1)S(1)}, u32[]{:S(2)}, u32[]{:S(2)}) %collective-permute-start.40) | collective-permute-done | bytes 262176 | tf_op jit(solution)/shard_map/ppermute | solution.py:43
  123.6 7.2 %collective-permute-done.44.refs_1_ = bf16[64,8,256]{2,1,0:T(8,128)(2,1)S(1)} collective-permute-done((bf16[64,8,256]{2,1,0:T(8,128)(2,1)S(1)}, bf16[64,8,256]{2,1,0:T(8,128)(2,1)S(1)}, u32[]{:S(2)}, u32[]{:S(2)}) %collective-permute-start.44) | collective-permute-done | bytes 262176 | tf_op jit(solution)/shard_map/ppermute | solution.py:43
  133.0 3.4 %collective-permute-done.41.refs_1_ = bf16[64,8,256]{2,1,0:T(8,128)(2,1)S(1)} collective-permute-done((bf16[64,8,256]{2,1,0:T(8,128)(2,1)S(1)}, bf16[64,8,256]{2,1,0:T(8,128)(2,1)S(1)}, u32[]{:S(2)}, u32[]{:S(2)}) %collective-permute-start.41) | collective-permute-done | bytes 262176 | tf_op jit(solution)/shard_map/ppermute | solution.py:43
  137.9 5.0 %collective-permute-done.45.refs_1_ = bf16[8,8192]{1,0:T(8,128)(2,1)S(1)} collective-permute-done((bf16[8,8192]{1,0:T(8,128)(2,1)S(1)}, bf16[8,8192]{1,0:T(8,128)(2,1)S(1)}, u32[]{:S(2)}, u32[]{:S(2)}) %collective-permute-start.45) | collective-permute-done | bytes 131104 | tf_op jit(solution)/shard_map/ppermute | solution.py:43
  (115 shorter events, 63.3 us)
Async XLA Ops:
  0.6 30.6 %collective-permute-start.11 = (bf16[8192,256]{1,0:T(8,128)(2,1)}, bf16[8192,256]{1,0:T(8,128)(2,1)}, u32[]{:S(2)}, u32[]{:S(2)}) collective-permute-start(bf16[8192,256]{1,0:T(8,128)(2,1)} %refs_2_.7), channel_id=1, source_target_pairs={{0,1},{1,0},{2,3},{3,2},{4,5},{5,4},{6,7},{7,6},{8,9},{9,8},{10,11... | collective-permute-start | bytes 12582920 | tf_op jit(solution)/shard_map/ppermute | solution.py:43
  10.2 13.9 %collective-permute-start.6 = (bf16[64,8,256]{2,1,0:T(8,128)(2,1)S(1)}, bf16[64,8,256]{2,1,0:T(8,128)(2,1)S(1)}, u32[]{:S(2)}, u32[]{:S(2)}) collective-permute-start(bf16[64,8,256]{2,1,0:T(8,128)(2,1)S(1)} %get-tuple-element.148.refs_0_), channel_id=1, source_target_pairs={{0,4},{4,0},{8,12},{12,8},{16,20},{20,16},{24,28},{28,24},{1,5},{5... | collective-permute-start | bytes 786440 | tf_op jit(solution)/shard_map/ppermute | solution.py:43
  11.7 10.9 %collective-permute-start.8 = (bf16[64,8,256]{2,1,0:T(8,128)(2,1)S(1)}, bf16[64,8,256]{2,1,0:T(8,128)(2,1)S(1)}, u32[]{:S(2)}, u32[]{:S(2)}) collective-permute-start(bf16[64,8,256]{2,1,0:T(8,128)(2,1)S(1)} %collective-permute-done.1.refs_0_), channel_id=1, source_target_pairs={{0,8},{4,12},{8,0},{12,4},{16,24},{20,28},{24,16},{28,20},{1,9},{5... | collective-permute-start | bytes 786440 | tf_op jit(solution)/shard_map/ppermute | solution.py:43
  19.3 15.8 %collective-permute-start.9 = (bf16[64,8,256]{2,1,0:T(8,128)(2,1)S(1)}, bf16[64,8,256]{2,1,0:T(8,128)(2,1)S(1)}, u32[]{:S(2)}, u32[]{:S(2)}) collective-permute-start(bf16[64,8,256]{2,1,0:T(8,128)(2,1)S(1)} %collective-permute-done.1.refs_0_), channel_id=1, source_target_pairs={{0,4},{4,0},{8,12},{12,8},{16,20},{20,16},{24,28},{28,24},{1,5},{5... | collective-permute-start | bytes 786440 | tf_op jit(solution)/shard_map/ppermute | solution.py:43
  22.6 15.6 %collective-permute-start.10 = (bf16[64,8,256]{2,1,0:T(8,128)(2,1)S(1)}, bf16[64,8,256]{2,1,0:T(8,128)(2,1)S(1)}, u32[]{:S(2)}, u32[]{:S(2)}) collective-permute-start(bf16[64,8,256]{2,1,0:T(8,128)(2,1)S(1)} %collective-permute-done.8.refs_1_), channel_id=1, source_target_pairs={{0,4},{4,0},{8,12},{12,8},{16,20},{20,16},{24,28},{28,24},{1,5},{5... | collective-permute-start | bytes 786440 | tf_op jit(solution)/shard_map/ppermute | solution.py:43
  28.1 14.3 %collective-permute-start.12 = (bf16[64,8,256]{2,1,0:T(8,128)(2,1)S(1)}, bf16[64,8,256]{2,1,0:T(8,128)(2,1)S(1)}, u32[]{:S(2)}, u32[]{:S(2)}) collective-permute-start(bf16[64,8,256]{2,1,0:T(8,128)(2,1)S(1)} %get-tuple-element.153), channel_id=1, source_target_pairs={{0,16},{4,20},{8,24},{12,28},{16,0},{20,4},{24,8},{28,12},{1,17},{... | collective-permute-start | bytes 786440 | tf_op jit(solution)/shard_map/ppermute | solution.py:43
  29.6 16.7 %collective-permute-start.2 = (bf16[64,8,256]{2,1,0:T(8,128)(2,1)S(1)}, bf16[64,8,256]{2,1,0:T(8,128)(2,1)S(1)}, u32[]{:S(2)}, u32[]{:S(2)}) collective-permute-start(bf16[64,8,256]{2,1,0:T(8,128)(2,1)S(1)} %get-tuple-element.172.refs_0_), channel_id=1, source_target_pairs={{0,8},{4,12},{8,0},{12,4},{16,24},{20,28},{24,16},{28,20},{1,9},{5... | collective-permute-start | bytes 786440 | tf_op jit(solution)/shard_map/ppermute | solution.py:43
  31.2 15.1 %collective-permute-start.3 = (bf16[64,8,256]{2,1,0:T(8,128)(2,1)S(1)}, bf16[64,8,256]{2,1,0:T(8,128)(2,1)S(1)}, u32[]{:S(2)}, u32[]{:S(2)}) collective-permute-start(bf16[64,8,256]{2,1,0:T(8,128)(2,1)S(1)} %get-tuple-element.172.refs_0_), channel_id=1, source_target_pairs={{0,4},{4,0},{8,12},{12,8},{16,20},{20,16},{24,28},{28,24},{1,5},{5... | collective-permute-start | bytes 786440 | tf_op jit(solution)/shard_map/ppermute | solution.py:43
  39.3 11.0 %collective-permute-start.16 = (bf16[64,8,256]{2,1,0:T(8,128)(2,1)S(1)}, bf16[64,8,256]{2,1,0:T(8,128)(2,1)S(1)}, u32[]{:S(2)}, u32[]{:S(2)}) collective-permute-start(bf16[64,8,256]{2,1,0:T(8,128)(2,1)S(1)} %get-tuple-element.160), channel_id=1, source_target_pairs={{0,16},{4,20},{8,24},{12,28},{16,0},{20,4},{24,8},{28,12},{1,17},{... | collective-permute-start | bytes 786440 | tf_op jit(solution)/shard_map/ppermute | solution.py:43
  40.8 10.7 %collective-permute-start.14 = (bf16[64,8,256]{2,1,0:T(8,128)(2,1)S(1)}, bf16[64,8,256]{2,1,0:T(8,128)(2,1)S(1)}, u32[]{:S(2)}, u32[]{:S(2)}) collective-permute-start(bf16[64,8,256]{2,1,0:T(8,128)(2,1)S(1)} %collective-permute-done.5.refs_0_), channel_id=1, source_target_pairs={{0,8},{4,12},{8,0},{12,4},{16,24},{20,28},{24,16},{28,20},{1,9},{5... | collective-permute-start | bytes 786440 | tf_op jit(solution)/shard_map/ppermute | solution.py:43
  56.4 15.4 %collective-permute-start.21 = (bf16[64,8,256]{2,1,0:T(8,128)(2,1)S(1)}, bf16[64,8,256]{2,1,0:T(8,128)(2,1)S(1)}, u32[]{:S(2)}, u32[]{:S(2)}) collective-permute-start(bf16[64,8,256]{2,1,0:T(8,128)(2,1)S(1)} %get-tuple-element.178), channel_id=1, source_target_pairs={{0,16},{4,20},{8,24},{12,28},{16,0},{20,4},{24,8},{28,12},{1,17},{... | collective-permute-start | bytes 786440 | tf_op jit(solution)/shard_map/ppermute | solution.py:43
  58.4 17.0 %collective-permute-start.20 = (bf16[64,8,256]{2,1,0:T(8,128)(2,1)S(1)}, bf16[64,8,256]{2,1,0:T(8,128)(2,1)S(1)}, u32[]{:S(2)}, u32[]{:S(2)}) collective-permute-start(bf16[64,8,256]{2,1,0:T(8,128)(2,1)S(1)} %shard_map.67.refs_0_), channel_id=1, source_target_pairs={{0,8},{4,12},{8,0},{12,4},{16,24},{20,28},{24,16},{28,20},{1,9},{5... | collective-permute-start | bytes 786440 | tf_op jit(solution)/shard_map/ppermute | solution.py:43
  61.1 16.3 %collective-permute-start.19 = (bf16[64,8,256]{2,1,0:T(8,128)(2,1)S(1)}, bf16[64,8,256]{2,1,0:T(8,128)(2,1)S(1)}, u32[]{:S(2)}, u32[]{:S(2)}) collective-permute-start(bf16[64,8,256]{2,1,0:T(8,128)(2,1)S(1)} %get-tuple-element.188), channel_id=1, source_target_pairs={{0,16},{4,20},{8,24},{12,28},{16,0},{20,4},{24,8},{28,12},{1,17},{... | collective-permute-start | bytes 786440 | tf_op jit(solution)/shard_map/ppermute | solution.py:43
  63.6 15.0 %collective-permute-start.25 = (bf16[64,8,256]{2,1,0:T(8,128)(2,1)S(1)}, bf16[64,8,256]{2,1,0:T(8,128)(2,1)S(1)}, u32[]{:S(2)}, u32[]{:S(2)}) collective-permute-start(bf16[64,8,256]{2,1,0:T(8,128)(2,1)S(1)} %shard_map.68.refs_0_), channel_id=1, source_target_pairs={{0,8},{4,12},{8,0},{12,4},{16,24},{20,28},{24,16},{28,20},{1,9},{5... | collective-permute-start | bytes 786440 | tf_op jit(solution)/shard_map/ppermute | solution.py:43
  64.1 14.6 %collective-permute-start.26 = (bf16[64,8,256]{2,1,0:T(8,128)(2,1)S(1)}, bf16[64,8,256]{2,1,0:T(8,128)(2,1)S(1)}, u32[]{:S(2)}, u32[]{:S(2)}) collective-permute-start(bf16[64,8,256]{2,1,0:T(8,128)(2,1)S(1)} %shard_map.68.refs_0_), channel_id=1, source_target_pairs={{0,4},{4,0},{8,12},{12,8},{16,20},{20,16},{24,28},{28,24},{1,5},{5... | collective-permute-start | bytes 786440 | tf_op jit(solution)/shard_map/ppermute | solution.py:43
  84.9 14.3 %collective-permute-start.34 = (bf16[64,8,256]{2,1,0:T(8,128)(2,1)S(1)}, bf16[64,8,256]{2,1,0:T(8,128)(2,1)S(1)}, u32[]{:S(2)}, u32[]{:S(2)}) collective-permute-start(bf16[64,8,256]{2,1,0:T(8,128)(2,1)S(1)} %get-tuple-element.203), channel_id=1, source_target_pairs={{0,16},{4,20},{8,24},{12,28},{16,0},{20,4},{24,8},{28,12},{1,17},{... | collective-permute-start | bytes 786440 | tf_op jit(solution)/shard_map/ppermute | solution.py:43
  85.7 14.7 %collective-permute-start.33 = (bf16[64,8,256]{2,1,0:T(8,128)(2,1)S(1)}, bf16[64,8,256]{2,1,0:T(8,128)(2,1)S(1)}, u32[]{:S(2)}, u32[]{:S(2)}) collective-permute-start(bf16[64,8,256]{2,1,0:T(8,128)(2,1)S(1)} %shard_map.74.refs_0_), channel_id=1, source_target_pairs={{0,8},{4,12},{8,0},{12,4},{16,24},{20,28},{24,16},{28,20},{1,9},{5... | collective-permute-start | bytes 786440 | tf_op jit(solution)/shard_map/ppermute | solution.py:43
  90.3 18.3 %collective-permute-start.32 = (bf16[64,8,256]{2,1,0:T(8,128)(2,1)S(1)}, bf16[64,8,256]{2,1,0:T(8,128)(2,1)S(1)}, u32[]{:S(2)}, u32[]{:S(2)}) collective-permute-start(bf16[64,8,256]{2,1,0:T(8,128)(2,1)S(1)} %get-tuple-element.217), channel_id=1, source_target_pairs={{0,16},{4,20},{8,24},{12,28},{16,0},{20,4},{24,8},{28,12},{1,17},{... | collective-permute-start | bytes 786440 | tf_op jit(solution)/shard_map/ppermute | solution.py:43
  91.6 18.2 %collective-permute-start.38 = (bf16[64,8,256]{2,1,0:T(8,128)(2,1)S(1)}, bf16[64,8,256]{2,1,0:T(8,128)(2,1)S(1)}, u32[]{:S(2)}, u32[]{:S(2)}) collective-permute-start(bf16[64,8,256]{2,1,0:T(8,128)(2,1)S(1)} %shard_map.76.refs_0_), channel_id=1, source_target_pairs={{0,8},{4,12},{8,0},{12,4},{16,24},{20,28},{24,16},{28,20},{1,9},{5... | collective-permute-start | bytes 786440 | tf_op jit(solution)/shard_map/ppermute | solution.py:43
  93.6 16.6 %collective-permute-start.36 = (bf16[64,8,256]{2,1,0:T(8,128)(2,1)S(1)}, bf16[64,8,256]{2,1,0:T(8,128)(2,1)S(1)}, u32[]{:S(2)}, u32[]{:S(2)}) collective-permute-start(bf16[64,8,256]{2,1,0:T(8,128)(2,1)S(1)} %shard_map.74.refs_0_), channel_id=1, source_target_pairs={{0,4},{4,0},{8,12},{12,8},{16,20},{20,16},{24,28},{28,24},{1,5},{5... | collective-permute-start | bytes 786440 | tf_op jit(solution)/shard_map/ppermute | solution.py:43
  103.1 12.6 %collective-permute-start.39 = (bf16[64,8,256]{2,1,0:T(8,128)(2,1)S(1)}, bf16[64,8,256]{2,1,0:T(8,128)(2,1)S(1)}, u32[]{:S(2)}, u32[]{:S(2)}) collective-permute-start(bf16[64,8,256]{2,1,0:T(8,128)(2,1)S(1)} %shard_map.76.refs_0_), channel_id=1, source_target_pairs={{0,4},{4,0},{8,12},{12,8},{16,20},{20,16},{24,28},{28,24},{1,5},{5... | collective-permute-start | bytes 786440 | tf_op jit(solution)/shard_map/ppermute | solution.py:43
  111.4 19.4 %collective-permute-start.44 = (bf16[64,8,256]{2,1,0:T(8,128)(2,1)S(1)}, bf16[64,8,256]{2,1,0:T(8,128)(2,1)S(1)}, u32[]{:S(2)}, u32[]{:S(2)}) collective-permute-start(bf16[64,8,256]{2,1,0:T(8,128)(2,1)S(1)} %get-tuple-element.233), channel_id=1, source_target_pairs={{0,16},{4,20},{8,24},{12,28},{16,0},{20,4},{24,8},{28,12},{1,17},{... | collective-permute-start | bytes 786440 | tf_op jit(solution)/shard_map/ppermute | solution.py:43
  120.8 15.6 %collective-permute-start.41 = (bf16[64,8,256]{2,1,0:T(8,128)(2,1)S(1)}, bf16[64,8,256]{2,1,0:T(8,128)(2,1)S(1)}, u32[]{:S(2)}, u32[]{:S(2)}) collective-permute-start(bf16[64,8,256]{2,1,0:T(8,128)(2,1)S(1)} %get-tuple-element.239), channel_id=1, source_target_pairs={{0,16},{4,20},{8,24},{12,28},{16,0},{20,4},{24,8},{28,12},{1,17},{... | collective-permute-start | bytes 786440 | tf_op jit(solution)/shard_map/ppermute | solution.py:43
  121.0 11.1 %collective-permute-start.42 = (bf16[8,8192]{1,0:T(8,128)(2,1)S(1)}, bf16[8,8192]{1,0:T(8,128)(2,1)S(1)}, u32[]{:S(2)}, u32[]{:S(2)}) collective-permute-start(bf16[8,8192]{1,0:T(8,128)(2,1)S(1)} %shard_map.80.refs_0_), channel_id=1, source_target_pairs={{0,1},{1,0},{2,3},{3,2},{4,5},{5,4},{6,7},{7,6},{8,9},{9,8},{10,11... | collective-permute-start | bytes 393224 | tf_op jit(solution)/shard_map/ppermute | solution.py:43
  (28 other events, 208.2 us)

commit v17 on v14

--- a/solution.py
+++ b/solution.py
@@ -11,7 +11,7 @@
 GROUPS = 2
 PARTS = CORES
 TILE_BLOCKS = 8
-UNROLL = 32
+UNROLL = 64
 VMEM_LIMIT = 8 * 1024 * 1024
 SIDE, NEXT = 1, 2
 

time: 147 us -> 145 us (0.986)
  Pallas kernels: 37.9 us -> 34.9 us
  transfers between devices with their start and end apart: 48 -> 48, of which waited for: 19 -> 19; matrix products, arithmetic and copies ran while one was open for 0% -> 0% of each run, Pallas kernels for 24% -> 23%
where the time goes in v17:
time: 145 us
  waiting for transfers between devices  56.2 us (39%)
  starting transfers between devices  52.3 us (36%)
  Pallas kernels  34.9 us (24%)
    ppermute x48, waiting for transfers between devices, swap(): return lax.ppermute(value, axis, [(i, i ^ mask) for i in range(size)])  56.2 us
    ppermute x48, starting transfers between devices, swap(): return lax.ppermute(value, axis, [(i, i ^ mask) for i in range(size)])  52.3 us
    pallas_call x8, Pallas kernels, expand(): pl.pallas_call(expand_kernel, in_specs=[VMEM] * (len(values) + 1), out_sp...  9.51 us
    pallas_call x8, Pallas kernels, combine_far(): pl.pallas_call(table_kernel, in_specs=[SMEM] + [VMEM] * len(shards), out_...  8.95 us
    pallas_call x4, Pallas kernels, combine(): pl.pallas_call(lookup_kernel, in_specs=[SMEM] + [VMEM] * len(tables), out...  4.62 us
    pallas_call x4, Pallas kernels, fill(): pl.pallas_call(functools.partial(fill_kernel, c, bool(before)), in_specs=...  3.62 us
    pallas_call x1, Pallas kernels, first_sums(): pl.pallas_call(first_sums_kernel, in_specs=[SMEM] + [HBM] * 3, out_specs=...  3.19 us
  transfers between devices with their start and end apart: 48, of which 19 were waited for; matrix products, arithmetic and copies ran while one was open for 0% of the time, Pallas kernels for 23%

profile of v17, /device:TPU:0, one launch (start us, length us, event | category | flops | bytes accessed | tf_op | source)
XLA Modules:
  0.0 144.9 jit_solution(7331704683338117652)
XLA Ops:
  1.1 3.2 %shard_map.59 = (bf16[64,8,256]{2,1,0:T(8,128)(2,1)S(1)}, bf16[64,8,256]{2,1,0:T(8,128)(2,1)S(1)}, bf16[64,8,256]{2,1,0:T(8,128)(2,1)S(1)}, bf16[64,8,256]{2,1,0:T(8,128)(2,1)S(1)}) custom-call(s32[1]{0:T(128)} %bitcast.core_ref, f32[32,8192]{1,0:T(8,128)} %vec_ref.17, f32[1,8192]{1,0:T(1,128)} %bitcast.2, bf16[8192,256]{1,0:T(8,128)(2,1)} %refs_2_.7), custom_call_target="tpu_custom_call" | custom-call | tf_op jit(solution)/shard_map/pallas_call | solution.py:228
  4.9 2.6 %collective-permute-start.1 = (bf16[64,8,256]{2,1,0:T(8,128)(2,1)S(1)}, bf16[64,8,256]{2,1,0:T(8,128)(2,1)S(1)}, u32[]{:S(2)}, u32[]{:S(2)}) collective-permute-start(bf16[64,8,256]{2,1,0:T(8,128)(2,1)S(1)} %get-tuple-element.137.refs_0_), channel_id=1, source_target_pairs={{0,8},{4,12},{8,0},{12,4},{16,24},{20,28},{24,16},{28,20},{1,9},{5... | collective-permute-start | bytes 786440 | tf_op jit(solution)/shard_map/ppermute | solution.py:43
  9.1 2.2 %collective-permute-start.8 = (bf16[64,8,256]{2,1,0:T(8,128)(2,1)S(1)}, bf16[64,8,256]{2,1,0:T(8,128)(2,1)S(1)}, u32[]{:S(2)}, u32[]{:S(2)}) collective-permute-start(bf16[64,8,256]{2,1,0:T(8,128)(2,1)S(1)} %collective-permute-done.3.refs_0_), channel_id=1, source_target_pairs={{0,8},{4,12},{8,0},{12,4},{16,24},{20,28},{24,16},{28,20},{1,9},{5... | collective-permute-start | bytes 786440 | tf_op jit(solution)/shard_map/ppermute | solution.py:43
  11.3 3.5 %collective-permute-done.1.refs_1_ = bf16[64,8,256]{2,1,0:T(8,128)(2,1)S(1)} collective-permute-done((bf16[64,8,256]{2,1,0:T(8,128)(2,1)S(1)}, bf16[64,8,256]{2,1,0:T(8,128)(2,1)S(1)}, u32[]{:S(2)}, u32[]{:S(2)}) %collective-permute-start.1) | collective-permute-done | bytes 262176 | tf_op jit(solution)/shard_map/ppermute | solution.py:43
  14.7 1.9 %collective-permute-start.7 = (bf16[64,8,256]{2,1,0:T(8,128)(2,1)S(1)}, bf16[64,8,256]{2,1,0:T(8,128)(2,1)S(1)}, u32[]{:S(2)}, u32[]{:S(2)}) collective-permute-start(bf16[64,8,256]{2,1,0:T(8,128)(2,1)S(1)} %collective-permute-done.1.refs_1_), channel_id=1, source_target_pairs={{0,4},{4,0},{8,12},{12,8},{16,20},{20,16},{24,28},{28,24},{1,5},{5... | collective-permute-start | bytes 786440 | tf_op jit(solution)/shard_map/ppermute | solution.py:43
  16.6 2.6 %collective-permute-start = (s32[64,8]{0,1:T(8,128)S(1)}, s32[64,8]{0,1:T(8,128)S(1)}, u32[]{:S(2)}, u32[]{:S(2)}) collective-permute-start(s32[64,8]{0,1:T(8,128)S(1)} %copy-done.3), channel_id=1, source_target_pairs={{0,16},{4,20},{8,24},{12,28},{16,0},{20,4},{24,8},{28,12},{1,17},{... | collective-permute-start | bytes 6152 | tf_op jit(solution)/shard_map/ppermute | solution.py:43
  19.2 1.9 %collective-permute-done = s32[64,8]{0,1:T(8,128)S(1)} collective-permute-done((s32[64,8]{0,1:T(8,128)S(1)}, s32[64,8]{0,1:T(8,128)S(1)}, u32[]{:S(2)}, u32[]{:S(2)}) %collective-permute-start) | collective-permute-done | bytes 2080 | tf_op jit(solution)/shard_map/ppermute | solution.py:43
  24.7 2.7 %collective-permute-start.12 = (bf16[64,8,256]{2,1,0:T(8,128)(2,1)S(1)}, bf16[64,8,256]{2,1,0:T(8,128)(2,1)S(1)}, u32[]{:S(2)}, u32[]{:S(2)}) collective-permute-start(bf16[64,8,256]{2,1,0:T(8,128)(2,1)S(1)} %get-tuple-element.142), channel_id=1, source_target_pairs={{0,16},{4,20},{8,24},{12,28},{16,0},{20,4},{24,8},{28,12},{1,17},{... | collective-permute-start | bytes 786440 | tf_op jit(solution)/shard_map/ppermute | solution.py:43
  28.9 2.2 %collective-permute-start.5 = (bf16[64,8,256]{2,1,0:T(8,128)(2,1)S(1)}, bf16[64,8,256]{2,1,0:T(8,128)(2,1)S(1)}, u32[]{:S(2)}, u32[]{:S(2)}) collective-permute-start(bf16[64,8,256]{2,1,0:T(8,128)(2,1)S(1)} %get-tuple-element.162.refs_0_), channel_id=1, source_target_pairs={{0,4},{4,0},{8,12},{12,8},{16,20},{20,16},{24,28},{28,24},{1,5},{5... | collective-permute-start | bytes 786440 | tf_op jit(solution)/shard_map/ppermute | solution.py:43
  31.2 2.3 %shard_map.61.refs_3_.emb_ref = bf16[8192,256]{1,0:T(8,128)(2,1)S(1)} custom-call(bf16[8192,256]{1,0:T(8,128)(2,1)} %collective-permute-done.11.src_ref), custom_call_target="tpu_custom_call" | custom-call | tf_op jit(solution)/shard_map/pallas_call | solution.py:243
  33.6 2.4 %collective-permute-done.10.refs_3_ = bf16[64,8,256]{2,1,0:T(8,128)(2,1)S(1)} collective-permute-done((bf16[64,8,256]{2,1,0:T(8,128)(2,1)S(1)}, bf16[64,8,256]{2,1,0:T(8,128)(2,1)S(1)}, u32[]{:S(2)}, u32[]{:S(2)}) %collective-permute-start.10) | collective-permute-done | bytes 262176 | tf_op jit(solution)/shard_map/ppermute | solution.py:43
  37.1 2.7 %collective-permute-start.14 = (bf16[64,8,256]{2,1,0:T(8,128)(2,1)S(1)}, bf16[64,8,256]{2,1,0:T(8,128)(2,1)S(1)}, u32[]{:S(2)}, u32[]{:S(2)}) collective-permute-start(bf16[64,8,256]{2,1,0:T(8,128)(2,1)S(1)} %get-tuple-element.149), channel_id=1, source_target_pairs={{0,16},{4,20},{8,24},{12,28},{16,0},{20,4},{24,8},{28,12},{1,17},{... | collective-permute-start | bytes 786440 | tf_op jit(solution)/shard_map/ppermute | solution.py:43
  45.8 2.9 %collective-permute-done.14.refs_1_ = bf16[64,8,256]{2,1,0:T(8,128)(2,1)S(1)} collective-permute-done((bf16[64,8,256]{2,1,0:T(8,128)(2,1)S(1)}, bf16[64,8,256]{2,1,0:T(8,128)(2,1)S(1)}, u32[]{:S(2)}, u32[]{:S(2)}) %collective-permute-start.14) | collective-permute-done | bytes 262176 | tf_op jit(solution)/shard_map/ppermute | solution.py:43
  60.7 2.0 %collective-permute-start.19 = (bf16[64,8,256]{2,1,0:T(8,128)(2,1)S(1)}, bf16[64,8,256]{2,1,0:T(8,128)(2,1)S(1)}, u32[]{:S(2)}, u32[]{:S(2)}) collective-permute-start(bf16[64,8,256]{2,1,0:T(8,128)(2,1)S(1)} %get-tuple-element.178), channel_id=1, source_target_pairs={{0,16},{4,20},{8,24},{12,28},{16,0},{20,4},{24,8},{28,12},{1,17},{... | collective-permute-start | bytes 786440 | tf_op jit(solution)/shard_map/ppermute | solution.py:43
  64.3 5.9 %collective-permute-done.21.refs_1_ = bf16[64,8,256]{2,1,0:T(8,128)(2,1)S(1)} collective-permute-done((bf16[64,8,256]{2,1,0:T(8,128)(2,1)S(1)}, bf16[64,8,256]{2,1,0:T(8,128)(2,1)S(1)}, u32[]{:S(2)}, u32[]{:S(2)}) %collective-permute-start.21) | collective-permute-done | bytes 262176 | tf_op jit(solution)/shard_map/ppermute | solution.py:43
  74.6 2.4 %collective-permute-done.19.refs_1_ = bf16[64,8,256]{2,1,0:T(8,128)(2,1)S(1)} collective-permute-done((bf16[64,8,256]{2,1,0:T(8,128)(2,1)S(1)}, bf16[64,8,256]{2,1,0:T(8,128)(2,1)S(1)}, u32[]{:S(2)}, u32[]{:S(2)}) %collective-permute-start.19) | collective-permute-done | bytes 262176 | tf_op jit(solution)/shard_map/ppermute | solution.py:43
  84.5 2.3 %collective-permute-start.33 = (bf16[64,8,256]{2,1,0:T(8,128)(2,1)S(1)}, bf16[64,8,256]{2,1,0:T(8,128)(2,1)S(1)}, u32[]{:S(2)}, u32[]{:S(2)}) collective-permute-start(bf16[64,8,256]{2,1,0:T(8,128)(2,1)S(1)} %shard_map.74.refs_0_), channel_id=1, source_target_pairs={{0,8},{4,12},{8,0},{12,4},{16,24},{20,28},{24,16},{28,20},{1,9},{5... | collective-permute-start | bytes 786440 | tf_op jit(solution)/shard_map/ppermute | solution.py:43
  89.7 2.8 %collective-permute-start.32 = (bf16[64,8,256]{2,1,0:T(8,128)(2,1)S(1)}, bf16[64,8,256]{2,1,0:T(8,128)(2,1)S(1)}, u32[]{:S(2)}, u32[]{:S(2)}) collective-permute-start(bf16[64,8,256]{2,1,0:T(8,128)(2,1)S(1)} %get-tuple-element.207), channel_id=1, source_target_pairs={{0,16},{4,20},{8,24},{12,28},{16,0},{20,4},{24,8},{28,12},{1,17},{... | collective-permute-start | bytes 786440 | tf_op jit(solution)/shard_map/ppermute | solution.py:43
  95.0 5.8 %collective-permute-done.34.refs_1_ = bf16[64,8,256]{2,1,0:T(8,128)(2,1)S(1)} collective-permute-done((bf16[64,8,256]{2,1,0:T(8,128)(2,1)S(1)}, bf16[64,8,256]{2,1,0:T(8,128)(2,1)S(1)}, u32[]{:S(2)}, u32[]{:S(2)}) %collective-permute-start.34) | collective-permute-done | bytes 262176 | tf_op jit(solution)/shard_map/ppermute | solution.py:43
  104.0 4.2 %collective-permute-done.32.refs_1_ = bf16[64,8,256]{2,1,0:T(8,128)(2,1)S(1)} collective-permute-done((bf16[64,8,256]{2,1,0:T(8,128)(2,1)S(1)}, bf16[64,8,256]{2,1,0:T(8,128)(2,1)S(1)}, u32[]{:S(2)}, u32[]{:S(2)}) %collective-permute-start.32) | collective-permute-done | bytes 262176 | tf_op jit(solution)/shard_map/ppermute | solution.py:43
  113.8 4.3 %collective-permute-done.40.refs_3_ = bf16[64,8,256]{2,1,0:T(8,128)(2,1)S(1)} collective-permute-done((bf16[64,8,256]{2,1,0:T(8,128)(2,1)S(1)}, bf16[64,8,256]{2,1,0:T(8,128)(2,1)S(1)}, u32[]{:S(2)}, u32[]{:S(2)}) %collective-permute-start.40) | collective-permute-done | bytes 262176 | tf_op jit(solution)/shard_map/ppermute | solution.py:43
  121.9 10.2 %collective-permute-done.44.refs_1_ = bf16[64,8,256]{2,1,0:T(8,128)(2,1)S(1)} collective-permute-done((bf16[64,8,256]{2,1,0:T(8,128)(2,1)S(1)}, bf16[64,8,256]{2,1,0:T(8,128)(2,1)S(1)}, u32[]{:S(2)}, u32[]{:S(2)}) %collective-permute-start.44) | collective-permute-done | bytes 262176 | tf_op jit(solution)/shard_map/ppermute | solution.py:43
  134.3 1.9 %collective-permute-done.41.refs_1_ = bf16[64,8,256]{2,1,0:T(8,128)(2,1)S(1)} collective-permute-done((bf16[64,8,256]{2,1,0:T(8,128)(2,1)S(1)}, bf16[64,8,256]{2,1,0:T(8,128)(2,1)S(1)}, u32[]{:S(2)}, u32[]{:S(2)}) %collective-permute-start.41) | collective-permute-done | bytes 262176 | tf_op jit(solution)/shard_map/ppermute | solution.py:43
  137.6 4.8 %collective-permute-done.45.refs_1_ = bf16[8,8192]{1,0:T(8,128)(2,1)S(1)} collective-permute-done((bf16[8,8192]{1,0:T(8,128)(2,1)S(1)}, bf16[8,8192]{1,0:T(8,128)(2,1)S(1)}, u32[]{:S(2)}, u32[]{:S(2)}) %collective-permute-start.45) | collective-permute-done | bytes 131104 | tf_op jit(solution)/shard_map/ppermute | solution.py:43
  (115 shorter events, 64.1 us)
Async XLA Ops:
  0.6 28.3 %collective-permute-start.11 = (bf16[8192,256]{1,0:T(8,128)(2,1)}, bf16[8192,256]{1,0:T(8,128)(2,1)}, u32[]{:S(2)}, u32[]{:S(2)}) collective-permute-start(bf16[8192,256]{1,0:T(8,128)(2,1)} %refs_2_.7), channel_id=1, source_target_pairs={{0,1},{1,0},{2,3},{3,2},{4,5},{5,4},{6,7},{7,6},{8,9},{9,8},{10,11... | collective-permute-start | bytes 12582920 | tf_op jit(solution)/shard_map/ppermute | solution.py:43
  7.6 16.0 %collective-permute-start.6 = (bf16[64,8,256]{2,1,0:T(8,128)(2,1)S(1)}, bf16[64,8,256]{2,1,0:T(8,128)(2,1)S(1)}, u32[]{:S(2)}, u32[]{:S(2)}) collective-permute-start(bf16[64,8,256]{2,1,0:T(8,128)(2,1)S(1)} %get-tuple-element.137.refs_0_), channel_id=1, source_target_pairs={{0,4},{4,0},{8,12},{12,8},{16,20},{20,16},{24,28},{28,24},{1,5},{5... | collective-permute-start | bytes 786440 | tf_op jit(solution)/shard_map/ppermute | solution.py:43
  9.1 12.7 %collective-permute-start.8 = (bf16[64,8,256]{2,1,0:T(8,128)(2,1)S(1)}, bf16[64,8,256]{2,1,0:T(8,128)(2,1)S(1)}, u32[]{:S(2)}, u32[]{:S(2)}) collective-permute-start(bf16[64,8,256]{2,1,0:T(8,128)(2,1)S(1)} %collective-permute-done.3.refs_0_), channel_id=1, source_target_pairs={{0,8},{4,12},{8,0},{12,4},{16,24},{20,28},{24,16},{28,20},{1,9},{5... | collective-permute-start | bytes 786440 | tf_op jit(solution)/shard_map/ppermute | solution.py:43
  21.1 12.4 %collective-permute-start.9 = (bf16[64,8,256]{2,1,0:T(8,128)(2,1)S(1)}, bf16[64,8,256]{2,1,0:T(8,128)(2,1)S(1)}, u32[]{:S(2)}, u32[]{:S(2)}) collective-permute-start(bf16[64,8,256]{2,1,0:T(8,128)(2,1)S(1)} %collective-permute-done.3.refs_0_), channel_id=1, source_target_pairs={{0,4},{4,0},{8,12},{12,8},{16,20},{20,16},{24,28},{28,24},{1,5},{5... | collective-permute-start | bytes 786440 | tf_op jit(solution)/shard_map/ppermute | solution.py:43
  21.8 14.2 %collective-permute-start.10 = (bf16[64,8,256]{2,1,0:T(8,128)(2,1)S(1)}, bf16[64,8,256]{2,1,0:T(8,128)(2,1)S(1)}, u32[]{:S(2)}, u32[]{:S(2)}) collective-permute-start(bf16[64,8,256]{2,1,0:T(8,128)(2,1)S(1)} %collective-permute-done.8.refs_1_), channel_id=1, source_target_pairs={{0,4},{4,0},{8,12},{12,8},{16,20},{20,16},{24,28},{28,24},{1,5},{5... | collective-permute-start | bytes 786440 | tf_op jit(solution)/shard_map/ppermute | solution.py:43
  24.7 16.6 %collective-permute-start.12 = (bf16[64,8,256]{2,1,0:T(8,128)(2,1)S(1)}, bf16[64,8,256]{2,1,0:T(8,128)(2,1)S(1)}, u32[]{:S(2)}, u32[]{:S(2)}) collective-permute-start(bf16[64,8,256]{2,1,0:T(8,128)(2,1)S(1)} %get-tuple-element.142), channel_id=1, source_target_pairs={{0,16},{4,20},{8,24},{12,28},{16,0},{20,4},{24,8},{28,12},{1,17},{... | collective-permute-start | bytes 786440 | tf_op jit(solution)/shard_map/ppermute | solution.py:43
  27.4 17.4 %collective-permute-start.4 = (bf16[64,8,256]{2,1,0:T(8,128)(2,1)S(1)}, bf16[64,8,256]{2,1,0:T(8,128)(2,1)S(1)}, u32[]{:S(2)}, u32[]{:S(2)}) collective-permute-start(bf16[64,8,256]{2,1,0:T(8,128)(2,1)S(1)} %get-tuple-element.162.refs_0_), channel_id=1, source_target_pairs={{0,8},{4,12},{8,0},{12,4},{16,24},{20,28},{24,16},{28,20},{1,9},{5... | collective-permute-start | bytes 786440 | tf_op jit(solution)/shard_map/ppermute | solution.py:43
  28.9 15.8 %collective-permute-start.5 = (bf16[64,8,256]{2,1,0:T(8,128)(2,1)S(1)}, bf16[64,8,256]{2,1,0:T(8,128)(2,1)S(1)}, u32[]{:S(2)}, u32[]{:S(2)}) collective-permute-start(bf16[64,8,256]{2,1,0:T(8,128)(2,1)S(1)} %get-tuple-element.162.refs_0_), channel_id=1, source_target_pairs={{0,4},{4,0},{8,12},{12,8},{16,20},{20,16},{24,28},{28,24},{1,5},{5... | collective-permute-start | bytes 786440 | tf_op jit(solution)/shard_map/ppermute | solution.py:43
  37.1 11.6 %collective-permute-start.14 = (bf16[64,8,256]{2,1,0:T(8,128)(2,1)S(1)}, bf16[64,8,256]{2,1,0:T(8,128)(2,1)S(1)}, u32[]{:S(2)}, u32[]{:S(2)}) collective-permute-start(bf16[64,8,256]{2,1,0:T(8,128)(2,1)S(1)} %get-tuple-element.149), channel_id=1, source_target_pairs={{0,16},{4,20},{8,24},{12,28},{16,0},{20,4},{24,8},{28,12},{1,17},{... | collective-permute-start | bytes 786440 | tf_op jit(solution)/shard_map/ppermute | solution.py:43
  55.4 14.7 %collective-permute-start.21 = (bf16[64,8,256]{2,1,0:T(8,128)(2,1)S(1)}, bf16[64,8,256]{2,1,0:T(8,128)(2,1)S(1)}, u32[]{:S(2)}, u32[]{:S(2)}) collective-permute-start(bf16[64,8,256]{2,1,0:T(8,128)(2,1)S(1)} %get-tuple-element.168), channel_id=1, source_target_pairs={{0,16},{4,20},{8,24},{12,28},{16,0},{20,4},{24,8},{28,12},{1,17},{... | collective-permute-start | bytes 786440 | tf_op jit(solution)/shard_map/ppermute | solution.py:43
  57.6 15.5 %collective-permute-start.20 = (bf16[64,8,256]{2,1,0:T(8,128)(2,1)S(1)}, bf16[64,8,256]{2,1,0:T(8,128)(2,1)S(1)}, u32[]{:S(2)}, u32[]{:S(2)}) collective-permute-start(bf16[64,8,256]{2,1,0:T(8,128)(2,1)S(1)} %shard_map.67.refs_0_), channel_id=1, source_target_pairs={{0,8},{4,12},{8,0},{12,4},{16,24},{20,28},{24,16},{28,20},{1,9},{5... | collective-permute-start | bytes 786440 | tf_op jit(solution)/shard_map/ppermute | solution.py:43
  60.7 16.3 %collective-permute-start.19 = (bf16[64,8,256]{2,1,0:T(8,128)(2,1)S(1)}, bf16[64,8,256]{2,1,0:T(8,128)(2,1)S(1)}, u32[]{:S(2)}, u32[]{:S(2)}) collective-permute-start(bf16[64,8,256]{2,1,0:T(8,128)(2,1)S(1)} %get-tuple-element.178), channel_id=1, source_target_pairs={{0,16},{4,20},{8,24},{12,28},{16,0},{20,4},{24,8},{28,12},{1,17},{... | collective-permute-start | bytes 786440 | tf_op jit(solution)/shard_map/ppermute | solution.py:43
  62.7 15.4 %collective-permute-start.25 = (bf16[64,8,256]{2,1,0:T(8,128)(2,1)S(1)}, bf16[64,8,256]{2,1,0:T(8,128)(2,1)S(1)}, u32[]{:S(2)}, u32[]{:S(2)}) collective-permute-start(bf16[64,8,256]{2,1,0:T(8,128)(2,1)S(1)} %shard_map.68.refs_0_), channel_id=1, source_target_pairs={{0,8},{4,12},{8,0},{12,4},{16,24},{20,28},{24,16},{28,20},{1,9},{5... | collective-permute-start | bytes 786440 | tf_op jit(solution)/shard_map/ppermute | solution.py:43
  63.8 14.4 %collective-permute-start.26 = (bf16[64,8,256]{2,1,0:T(8,128)(2,1)S(1)}, bf16[64,8,256]{2,1,0:T(8,128)(2,1)S(1)}, u32[]{:S(2)}, u32[]{:S(2)}) collective-permute-start(bf16[64,8,256]{2,1,0:T(8,128)(2,1)S(1)} %shard_map.68.refs_0_), channel_id=1, source_target_pairs={{0,4},{4,0},{8,12},{12,8},{16,20},{20,16},{24,28},{28,24},{1,5},{5... | collective-permute-start | bytes 786440 | tf_op jit(solution)/shard_map/ppermute | solution.py:43
  83.4 17.4 %collective-permute-start.34 = (bf16[64,8,256]{2,1,0:T(8,128)(2,1)S(1)}, bf16[64,8,256]{2,1,0:T(8,128)(2,1)S(1)}, u32[]{:S(2)}, u32[]{:S(2)}) collective-permute-start(bf16[64,8,256]{2,1,0:T(8,128)(2,1)S(1)} %get-tuple-element.193), channel_id=1, source_target_pairs={{0,16},{4,20},{8,24},{12,28},{16,0},{20,4},{24,8},{28,12},{1,17},{... | collective-permute-start | bytes 786440 | tf_op jit(solution)/shard_map/ppermute | solution.py:43
  84.5 17.4 %collective-permute-start.33 = (bf16[64,8,256]{2,1,0:T(8,128)(2,1)S(1)}, bf16[64,8,256]{2,1,0:T(8,128)(2,1)S(1)}, u32[]{:S(2)}, u32[]{:S(2)}) collective-permute-start(bf16[64,8,256]{2,1,0:T(8,128)(2,1)S(1)} %shard_map.74.refs_0_), channel_id=1, source_target_pairs={{0,8},{4,12},{8,0},{12,4},{16,24},{20,28},{24,16},{28,20},{1,9},{5... | collective-permute-start | bytes 786440 | tf_op jit(solution)/shard_map/ppermute | solution.py:43
  89.7 18.5 %collective-permute-start.32 = (bf16[64,8,256]{2,1,0:T(8,128)(2,1)S(1)}, bf16[64,8,256]{2,1,0:T(8,128)(2,1)S(1)}, u32[]{:S(2)}, u32[]{:S(2)}) collective-permute-start(bf16[64,8,256]{2,1,0:T(8,128)(2,1)S(1)} %get-tuple-element.207), channel_id=1, source_target_pairs={{0,16},{4,20},{8,24},{12,28},{16,0},{20,4},{24,8},{28,12},{1,17},{... | collective-permute-start | bytes 786440 | tf_op jit(solution)/shard_map/ppermute | solution.py:43
  92.5 16.9 %collective-permute-start.38 = (bf16[64,8,256]{2,1,0:T(8,128)(2,1)S(1)}, bf16[64,8,256]{2,1,0:T(8,128)(2,1)S(1)}, u32[]{:S(2)}, u32[]{:S(2)}) collective-permute-start(bf16[64,8,256]{2,1,0:T(8,128)(2,1)S(1)} %shard_map.76.refs_0_), channel_id=1, source_target_pairs={{0,8},{4,12},{8,0},{12,4},{16,24},{20,28},{24,16},{28,20},{1,9},{5... | collective-permute-start | bytes 786440 | tf_op jit(solution)/shard_map/ppermute | solution.py:43
  92.5 18.1 %collective-permute-start.36 = (bf16[64,8,256]{2,1,0:T(8,128)(2,1)S(1)}, bf16[64,8,256]{2,1,0:T(8,128)(2,1)S(1)}, u32[]{:S(2)}, u32[]{:S(2)}) collective-permute-start(bf16[64,8,256]{2,1,0:T(8,128)(2,1)S(1)} %shard_map.74.refs_0_), channel_id=1, source_target_pairs={{0,4},{4,0},{8,12},{12,8},{16,20},{20,16},{24,28},{28,24},{1,5},{5... | collective-permute-start | bytes 786440 | tf_op jit(solution)/shard_map/ppermute | solution.py:43
  103.5 10.3 %collective-permute-start.39 = (bf16[64,8,256]{2,1,0:T(8,128)(2,1)S(1)}, bf16[64,8,256]{2,1,0:T(8,128)(2,1)S(1)}, u32[]{:S(2)}, u32[]{:S(2)}) collective-permute-start(bf16[64,8,256]{2,1,0:T(8,128)(2,1)S(1)} %shard_map.76.refs_0_), channel_id=1, source_target_pairs={{0,4},{4,0},{8,12},{12,8},{16,20},{20,16},{24,28},{28,24},{1,5},{5... | collective-permute-start | bytes 786440 | tf_op jit(solution)/shard_map/ppermute | solution.py:43
  111.7 20.4 %collective-permute-start.44 = (bf16[64,8,256]{2,1,0:T(8,128)(2,1)S(1)}, bf16[64,8,256]{2,1,0:T(8,128)(2,1)S(1)}, u32[]{:S(2)}, u32[]{:S(2)}) collective-permute-start(bf16[64,8,256]{2,1,0:T(8,128)(2,1)S(1)} %get-tuple-element.223), channel_id=1, source_target_pairs={{0,16},{4,20},{8,24},{12,28},{16,0},{20,4},{24,8},{28,12},{1,17},{... | collective-permute-start | bytes 786440 | tf_op jit(solution)/shard_map/ppermute | solution.py:43
  119.1 17.1 %collective-permute-start.41 = (bf16[64,8,256]{2,1,0:T(8,128)(2,1)S(1)}, bf16[64,8,256]{2,1,0:T(8,128)(2,1)S(1)}, u32[]{:S(2)}, u32[]{:S(2)}) collective-permute-start(bf16[64,8,256]{2,1,0:T(8,128)(2,1)S(1)} %get-tuple-element.229), channel_id=1, source_target_pairs={{0,16},{4,20},{8,24},{12,28},{16,0},{20,4},{24,8},{28,12},{1,17},{... | collective-permute-start | bytes 786440 | tf_op jit(solution)/shard_map/ppermute | solution.py:43
  119.3 14.0 %collective-permute-start.42 = (bf16[8,8192]{1,0:T(8,128)(2,1)S(1)}, bf16[8,8192]{1,0:T(8,128)(2,1)S(1)}, u32[]{:S(2)}, u32[]{:S(2)}) collective-permute-start(bf16[8,8192]{1,0:T(8,128)(2,1)S(1)} %shard_map.80.refs_0_), channel_id=1, source_target_pairs={{0,1},{1,0},{2,3},{3,2},{4,5},{5,4},{6,7},{7,6},{8,9},{9,8},{10,11... | collective-permute-start | bytes 393224 | tf_op jit(solution)/shard_map/ppermute | solution.py:43
  119.8 13.5 %collective-permute-start.43 = (bf16[8,8192]{1,0:T(8,128)(2,1)S(1)}, bf16[8,8192]{1,0:T(8,128)(2,1)S(1)}, u32[]{:S(2)}, u32[]{:S(2)}) collective-permute-start(bf16[8,8192]{1,0:T(8,128)(2,1)S(1)} %collective-permute-done.35.refs_1_), channel_id=1, source_target_pairs={{0,1},{1,0},{2,3},{3,2},{4,5},{5,4},{6,7},{7,6},{8,9},{9,8},{10,11... | collective-permute-start | bytes 393224 | tf_op jit(solution)/shard_map/ppermute | solution.py:43
  (28 other events, 208.4 us)
